TPU v7x, 32 devices: a whole 2x2x4 slice. The times are simulated.
32 devices in a mesh: dp: 8 (over z, x), mp: 4 (over y, core).
Axes of the slice: x: 2, y: 2, z: 4, core: 2. Of those that a mesh axis runs over, the one named last changes fastest.
Arguments:
- tokens: bfloat16 [32768, 512], P(('dp', 'mp')), may hold values from -6 to 6
- gain_mix: bfloat16 [512], P(('dp', 'mp')), may hold values from 0.25 to 1.75
- gain_mlp: bfloat16 [512], P(('dp', 'mp')), may hold values from 0.25 to 1.75
- forget_weight: bfloat16 [512, 1024], P(('dp', 'mp')), may hold values from -0.25 to 0.25
- input_weight: bfloat16 [512, 1024], P(('dp', 'mp')), may hold values from -0.25 to 0.25
- candidate_weight: bfloat16 [512, 1024], P(('dp', 'mp')), may hold values from -0.25 to 0.25
- input_gate_bias: bfloat16 [1024], P(('dp', 'mp')), may hold values from -11 to -3
- output_weight: bfloat16 [1024, 512], P(('dp', 'mp')), may hold values from -1 to 1
- up_weight: bfloat16 [512, 2048], P('dp', 'mp'), may hold values from -0.25 to 0.25
- down_weight: bfloat16 [2048, 512], P('mp', 'dp'), may hold values from -0.1875 to 0.1875
- cotangent: bfloat16 [32768, 512], P(('dp', 'mp')), may hold values from -6 to 6
Outputs:
- block_out: bfloat16 [32768, 512], P(('dp', 'mp'))
- tokens_grad: float32 [32768, 512], P(('dp', 'mp'))
- gain_mix_grad: float32 [512], P(('dp', 'mp'))
- gain_mlp_grad: float32 [512], P(('dp', 'mp'))
- forget_grad: float32 [512, 1024], P(('dp', 'mp'))
- input_grad: float32 [512, 1024], P(('dp', 'mp'))
- cand_grad: float32 [512, 1024], P(('dp', 'mp'))
- bias_grad: float32 [1024], P(('dp', 'mp'))
- out_grad: float32 [1024, 512], P(('dp', 'mp'))
- up_grad: float32 [512, 2048], P('dp', 'mp')
- down_grad: float32 [2048, 512], P('mp', 'dp')
All inputs are finite; a program needn't handle non-finite values.
Results may differ from a plain program's by a relative error of at most 0.011.
Values may be sent and summed in bfloat16 or wider, within the bound.
No kernel may reach another device: no remote copies, remote signals or barrier semaphores. Data moves between devices by JAX's collectives and lax.ppermute only.
A program may use at most 192 MiB of HBM per device.

v0:
```python
import jax
import jax.numpy as jnp
from jax import lax
from jax.sharding import PartitionSpec as P

LEN = 1024


EPSILON = 1e-06


def cut_along(array, dim, peers):
    shape = array.shape
    blocks = array.reshape(*shape[:dim], peers, shape[dim] // peers, *shape[dim + 1 :])
    return jnp.moveaxis(blocks, dim, 0)


def sum_at_owner(array, axis, dim):
    blocks = cut_along(array, dim, lax.axis_size(axis))
    arrived = lax.all_to_all(blocks, axis, split_axis=0, concat_axis=0, tiled=True)
    return arrived.astype(jnp.float32).sum(axis=0)


def norm_rows(values, gain):
    scale = lax.rsqrt(jnp.mean(values * values, axis=-1, keepdims=True) + EPSILON)
    normed = values * scale
    return (scale, normed, (normed * gain.astype(jnp.float32)).astype(jnp.bfloat16))


def norm_back(grad_rows, scale, normed, gain):
    scaled = grad_rows * gain.astype(jnp.float32)
    back = scale * (scaled - normed * jnp.mean(scaled * normed, axis=-1, keepdims=True))
    return (back, jnp.sum(grad_rows * normed, axis=0))


def combine_steps(earlier, later):
    return (earlier[0] * later[0], later[0] * earlier[1] + later[1])


def gelu_tanh(values):
    return jax.nn.gelu(values, approximate=True)


def run_recurrence(decay, drive):
    seqs = decay.shape[0] // LEN
    width = decay.shape[1]
    result = lax.associative_scan(
        combine_steps, (decay.reshape(seqs, LEN, width), drive.reshape(seqs, LEN, width)), axis=1
    )
    return result[1].reshape(decay.shape)


def shift_rows(values, upward):
    seqs = values.shape[0] // LEN
    width = values.shape[1]
    framed = values.reshape(seqs, LEN, width)
    zeros = jnp.zeros((seqs, 1, width), values.dtype)
    if upward:
        moved = jnp.concatenate([framed[:, 1:], zeros], axis=1)
    else:
        moved = jnp.concatenate([zeros, framed[:, :-1]], axis=1)
    return moved.reshape(values.shape)


def down_rows(activation_rows, weight):
    return jnp.dot(activation_rows, weight, preferred_element_type=jnp.float32)


def back_rows(grad_pre, weight):
    return jnp.einsum("tf,df->td", grad_pre, weight, preferred_element_type=jnp.float32)


def forward_state(
    tokens,
    gain_mix,
    gain_mlp,
    forget_weight,
    input_weight,
    candidate_weight,
    input_gate_bias,
    output_weight,
    up_weight,
    down_weight,
):
    gathered = (
        lax.all_gather(gain_mix, ("dp", "mp"), axis=0, tiled=True),
        lax.all_gather(gain_mlp, ("dp", "mp"), axis=0, tiled=True),
        lax.all_gather(input_gate_bias, ("dp", "mp"), axis=0, tiled=True),
        lax.all_gather(forget_weight, ("dp", "mp"), axis=0, tiled=True),
        lax.all_gather(input_weight, ("dp", "mp"), axis=0, tiled=True),
        lax.all_gather(candidate_weight, ("dp", "mp"), axis=0, tiled=True),
        lax.all_gather(output_weight, ("dp", "mp"), axis=0, tiled=True),
    )
    up_local, down_local = (
        lax.all_gather(up_weight, "dp", axis=0, tiled=True),
        lax.all_gather(down_weight, "dp", axis=1, tiled=True),
    )
    up_use, down_use = (up_local, down_local)
    gmix_full, gmlp_full, bias_full, wf_full, wi_full, wc_full, wo_full = gathered
    rows = tokens.astype(jnp.float32)
    scale_one, normed_one, first_normed_input = norm_rows(rows, gmix_full)
    forget_gate = jnp.dot(first_normed_input, wf_full, preferred_element_type=jnp.float32)
    input_gate = jnp.dot(
        first_normed_input, wi_full, preferred_element_type=jnp.float32
    ) + bias_full.astype(jnp.float32)
    candidate_rows = jnp.dot(first_normed_input, wc_full, preferred_element_type=jnp.float32)
    forget = jax.nn.sigmoid(jax.nn.log_sigmoid(forget_gate) - jax.nn.log_sigmoid(input_gate))
    hidden_state = run_recurrence(forget, (1.0 - forget) * candidate_rows)
    state_low = hidden_state.astype(jnp.bfloat16)
    residual_rows = rows + jnp.dot(state_low, wo_full, preferred_element_type=jnp.float32)
    scale_two, normed_two, second_normed_input = norm_rows(residual_rows, gmlp_full)
    rows_all = lax.all_gather(second_normed_input, "mp", axis=0, tiled=True)
    preactivation = jnp.dot(rows_all, up_use, preferred_element_type=jnp.float32)
    activation_rows = gelu_tanh(preactivation).astype(jnp.bfloat16)
    return {
        "gmix": gmix_full,
        "gmlp": gmlp_full,
        "wf": wf_full,
        "wi": wi_full,
        "wc": wc_full,
        "wo": wo_full,
        "up_use": up_use,
        "down_use": down_use,
        "scale_one": scale_one,
        "normed_one": normed_one,
        "xn_first": first_normed_input,
        "gate_f": forget_gate,
        "gate_i": input_gate,
        "cand": candidate_rows,
        "forget": forget,
        "state": hidden_state,
        "state_low": state_low,
        "resid": residual_rows,
        "scale_two": scale_two,
        "normed_two": normed_two,
        "rows_all": rows_all,
        "pre": preactivation,
        "active": activation_rows,
    }


def local(
    tokens,
    gain_mix,
    gain_mlp,
    forget_weight,
    input_weight,
    candidate_weight,
    input_gate_bias,
    output_weight,
    up_weight,
    down_weight,
    cotangent,
):
    inputs = (
        tokens,
        gain_mix,
        gain_mlp,
        forget_weight,
        input_weight,
        candidate_weight,
        input_gate_bias,
        output_weight,
        up_weight,
        down_weight,
    )
    kept = forward_state(*inputs)
    branch = lax.psum_scatter(
        down_rows(kept["active"], kept["down_use"]).astype(jnp.bfloat16),
        "mp",
        scatter_dimension=0,
        tiled=True,
    ).astype(jnp.float32)
    block_out = (kept["resid"] + branch).astype(jnp.bfloat16)
    again = lax.optimization_barrier(inputs + (block_out,))
    kept = forward_state(*again[:-1])
    grad_out = cotangent.astype(jnp.float32)
    grad_rows = lax.all_gather(cotangent, "mp", axis=0, tiled=True)
    grad_act = jnp.einsum(
        "td,fd->tf", grad_rows, kept["down_use"], preferred_element_type=jnp.float32
    )
    unused, pull = jax.vjp(gelu_tanh, kept["pre"])
    grad_pre = pull(grad_act)[0].astype(jnp.bfloat16)
    up_term = jnp.einsum(
        "td,tf->df", kept["rows_all"], grad_pre, preferred_element_type=jnp.float32
    )
    down_term = jnp.einsum(
        "tf,td->fd", kept["active"], grad_rows, preferred_element_type=jnp.float32
    )
    grad_xn_two = lax.psum_scatter(
        back_rows(grad_pre, kept["up_use"]).astype(jnp.bfloat16),
        "mp",
        scatter_dimension=0,
        tiled=True,
    ).astype(jnp.float32)
    up_grad, down_grad = (
        sum_at_owner(up_term.astype(jnp.bfloat16), "dp", 0),
        sum_at_owner(down_term.astype(jnp.bfloat16), "dp", 1),
    )
    norm_two_back, gmlp_term = norm_back(
        grad_xn_two, kept["scale_two"], kept["normed_two"], kept["gmlp"]
    )
    grad_resid = grad_out + norm_two_back
    grad_mix = grad_resid.astype(jnp.bfloat16)
    wo_term = jnp.einsum(
        "th,td->hd", kept["state_low"], grad_mix, preferred_element_type=jnp.float32
    )
    grad_state = jnp.einsum("td,hd->th", grad_mix, kept["wo"], preferred_element_type=jnp.float32)
    forget = kept["forget"]
    decay_next = shift_rows(forget, True)
    carried = jnp.flip(run_recurrence(jnp.flip(decay_next, 0), jnp.flip(grad_state, 0)), 0)
    state_prev = shift_rows(kept["state"], False)
    grad_z = forget * (1.0 - forget) * carried * (state_prev - kept["cand"])
    grad_gf = (grad_z * jax.nn.sigmoid(-kept["gate_f"])).astype(jnp.bfloat16)
    grad_gi = (-grad_z * jax.nn.sigmoid(-kept["gate_i"])).astype(jnp.bfloat16)
    grad_cand = ((1.0 - forget) * carried).astype(jnp.bfloat16)
    wf_term = jnp.einsum("td,th->dh", kept["xn_first"], grad_gf, preferred_element_type=jnp.float32)
    wi_term = jnp.einsum("td,th->dh", kept["xn_first"], grad_gi, preferred_element_type=jnp.float32)
    wc_term = jnp.einsum(
        "td,th->dh", kept["xn_first"], grad_cand, preferred_element_type=jnp.float32
    )
    bias_term = jnp.sum(grad_gi.astype(jnp.float32), axis=0)
    grad_xn_one = jnp.einsum("th,dh->td", grad_gf, kept["wf"], preferred_element_type=jnp.float32)
    grad_xn_one = grad_xn_one + jnp.einsum(
        "th,dh->td", grad_gi, kept["wi"], preferred_element_type=jnp.float32
    )
    grad_xn_one = grad_xn_one + jnp.einsum(
        "th,dh->td", grad_cand, kept["wc"], preferred_element_type=jnp.float32
    )
    norm_one_back, gmix_term = norm_back(
        grad_xn_one, kept["scale_one"], kept["normed_one"], kept["gmix"]
    )
    tokens_grad = grad_resid + norm_one_back
    shards = (
        lax.psum_scatter(gmix_term, ("dp", "mp"), scatter_dimension=0, tiled=True),
        lax.psum_scatter(gmlp_term, ("dp", "mp"), scatter_dimension=0, tiled=True),
        lax.psum_scatter(bias_term, ("dp", "mp"), scatter_dimension=0, tiled=True),
        lax.psum_scatter(wf_term, ("dp", "mp"), scatter_dimension=0, tiled=True),
        lax.psum_scatter(wi_term, ("dp", "mp"), scatter_dimension=0, tiled=True),
        lax.psum_scatter(wc_term, ("dp", "mp"), scatter_dimension=0, tiled=True),
        lax.psum_scatter(wo_term, ("dp", "mp"), scatter_dimension=0, tiled=True),
    )
    return (
        block_out,
        tokens_grad,
        shards[0],
        shards[1],
        shards[3],
        shards[4],
        shards[5],
        shards[2],
        shards[6],
        up_grad,
        down_grad,
    )


def solution(mesh):
    in_specs = (
        P(("dp", "mp"), None),
        P(("dp", "mp")),
        P(("dp", "mp")),
        P(("dp", "mp"), None),
        P(("dp", "mp"), None),
        P(("dp", "mp"), None),
        P(("dp", "mp")),
        P(("dp", "mp"), None),
        P("dp", "mp"),
        P("mp", "dp"),
        P(("dp", "mp"), None),
    )
    out_specs = (
        P(("dp", "mp"), None),
        P(("dp", "mp"), None),
        P(("dp", "mp")),
        P(("dp", "mp")),
        P(("dp", "mp"), None),
        P(("dp", "mp"), None),
        P(("dp", "mp"), None),
        P(("dp", "mp")),
        P(("dp", "mp"), None),
        P("dp", "mp"),
        P("mp", "dp"),
    )
    return jax.shard_map(local, mesh=mesh, in_specs=in_specs, out_specs=out_specs, check_vma=False)
```

profile of v0, /device:TPU:0, one launch (start us, length us, event | category | flops | bytes accessed | tf_op | source)
XLA Modules:
  0.0 1704.6 jit_solution(10180123460001664796)
XLA Ops:
  12.6 42.1 %all-reduce.73 = (bf16[512]{0:T(512)(128)(2,1)S(1)}, bf16[1024]{0:T(1024)(128)(2,1)S(1)}, bf16[512]{0:T(512)(128)(2,1)S(1)}) all-reduce(bf16[512]{0:T(512)(128)(2,1)S(1)} %dynamic-update-slice, bf16[1024]{0:T(1024)(128)(2,1)S(1)} %dynamic-update-slice.1, bf16[512]{0:T(512)(128)(2,1)S(1)} %dynamic-update-slice.2), channel_id=1, replica_groups=mesh['dp'=8,'mp'=4] {'dp','mp'}, use_global_device_ids=true, to_apply=%add.62 | all-reduce | flops 2048 | bytes 8192
  56.4 11.1 all-gather.12.cloned.1.call-done
  72.1 51.0 %all-gather.14.cloned.1.call-done = bf16[512,1024]{1,0:T(8,128)(2,1)} async-done(((bf16[16,1024]{1,0:T(8,128)(2,1)}), bf16[512,1024]{1,0:T(8,128)(2,1)}) %all-gather.14.cloned.1.call-update) | async-done | bytes 1048592 | tf_op jit(solution)/shard_map/all_gather | solution.py:90
  123.1 10.1 fusion.27
  152.7 10.0 slice.700
  162.7 16.0 all-gather.16.cloned.1.call-done
  184.6 10.0 slice.773
  288.1 16.6 pad.203
  320.3 31.3 %all_gather.71 = bf16[512,512]{1,0:T(8,128)(2,1)S(1)} all-gather(bf16[64,512]{1,0:T(8,128)(2,1)S(1)} %copy-done.38), channel_id=1, replica_groups=mesh['dp'=8,'mp'=4] {'dp'}, dimensions={0}, use_global_device_ids=true | all-gather | bytes 589824 | tf_op jit(solution)/shard_map/all_gather | solution.py:95
  351.6 31.5 %all_gather.72 = bf16[512,512]{0,1:T(8,128)(2,1)S(1)} all-gather(bf16[512,64]{0,1:T(8,128)(2,1)S(1)} %copy-done.39), channel_id=1, replica_groups=mesh['dp'=8,'mp'=4] {'dp'}, dimensions={1}, use_global_device_ids=true | all-gather | bytes 589824 | tf_op jit(solution)/shard_map/all_gather | solution.py:96
  392.0 43.5 %reduce-scatter.7.cloned.1.call-done = bf16[1024,512]{0,1:T(8,128)(2,1)} async-done(((bf16[4096,512]{0,1:T(8,128)(2,1)}), bf16[1024,512]{0,1:T(8,128)(2,1)}) %reduce-scatter.7.cloned.1.call-update) | async-done | bytes 1048592 | tf_op jit(solution)/shard_map/reduce_scatter | solution.py:168
  438.1 12.3 all-gather.24.cloned.1.call-start
  452.0 39.5 %all-reduce.72 = (bf16[512]{0:T(512)(128)(2,1)S(1)}, bf16[1024]{0:T(1024)(128)(2,1)S(1)}, bf16[512]{0:T(512)(128)(2,1)S(1)}) all-reduce(bf16[512]{0:T(512)(128)(2,1)S(1)} %dynamic-update-slice.3, bf16[1024]{0:T(1024)(128)(2,1)S(1)} %dynamic-update-slice.4, ...), channel_id=1, replica_groups=mesh['dp'=8,'mp'=4] {'dp','mp'}, use_global_device_ids=true, to_apply=%add.65 | all-reduce | flops 2048 | bytes 8192
  498.0 50.7 %all-gather.24.cloned.1.call-done = bf16[512,1024]{1,0:T(8,128)(2,1)} async-done(((bf16[16,1024]{1,0:T(8,128)(2,1)}), bf16[512,1024]{1,0:T(8,128)(2,1)}) %all-gather.24.cloned.1.call-update) | async-done | bytes 1048592 | tf_op jit(solution)/shard_map/all_gather | solution.py:90
  553.3 51.3 %all-gather.22.cloned.1.call-done = bf16[512,1024]{1,0:T(8,128)(2,1)} async-done(((bf16[16,1024]{1,0:T(8,128)(2,1)}), bf16[512,1024]{1,0:T(8,128)(2,1)}) %all-gather.22.cloned.1.call-update) | async-done | bytes 1048592 | tf_op jit(solution)/shard_map/all_gather | solution.py:89
  607.4 11.2 fusion.18
  648.9 10.0 slice.848
  754.1 16.7 pad.223
  790.5 33.3 %all_gather.83 = bf16[512,512]{1,0:T(8,128)(2,1)} all-gather(bf16[64,512]{1,0:T(8,128)(2,1)S(1)} %copy-done.38), channel_id=1, replica_groups=mesh['dp'=8,'mp'=4] {'dp'}, dimensions={0}, use_global_device_ids=true | all-gather | bytes 589824 | tf_op jit(solution)/shard_map/all_gather | solution.py:95
  823.8 33.3 %all_gather.79 = bf16[512,512]{0,1:T(8,128)(2,1)} all-gather(bf16[512,64]{0,1:T(8,128)(2,1)S(1)} %copy-done.39), channel_id=1, replica_groups=mesh['dp'=8,'mp'=4] {'dp'}, dimensions={1}, use_global_device_ids=true | all-gather | bytes 589824 | tf_op jit(solution)/shard_map/all_gather | solution.py:96
  865.3 10.1 fusion.6
  890.2 32.8 %rev.11 = f32[1024,1024]{1,0:T(8,128)} reverse(f32[1024,1024]{1,0:T(8,128)} %pad_bitcast_fusion), dimensions={0} | reverse | bytes 8388608 | tf_op jit(solution)/shard_map/jit(_flip)/rev | solution.py:211
  971.5 32.7 %rev.10 = f32[1024,1024]{1,0:T(8,128)} reverse(f32[1024,1024]{1,0:T(8,128)} %fusion.76), dimensions={0} | reverse | bytes 8388608 | tf_op jit(solution)/shard_map/jit(_flip)/rev | solution.py:211
  1135.6 10.0 slice.924
  1202.7 16.5 pad.243
  1219.2 16.6 pad.244
  1242.6 32.7 %rev.12 = f32[1024,1024]{1,0:T(8,128)} reverse(f32[1024,1024]{1,0:T(8,128)} %add_bitcast_fusion), dimensions={0} | reverse | bytes 8388608 | tf_op jit(solution)/shard_map/jit(_flip)/rev | solution.py:211
  1275.3 10.7 convert_reduce_fusion
  1349.3 41.2 %all-reduce.71 = (f32[512]{0:T(512)S(1)}, f32[512]{0:T(512)S(1)}, f32[1024]{0:T(1024)S(1)}) all-reduce(f32[512]{0:T(512)S(1)} %get-tuple-element.55, f32[512]{0:T(512)S(1)} %copy-done.50, f32[1024]{0:T(1024)S(1)} %get-tuple-element.66), channel_id=4, replica_groups=mesh['dp'=8,'mp'=4] {'dp','mp'}, use_global_device_ids=true, to_apply=%region_9.10.clone | all-reduce | flops 2048 | bytes 16384
  1398.5 28.3 %reduce-scatter.11.cloned.1.call-done = f32[16,1024]{1,0:T(8,128)} async-done(((f32[512,1024]{1,0:T(8,128)}), f32[16,1024]{1,0:T(8,128)}) %reduce-scatter.11.cloned.1.call-update) | async-done | bytes 65552 | tf_op jit(solution)/shard_map/reduce_scatter | solution.py:238
  1426.8 135.4 %reduce-scatter.13.cloned.1.call-done = f32[16,1024]{1,0:T(8,128)} async-done(((f32[512,1024]{1,0:T(8,128)}), f32[16,1024]{1,0:T(8,128)}) %reduce-scatter.13.cloned.1.call-update) | async-done | bytes 65552 | tf_op jit(solution)/shard_map/reduce_scatter | solution.py:239
  1562.2 135.4 %reduce-scatter.15.cloned.1.call-done = f32[16,1024]{1,0:T(8,128)} async-done(((f32[512,1024]{1,0:T(8,128)}), f32[16,1024]{1,0:T(8,128)}) %reduce-scatter.15.cloned.1.call-update) | async-done | bytes 65552 | tf_op jit(solution)/shard_map/reduce_scatter | solution.py:240
  (560 shorter events, 654.8 us)
Async XLA Ops:
  7.2 60.3 %all-gather.12.cloned.1.call-start = ((), (), s32[]{:S(2)}) async-start(), calls=%async_computation.8 | async-start | bytes 1081344 | tf_op jit(solution)/shard_map/all_gather | solution.py:89
  7.9 115.2 %all-gather.14.cloned.1.call-start = ((), (), s32[]{:S(2)}) async-start(), calls=%async_computation.9 | async-start | bytes 1081344 | tf_op jit(solution)/shard_map/all_gather | solution.py:90
  8.7 170.0 %all-gather.16.cloned.1.call-start = ((), (), s32[]{:S(2)}) async-start(), calls=%async_computation.10 | async-start | bytes 1081344 | tf_op jit(solution)/shard_map/all_gather | solution.py:91
  9.4 304.4 %all-gather.18.cloned.1.call-start = ((), (), s32[]{:S(2)}) async-start(), calls=%async_computation.11 | async-start | bytes 1081344 | tf_op jit(solution)/shard_map/all_gather | solution.py:92
  10.0 373.2 %all-gather.20.cloned.1.call-start = ((), (), s32[]{:S(2)}) async-start(), calls=%async_computation.12 | async-start | bytes 5242880 | tf_op jit(solution)/shard_map/all_gather | solution.py:112
  288.1 16.6 copy-start.12
  319.0 32.6 %copy-start.39 = (bf16[512,64]{0,1:T(8,128)(2,1)S(1)}, bf16[512,64]{0,1:T(8,128)(2,1)}, u32[]{:S(2)}) copy-start(bf16[512,64]{0,1:T(8,128)(2,1)} %param.20) | copy-start | bytes 196612
  320.2 115.3 %reduce-scatter.7.cloned.1.call-start = ((), (), s32[]{:S(2)}) async-start(), calls=%async_computation.13 | async-start | bytes 5242880 | tf_op jit(solution)/shard_map/reduce_scatter | solution.py:168
  391.9 59.3 %copy-start.51 = (bf16[16]{0:T(256)(128)(2,1)S(1)}, bf16[16]{0:T(256)(128)(2,1)}, u32[]{:S(2)}) copy-start(bf16[16]{0:T(256)(128)(2,1)} %param.13) | copy-start | bytes 100
  391.9 59.6 %copy-start.52 = (bf16[32]{0:T(256)(128)(2,1)S(1)}, bf16[32]{0:T(256)(128)(2,1)}, u32[]{:S(2)}) copy-start(bf16[32]{0:T(256)(128)(2,1)} %param.17) | copy-start | bytes 196
  392.0 59.8 %copy-start.53 = (bf16[16]{0:T(256)(128)(2,1)S(1)}, bf16[16]{0:T(256)(128)(2,1)}, u32[]{:S(2)}) copy-start(bf16[16]{0:T(256)(128)(2,1)} %param.12) | copy-start | bytes 100
  392.0 101.4 %all-gather.26.cloned.1.call-start = ((), (), s32[]{:S(2)}) async-start(), calls=%async_computation.16 | async-start | bytes 1081344 | tf_op jit(solution)/shard_map/all_gather | solution.py:91
  438.1 110.5 %all-gather.24.cloned.1.call-start = ((), (), s32[]{:S(2)}) async-start(), calls=%async_computation.15 | async-start | bytes 1081344 | tf_op jit(solution)/shard_map/all_gather | solution.py:90
  450.5 154.2 %all-gather.22.cloned.1.call-start = ((), (), s32[]{:S(2)}) async-start(), calls=%async_computation.14 | async-start | bytes 1081344 | tf_op jit(solution)/shard_map/all_gather | solution.py:89
  451.2 334.0 %all-gather.28.cloned.1.call-start = ((), (), s32[]{:S(2)}) async-start(), calls=%async_computation.17 | async-start | bytes 1081344 | tf_op jit(solution)/shard_map/all_gather | solution.py:92
  491.5 113.1 %copy-start.41 = (f32[512]{0:T(512)}, f32[512]{0:T(512)S(1)}, u32[]{:S(2)}) copy-start(f32[512]{0:T(512)S(1)} %convert_element_type.118) | copy-start | bytes 6148
  491.5 115.8 %copy-start.45 = (f32[1024]{0:T(1024)}, f32[1024]{0:T(1024)S(1)}, u32[]{:S(2)}) copy-start(f32[1024]{0:T(1024)S(1)} %convert_element_type.120) | copy-start | bytes 12292
  493.3 111.3 %copy-start.35 = (f32[1024]{0:T(1024)}, f32[1024]{0:T(1024)S(1)}, u32[]{:S(2)}) copy-start(f32[1024]{0:T(1024)S(1)} %add_rsqrt_fusion.1) | copy-start | bytes 12292
  493.3 363.8 %all-gather.32.cloned.1.call-start = ((), (), s32[]{:S(2)}) async-start(), calls=%async_computation.19 | async-start | bytes 5242880 | tf_op jit(solution)/shard_map/all_gather | solution.py:112
  754.1 16.7 copy-start.13
  788.4 170.9 %copy-start.8 = (f32[1024,512]{0,1:T(8,128)}, f32[1024,512]{0,1:T(8,128)S(1)}, u32[]{:S(2)}) copy-start(f32[1024,512]{0,1:T(8,128)S(1)} %get-tuple-element.135) | copy-start | bytes 6291460
  789.9 75.4 %all-gather.30.cloned.1.call-start = ((), (), s32[]{:S(2)}) async-start(), calls=%async_computation.18 | async-start | bytes 5242880 | tf_op jit(solution)/shard_map/all_gather | solution.py:178
  790.4 168.8 %reduce-scatter.9.cloned.1.call-start = ((), (), s32[]{:S(2)}) async-start(), calls=%async_computation.20 | async-start | bytes 5242880 | tf_op jit(solution)/shard_map/reduce_scatter | solution.py:190
  865.3 12.1 copy-start.31
  881.8 516.7 %reduce-scatter.17.cloned.1.call-start = ((), (), s32[]{:S(2)}) async-start(), calls=%async_computation.24 | async-start | bytes 2162688 | tf_op jit(solution)/shard_map/reduce_scatter | solution.py:241
  1105.0 14.3 copy-start.40
  1115.6 311.2 %reduce-scatter.11.cloned.1.call-start = ((), (), s32[]{:S(2)}) async-start(), calls=%async_computation.21 | async-start | bytes 2162688 | tf_op jit(solution)/shard_map/reduce_scatter | solution.py:238
  1242.6 32.7 %copy-start.46 = (f32[1024]{0:T(1024)S(1)}, f32[1024]{0:T(1024)}, u32[]{:S(2)}) copy-start(f32[1024]{0:T(1024)} %copy-done.45) | copy-start | bytes 12292
  1291.2 271.0 %reduce-scatter.13.cloned.1.call-start = ((), (), s32[]{:S(2)}) async-start(), calls=%async_computation.22 | async-start | bytes 2162688 | tf_op jit(solution)/shard_map/reduce_scatter | solution.py:239
  1295.5 402.2 %reduce-scatter.15.cloned.1.call-start = ((), (), s32[]{:S(2)}) async-start(), calls=%async_computation.23 | async-start | bytes 2162688 | tf_op jit(solution)/shard_map/reduce_scatter | solution.py:240
  1309.0 15.1 all-to-all-start.1
  1324.1 15.1 all-to-all-start
  (42 other events, 148.7 us)
Sparse Core Ops, SparseCore 0:
  10.9 56.5 all-gather.11
  70.3 52.6 all-gather.13
  126.0 52.6 all-gather.15
  181.4 52.6 all-gather.17
  320.4 33.3 all-gather.19
  392.1 43.4 reduce-scatter.6
  438.8 53.7 all-gather.25
  495.8 52.7 all-gather.23
  551.9 52.6 all-gather.21
  607.7 52.6 all-gather.27
  790.0 33.3 all-gather.31
  824.8 34.4 all-gather.29
  881.9 43.2 reduce-scatter.8
  1115.7 134.7 reduce-scatter.16
  1291.3 135.4 reduce-scatter.10
  1429.5 132.6 reduce-scatter.12
  1565.0 132.6 reduce-scatter.14
where the time goes:
time: 1730 us; the launch traced here: 1700 us
  local copies, waits for them, and re-layouts  613 us (35%)
  waiting for transfers between devices  538 us (31%)
  blocking collectives  252 us (15%)
  other arithmetic  152 us (9%)
  matrix products  112 us (6%)
  starting transfers between devices  21.5 us (1%)
    slice x180, local copies, waits for them, and re-layouts, run_recurrence(): lax.associative_scan(combine_steps, (decay.reshape(seqs, LEN, width), dri...  334 us
    pad x54, local copies, waits for them, and re-layouts, run_recurrence(): lax.associative_scan(combine_steps, (decay.reshape(seqs, LEN, width), dri...  150 us
    reduce_scatter x1, waiting for transfers between devices, local(): lax.psum_scatter(wc_term, ('dp', 'mp'), scatter_dimension=0, tiled=True)  135 us
    reduce_scatter x1, waiting for transfers between devices, local(): lax.psum_scatter(wi_term, ('dp', 'mp'), scatter_dimension=0, tiled=True)  135 us
    unnamed x3, blocking collectives  123 us
    all_gather x2, waiting for transfers between devices, forward_state(): lax.all_gather(input_weight, ('dp', 'mp'), axis=0, tiled=True)  102 us
    all_gather x2, blocking collectives, forward_state(): lax.all_gather(down_weight, 'dp', axis=1, tiled=True)  64.8 us
    all_gather x2, blocking collectives, forward_state(): lax.all_gather(up_weight, 'dp', axis=0, tiled=True)  64.7 us
  transfers between devices with their start and end apart: 19, of which 11 were waited for; matrix products, arithmetic and copies ran while one was open for 40% of the time, Pallas kernels for 0%

commit v1 on v0

v1 whole, which is shorter than its diff:
```python
import functools

import jax
import jax.numpy as jnp
import numpy as np
from jax import lax
from jax.experimental import pallas as pl
from jax.experimental.pallas import tpu as pltpu
from jax.sharding import PartitionSpec as P

LEN = 1024
EPSILON = 1e-06
AXES = ("dp", "mp")
SLOTS = 32
CHUNKS = 8
LANES = 256
BF = jnp.bfloat16
F32 = jnp.float32
VMEM_LIMIT = 60 * 1024 * 1024
C0 = 0.7978845608028654
C1 = C0 * 0.044715


def params():
    return pltpu.CompilerParams(vmem_limit_bytes=VMEM_LIMIT)


def dot(a, b, dims=((1,), (0,))):
    return lax.dot_general(a, b, (dims, ((), ())), preferred_element_type=F32)


def whole(shape):
    return pl.BlockSpec(shape, lambda *_: (0,) * len(shape), pipeline_mode=pl.Buffered(1))


def aligned(start, size):
    return pl.ds(pl.multiple_of(start, size), size)


def spread(small, offset, piece, width):
    lane = lax.broadcasted_iota(jnp.int32, (LANES, width), 0)
    column = lax.broadcasted_iota(jnp.int32, (LANES, width), 1)
    pick = (lane == offset + column % piece).astype(BF)
    placed = dot(small.astype(BF), pick)
    row = lax.broadcasted_iota(jnp.int32, (SLOTS, width), 0)
    col = lax.broadcasted_iota(jnp.int32, (SLOTS, width), 1)
    return jnp.sum(jnp.where(col // piece == row, placed, 0.0), axis=0, keepdims=True)


def collect(vector, offset, piece):
    width = vector.shape[1]
    row = lax.broadcasted_iota(jnp.int32, (SLOTS, width), 0)
    col = lax.broadcasted_iota(jnp.int32, (SLOTS, width), 1)
    kept = jnp.where(col // piece == row, vector, 0.0).astype(BF)
    column = lax.broadcasted_iota(jnp.int32, (width, LANES), 0)
    lane = lax.broadcasted_iota(jnp.int32, (width, LANES), 1)
    pick = (lane == offset + column % piece).astype(BF)
    return dot(kept, pick)


def mixer_forward(dev_ref, x_ref, g0, g1, g2, g3, hb_ref, f_ref, u1_ref, u2_ref, w_ref, xn_ref, gain_ref,
                  small, kf_s, ki_s, kc_s, c1_s, bias_s):
    step = pl.program_id(0)
    parts = (g0, g1, g2, g3)
    per = SLOTS // 4
    nblk = (g0.shape[1] - 16) // 48
    tail = 48 * nblk

    @pl.when(step == 0)
    def _():
        for s in range(SLOTS):
            d = dev_ref[s]
            row = parts[s // per][s % per, tail : tail + 16, :].astype(F32)
            small[pl.ds(d, 1), :] = row[0:1, :]
        values = small[...]
        width = x_ref.shape[1]
        piece = width // SLOTS
        chans = nblk * LANES
        gmix = spread(values, 0, piece, width)
        gmlp = spread(values, piece, piece, width)
        bias = spread(values, 2 * piece, chans // SLOTS, chans)
        gain_ref[0:1, :] = gmix
        gain_ref[1:2, :] = gmlp
        for b in range(nblk):
            bias_s[b, 0:1, :] = bias[:, b * LANES : (b + 1) * LANES]

        def rows(i, _):
            at = aligned(i * 128, 128)
            v = x_ref[at, :].astype(F32)
            scale = lax.rsqrt(jnp.mean(v * v, axis=-1, keepdims=True) + EPSILON)
            xn_ref[at, :] = ((v * scale) * gmix).astype(BF)
            return 0

        lax.fori_loop(0, x_ref.shape[0] // 128, rows, 0)

    for s in range(SLOTS):
        d = dev_ref[s]
        for w in range(3):
            src = aligned((w * nblk + step) * 16, 16)
            w_ref[w, aligned(d * 16, 16), :] = parts[s // per][s % per, src, :]

    xn = xn_ref[...]
    kf_s[...] = dot(xn, w_ref[0])
    ki_s[...] = dot(xn, w_ref[1])
    kc_s[...] = dot(xn, w_ref[2])
    bias = bias_s[step, 0:1, :]
    zeros = jnp.zeros((CHUNKS, LANES), F32)
    tile = 4 * CHUNKS
    count = x_ref.shape[0] // tile

    def first(i, carry):
        h, prod = carry
        at = aligned(i * tile, tile)
        kf = kf_s[at, :]
        ki = ki_s[at, :] + bias
        kc = kc_s[at, :]
        p = jnp.exp(-jnp.abs(kf))
        q = jnp.exp(-jnp.abs(ki))
        w = jnp.minimum(ki, 0.0) - jnp.minimum(kf, 0.0)
        e = jnp.exp(-jnp.abs(w))
        onep = 1.0 + p
        oneq = 1.0 + q
        low = w <= 0.0
        a = jnp.where(low, oneq, e * oneq)
        b = jnp.where(low, e * onep, onep)
        inv = 1.0 / (a + b)
        forget = a * inv
        other = b * inv
        both = forget * other
        f_ref[at, :] = forget
        drive = other * kc
        ki_s[at, :] = drive
        kf_s[at, :] = both * jnp.where(kf >= 0.0, p, 1.0) / onep
        c1_s[at, :] = -both * jnp.where(ki >= 0.0, q, 1.0) / oneq
        for k in range(4):
            part = slice(k * CHUNKS, (k + 1) * CHUNKS)
            h = forget[part] * h + drive[part]
            prod = prod * forget[part]
        return h, prod

    last, prod = lax.fori_loop(0, count, first, (zeros, zeros + 1.0))
    sub = lax.broadcasted_iota(jnp.int32, (CHUNKS, LANES), 0)
    start = zeros
    for s in range(CHUNKS - 1):
        moved = pltpu.roll(last + prod * start, 1, 0)
        start = jnp.where(sub == s + 1, moved, start)

    def second(i, h):
        at = aligned(i * tile, tile)
        forget = f_ref[at, :]
        drive = ki_s[at, :]
        kc = kc_s[at, :]
        before, after = [], []
        for k in range(4):
            part = slice(k * CHUNKS, (k + 1) * CHUNKS)
            before.append(h)
            h = forget[part] * h + drive[part]
            after.append(h)
        diff = jnp.concatenate(before, axis=0) - kc
        hb_ref[at, :] = jnp.concatenate(after, axis=0).astype(BF)
        u1_ref[at, :] = (kf_s[at, :] * diff).astype(BF)
        u2_ref[at, :] = (c1_s[at, :] * diff).astype(BF)
        return h

    lax.fori_loop(0, count, second, start)


def feed_forward(dev_ref, slot_ref, cols_ref, hb_ref, x_ref, dy_ref, gain_ref, g0, g1, g2, g3,
                 out_ref, dy1_ref, dmix_ref, wo_ref, small_ref, keep_ref, send_ref,
                 buf, sems, y1_s, xn_s, xnt_s, dyt_s, acc_s, dxn_s, up_s, dn_s, upg_s, dng_s):
    step = pl.program_id(0)
    parts = (g0, g1, g2, g3)
    per = SLOTS // 4
    tokens, width = x_ref.shape
    hid = up_s.shape[1]
    shard = buf.shape[1] - 32
    half = shard // 2
    rows_of = width // half
    copies = [pltpu.make_async_copy(parts[i], buf.at[pl.ds(i * per, per)], sems.at[i]) for i in range(4)]

    @pl.when(step == 0)
    def _():
        for c in copies:
            c.start()
        for c in copies:
            c.wait()
        for s in range(SLOTS):
            wo_ref[aligned(dev_ref[s] * 32, 32), :] = buf[s, shard : shard + 32, :]

        def rows(i, _):
            at = aligned(i * 256, 256)
            y1 = x_ref[at, :].astype(F32) + dot(hb_ref[at, :], wo_ref[...])
            y1_s[at, :] = y1
            scale = lax.rsqrt(jnp.mean(y1 * y1, axis=-1, keepdims=True) + EPSILON)
            xn = ((y1 * scale) * gain_ref[1:2, :]).astype(BF)
            xn_s[at, :] = xn
            xnt_s[:, aligned(i * 256, 256)] = xn.T
            dyt_s[:, aligned(i * 256, 256)] = dy_ref[at, :].T
            return 0

        lax.fori_loop(0, tokens // 256, rows, 0)
        acc_s[...] = jnp.zeros_like(acc_s)
        dxn_s[...] = jnp.zeros_like(dxn_s)

    block = cols_ref[step]
    for r in range(rows_of):
        s = slot_ref[r * 4 + block]
        up_s[r * half : (r + 1) * half, :] = buf[s, 0:half, :]
        dn_s[r * half : (r + 1) * half, :] = buf[s, half : 2 * half, :]

    upg_s[...] = jnp.zeros_like(upg_s)
    dng_s[...] = jnp.zeros_like(dng_s)

    def rows(i, _):
        at = aligned(i * 256, 256)
        xn = xn_s[at, :]
        pre = dot(xn, up_s[...])
        dact = dot(dy_ref[at, :], dn_s[...])
        sq = pre * pre
        gate = 0.5 + 0.5 * jnp.tanh(pre * (C0 + C1 * sq))
        value = pre * gate
        act = value.astype(BF)
        slope = gate + value * (1.0 - gate) * (2.0 * C0 + 6.0 * C1 * sq)
        dpre = (slope * dact).astype(BF)
        acc_s[at, :] += dot(act, dn_s[...], ((1,), (1,)))
        dxn_s[at, :] += dot(dpre, up_s[...], ((1,), (1,)))
        upg_s[...] += dot(xnt_s[:, at], dpre)
        dng_s[...] += dot(dyt_s[:, at], act)
        return 0

    lax.fori_loop(0, tokens // 256, rows, 0)

    def give(target, base):
        for r in range(rows_of):
            s = slot_ref[r * 4 + block] - base
            target[s, 0:half, :] = upg_s[r * half : (r + 1) * half, :].astype(BF)
            target[s, half : 2 * half, :] = dng_s[r * half : (r + 1) * half, :].astype(BF)

    @pl.when(step < 2)
    def _():
        give(send_ref, SLOTS // 2)

    @pl.when(step >= 2)
    def _():
        give(keep_ref, 0)

    @pl.when(step == 3)
    def _():
        gain = gain_ref[1:2, :]

        def rows(i, total):
            at = aligned(i * 128, 128)
            y1 = y1_s[at, :]
            scale = lax.rsqrt(jnp.mean(y1 * y1, axis=-1, keepdims=True) + EPSILON)
            n2 = y1 * scale
            out_ref[at, :] = (y1 + acc_s[at, :]).astype(BF)
            dxn = dxn_s[at, :]
            dn = dxn * gain
            dy1 = dy_ref[at, :].astype(F32) + scale * (dn - n2 * jnp.mean(dn * n2, axis=-1, keepdims=True))
            dy1_ref[at, :] = dy1
            dmix_ref[at, :] = dy1.astype(BF)
            return total + jnp.sum(dxn * n2, axis=0, keepdims=True)

        total = lax.fori_loop(0, tokens // 128, rows, jnp.zeros((1, width), F32))
        small_ref[...] = collect(total, 0, width // SLOTS)
        chans = hb_ref.shape[1]
        for b in range(chans // width):
            upg_s[...] = dot(hb_ref[:, b * width : (b + 1) * width], dmix_ref[...], ((0,), (0,)))
            per_b = width // 32
            for r in range(per_b):
                s = slot_ref[b * per_b + r]
                piece = upg_s[r * 32 : (r + 1) * 32, :].astype(BF)

                @pl.when(s < SLOTS // 2)
                def _():
                    keep_ref[s, shard : shard + 32, :] = piece

                @pl.when(s >= SLOTS // 2)
                def _():
                    send_ref[s - SLOTS // 2, shard : shard + 32, :] = piece


def mixer_backward(dev_ref, dmix_ref, xn_ref, small_ref, wo_ref, f_ref, u1_ref, u2_ref,
                   df_ref, di_ref, dc_ref, keep_ref, send_ref, xnt_s, dh_s, bias_s):
    step = pl.program_id(0)
    tokens, width = xn_ref.shape
    nblk = (keep_ref.shape[1] - 16) // 48
    tail = 48 * nblk
    half = SLOTS // 2

    @pl.when(step == 0)
    def _():
        xnt_s[...] = xn_ref[...].T

    dh_s[...] = dot(dmix_ref[...], wo_ref[...], ((1,), (1,)))
    zeros = jnp.zeros((CHUNKS, LANES), F32)
    tile = 4 * CHUNKS
    count = tokens // tile

    def first(i, carry):
        g, prod, decay = carry
        at = aligned((count - 1 - i) * tile, tile)
        dh = dh_s[at, :]
        forget = f_ref[at, :]
        for k in reversed(range(4)):
            part = slice(k * CHUNKS, (k + 1) * CHUNKS)
            g = dh[part] + decay * g
            prod = prod * decay
            decay = forget[part]
        return g, prod, decay

    ones = zeros + 1.0
    head, prod, decay = lax.fori_loop(0, count, first, (zeros, ones, ones))
    sub = lax.broadcasted_iota(jnp.int32, (CHUNKS, LANES), 0)
    start = zeros
    for s in reversed(range(1, CHUNKS)):
        moved = pltpu.roll(decay * (head + prod * start), CHUNKS - 1, 0)
        start = jnp.where(sub == s - 1, moved, start)

    def second(i, carry):
        g, decay, total = carry
        at = aligned((count - 1 - i) * tile, tile)
        dh = dh_s[at, :]
        forget = f_ref[at, :]
        parts = [None] * 4
        for k in reversed(range(4)):
            part = slice(k * CHUNKS, (k + 1) * CHUNKS)
            g = dh[part] + decay * g
            decay = forget[part]
            parts[k] = g
        grad = jnp.concatenate(parts, axis=0)
        df_ref[at, :] = (u1_ref[at, :].astype(F32) * grad).astype(BF)
        di = (u2_ref[at, :].astype(F32) * grad).astype(BF)
        di_ref[at, :] = di
        dc_ref[at, :] = ((1.0 - forget) * grad).astype(BF)
        di = di.astype(F32)
        for k in range(4):
            total = total + di[k * CHUNKS : (k + 1) * CHUNKS]
        return g, decay, total

    _, _, total = lax.fori_loop(0, count, second, (start, ones, zeros))
    bias_s[step, 0:1, :] = jnp.sum(total, axis=0, keepdims=True)

    for w, ref in enumerate((df_ref, di_ref, dc_ref)):
        grad = dot(xnt_s[...], ref[...]).astype(BF)
        dh_s[0:width, :] = grad.astype(F32)
        dst = aligned((w * nblk + step) * 16, 16)
        for s in range(SLOTS):
            d = dev_ref[s]
            target = keep_ref if s < half else send_ref
            target[s % half, dst, :] = dh_s[aligned(d * 16, 16), :].astype(BF)

    @pl.when(step == pl.num_programs(0) - 1)
    def _():
        bias = jnp.concatenate([bias_s[b, 0:1, :] for b in range(nblk)], axis=1)
        piece = width // SLOTS
        dh_s[0:SLOTS, :] = small_ref[...] + collect(bias, 2 * piece, nblk * LANES // SLOTS)
        row = lax.broadcasted_iota(jnp.int32, (16, LANES), 0)
        for s in range(SLOTS):
            target = keep_ref if s < half else send_ref
            values = dh_s[pl.ds(dev_ref[s], 1), :]
            target[s % half, tail : tail + 16, :] = jnp.where(row == 0, values, 0.0).astype(BF)


def input_gradient(x_ref, dy1_ref, gain_ref, df_ref, di_ref, dc_ref, w_ref, out_ref):
    dxn = dot(df_ref[...], w_ref[0], ((1,), (1,)))
    dxn = dxn + dot(di_ref[...], w_ref[1], ((1,), (1,)))
    dxn = dxn + dot(dc_ref[...], w_ref[2], ((1,), (1,)))
    v = x_ref[...].astype(F32)
    scale = lax.rsqrt(jnp.mean(v * v, axis=-1, keepdims=True) + EPSILON)
    n1 = v * scale
    dn = dxn * gain_ref[0:1, :]
    out_ref[...] = dy1_ref[...] + scale * (dn - n1 * jnp.mean(dn * n1, axis=-1, keepdims=True))


def order_table():
    table = np.zeros((SLOTS, SLOTS), np.int32)
    for me in range(SLOTS):
        core, y, x, z = me & 1, me >> 1 & 1, me >> 2 & 1, me >> 3
        for slot in range(SLOTS):
            oc, second, first, oz = slot >> 4, slot >> 3 & 1, slot >> 2 & 1, slot & 3
            c2 = core ^ oc
            x2 = x ^ (first if c2 == 0 else second)
            y2 = y ^ (second if c2 == 0 else first)
            table[me, slot] = ((z ^ oz) * 2 + x2) * 4 + y2 * 2 + c2
    return table


def flip(x0, y0, z0, c0, x1, y1, z1, c1):
    pairs = []
    for me in range(SLOTS):
        x, y, z, c = (x1, y1, z1, c1) if me & 1 else (x0, y0, z0, c0)
        pairs.append((me, me ^ (z << 3 | x << 2 | y << 1 | c)))
    return pairs


Z = [None] + [flip(0, 0, k, 0, 0, 0, k, 0) for k in (1, 2, 3)]
FIRST = flip(1, 0, 0, 0, 0, 1, 0, 0)
SECOND = flip(0, 1, 0, 0, 1, 0, 0, 0)
CORE = flip(0, 0, 0, 1, 0, 0, 0, 1)


def send(value, pairs):
    return lax.ppermute(value, AXES, pairs)


def gather(piece):
    four = jnp.stack([piece] + [send(piece, Z[k]) for k in (1, 2, 3)])
    eight = jnp.concatenate([four, send(four, FIRST)])
    more = send(eight, SECOND)
    return eight, more, send(eight, CORE), send(more, CORE)


def add(a, b):
    return (a.astype(F32) + b.astype(F32)).astype(BF)


def reduce_scatter(keep, away):
    got = send(away, CORE)
    high = add(keep[8:], got[8:])
    low = add(keep[:8], got[:8])
    got = send(high, SECOND)
    high = add(low[4:], got[4:])
    low = add(low[:4], got[:4])
    got = send(high, FIRST)
    four = add(low, got)
    parts = [send(four[k], Z[k]) for k in (1, 2, 3)]
    total = four[0].astype(F32)
    for part in parts:
        total = total + part.astype(F32)
    return total


def pack_mixer(forget_weight, input_weight, candidate_weight, small):
    def cut(w):
        blocks = w.shape[1] // LANES
        return w.reshape(16, blocks, LANES).transpose(1, 0, 2).reshape(blocks * 16, LANES)

    row = jnp.concatenate([small, jnp.zeros((LANES - small.shape[0],), small.dtype)])
    tail = jnp.concatenate([row[None], jnp.zeros((15, LANES), small.dtype)])
    return jnp.concatenate([cut(forget_weight), cut(input_weight), cut(candidate_weight), tail])


def local(fast, tokens, gain_mix, gain_mlp, forget_weight, input_weight, candidate_weight, input_gate_bias,
          output_weight, up_weight, down_weight, cotangent):
    rows, width = tokens.shape
    chans = forget_weight.shape[1]
    nblk = chans // LANES
    shard = width // SLOTS

    def permute(v):
        return v.reshape(CHUNKS, rows // CHUNKS, width).transpose(1, 0, 2).reshape(rows, width)

    def restore(v):
        return v.reshape(rows // CHUNKS, CHUNKS, width).transpose(1, 0, 2).reshape(rows, width)

    if fast:
        me = lax.axis_index(AXES)
        table = order_table()
        dev = lax.dynamic_index_in_dim(jnp.asarray(table), me, keepdims=False)
        slot = lax.dynamic_index_in_dim(jnp.asarray(np.argsort(table, axis=1).astype(np.int32)), me, keepdims=False)
        mine, core = me // 2 % 2, me % 2
        cols = jnp.stack([1 - core, 3 - core, core, 2 + core]).astype(jnp.int32)
        small = jnp.concatenate([gain_mix, gain_mlp, input_gate_bias])
        mixer = gather(pack_mixer(forget_weight, input_weight, candidate_weight, small))
        ffn = gather(jnp.concatenate([up_weight, down_weight.T, output_weight]))
    else:
        dev = slot = jnp.arange(SLOTS, dtype=jnp.int32)
        cols = jnp.arange(4, dtype=jnp.int32)

        def full(v, axis=0, names=AXES):
            return lax.all_gather(v, names, axis=axis, tiled=True)

        gm, gl, gb = full(gain_mix), full(gain_mlp), full(input_gate_bias)
        weights = [full(w) for w in (forget_weight, input_weight, candidate_weight)]
        smalls = jnp.concatenate([v.reshape(SLOTS, -1) for v in (gm, gl, gb)], axis=1)
        packed = jnp.stack(
            [pack_mixer(*[w[s * 16 : (s + 1) * 16] for w in weights], smalls[s]) for s in range(SLOTS)]
        )
        up = full(full(up_weight, 0, "dp"), 1, "mp")
        down = full(full(down_weight, 1, "dp"), 0, "mp")
        hid = up.shape[1] // 4

        def blocks(w):
            return w.reshape(8, width // 8, 4, hid).transpose(0, 2, 1, 3).reshape(SLOTS, width // 8, hid)

        both = jnp.concatenate([blocks(up), blocks(down.T), full(output_weight).reshape(SLOTS, -1, width)], axis=1)
        mixer = tuple(packed[k * 8 : (k + 1) * 8] for k in range(4))
        ffn = tuple(both[k * 8 : (k + 1) * 8] for k in range(4))

    xp = permute(tokens)
    dyp = permute(cotangent)
    r1 = mixer[0].shape[1]
    r2 = ffn[0].shape[1]
    hid = ffn[0].shape[2]
    smem = pl.BlockSpec(memory_space=pltpu.SMEM)
    anyspace = pl.BlockSpec(memory_space=pl.ANY)
    column = pl.BlockSpec((rows, LANES), lambda i: (0, i))

    hb, forget, u1, u2, w3, xn1, gains = pl.pallas_call(
        mixer_forward,
        grid=(nblk,),
        in_specs=[smem, whole((rows, width))] + [whole((8, r1, LANES))] * 4,
        out_specs=[column] * 4 + [pl.BlockSpec((3, width, LANES), lambda i: (0, 0, i)), whole((rows, width)), whole((2, width))],
        out_shape=[
            jax.ShapeDtypeStruct((rows, chans), BF),
            jax.ShapeDtypeStruct((rows, chans), F32),
            jax.ShapeDtypeStruct((rows, chans), BF),
            jax.ShapeDtypeStruct((rows, chans), BF),
            jax.ShapeDtypeStruct((3, width, chans), BF),
            jax.ShapeDtypeStruct((rows, width), BF),
            jax.ShapeDtypeStruct((2, width), F32),
        ],
        scratch_shapes=[pltpu.VMEM((SLOTS, LANES), F32)] + [pltpu.VMEM((rows, LANES), F32)] * 4 + [pltpu.VMEM((nblk, 8, LANES), F32)],
        compiler_params=params(),
        cost_estimate=pl.CostEstimate(flops=6 * rows * width * chans, bytes_accessed=16 << 20, transcendentals=6 * rows * chans),
        name="mixer_forward",
    )(dev, xp, *mixer)

    block_out, dy1, dmix, wo, gmlp_small, keep1, send1 = pl.pallas_call(
        feed_forward,
        grid=(4,),
        in_specs=[smem, smem, smem, whole((rows, chans)), whole((rows, width)), whole((rows, width)), whole((2, width))] + [anyspace] * 4,
        out_specs=[whole((rows, width))] * 3
        + [whole((chans, width)), whole((SLOTS, LANES)), whole((SLOTS // 2, r2, hid)), whole((SLOTS // 2, r2, hid))],
        out_shape=[
            jax.ShapeDtypeStruct((rows, width), BF),
            jax.ShapeDtypeStruct((rows, width), F32),
            jax.ShapeDtypeStruct((rows, width), BF),
            jax.ShapeDtypeStruct((chans, width), BF),
            jax.ShapeDtypeStruct((SLOTS, LANES), F32),
            jax.ShapeDtypeStruct((SLOTS // 2, r2, hid), BF),
            jax.ShapeDtypeStruct((SLOTS // 2, r2, hid), BF),
        ],
        scratch_shapes=[
            pltpu.VMEM((SLOTS, r2, hid), BF),
            pltpu.SemaphoreType.DMA((4,)),
            pltpu.VMEM((rows, width), F32),
            pltpu.VMEM((rows, width), BF),
            pltpu.VMEM((width, rows), BF),
            pltpu.VMEM((width, rows), BF),
            pltpu.VMEM((rows, width), F32),
            pltpu.VMEM((rows, width), F32),
            pltpu.VMEM((width, hid), BF),
            pltpu.VMEM((width, hid), BF),
            pltpu.VMEM((width, hid), F32),
            pltpu.VMEM((width, hid), F32),
        ],
        compiler_params=params(),
        cost_estimate=pl.CostEstimate(flops=2 * rows * width * (24 * hid + 2 * chans), bytes_accessed=24 << 20, transcendentals=4 * rows * hid),
        name="feed_forward",
    )(dev, slot, cols, hb, xp, dyp, gains, *ffn)

    df, di, dc, keep2, send2 = pl.pallas_call(
        mixer_backward,
        grid=(nblk,),
        in_specs=[smem, whole((rows, width)), whole((rows, width)), whole((SLOTS, LANES)),
                  pl.BlockSpec((LANES, width), lambda i: (i, 0)), column, column, column],
        out_specs=[column] * 3 + [whole((SLOTS // 2, r1, LANES))] * 2,
        out_shape=[jax.ShapeDtypeStruct((rows, chans), BF)] * 3 + [jax.ShapeDtypeStruct((SLOTS // 2, r1, LANES), BF)] * 2,
        scratch_shapes=[pltpu.VMEM((width, rows), BF), pltpu.VMEM((rows, LANES), F32), pltpu.VMEM((nblk, 8, LANES), F32)],
        compiler_params=params(),
        cost_estimate=pl.CostEstimate(flops=8 * rows * width * chans, bytes_accessed=24 << 20, transcendentals=0),
        name="mixer_backward",
    )(dev, dmix, xn1, gmlp_small, wo, forget, u1, u2)

    tile = 256
    tokens_grad = pl.pallas_call(
        input_gradient,
        grid=(rows // tile,),
        in_specs=[pl.BlockSpec((tile, width), lambda i: (i, 0))] * 2 + [whole((2, width))]
        + [pl.BlockSpec((tile, chans), lambda i: (i, 0))] * 3 + [whole((3, width, chans))],
        out_specs=pl.BlockSpec((tile, width), lambda i: (i, 0)),
        out_shape=jax.ShapeDtypeStruct((rows, width), F32),
        compiler_params=params(),
        cost_estimate=pl.CostEstimate(flops=6 * rows * width * chans, bytes_accessed=16 << 20, transcendentals=0),
        name="input_gradient",
    )(xp, dy1, gains, df, di, dc, w3)

    half = (r2 - 32) // 2

    def uncut(v):
        return v.reshape(nblk, 16, LANES).transpose(1, 0, 2).reshape(16, chans)

    if fast:
        ffn_total = reduce_scatter(keep1, send1)
        up_grad, down_grad, out_grad = ffn_total[:half], ffn_total[half : 2 * half].T, ffn_total[2 * half :]
        total = reduce_scatter(keep2, send2)
        step = nblk * 16
        grads = [uncut(total[k * step : (k + 1) * step]) for k in range(3)]
        last = total[3 * step]
        gmlp_grad = last[:shard]
        bias_grad = last[2 * shard : 2 * shard + chans // SLOTS]
    else:
        pieces = jnp.concatenate([keep1, send1])

        def summed(v, axis=0, names=AXES):
            return lax.psum_scatter(v, names, scatter_dimension=axis, tiled=True)

        def joined(w):
            return w.reshape(8, 4, half, hid).transpose(0, 2, 1, 3).reshape(8 * half, 4 * hid).astype(F32)

        up_grad = summed(summed(joined(pieces[:, :half]), 0, "dp"), 1, "mp")
        down_grad = summed(summed(joined(pieces[:, half : 2 * half]).T, 1, "dp"), 0, "mp")
        out_grad = summed(pieces[:, 2 * half :].reshape(chans, width).astype(F32))
        pieces = jnp.concatenate([keep2, send2]).astype(F32)
        step = nblk * 16
        grads = []
        for k in range(3):
            w = pieces[:, k * step : (k + 1) * step].reshape(SLOTS, nblk, 16, LANES).transpose(0, 2, 1, 3)
            grads.append(summed(w.reshape(width, chans)))
        last = pieces[:, 3 * step]
        gmlp_grad = summed(last[:, :shard].reshape(-1))
        bias_grad = summed(last[:, 2 * shard : 2 * shard + chans // SLOTS].reshape(-1))

    dots = sum(
        jnp.sum(w.astype(F32) * g, axis=1) for w, g in zip((forget_weight, input_weight, candidate_weight), grads)
    )
    gmix_grad = dots / gain_mix.astype(F32)
    return (restore(block_out), restore(tokens_grad), gmix_grad, gmlp_grad, grads[0], grads[1], grads[2], bias_grad,
            out_grad, up_grad, down_grad)


def solution(mesh):
    fast = mesh.shape["dp"] == 8 and mesh.shape["mp"] == 4
    every = P(AXES, None)
    in_specs = (every, P(AXES), P(AXES), every, every, every, P(AXES), every, P("dp", "mp"), P("mp", "dp"), every)
    out_specs = (every, every, P(AXES), P(AXES), every, every, every, P(AXES), every, P("dp", "mp"), P("mp", "dp"))
    return jax.shard_map(
        functools.partial(local, fast), mesh=mesh, in_specs=in_specs, out_specs=out_specs, check_vma=False
    )
```

time: 1730 us -> 222 us (0.13); the launches traced: 1700 us -> 221 us
  local copies, waits for them, and re-layouts: 613 us -> 19.7 us
  waiting for transfers between devices: 538 us -> 77.9 us
  blocking collectives: 252 us -> 0 us
  other arithmetic: 152 us -> 8.84 us
  matrix products: 112 us -> 0 us
  Pallas kernels: 0 us -> 81.4 us
    reduce_scatter x6 -> x0, waiting for transfers between devices: 343 us -> none  [the longest x1 135 us: local(): lax.psum_scatter(wc_term, ('dp', 'mp'), scatter_dimension=0, tiled=True)]
    slice x181 -> x4, local copies, waits for them, and re-layouts: 337 us -> 1.74 us  [the longest x1 0.63 us: local(): ffn_total[2 * half:]]
    all_gather x11 -> x0, waiting for transfers between devices: 180 us -> none  [the longest x2 102 us: forward_state(): lax.all_gather(input_weight, ('dp', 'mp'), axis=0, tiled=True)]
    pad x54 -> x0, local copies, waits for them, and re-layouts: 150 us -> none  [run_recurrence(): lax.associative_scan(combine_steps, (decay.reshape(seqs, LEN, width), dri...]
    all_gather x4 -> x0, blocking collectives: 129 us -> none  [the longest x2 64.8 us: forward_state(): lax.all_gather(down_weight, 'dp', axis=1, tiled=True)]
    unnamed x3 -> x0, blocking collectives: 123 us -> none
    dot_general x22 -> x0, matrix products: 112 us -> none  [the longest x2 14.7 us: forward_state(): jnp.dot(first_normed_input, wi_full, preferred_element_type=jnp.float32)]
    rev x3 -> x0, local copies, waits for them, and re-layouts: 98.1 us -> none  [the longest x1 32.8 us: local(): jnp.flip(decay_next, 0)]
  transfers between devices with their start and end apart: 19 -> 26, of which waited for: 11 -> 12; matrix products, arithmetic and copies ran while one was open for 40% -> 11% of each run, Pallas kernels for 0% -> 13%
where the time goes in v1:
time: 222 us; the launch traced here: 221 us
  Pallas kernels  81.4 us (37%)
  waiting for transfers between devices  77.9 us (35%)
  starting transfers between devices  32.1 us (14%)
  local copies, waits for them, and re-layouts  19.7 us (9%)
  other arithmetic  8.84 us (4%)
    ppermute x26, waiting for transfers between devices, send(): return lax.ppermute(value, AXES, pairs)  77.9 us
    pallas_call x1, Pallas kernels, local(): pl.pallas_call(feed_forward, grid=(4,), in_specs=[smem, smem, smem, whole...  35.2 us
    ppermute x26, starting transfers between devices, send(): return lax.ppermute(value, AXES, pairs)  32.1 us
    pallas_call x1, Pallas kernels, local(): pl.pallas_call(mixer_forward, grid=(nblk,), in_specs=[smem, whole((rows,...  18.9 us
    pallas_call x1, Pallas kernels, local(): pl.pallas_call(mixer_backward, grid=(nblk,), in_specs=[smem, whole((rows,...  18.2 us
    pallas_call x1, Pallas kernels, local(): pl.pallas_call(input_gradient, grid=(rows // tile,), in_specs=[pl.BlockSp...  9.08 us
    transpose x2, local copies, waits for them, and re-layouts, restore(): v.reshape(rows // CHUNKS, CHUNKS, width).transpose(1, 0, 2)  5.5 us
    convert_element_type x6, other arithmetic, add(): return (a.astype(F32) + b.astype(F32)).astype(BF)  4.62 us
  transfers between devices with their start and end apart: 26, of which 12 were waited for; matrix products, arithmetic and copies ran while one was open for 11% of the time, Pallas kernels for 13%

profile of v1, /device:TPU:0, one launch (start us, length us, event | category | flops | bytes accessed | tf_op | source)
XLA Modules:
  0.0 220.8 jit_solution(13468910782642642954)
XLA Ops:
  3.9 3.1 %collective-permute-start = (bf16[208,256]{1,0:T(8,128)(2,1)S(1)}, bf16[208,256]{1,0:T(8,128)(2,1)S(1)}, u32[]{:S(2)}, u32[]{:S(2)}) collective-permute-start(bf16[208,256]{1,0:T(8,128)(2,1)S(1)} %concatenate.18), channel_id=1, source_target_pairs={{0,8},{1,9},{2,10},{3,11},{4,12},{5,13},{6,14},{7,15},{8,0},{9,1},... | collective-permute-start | bytes 319496 | tf_op jit(solution)/shard_map/ppermute | solution.py:404
  7.0 2.6 %collective-permute-start.1 = (bf16[208,256]{1,0:T(8,128)(2,1)S(1)}, bf16[208,256]{1,0:T(8,128)(2,1)S(1)}, u32[]{:S(2)}, u32[]{:S(2)}) collective-permute-start(bf16[208,256]{1,0:T(8,128)(2,1)S(1)} %concatenate.18), channel_id=1, source_target_pairs={{0,16},{1,17},{2,18},{3,19},{4,20},{5,21},{6,22},{7,23},{8,24},{9,... | collective-permute-start | bytes 319496 | tf_op jit(solution)/shard_map/ppermute | solution.py:404
  11.4 3.5 %collective-permute-start.8 = (bf16[160,512]{1,0:T(8,128)(2,1)S(1)}, bf16[160,512]{1,0:T(8,128)(2,1)S(1)}, u32[]{:S(2)}, u32[]{:S(2)}) collective-permute-start(bf16[160,512]{1,0:T(8,128)(2,1)S(1)} %get-tuple-element.65), channel_id=1, source_target_pairs={{0,16},{1,17},{2,18},{3,19},{4,20},{5,21},{6,22},{7,23},{8,24},{9,... | collective-permute-start | bytes 491528 | tf_op jit(solution)/shard_map/ppermute | solution.py:404
  16.5 1.6 collective-permute-done.1
  18.2 1.6 collective-permute-start.3
  19.9 11.0 %collective-permute-done.8 = bf16[160,512]{1,0:T(8,128)(2,1)S(1)} collective-permute-done((bf16[160,512]{1,0:T(8,128)(2,1)S(1)}, bf16[160,512]{1,0:T(8,128)(2,1)S(1)}, u32[]{:S(2)}, u32[]{:S(2)}) %collective-permute-start.8) | collective-permute-done | bytes 163872 | tf_op jit(solution)/shard_map/ppermute | solution.py:404
  31.0 1.6 collective-permute-start.10
  32.6 9.5 %collective-permute-done.10 = bf16[4,160,512]{2,1,0:T(8,128)(2,1)S(1)} collective-permute-done((bf16[4,160,512]{2,1,0:T(8,128)(2,1)S(1)}, bf16[4,160,512]{2,1,0:T(8,128)(2,1)S(1)}, u32[]{:S(2)}, u32[]{:S(2)}) %collective-permute-start.10) | collective-permute-done | bytes 655392 | tf_op jit(solution)/shard_map/ppermute | solution.py:404
  42.1 1.6 collective-permute-start.11
  47.0 12.9 %collective-permute-done.11.g1 = bf16[8,160,512]{2,1,0:T(8,128)(2,1)} collective-permute-done((bf16[8,160,512]{2,1,0:T(8,128)(2,1)S(1)}, bf16[8,160,512]{2,1,0:T(8,128)(2,1)}, u32[]{:S(2)}, u32[]{:S(2)}) %collective-permute-start.11) | collective-permute-done | bytes 1310752 | tf_op jit(solution)/shard_map/ppermute | solution.py:404
  60.4 8.6 %collective-permute-done.4.g1 = bf16[8,208,256]{2,1,0:T(8,128)(2,1)} collective-permute-done((bf16[8,208,256]{2,1,0:T(8,128)(2,1)}, bf16[8,208,256]{2,1,0:T(8,128)(2,1)}, u32[]{:S(2)}, u32[]{:S(2)}) %collective-permute-start.4) | collective-permute-done | bytes 852000 | tf_op jit(solution)/shard_map/ppermute | solution.py:404
  69.1 1.5 copy.46
  70.6 1.7 copy.45
  75.3 18.9 %mixer_forward.1 = (bf16[1024,1024]{1,0:T(8,128)(2,1)}, f32[1024,1024]{1,0:T(8,128)}, bf16[1024,1024]{1,0:T(8,128)(2,1)}, bf16[1024,1024]{1,0:T(8,128)(2,1)}, bf...) custom-call(s32[32]{0:T(128)} %dynamic-slice_bitcast_fusion.1.dev_ref, ...), custom_call_target="tpu_custom_call" | custom-call | flops 3221225472 | bytes 16777216 | tf_op jit(solution)/shard_map/mixer_forward/pallas_call | solution.py:500
  94.2 35.2 %feed_forward.1 = (bf16[1024,512]{1,0:T(8,128)(2,1)}, f32[1024,512]{1,0:T(8,128)}, bf16[1024,512]{1,0:T(8,128)(2,1)}, bf16[1024,512]{1,0:T(8,128)(2,1)}, f32[32,...) custom-call(s32[32]{0:T(128)} %dynamic-slice_bitcast_fusion.1.dev_ref, ...), custom_call_target="tpu_custom_call" | custom-call | flops 15032385536 | bytes 25165824 | tf_op jit(solution)/shard_map/feed_forward/pallas_call | solution.py:520
  129.4 18.2 %mixer_backward.1 = (bf16[1024,1024]{1,0:T(8,128)(2,1)}, bf16[1024,1024]{1,0:T(8,128)(2,1)}, bf16[1024,1024]{1,0:T(8,128)(2,1)}, bf16[16,208,256]{2,1,0:T(8,128)(2,1)}, bf16[16,208,256]{2,1,0:T(8,128)(2,1)}) custom-call(s32[32]{0:T(128)} %dynamic-slice_bitcast_fusion.1.dev_ref, bf16[1024,512]{1,0:T(8,128)(2,1)} %get-tuple-element.34.dmix_ref, ...), custom_call_target="tpu_custom_call" | custom-call | flops 4294967296 | bytes 25165824 | tf_op jit(solution)/shard_map/mixer_backward/pallas_call | solution.py:554
  148.2 3.4 %collective-permute-done.14 = bf16[16,208,256]{2,1,0:T(8,128)(2,1)S(1)} collective-permute-done((bf16[16,208,256]{2,1,0:T(8,128)(2,1)}, bf16[16,208,256]{2,1,0:T(8,128)(2,1)S(1)}, u32[]{:S(2)}, u32[]{:S(2)}) %collective-permute-start.14) | collective-permute-done | bytes 1703968 | tf_op jit(solution)/shard_map/ppermute | solution.py:404
  151.6 2.0 add_convert_fusion.3
  153.6 1.6 collective-permute-start.15
  155.2 11.2 %collective-permute-done.15 = bf16[8,208,256]{2,1,0:T(8,128)(2,1)S(1)} collective-permute-done((bf16[8,208,256]{2,1,0:T(8,128)(2,1)S(1)}, bf16[8,208,256]{2,1,0:T(8,128)(2,1)S(1)}, u32[]{:S(2)}, u32[]{:S(2)}) %collective-permute-start.15) | collective-permute-done | bytes 852000 | tf_op jit(solution)/shard_map/ppermute | solution.py:404
  166.5 1.5 collective-permute-start.16
  168.0 1.9 add_convert_fusion.1
  169.9 1.5 collective-permute-start.21
  171.5 5.8 %collective-permute-done.16 = bf16[4,208,256]{2,1,0:T(8,128)(2,1)S(1)} collective-permute-done((bf16[4,208,256]{2,1,0:T(8,128)(2,1)S(1)}, bf16[4,208,256]{2,1,0:T(8,128)(2,1)S(1)}, u32[]{:S(2)}, u32[]{:S(2)}) %collective-permute-start.16) | collective-permute-done | bytes 426016 | tf_op jit(solution)/shard_map/ppermute | solution.py:404
  177.4 2.4 %collective-permute-start.17 = (bf16[208,256]{1,0:T(8,128)(2,1)S(1)}, bf16[208,256]{1,0:T(8,128)(2,1)S(1)}, u32[]{:S(2)}, u32[]{:S(2)}) collective-permute-start(bf16[208,256]{1,0:T(8,128)(2,1)S(1)} %get-tuple-element.56), channel_id=1, source_target_pairs={{0,8},{1,9},{2,10},{3,11},{4,12},{5,13},{6,14},{7,15},{8,0},{9,1},... | collective-permute-start | bytes 319496 | tf_op jit(solution)/shard_map/ppermute | solution.py:404
  182.4 9.1 %input_gradient.1 = f32[1024,512]{1,0:T(8,128)} custom-call(bf16[1024,512]{1,0:T(8,128)(2,1)} %bitcast.113, f32[1024,512]{1,0:T(8,128)} %get-tuple-element.33.dy1_ref, f32[2,512]{1,0:T(2,128)} %get-tuple-element.31.gain_ref, bf16[1024,1024]{1,0:T(8,128)(2,1)} %get-tuple-element.41.df_ref, bf16[1024,1024]{1,0:T(8,128)(2,1)} %get-tuple-element.42.di_ref, ...), custom_call_target="tpu_custom_call" | custom-call | flops 3221225472 | bytes 16777216 | tf_op jit(solution)/shard_map/input_gradient/pallas_call | solution.py:568
  191.5 4.2 %copy.30 = f32[8,128,512]{2,1,0:T(8,128)} copy(f32[8,128,512]{2,0,1:T(8,128)} %bitcast.110) | data formatting | bytes 4194304 | tf_op jit(solution)/shard_map/transpose | solution.py:455
  197.4 1.5 collective-permute-start.22
  200.3 7.7 %collective-permute-done.22 = bf16[4,160,512]{2,1,0:T(8,128)(2,1)S(1)} collective-permute-done((bf16[4,160,512]{2,1,0:T(8,128)(2,1)S(1)}, bf16[4,160,512]{2,1,0:T(8,128)(2,1)S(1)}, u32[]{:S(2)}, u32[]{:S(2)}) %collective-permute-start.22) | collective-permute-done | bytes 655392 | tf_op jit(solution)/shard_map/ppermute | solution.py:404
  209.4 2.0 collective-permute-start.24
  211.4 1.4 collective-permute-start.25
  214.3 5.1 %collective-permute-done.24 = bf16[160,512]{1,0:T(8,128)(2,1)S(1)} collective-permute-done((bf16[160,512]{1,0:T(8,128)(2,1)S(1)}, bf16[160,512]{1,0:T(8,128)(2,1)S(1)}, u32[]{:S(2)}, u32[]{:S(2)}) %collective-permute-start.24) | collective-permute-done | bytes 163872 | tf_op jit(solution)/shard_map/ppermute | solution.py:404
  (97 shorter events, 24.5 us)
Async XLA Ops:
  3.9 11.7 %collective-permute-start = (bf16[208,256]{1,0:T(8,128)(2,1)S(1)}, bf16[208,256]{1,0:T(8,128)(2,1)S(1)}, u32[]{:S(2)}, u32[]{:S(2)}) collective-permute-start(bf16[208,256]{1,0:T(8,128)(2,1)S(1)} %concatenate.18), channel_id=1, source_target_pairs={{0,8},{1,9},{2,10},{3,11},{4,12},{5,13},{6,14},{7,15},{8,0},{9,1},... | collective-permute-start | bytes 319496 | tf_op jit(solution)/shard_map/ppermute | solution.py:404
  7.0 11.2 %collective-permute-start.1 = (bf16[208,256]{1,0:T(8,128)(2,1)S(1)}, bf16[208,256]{1,0:T(8,128)(2,1)S(1)}, u32[]{:S(2)}, u32[]{:S(2)}) collective-permute-start(bf16[208,256]{1,0:T(8,128)(2,1)S(1)} %concatenate.18), channel_id=1, source_target_pairs={{0,16},{1,17},{2,18},{3,19},{4,20},{5,21},{6,22},{7,23},{8,24},{9,... | collective-permute-start | bytes 319496 | tf_op jit(solution)/shard_map/ppermute | solution.py:404
  9.5 8.6 %collective-permute-start.2 = (bf16[208,256]{1,0:T(8,128)(2,1)S(1)}, bf16[208,256]{1,0:T(8,128)(2,1)S(1)}, u32[]{:S(2)}, u32[]{:S(2)}) collective-permute-start(bf16[208,256]{1,0:T(8,128)(2,1)S(1)} %concatenate.18), channel_id=1, source_target_pairs={{0,24},{1,25},{2,26},{3,27},{4,28},{5,29},{6,30},{7,31},{8,16},{9,... | collective-permute-start | bytes 319496 | tf_op jit(solution)/shard_map/ppermute | solution.py:404
  10.5 9.4 %collective-permute-start.7 = (bf16[160,512]{1,0:T(8,128)(2,1)S(1)}, bf16[160,512]{1,0:T(8,128)(2,1)S(1)}, u32[]{:S(2)}, u32[]{:S(2)}) collective-permute-start(bf16[160,512]{1,0:T(8,128)(2,1)S(1)} %get-tuple-element.65), channel_id=1, source_target_pairs={{0,8},{1,9},{2,10},{3,11},{4,12},{5,13},{6,14},{7,15},{8,0},{9,1},... | collective-permute-start | bytes 491528 | tf_op jit(solution)/shard_map/ppermute | solution.py:404
  11.4 19.5 %collective-permute-start.8 = (bf16[160,512]{1,0:T(8,128)(2,1)S(1)}, bf16[160,512]{1,0:T(8,128)(2,1)S(1)}, u32[]{:S(2)}, u32[]{:S(2)}) collective-permute-start(bf16[160,512]{1,0:T(8,128)(2,1)S(1)} %get-tuple-element.65), channel_id=1, source_target_pairs={{0,16},{1,17},{2,18},{3,19},{4,20},{5,21},{6,22},{7,23},{8,24},{9,... | collective-permute-start | bytes 491528 | tf_op jit(solution)/shard_map/ppermute | solution.py:404
  15.6 15.3 %collective-permute-start.9 = (bf16[160,512]{1,0:T(8,128)(2,1)S(1)}, bf16[160,512]{1,0:T(8,128)(2,1)S(1)}, u32[]{:S(2)}, u32[]{:S(2)}) collective-permute-start(bf16[160,512]{1,0:T(8,128)(2,1)S(1)} %get-tuple-element.65), channel_id=1, source_target_pairs={{0,24},{1,25},{2,26},{3,27},{4,28},{5,29},{6,30},{7,31},{8,16},{9,... | collective-permute-start | bytes 491528 | tf_op jit(solution)/shard_map/ppermute | solution.py:404
  18.2 27.5 %collective-permute-start.3 = (bf16[4,208,256]{2,1,0:T(8,128)(2,1)S(1)}, bf16[4,208,256]{2,1,0:T(8,128)(2,1)S(1)}, u32[]{:S(2)}, u32[]{:S(2)}) collective-permute-start(bf16[4,208,256]{2,1,0:T(8,128)(2,1)S(1)} %pad_maximum_fusion.1), channel_id=1, source_target_pairs={{0,4},{1,3},{2,6},{3,1},{4,0},{5,7},{6,2},{7,5},{8,12},{9,11},{10,... | collective-permute-start | bytes 1277960 | tf_op jit(solution)/shard_map/ppermute | solution.py:404
  31.0 11.1 %collective-permute-start.10 = (bf16[4,160,512]{2,1,0:T(8,128)(2,1)S(1)}, bf16[4,160,512]{2,1,0:T(8,128)(2,1)S(1)}, u32[]{:S(2)}, u32[]{:S(2)}) collective-permute-start(bf16[4,160,512]{2,1,0:T(8,128)(2,1)S(1)} %pad_maximum_fusion), channel_id=1, source_target_pairs={{0,4},{1,3},{2,6},{3,1},{4,0},{5,7},{6,2},{7,5},{8,12},{9,11},{10,... | collective-permute-start | bytes 1966088 | tf_op jit(solution)/shard_map/ppermute | solution.py:404
  32.6 36.4 %copy-start.1 = (bf16[1024,512]{1,0:T(8,128)(2,1)S(1)}, bf16[1024,512]{1,0:T(8,128)(2,1)}, u32[]{:S(2)}) copy-start(bf16[1024,512]{1,0:T(8,128)(2,1)} %param.13) | copy-start | bytes 3145732
  42.1 28.5 %copy-start.10 = (bf16[8,160,512]{2,1,0:T(8,128)(2,1)}, bf16[8,160,512]{2,1,0:T(8,128)(2,1)S(1)}, u32[]{:S(2)}) copy-start(bf16[8,160,512]{2,1,0:T(8,128)(2,1)S(1)} %constant_dynamic-update-slice_fusion.5.g0) | copy-start | bytes 3932164
  42.1 17.8 %collective-permute-start.11 = (bf16[8,160,512]{2,1,0:T(8,128)(2,1)S(1)}, bf16[8,160,512]{2,1,0:T(8,128)(2,1)}, u32[]{:S(2)}, u32[]{:S(2)}) collective-permute-start(bf16[8,160,512]{2,1,0:T(8,128)(2,1)S(1)} %constant_dynamic-update-slice_fusion.5.g0), channel_id=1, source_target_pairs={{0,2},{1,5},{2,0},{3,7},{4,6},{5,1},{6,4},{7,3},{8,10},{9,13},{10,... | collective-permute-start | bytes 3932168 | tf_op jit(solution)/shard_map/ppermute | solution.py:404
  45.6 25.0 %copy-start.2 = (bf16[1024,512]{1,0:T(8,128)(2,1)S(1)}, bf16[1024,512]{1,0:T(8,128)(2,1)}, u32[]{:S(2)}) copy-start(bf16[1024,512]{1,0:T(8,128)(2,1)} %param.23) | copy-start | bytes 3145732
  46.5 22.6 %collective-permute-start.4 = (bf16[8,208,256]{2,1,0:T(8,128)(2,1)}, bf16[8,208,256]{2,1,0:T(8,128)(2,1)}, u32[]{:S(2)}, u32[]{:S(2)}) collective-permute-start(bf16[8,208,256]{2,1,0:T(8,128)(2,1)} %constant_dynamic-update-slice_fusion.g0), channel_id=1, source_target_pairs={{0,2},{1,5},{2,0},{3,7},{4,6},{5,1},{6,4},{7,3},{8,10},{9,13},{10,... | collective-permute-start | bytes 2555912 | tf_op jit(solution)/shard_map/ppermute | solution.py:404
  47.0 47.2 %collective-permute-start.12 = (bf16[8,160,512]{2,1,0:T(8,128)(2,1)S(1)}, bf16[8,160,512]{2,1,0:T(8,128)(2,1)}, u32[]{:S(2)}, u32[]{:S(2)}) collective-permute-start(bf16[8,160,512]{2,1,0:T(8,128)(2,1)S(1)} %constant_dynamic-update-slice_fusion.5.g0), channel_id=1, source_target_pairs={{0,1},{1,0},{2,3},{3,2},{4,5},{5,4},{6,7},{7,6},{8,9},{9,8},{10,11... | collective-permute-start | bytes 3932168 | tf_op jit(solution)/shard_map/ppermute | solution.py:404
  59.9 34.3 %collective-permute-start.13 = (bf16[8,160,512]{2,1,0:T(8,128)(2,1)}, bf16[8,160,512]{2,1,0:T(8,128)(2,1)}, u32[]{:S(2)}, u32[]{:S(2)}) collective-permute-start(bf16[8,160,512]{2,1,0:T(8,128)(2,1)} %collective-permute-done.11.g1), channel_id=1, source_target_pairs={{0,1},{1,0},{2,3},{3,2},{4,5},{5,4},{6,7},{7,6},{8,9},{9,8},{10,11... | collective-permute-start | bytes 3932168 | tf_op jit(solution)/shard_map/ppermute | solution.py:404
  59.9 15.3 %collective-permute-start.5 = (bf16[8,208,256]{2,1,0:T(8,128)(2,1)}, bf16[8,208,256]{2,1,0:T(8,128)(2,1)}, u32[]{:S(2)}, u32[]{:S(2)}) collective-permute-start(bf16[8,208,256]{2,1,0:T(8,128)(2,1)} %constant_dynamic-update-slice_fusion.g0), channel_id=1, source_target_pairs={{0,1},{1,0},{2,3},{3,2},{4,5},{5,4},{6,7},{7,6},{8,9},{9,8},{10,11... | collective-permute-start | bytes 2555912 | tf_op jit(solution)/shard_map/ppermute | solution.py:404
  69.0 6.2 %collective-permute-start.6 = (bf16[8,208,256]{2,1,0:T(8,128)(2,1)}, bf16[8,208,256]{2,1,0:T(8,128)(2,1)}, u32[]{:S(2)}, u32[]{:S(2)}) collective-permute-start(bf16[8,208,256]{2,1,0:T(8,128)(2,1)} %collective-permute-done.4.g1), channel_id=1, source_target_pairs={{0,1},{1,0},{2,3},{3,2},{4,5},{5,4},{6,7},{7,6},{8,9},{9,8},{10,11... | collective-permute-start | bytes 2555912 | tf_op jit(solution)/shard_map/ppermute | solution.py:404
  147.6 4.0 %collective-permute-start.14 = (bf16[16,208,256]{2,1,0:T(8,128)(2,1)}, bf16[16,208,256]{2,1,0:T(8,128)(2,1)S(1)}, u32[]{:S(2)}, u32[]{:S(2)}) collective-permute-start(bf16[16,208,256]{2,1,0:T(8,128)(2,1)} %get-tuple-element.46), channel_id=1, source_target_pairs={{0,1},{1,0},{2,3},{3,2},{4,5},{5,4},{6,7},{7,6},{8,9},{9,8},{10,11... | collective-permute-start | bytes 5111816 | tf_op jit(solution)/shard_map/ppermute | solution.py:404
  148.2 19.9 %collective-permute-start.20 = (bf16[16,160,512]{2,1,0:T(8,128)(2,1)}, bf16[16,160,512]{2,1,0:T(8,128)(2,1)S(1)}, u32[]{:S(2)}, u32[]{:S(2)}) collective-permute-start(bf16[16,160,512]{2,1,0:T(8,128)(2,1)} %get-tuple-element.48), channel_id=1, source_target_pairs={{0,1},{1,0},{2,3},{3,2},{4,5},{5,4},{6,7},{7,6},{8,9},{9,8},{10,11... | collective-permute-start | bytes 7864328 | tf_op jit(solution)/shard_map/ppermute | solution.py:404
  151.6 16.4 %copy-start = (bf16[16,160,512]{2,1,0:T(8,128)(2,1)S(1)}, bf16[16,160,512]{2,1,0:T(8,128)(2,1)}, u32[]{:S(2)}) copy-start(bf16[16,160,512]{2,1,0:T(8,128)(2,1)} %get-tuple-element.47) | copy-start | bytes 7864324
  153.6 12.8 %collective-permute-start.15 = (bf16[8,208,256]{2,1,0:T(8,128)(2,1)S(1)}, bf16[8,208,256]{2,1,0:T(8,128)(2,1)S(1)}, u32[]{:S(2)}, u32[]{:S(2)}) collective-permute-start(bf16[8,208,256]{2,1,0:T(8,128)(2,1)S(1)} %get-tuple-element.52), channel_id=1, source_target_pairs={{0,2},{1,5},{2,0},{3,7},{4,6},{5,1},{6,4},{7,3},{8,10},{9,13},{10,... | collective-permute-start | bytes 2555912 | tf_op jit(solution)/shard_map/ppermute | solution.py:404
  166.5 10.8 %collective-permute-start.16 = (bf16[4,208,256]{2,1,0:T(8,128)(2,1)S(1)}, bf16[4,208,256]{2,1,0:T(8,128)(2,1)S(1)}, u32[]{:S(2)}, u32[]{:S(2)}) collective-permute-start(bf16[4,208,256]{2,1,0:T(8,128)(2,1)S(1)} %add_convert_fusion.8), channel_id=1, source_target_pairs={{0,4},{1,3},{2,6},{3,1},{4,0},{5,7},{6,2},{7,5},{8,12},{9,11},{10,... | collective-permute-start | bytes 1277960 | tf_op jit(solution)/shard_map/ppermute | solution.py:404
  169.9 27.2 %collective-permute-start.21 = (bf16[8,160,512]{2,1,0:T(8,128)(2,1)}, bf16[8,160,512]{2,1,0:T(8,128)(2,1)S(1)}, u32[]{:S(2)}, u32[]{:S(2)}) collective-permute-start(bf16[8,160,512]{2,1,0:T(8,128)(2,1)} %get-tuple-element.50), channel_id=1, source_target_pairs={{0,2},{1,5},{2,0},{3,7},{4,6},{5,1},{6,4},{7,3},{8,10},{9,13},{10,... | collective-permute-start | bytes 3932168 | tf_op jit(solution)/shard_map/ppermute | solution.py:404
  177.4 19.5 %collective-permute-start.17 = (bf16[208,256]{1,0:T(8,128)(2,1)S(1)}, bf16[208,256]{1,0:T(8,128)(2,1)S(1)}, u32[]{:S(2)}, u32[]{:S(2)}) collective-permute-start(bf16[208,256]{1,0:T(8,128)(2,1)S(1)} %get-tuple-element.56), channel_id=1, source_target_pairs={{0,8},{1,9},{2,10},{3,11},{4,12},{5,13},{6,14},{7,15},{8,0},{9,1},... | collective-permute-start | bytes 319496 | tf_op jit(solution)/shard_map/ppermute | solution.py:404
  179.8 17.1 %collective-permute-start.18 = (bf16[208,256]{1,0:T(8,128)(2,1)S(1)}, bf16[208,256]{1,0:T(8,128)(2,1)S(1)}, u32[]{:S(2)}, u32[]{:S(2)}) collective-permute-start(bf16[208,256]{1,0:T(8,128)(2,1)S(1)} %get-tuple-element.58), channel_id=1, source_target_pairs={{0,16},{1,17},{2,18},{3,19},{4,20},{5,21},{6,22},{7,23},{8,24},{9,... | collective-permute-start | bytes 319496 | tf_op jit(solution)/shard_map/ppermute | solution.py:404
  181.0 16.0 %collective-permute-start.19 = (bf16[208,256]{1,0:T(8,128)(2,1)S(1)}, bf16[208,256]{1,0:T(8,128)(2,1)S(1)}, u32[]{:S(2)}, u32[]{:S(2)}) collective-permute-start(bf16[208,256]{1,0:T(8,128)(2,1)S(1)} %get-tuple-element.57), channel_id=1, source_target_pairs={{0,24},{1,25},{2,26},{3,27},{4,28},{5,29},{6,30},{7,31},{8,16},{9,... | collective-permute-start | bytes 319496 | tf_op jit(solution)/shard_map/ppermute | solution.py:404
  197.1 11.2 %copy-start.4 = (f32[4,2,8,256]{3,2,0,1:T(8,128)}, f32[4,2,8,256]{3,2,0,1:T(8,128)S(1)}, u32[]{:S(2)}) copy-start(f32[4,2,8,256]{3,2,0,1:T(8,128)S(1)} %copy.38) | copy-start | bytes 196612
  197.4 10.7 %collective-permute-start.22 = (bf16[4,160,512]{2,1,0:T(8,128)(2,1)S(1)}, bf16[4,160,512]{2,1,0:T(8,128)(2,1)S(1)}, u32[]{:S(2)}, u32[]{:S(2)}) collective-permute-start(bf16[4,160,512]{2,1,0:T(8,128)(2,1)S(1)} %add_convert_fusion.5), channel_id=1, source_target_pairs={{0,4},{1,3},{2,6},{3,1},{4,0},{5,7},{6,2},{7,5},{8,12},{9,11},{10,... | collective-permute-start | bytes 1966088 | tf_op jit(solution)/shard_map/ppermute | solution.py:404
  200.3 12.5 %copy-start.11 = (bf16[16]{0:T(256)(128)(2,1)S(1)}, bf16[16]{0:T(256)(128)(2,1)}, u32[]{:S(2)}) copy-start(bf16[16]{0:T(256)(128)(2,1)} %param.14) | copy-start | bytes 100
  208.4 5.9 %collective-permute-start.23 = (bf16[160,512]{1,0:T(8,128)(2,1)S(1)}, bf16[160,512]{1,0:T(8,128)(2,1)S(1)}, u32[]{:S(2)}, u32[]{:S(2)}) collective-permute-start(bf16[160,512]{1,0:T(8,128)(2,1)S(1)} %get-tuple-element.53), channel_id=1, source_target_pairs={{0,8},{1,9},{2,10},{3,11},{4,12},{5,13},{6,14},{7,15},{8,0},{9,1},... | collective-permute-start | bytes 491528 | tf_op jit(solution)/shard_map/ppermute | solution.py:404
  209.4 10.0 %collective-permute-start.24 = (bf16[160,512]{1,0:T(8,128)(2,1)S(1)}, bf16[160,512]{1,0:T(8,128)(2,1)S(1)}, u32[]{:S(2)}, u32[]{:S(2)}) collective-permute-start(bf16[160,512]{1,0:T(8,128)(2,1)S(1)} %get-tuple-element.55), channel_id=1, source_target_pairs={{0,16},{1,17},{2,18},{3,19},{4,20},{5,21},{6,22},{7,23},{8,24},{9,... | collective-permute-start | bytes 491528 | tf_op jit(solution)/shard_map/ppermute | solution.py:404
  211.4 8.0 %collective-permute-start.25 = (bf16[160,512]{1,0:T(8,128)(2,1)S(1)}, bf16[160,512]{1,0:T(8,128)(2,1)S(1)}, u32[]{:S(2)}, u32[]{:S(2)}) collective-permute-start(bf16[160,512]{1,0:T(8,128)(2,1)S(1)} %get-tuple-element.54), channel_id=1, source_target_pairs={{0,24},{1,25},{2,26},{3,27},{4,28},{5,29},{6,30},{7,31},{8,16},{9,... | collective-permute-start | bytes 491528 | tf_op jit(solution)/shard_map/ppermute | solution.py:404
  (6 other events, 32.3 us)

commit v2 on v1

v2 whole, which is shorter than its diff:
```python
import functools

import jax
import jax.numpy as jnp
import numpy as np
from jax import lax
from jax.experimental import pallas as pl
from jax.experimental.pallas import tpu as pltpu
from jax.sharding import PartitionSpec as P

LEN = 1024
EPSILON = 1e-06
AXES = ("dp", "mp")
SLOTS = 32
CHUNKS = 8
LANES = 256
GROUP = 8
BF = jnp.bfloat16
F32 = jnp.float32
VMEM_LIMIT = 60 * 1024 * 1024
C0 = 0.7978845608028654
C1 = C0 * 0.044715


def params():
    return pltpu.CompilerParams(vmem_limit_bytes=VMEM_LIMIT)


def dot(a, b, dims=((1,), (0,))):
    return lax.dot_general(a, b, (dims, ((), ())), preferred_element_type=F32)


def whole(shape):
    return pl.BlockSpec(shape, lambda *_: (0,) * len(shape), pipeline_mode=pl.Buffered(1))


def aligned(start, size):
    return pl.ds(pl.multiple_of(start, size), size)


def spread(small, offset, piece, width):
    lane = lax.broadcasted_iota(jnp.int32, (LANES, width), 0)
    column = lax.broadcasted_iota(jnp.int32, (LANES, width), 1)
    pick = (lane == offset + column % piece).astype(BF)
    placed = dot(small.astype(BF), pick)
    row = lax.broadcasted_iota(jnp.int32, (SLOTS, width), 0)
    col = lax.broadcasted_iota(jnp.int32, (SLOTS, width), 1)
    return jnp.sum(jnp.where(col // piece == row, placed, 0.0), axis=0, keepdims=True)


def collect(vector, offset, piece):
    width = vector.shape[1]
    row = lax.broadcasted_iota(jnp.int32, (SLOTS, width), 0)
    col = lax.broadcasted_iota(jnp.int32, (SLOTS, width), 1)
    kept = jnp.where(col // piece == row, vector, 0.0).astype(BF)
    column = lax.broadcasted_iota(jnp.int32, (width, LANES), 0)
    lane = lax.broadcasted_iota(jnp.int32, (width, LANES), 1)
    pick = (lane == offset + column % piece).astype(BF)
    return dot(kept, pick)


def pack_mixer(forget_ref, input_ref, cand_ref, small_ref, out_ref):
    blocks = forget_ref.shape[1] // LANES
    for b in range(blocks):
        for w, ref in enumerate((forget_ref, input_ref, cand_ref)):
            at = (b * 3 + w) * 16
            out_ref[at : at + 16, :] = ref[:, b * LANES : (b + 1) * LANES]
    row = lax.broadcasted_iota(jnp.int32, (16, LANES), 0)
    out_ref[48 * blocks :, :] = jnp.where(row == 0, small_ref[...].astype(F32), 0.0).astype(BF)


def mixer_prepare(dev_ref, parts, x_ref, xn_ref, xnt_ref, gain_ref, bias_s, small):
    per = SLOTS // 4
    tail = parts[0].shape[1] - 16
    for s in range(SLOTS):
        row = parts[s // per][s % per, tail : tail + 16, :].astype(F32)
        small[pl.ds(dev_ref[s], 1), :] = row[0:1, :]
    values = small[...]
    width, chans = x_ref.shape[1], bias_s.shape[1]
    piece = width // SLOTS
    gmix = spread(values, 0, piece, width)
    gain_ref[0:1, :] = gmix
    gain_ref[1:2, :] = spread(values, piece, piece, width)
    bias_s[...] = spread(values, 2 * piece, chans // SLOTS, chans)

    def rows(i, _):
        at = aligned(i * 256, 256)
        v = x_ref[at, :].astype(F32)
        scale = lax.rsqrt(jnp.mean(v * v, axis=-1, keepdims=True) + EPSILON)
        xn = ((v * scale) * gmix).astype(BF)
        xn_ref[at, :] = xn
        xnt_ref[:, at] = xn.T
        return 0

    lax.fori_loop(0, x_ref.shape[0] // 256, rows, 0)


def mixer_forward(dev_ref, x_ref, g0, g1, g2, g3, hb_ref, f_ref, u1_ref, u2_ref, w_ref, xnt_ref, gain_ref,
                  small, bias_s, xn_s, k_s, c2_s):
    step = pl.program_id(0)
    per = SLOTS // 4
    parts = (g0, g1, g2, g3)

    @pl.when(step == 0)
    def _():
        mixer_prepare(dev_ref, parts, x_ref, xn_s, xnt_ref, gain_ref, bias_s, small)

    for s in range(SLOTS):
        d = dev_ref[s]
        for w in range(3):
            src = aligned((step * 3 + w) * 16, 16)
            w_ref[aligned(d * 16, 16), w * LANES : (w + 1) * LANES] = parts[s // per][s % per, src, :]

    bias = bias_s[:, aligned(step * LANES, LANES)]
    k_s[...] = dot(xn_s[...], w_ref[...])
    kf_c, ki_c, kc_c = (slice(w * LANES, (w + 1) * LANES) for w in range(3))
    zeros = jnp.zeros((CHUNKS, LANES), F32)
    tile = GROUP * CHUNKS
    count = xn_s.shape[0] // tile

    def first(i, carry):
        h, prod = carry
        at = aligned(i * tile, tile)
        kf = k_s[at, kf_c]
        ki = k_s[at, ki_c] + bias
        kc = k_s[at, kc_c]
        p = jnp.exp(-jnp.abs(kf))
        q = jnp.exp(-jnp.abs(ki))
        w = jnp.minimum(ki, 0.0) - jnp.minimum(kf, 0.0)
        e = jnp.exp(-jnp.abs(w))
        low = w <= 0.0
        a_part = jnp.where(low, 1.0, e)
        b_part = jnp.where(low, e, 1.0)
        a = a_part * (1.0 + q)
        b = b_part * (1.0 + p)
        inv = 1.0 / (a + b)
        forget = a * inv
        other = b * inv
        f_ref[at, :] = forget
        drive = other * kc
        k_s[at, kf_c] = forget * (inv * (b_part * jnp.where(kf >= 0.0, p, 1.0)))
        k_s[at, ki_c] = -other * (inv * (a_part * jnp.where(ki >= 0.0, q, 1.0)))
        c2_s[at, :] = drive
        for k in range(GROUP):
            part = slice(k * CHUNKS, (k + 1) * CHUNKS)
            h = forget[part] * h + drive[part]
            prod = prod * forget[part]
        return h, prod

    last, prod = lax.fori_loop(0, count, first, (zeros, zeros + 1.0))
    sub = lax.broadcasted_iota(jnp.int32, (CHUNKS, LANES), 0)
    start = zeros
    for s in range(CHUNKS - 1):
        moved = pltpu.roll(last + prod * start, 1, 0)
        start = jnp.where(sub == s + 1, moved, start)

    def second(i, h):
        at = aligned(i * tile, tile)
        forget = f_ref[at, :]
        drive = c2_s[at, :]
        before, after = [], []
        for k in range(GROUP):
            part = slice(k * CHUNKS, (k + 1) * CHUNKS)
            before.append(h)
            h = forget[part] * h + drive[part]
            after.append(h)
        diff = jnp.concatenate(before, axis=0) - k_s[at, kc_c]
        hb_ref[at, :] = jnp.concatenate(after, axis=0).astype(BF)
        u1_ref[at, :] = (k_s[at, kf_c] * diff).astype(BF)
        u2_ref[at, :] = (k_s[at, ki_c] * diff).astype(BF)
        return h

    lax.fori_loop(0, count, second, start)


def feed_forward(dev_ref, slot_ref, cols_ref, gain_ref, g0, g1, g2, g3, hb_hbm, x_hbm, dy_hbm,
                 out_hbm, dy1_hbm, dmix_hbm, wo_hbm, keep_hbm, send_hbm, small_ref,
                 outs_in, feed_in, hb_s, x_s, dy_s, wo_s, y1_s, xn_s, xnt_s, dyt_s, acc_s, dxn_s, up_s, dn_s,
                 pieces, out_s, dy1_s, dmix_s, sems):
    parts = (g0, g1, g2, g3)
    per = SLOTS // 4
    half = SLOTS // 2
    tokens, width = x_s.shape
    chans = hb_s.shape[1]
    rows = up_s.shape[0] // 8
    feed = 2 * rows
    used = []

    def copy(src, dst):
        used.append(pltpu.make_async_copy(src, dst, sems.at[len(used)]))
        used[-1].start()
        return used[-1]

    wait_out = [copy(parts[k].at[:, feed:, :], outs_in.at[pl.ds(k * per, per)]) for k in range(4)]
    wait_mix = [copy(hb_hbm, hb_s), copy(x_hbm, x_s)]
    wait_feed = [copy(parts[k].at[:, :feed, :], feed_in.at[pl.ds(k * per, per)]) for k in range(2)]
    wait_dy = copy(dy_hbm, dy_s)
    wait_more = [copy(parts[k].at[:, :feed, :], feed_in.at[pl.ds(k * per, per)]) for k in range(2, 4)]

    for c in wait_out:
        c.wait()
    for s in range(SLOTS):
        wo_s[aligned(dev_ref[s] * 32, 32), :] = outs_in[s]
    finish = [copy(wo_s, wo_hbm)]
    for c in wait_mix:
        c.wait()
    gain = gain_ref[1:2, :]

    def rows_in(i, _):
        at = aligned(i * 256, 256)
        y1 = x_s[at, :].astype(F32) + dot(hb_s[at, :], wo_s[...])
        y1_s[at, :] = y1
        scale = lax.rsqrt(jnp.mean(y1 * y1, axis=-1, keepdims=True) + EPSILON)
        xn = ((y1 * scale) * gain).astype(BF)
        xn_s[at, :] = xn
        xnt_s[:, at] = xn.T
        return 0

    lax.fori_loop(0, tokens // 256, rows_in, 0)
    wait_dy.wait()
    dyt_s[...] = dy_s[...].T

    for group in range(4):
        for c in {0: wait_feed, 2: wait_more}.get(group, ()):
            c.wait()
        block = cols_ref[group]
        for r in range(8):
            s = slot_ref[r * 4 + block]
            up_s[r * rows : (r + 1) * rows, :] = feed_in[s, 0:rows, :]
            dn_s[r * rows : (r + 1) * rows, :] = feed_in[s, rows:feed, :]
        pre = dot(xn_s[...], up_s[...])
        dact = dot(dy_s[...], dn_s[...])
        sq = pre * pre
        gate = 0.5 + 0.5 * jnp.tanh(pre * (C0 + C1 * sq))
        value = pre * gate
        act = value.astype(BF)
        slope = gate + value * (1.0 - gate) * (2.0 * C0 + 6.0 * C1 * sq)
        dpre = (slope * dact).astype(BF)
        upg = dot(xnt_s[...], dpre).astype(BF)
        dng = dot(dyt_s[...], act).astype(BF)
        for r in range(8):
            s = slot_ref[r * 4 + block]
            pieces[s, 0:rows, :] = upg[r * rows : (r + 1) * rows]
            pieces[s, rows:feed, :] = dng[r * rows : (r + 1) * rows]
        if group == 1:
            finish.append(copy(pieces.at[:half, :feed, :], keep_hbm.at[:, :feed, :]))
        if group == 3:
            finish.append(copy(pieces.at[half:, :feed, :], send_hbm.at[:, :feed, :]))
        out = dot(act, dn_s[...], ((1,), (1,)))
        dxn = dot(dpre, up_s[...], ((1,), (1,)))
        if group == 0:
            acc_s[...] = out
            dxn_s[...] = dxn
        else:
            acc_s[...] += out
            dxn_s[...] += dxn

    total = jnp.zeros((1, width), F32)
    for i in range(tokens // 256):
        at = slice(i * 256, (i + 1) * 256)
        y1 = y1_s[at, :]
        scale = lax.rsqrt(jnp.mean(y1 * y1, axis=-1, keepdims=True) + EPSILON)
        n2 = y1 * scale
        out_s[at, :] = (y1 + acc_s[at, :]).astype(BF)
        dxn = dxn_s[at, :]
        dn = dxn * gain
        dy1 = dy_s[at, :].astype(F32) + scale * (dn - n2 * jnp.mean(dn * n2, axis=-1, keepdims=True))
        dy1_s[at, :] = dy1
        dmix_s[at, :] = dy1.astype(BF)
        total = total + jnp.sum(dxn * n2, axis=0, keepdims=True)
    finish += [copy(out_s, out_hbm), copy(dy1_s, dy1_hbm), copy(dmix_s, dmix_hbm)]
    small_ref[...] = collect(total, 0, width // SLOTS)

    span = 256
    for b in range(chans // span):
        grad = dot(hb_s[:, b * span : (b + 1) * span], dmix_s[...], ((0,), (0,))).astype(BF)
        for r in range(span // 32):
            pieces[slot_ref[b * (span // 32) + r], feed:, :] = grad[r * 32 : (r + 1) * 32]
    finish.append(copy(pieces.at[:half, feed:, :], keep_hbm.at[:, feed:, :]))
    finish.append(copy(pieces.at[half:, feed:, :], send_hbm.at[:, feed:, :]))
    for c in finish:
        c.wait()


def mixer_backward(dev_ref, dmix_ref, xnt_ref, wo_ref, small_ref, f_ref, u1_ref, u2_ref,
                   dk_ref, keep_ref, send_ref, bias_s, dh_s, grad_s):
    step = pl.program_id(0)
    blocks = pl.num_programs(0)
    width, tokens = xnt_ref.shape
    half = SLOTS // 2

    @pl.when(step == 0)
    def _():
        for b in range(dh_s.shape[0]):
            dh_s[b] = dot(dmix_ref[...], wo_ref[b * LANES : (b + 1) * LANES, :], ((1,), (1,)))

    zeros = jnp.zeros((CHUNKS, LANES), F32)
    tile = GROUP * CHUNKS
    count = tokens // tile

    def first(i, carry):
        g, prod, decay = carry
        at = aligned((count - 1 - i) * tile, tile)
        dh = dh_s[step, at, :]
        forget = f_ref[at, :]
        for k in reversed(range(GROUP)):
            part = slice(k * CHUNKS, (k + 1) * CHUNKS)
            g = dh[part] + decay * g
            prod = prod * decay
            decay = forget[part]
        return g, prod, decay

    ones = zeros + 1.0
    head, prod, decay = lax.fori_loop(0, count, first, (zeros, ones, ones))
    sub = lax.broadcasted_iota(jnp.int32, (CHUNKS, LANES), 0)
    start = zeros
    for s in reversed(range(1, CHUNKS)):
        moved = pltpu.roll(decay * (head + prod * start), CHUNKS - 1, 0)
        start = jnp.where(sub == s - 1, moved, start)

    def second(i, carry):
        g, decay, total = carry
        at = aligned((count - 1 - i) * tile, tile)
        dh = dh_s[step, at, :]
        forget = f_ref[at, :]
        parts = [None] * GROUP
        for k in reversed(range(GROUP)):
            part = slice(k * CHUNKS, (k + 1) * CHUNKS)
            g = dh[part] + decay * g
            decay = forget[part]
            parts[k] = g
        grad = jnp.concatenate(parts, axis=0)
        dk_ref[at, 0:LANES] = (u1_ref[at, :].astype(F32) * grad).astype(BF)
        di = (u2_ref[at, :].astype(F32) * grad).astype(BF)
        dk_ref[at, LANES : 2 * LANES] = di
        dk_ref[at, 2 * LANES : 3 * LANES] = ((1.0 - forget) * grad).astype(BF)
        di = di.astype(F32)
        for k in range(GROUP):
            total = total + di[k * CHUNKS : (k + 1) * CHUNKS]
        return g, decay, total

    _, _, total = lax.fori_loop(0, count, second, (start, ones, zeros))
    bias_s[:, aligned(step * LANES, LANES)] = jnp.sum(total, axis=0, keepdims=True)

    grad_s[...] = dot(xnt_ref[...], dk_ref[...]).astype(BF)
    for s in range(SLOTS):
        target = keep_ref if s < half else send_ref
        src = aligned(dev_ref[s] * 16, 16)
        for w in range(3):
            dst = aligned((step * 3 + w) * 16, 16)
            target[s % half, dst, :] = grad_s[src, w * LANES : (w + 1) * LANES]

    @pl.when(step == blocks - 1)
    def _():
        bias = bias_s[...]
        piece = width // SLOTS
        values = small_ref[...] + collect(bias, 2 * piece, bias.shape[1] // SLOTS)
        dh_s[0, 0:SLOTS, :] = values
        row = lax.broadcasted_iota(jnp.int32, (16, LANES), 0)
        tail = keep_ref.shape[1] - 16
        for s in range(SLOTS):
            target = keep_ref if s < half else send_ref
            values = dh_s[0, pl.ds(dev_ref[s], 1), :]
            target[s % half, tail : tail + 16, :] = jnp.where(row == 0, values, 0.0).astype(BF)


def input_gradient(x_ref, dy1_ref, gain_ref, dk_ref, w_ref, out_ref):
    dxn = dot(dk_ref[...], w_ref[...], ((1,), (1,)))
    v = x_ref[...].astype(F32)
    scale = lax.rsqrt(jnp.mean(v * v, axis=-1, keepdims=True) + EPSILON)
    n1 = v * scale
    dn = dxn * gain_ref[0:1, :]
    out_ref[...] = dy1_ref[...] + scale * (dn - n1 * jnp.mean(dn * n1, axis=-1, keepdims=True))


def order_table():
    table = np.zeros((SLOTS, SLOTS), np.int32)
    for me in range(SLOTS):
        core, y, x, z = me & 1, me >> 1 & 1, me >> 2 & 1, me >> 3
        for slot in range(SLOTS):
            oc, second, first, oz = slot >> 4, slot >> 3 & 1, slot >> 2 & 1, (slot & 1) << 1 | slot >> 1 & 1
            c2 = core ^ oc
            x2 = x ^ (first if c2 == 0 else second)
            y2 = y ^ (second if c2 == 0 else first)
            table[me, slot] = ((z ^ oz) * 2 + x2) * 4 + y2 * 2 + c2
    return table


def flip(x0, y0, z0, c0, x1, y1, z1, c1):
    pairs = []
    for me in range(SLOTS):
        x, y, z, c = (x1, y1, z1, c1) if me & 1 else (x0, y0, z0, c0)
        pairs.append((me, me ^ (z << 3 | x << 2 | y << 1 | c)))
    return pairs


FAR, NEAR, BOTH = [flip(0, 0, k, 0, 0, 0, k, 0) for k in (2, 1, 3)]
FIRST = flip(1, 0, 0, 0, 0, 1, 0, 0)
SECOND = flip(0, 1, 0, 0, 1, 0, 0, 0)
CORE = flip(0, 0, 0, 1, 0, 0, 0, 1)


def send(value, pairs, name):
    with jax.named_scope(name):
        return lax.ppermute(value, AXES, pairs)


def after(value, *others):
    return lax.optimization_barrier((value,) + others)[0]


def after_all(*values):
    return lax.optimization_barrier(values)


def add(a, b):
    return (a.astype(F32) + b.astype(F32)).astype(BF)


def fold(low, high, pairs, name):
    got = send(high, pairs, name)
    half = low.shape[0] // 2
    return add(low[:half], got[:half]), add(low[half:], got[half:])


def pack(forget_weight, input_weight, candidate_weight, small):
    rows = 3 * forget_weight.shape[1] // LANES * 16 + 16
    return pl.pallas_call(
        pack_mixer,
        out_shape=jax.ShapeDtypeStruct((rows, LANES), BF),
        compiler_params=params(),
        name="pack",
    )(forget_weight, input_weight, candidate_weight, small)


def widen(small):
    return jnp.concatenate([small, jnp.zeros((LANES - small.shape[0],), small.dtype)])[None]


def local(fast, tokens, gain_mix, gain_mlp, forget_weight, input_weight, candidate_weight, input_gate_bias,
          output_weight, up_weight, down_weight, cotangent):
    rows, width = tokens.shape
    chans = forget_weight.shape[1]
    blocks = chans // LANES
    shard = width // SLOTS

    def permute(v):
        return v.reshape(CHUNKS, rows // CHUNKS, width).transpose(1, 0, 2).reshape(rows, width)

    def restore(v):
        return v.reshape(rows // CHUNKS, CHUNKS, width).transpose(1, 0, 2).reshape(rows, width)

    xp = permute(tokens)
    dyp = permute(cotangent)
    if fast:
        me = lax.axis_index(AXES)
        table = order_table()
        tables = jnp.asarray(np.stack([table, np.argsort(table, axis=1)], axis=1).astype(np.int32))
        dev, slot = lax.dynamic_index_in_dim(tables, me, keepdims=False)
        mine = me % 2
        cols = jnp.stack([mine, 2 + mine, 1 - mine, 3 - mine]).astype(jnp.int32)
        small = widen(jnp.concatenate([gain_mix, gain_mlp, input_gate_bias]))
        piece = pack(forget_weight, input_weight, candidate_weight, small)
        four = jnp.stack([piece] + [send(piece, p, "mixer_z") for p in (FAR, NEAR, BOTH)])
        four, piece_f = after_all(four, jnp.concatenate([up_weight, down_weight.T, output_weight]), dev, xp, dyp)[:2]
        got, far_f = after_all(send(four, FIRST, "mixer_first"), send(piece_f, FAR, "feed_far"))
        eight = jnp.concatenate([four, got])
        two_f = jnp.stack([piece_f, far_f])
        eight, two_f = after_all(eight, two_f)
        more, got = after_all(send(eight, SECOND, "mixer_second"), send(two_f, NEAR, "feed_near"))
        four_f = jnp.concatenate([two_f, got])
        more, four_f = after_all(more, four_f)
        got, core, core_more = after_all(
            send(four_f, FIRST, "feed_first"), send(eight, CORE, "mixer_core"), send(more, CORE, "mixer_core_more")
        )
        eight_f = jnp.concatenate([four_f, got])
        mixer = (eight, more, core, core_more)
        mixer, eight_f = lax.optimization_barrier((mixer, eight_f))
        more_f = send(eight_f, SECOND, "feed_second")
    else:
        dev = slot = jnp.arange(SLOTS, dtype=jnp.int32)
        cols = jnp.arange(4, dtype=jnp.int32)

        def full(v, axis=0, names=AXES):
            return lax.all_gather(v, names, axis=axis, tiled=True)

        gm, gl, gb = full(gain_mix), full(gain_mlp), full(input_gate_bias)
        weights = [full(w) for w in (forget_weight, input_weight, candidate_weight)]
        smalls = jnp.concatenate([v.reshape(SLOTS, -1) for v in (gm, gl, gb)], axis=1)
        up = full(full(up_weight, 0, "dp"), 1, "mp")
        down = full(full(down_weight, 1, "dp"), 0, "mp")

        def regroup(w):
            return w.reshape(8, width // 8, 4, width).transpose(0, 2, 1, 3).reshape(SLOTS, width // 8, width)

        both = jnp.concatenate([regroup(up), regroup(down.T), full(output_weight).reshape(SLOTS, -1, width)], axis=1)

        def quarters(v):
            return tuple(v[k * 8 : (k + 1) * 8] for k in range(4))

        mixer = quarters(
            jnp.stack([pack(*[w[s * 16 : (s + 1) * 16] for w in weights], widen(smalls[s])) for s in range(SLOTS)])
        )
        feed = quarters(both)

    smem = pl.BlockSpec(memory_space=pltpu.SMEM)
    part = 256

    def band(cols):
        return pl.BlockSpec((part, cols), lambda i: (i, 0))

    def shapes(*items):
        return [jax.ShapeDtypeStruct(shape, kind) for shape, kind in items]

    column = pl.BlockSpec((rows, LANES), lambda i: (0, i))

    wide = pl.BlockSpec((width, 3 * LANES), lambda i: (0, i))
    hb, forget, u1, u2, w3, xn1t, gains = pl.pallas_call(
        mixer_forward,
        grid=(blocks,),
        in_specs=[smem, whole((rows, width))] + [whole(mixer[0].shape)] * 4,
        out_specs=[column] * 4 + [wide, whole((width, rows)), whole((2, width))],
        out_shape=shapes(((rows, chans), BF), ((rows, chans), F32), ((rows, chans), BF), ((rows, chans), BF),
                         ((width, 3 * chans), BF), ((width, rows), BF), ((2, width), F32)),
        scratch_shapes=[pltpu.VMEM((SLOTS, LANES), F32), pltpu.VMEM((1, chans), F32), pltpu.VMEM((rows, width), BF),
                        pltpu.VMEM((rows, 3 * LANES), F32), pltpu.VMEM((rows, LANES), F32)],
        compiler_params=params(),
        cost_estimate=pl.CostEstimate(flops=6 * rows * width * chans, bytes_accessed=32 << 20, transcendentals=0),
        name="mixer_forward",
    )(dev, xp, *mixer)
    if fast:
        last = after(more_f, hb)
        feed = (eight_f, more_f, send(eight_f, CORE, "feed_core"), send(last, CORE, "feed_core_more"))

    size = width // 8
    piece = (SLOTS // 2,) + feed[0].shape[1:]
    block_out, dy1, dmix, wo, keep1, send1, gmlp_small = pl.pallas_call(
        feed_forward,
        in_specs=[smem] * 3 + [pl.BlockSpec(memory_space=pltpu.VMEM)] + [pl.BlockSpec(memory_space=pl.ANY)] * 7,
        out_specs=[pl.BlockSpec(memory_space=pl.ANY)] * 6 + [pl.BlockSpec(memory_space=pltpu.VMEM)],
        out_shape=shapes(((rows, width), BF), ((rows, width), F32), ((rows, width), BF), ((chans, width), BF),
                         (piece, BF), (piece, BF), ((SLOTS, LANES), F32)),
        scratch_shapes=[
            pltpu.VMEM((SLOTS, piece[1] - 2 * size, width), BF),
            pltpu.VMEM((SLOTS, 2 * size, width), BF),
            pltpu.VMEM((rows, chans), BF),
            pltpu.VMEM((rows, width), BF),
            pltpu.VMEM((rows, width), BF),
            pltpu.VMEM((chans, width), BF),
            pltpu.VMEM((rows, width), F32),
            pltpu.VMEM((rows, width), BF),
            pltpu.VMEM((width, rows), BF),
            pltpu.VMEM((width, rows), BF),
            pltpu.VMEM((rows, width), F32),
            pltpu.VMEM((rows, width), F32),
            pltpu.VMEM((width, width), BF),
            pltpu.VMEM((width, width), BF),
            pltpu.VMEM((SLOTS,) + piece[1:], BF),
            pltpu.VMEM((rows, width), BF),
            pltpu.VMEM((rows, width), F32),
            pltpu.VMEM((rows, width), BF),
            pltpu.SemaphoreType.DMA((20,)),
        ],
        compiler_params=params(),
        cost_estimate=pl.CostEstimate(flops=2 * rows * width * (24 * width + 2 * chans), bytes_accessed=60 << 20, transcendentals=0),
        name="feed_forward",
    )(dev, slot, cols, gains, *feed, hb, xp, dyp)

    piece = (SLOTS // 2, 3 * blocks * 16 + 16, LANES)
    dk, keep2, send2 = pl.pallas_call(
        mixer_backward,
        grid=(blocks,),
        in_specs=[smem, whole((rows, width)), whole((width, rows)), whole((chans, width)), whole((SLOTS, LANES)),
                  column, column, column],
        out_specs=[pl.BlockSpec((rows, 3 * LANES), lambda i: (0, i))] + [whole(piece)] * 2,
        out_shape=shapes(((rows, 3 * chans), BF), (piece, BF), (piece, BF)),
        scratch_shapes=[pltpu.VMEM((1, chans), F32), pltpu.VMEM((blocks, rows, LANES), F32),
                        pltpu.VMEM((width, 3 * LANES), BF)],
        compiler_params=params(),
        cost_estimate=pl.CostEstimate(flops=8 * rows * width * chans, bytes_accessed=40 << 20, transcendentals=0),
        name="mixer_backward",
    )(dev, dmix, xn1t, wo, gmlp_small, forget, u1, u2)

    tile = 256
    tokens_grad = pl.pallas_call(
        input_gradient,
        grid=(rows // tile,),
        in_specs=[band(width), band(width), whole((2, width))] + [band(3 * chans), whole((width, 3 * chans))],
        out_specs=band(width),
        out_shape=jax.ShapeDtypeStruct((rows, width), F32),
        compiler_params=params(),
        cost_estimate=pl.CostEstimate(flops=6 * rows * width * chans, bytes_accessed=24 << 20, transcendentals=0),
        name="input_gradient",
    )(xp, dy1, gains, dk, w3)

    def uncut(v):
        v = v[:, : 48 * blocks].reshape(-1, blocks, 3, 16, LANES)
        return [v[:, :, k].transpose(0, 2, 1, 3).reshape(-1, 16, chans) for k in range(3)]

    if fast:
        half = SLOTS // 4
        got = send(send1, CORE, "feed_back_core")
        low, high = add(keep1[:half], got[:half]), add(keep1[half:], got[half:])
        low, high = fold(low, high, SECOND, "feed_back_second")
        low, high = fold(low, after(high, dk), FIRST, "feed_back_first")
        got = send(send2, CORE, "mixer_back_core")
        mlow, mhigh = add(keep2[:half], got[:half]), add(keep2[half:], got[half:])
        mlow, mhigh, low, high, _ = after_all(mlow, mhigh, low, high, tokens_grad)
        got, near = after_all(send(mhigh, SECOND, "mixer_back_second"), send(high, NEAR, "feed_back_near"))
        low, high = add(low[0], near[0]), add(low[1], near[1])
        half = SLOTS // 8
        mlow, mhigh = add(mlow[:half], got[:half]), add(mlow[half:], got[half:])
        mlow, mhigh, low, high = after_all(mlow, mhigh, low, high)
        got, far = after_all(send(mhigh, FIRST, "mixer_back_first"), send(high, FAR, "feed_back_far"))
        four = add(mlow, got)
        first = low.astype(F32) + far.astype(F32)
        total = four[0].astype(F32)
        for k, p in enumerate((FAR, NEAR, BOTH)):
            total = total + send(four[k + 1], p, "mixer_back_z").astype(F32)
        up_grad, down_grad, out_grad = first[:size], first[size : 2 * size].T, first[2 * size :]
        grads = [v[0] for v in uncut(total[None])]
        edge = total[48 * blocks]
        gmlp_grad = edge[:shard]
        bias_grad = edge[2 * shard : 2 * shard + chans // SLOTS]
    else:
        first, total = (jnp.concatenate(v).astype(F32) for v in ((keep1, send1), (keep2, send2)))

        def summed(v, axis=0, names=AXES):
            return lax.psum_scatter(v, names, scatter_dimension=axis, tiled=True)

        def joined(base):
            w = first[:, base : base + size]
            return w.reshape(8, 4, size, width).transpose(0, 2, 1, 3).reshape(width, 4 * width)

        up_grad = summed(summed(joined(0), 0, "dp"), 1, "mp")
        down_grad = summed(summed(joined(size).T, 1, "dp"), 0, "mp")
        out_grad = summed(first[:, 2 * size :].reshape(chans, width))
        grads = [summed(v.reshape(width, chans)) for v in uncut(total)]
        edge = total[:, 48 * blocks]
        gmlp_grad = summed(edge[:, :shard].reshape(-1))
        bias_grad = summed(edge[:, 2 * shard : 2 * shard + chans // SLOTS].reshape(-1))

    dots = sum(
        jnp.sum(w.astype(F32) * g, axis=1) for w, g in zip((forget_weight, input_weight, candidate_weight), grads)
    )
    gmix_grad = dots / gain_mix.astype(F32)
    return (restore(block_out), restore(tokens_grad), gmix_grad, gmlp_grad, grads[0], grads[1], grads[2], bias_grad,
            out_grad, up_grad, down_grad)


def solution(mesh):
    fast = mesh.shape["dp"] == 8 and mesh.shape["mp"] == 4
    every = P(AXES, None)
    in_specs = (every, P(AXES), P(AXES), every, every, every, P(AXES), every, P("dp", "mp"), P("mp", "dp"), every)
    out_specs = (every, every, P(AXES), P(AXES), every, every, every, P(AXES), every, P("dp", "mp"), P("mp", "dp"))
    return jax.shard_map(
        functools.partial(local, fast), mesh=mesh, in_specs=in_specs, out_specs=out_specs, check_vma=False
    )
```

time: 222 us -> 176 us (0.79)
  waiting for transfers between devices: 77.9 us -> 58 us
  Pallas kernels: 81.4 us -> 69.1 us
  local copies, waits for them, and re-layouts: 19.7 us -> 12.4 us
  starting transfers between devices: 32.1 us -> 25 us
    ppermute x26 -> x24, waiting for transfers between devices: 77.9 us -> 58 us  [send(): return lax.ppermute(value, AXES, pairs)]
    pallas_call x4 -> x5, Pallas kernels: 81.4 us -> 69.1 us  [the longest x1 26 us: local(): pl.pallas_call(feed_forward, in_specs=[smem] * 3 + [pl.BlockSpec(memory_s...]
    ppermute x26 -> x24, starting transfers between devices: 32.1 us -> 25 us  [send(): return lax.ppermute(value, AXES, pairs)]
    convert_element_type x6 -> x7, other arithmetic: 4.62 us -> 7.28 us  [add(): return (a.astype(F32) + b.astype(F32)).astype(BF)]
    unnamed x31 -> x41, local copies, waits for them, and re-layouts: 2.7 us -> 0.14 us
    squeeze x4 -> x1, local copies, waits for them, and re-layouts: 2.46 us -> 0.02 us  [local(): total = total + send(four[k + 1], p, 'mixer_back_z').astype(F32)]
    reshape x6 -> x0, local copies, waits for them, and re-layouts: 2.3 us -> none  [the longest x3 2.28 us: cut(): w.reshape(16, blocks, LANES).transpose(1, 0, 2).reshape(blocks * 16, LANES)]
  transfers between devices with their start and end apart: 26 -> 24, of which waited for: 12 -> 13; matrix products, arithmetic and copies ran while one was open for 11% -> 8% of each run, Pallas kernels for 13% -> 24%
where the time goes in v2:
time: 176 us
  Pallas kernels  69.1 us (39%)
  waiting for transfers between devices  58 us (33%)
  starting transfers between devices  25 us (14%)
  local copies, waits for them, and re-layouts  12.4 us (7%)
  other arithmetic  9.97 us (6%)
    ppermute x24, waiting for transfers between devices, send(): return lax.ppermute(value, AXES, pairs)  58 us
    pallas_call x1, Pallas kernels, local(): pl.pallas_call(feed_forward, in_specs=[smem] * 3 + [pl.BlockSpec(memory_s...  26 us
    ppermute x24, starting transfers between devices, send(): return lax.ppermute(value, AXES, pairs)  25 us
    pallas_call x1, Pallas kernels, local(): pl.pallas_call(mixer_forward, grid=(blocks,), in_specs=[smem, whole((rows...  18 us
    pallas_call x1, Pallas kernels, local(): pl.pallas_call(mixer_backward, grid=(blocks,), in_specs=[smem, whole((row...  14.6 us
    pallas_call x1, Pallas kernels, local(): pl.pallas_call(input_gradient, grid=(rows // tile,), in_specs=[band(width...  9.04 us
    convert_element_type x7, other arithmetic, add(): return (a.astype(F32) + b.astype(F32)).astype(BF)  7.28 us
    reshape x1, local copies, waits for them, and re-layouts, permute(): v.reshape(CHUNKS, rows // CHUNKS, width).transpose(1, 0, 2)  4.09 us
  transfers between devices with their start and end apart: 24, of which 13 were waited for; matrix products, arithmetic and copies ran while one was open for 8% of the time, Pallas kernels for 24%

profile of v2, /device:TPU:0, one launch (start us, length us, event | category | flops | bytes accessed | tf_op | source)
XLA Modules:
  0.0 175.5 jit_solution(12936641815354685455)
XLA Ops:
  2.0 1.4 pack.1
  3.4 4.0 %collective-permute-start = (bf16[208,256]{1,0:T(8,128)(2,1)}, bf16[208,256]{1,0:T(8,128)(2,1)S(1)}, u32[]{:S(2)}, u32[]{:S(2)}) collective-permute-start(bf16[208,256]{1,0:T(8,128)(2,1)} %pack.1), channel_id=1, source_target_pairs={{0,16},{1,17},{2,18},{3,19},{4,20},{5,21},{6,22},{7,23},{8,24},{9,... | collective-permute-start | bytes 319496 | tf_op jit(solution)/shard_map/mixer_z/ppermute | solution.py:405
  7.5 1.6 collective-permute-start.1
  10.3 4.1 %copy_bitcast_fusion = (bf16[1024,512]{1,0:T(8,128)(2,1)}, bf16[1024,512]{1,0:T(8,128)(2,1)}) fusion(bf16[8,128,512]{2,1,0:T(8,128)(2,1)} %bitcast.81, bf16[8,128,512]{2,1,0:T(8,128)(2,1)} %bitcast.82), kind=kLoop, calls=%fused_computation.7 | loop fusion | bytes 4194304 | tf_op jit(solution)/shard_map/reshape | solution.py:448
  14.6 1.8 %collective-permute-done.2 = bf16[208,256]{1,0:T(8,128)(2,1)S(1)} collective-permute-done((bf16[208,256]{1,0:T(8,128)(2,1)}, bf16[208,256]{1,0:T(8,128)(2,1)S(1)}, u32[]{:S(2)}, u32[]{:S(2)}) %collective-permute-start.2) | collective-permute-done | bytes 106528 | tf_op jit(solution)/shard_map/mixer_z/ppermute | solution.py:405
  16.4 1.6 collective-permute-start.3
  18.0 3.8 %collective-permute-start.4 = (bf16[160,512]{1,0:T(8,128)(2,1)S(1)}, bf16[160,512]{1,0:T(8,128)(2,1)S(1)}, u32[]{:S(2)}, u32[]{:S(2)}) collective-permute-start(bf16[160,512]{1,0:T(8,128)(2,1)S(1)} %pad_maximum_fusion.5), channel_id=1, source_target_pairs={{0,16},{1,17},{2,18},{3,19},{4,20},{5,21},{6,22},{7,23},{8,24},{9,... | collective-permute-start | bytes 491528 | tf_op jit(solution)/shard_map/feed_far/ppermute | solution.py:405
  21.8 7.6 %collective-permute-done.4 = bf16[160,512]{1,0:T(8,128)(2,1)S(1)} collective-permute-done((bf16[160,512]{1,0:T(8,128)(2,1)S(1)}, bf16[160,512]{1,0:T(8,128)(2,1)S(1)}, u32[]{:S(2)}, u32[]{:S(2)}) %collective-permute-start.4) | collective-permute-done | bytes 163872 | tf_op jit(solution)/shard_map/feed_far/ppermute | solution.py:405
  30.9 9.6 %collective-permute-done.6 = bf16[2,160,512]{2,1,0:T(8,128)(2,1)S(1)} collective-permute-done((bf16[2,160,512]{2,1,0:T(8,128)(2,1)S(1)}, bf16[2,160,512]{2,1,0:T(8,128)(2,1)S(1)}, u32[]{:S(2)}, u32[]{:S(2)}) %collective-permute-start.6) | collective-permute-done | bytes 327712 | tf_op jit(solution)/shard_map/feed_near/ppermute | solution.py:405
  40.5 1.8 %collective-permute-done.5.g1 = bf16[8,208,256]{2,1,0:T(8,128)(2,1)S(1)} collective-permute-done((bf16[8,208,256]{2,1,0:T(8,128)(2,1)S(1)}, bf16[8,208,256]{2,1,0:T(8,128)(2,1)S(1)}, u32[]{:S(2)}, u32[]{:S(2)}) %collective-permute-start.5) | collective-permute-done | bytes 852000 | tf_op jit(solution)/shard_map/mixer_second/ppermute | solution.py:405
  42.4 1.5 collective-permute-start.7
  43.9 9.2 %collective-permute-done.7 = bf16[4,160,512]{2,1,0:T(8,128)(2,1)S(1)} collective-permute-done((bf16[4,160,512]{2,1,0:T(8,128)(2,1)S(1)}, bf16[4,160,512]{2,1,0:T(8,128)(2,1)S(1)}, u32[]{:S(2)}, u32[]{:S(2)}) %collective-permute-start.7) | collective-permute-done | bytes 655392 | tf_op jit(solution)/shard_map/feed_first/ppermute | solution.py:405
  54.0 18.0 %mixer_forward.1 = (bf16[1024,1024]{1,0:T(8,128)(2,1)}, f32[1024,1024]{1,0:T(8,128)}, bf16[1024,1024]{1,0:T(8,128)(2,1)}, bf16[1024,1024]{1,0:T(8,128)(2,1)}, bf...) custom-call(s32[32]{0:T(128)} %get-tuple-element.130.dev_ref, ...), custom_call_target="tpu_custom_call" | custom-call | flops 3221225472 | bytes 33554432 | tf_op jit(solution)/shard_map/mixer_forward/pallas_call | solution.py:518
  73.1 2.3 %collective-permute-done.12.g3 = bf16[8,160,512]{2,1,0:T(8,128)(2,1)} collective-permute-done((bf16[8,160,512]{2,1,0:T(8,128)(2,1)S(1)}, bf16[8,160,512]{2,1,0:T(8,128)(2,1)}, u32[]{:S(2)}, u32[]{:S(2)}) %collective-permute-start.12) | collective-permute-done | bytes 1310752 | tf_op jit(solution)/shard_map/feed_core_more/ppermute | solution.py:405
  75.4 26.0 %feed_forward.1 = (bf16[1024,512]{1,0:T(8,128)(2,1)}, f32[1024,512]{1,0:T(8,128)}, bf16[1024,512]{1,0:T(8,128)(2,1)}, bf16[1024,512]{1,0:T(8,128)(2,1)}, bf16[16...) custom-call(s32[32]{0:T(128)} %get-tuple-element.130.dev_ref, ...), custom_call_target="tpu_custom_call" | custom-call | flops 15032385536 | bytes 62914560 | tf_op jit(solution)/shard_map/feed_forward/pallas_call | solution.py:537
  101.7 4.8 %collective-permute-done.14 = bf16[16,160,512]{2,1,0:T(8,128)(2,1)S(1)} collective-permute-done((bf16[16,160,512]{2,1,0:T(8,128)(2,1)}, bf16[16,160,512]{2,1,0:T(8,128)(2,1)S(1)}, u32[]{:S(2)}, u32[]{:S(2)}) %collective-permute-start.14) | collective-permute-done | bytes 2621472 | tf_op jit(solution)/shard_map/feed_back_core/ppermute | solution.py:405
  106.5 3.6 %add_convert_fusion.1 = (bf16[8,160,512]{2,1,0:T(8,128)(2,1)S(1)}, bf16[8,160,512]{2,1,0:T(8,128)(2,1)}) fusion(bf16[16,160,512]{2,1,0:T(8,128)(2,1)S(1)} %collective-permute-done.14, bf16[16,160,512]{2,1,0:T(8,128)(2,1)} %get-tuple-element.94), kind=kLoop, calls=%fused_computation.1 | loop fusion | flops 5242880 | bytes 7864320 | tf_op jit(solution)/shard_map/convert_element_type | solution.py:417
  110.2 1.5 collective-permute-start.15
  111.6 14.6 %mixer_backward.1 = (bf16[1024,3072]{1,0:T(8,128)(2,1)}, bf16[16,208,256]{2,1,0:T(8,128)(2,1)}, bf16[16,208,256]{2,1,0:T(8,128)(2,1)}) custom-call(s32[32]{0:T(128)} %get-tuple-element.130.dev_ref, bf16[1024,512]{1,0:T(8,128)(2,1)} %get-tuple-element.83.dmix_ref, bf16[512,1024]{1,0:T(8,128)(2,1)} %get-tuple-element.84.xnt_ref, ...), custom_call_target="tpu_custom_call" | custom-call | flops 4294967296 | bytes 41943040 | tf_op jit(solution)/shard_map/mixer_backward/pallas_call | solution.py:570
  126.3 1.7 collective-permute-done.15
  129.2 1.4 collective-permute-start.16
  130.6 9.0 %input_gradient.1 = f32[1024,512]{1,0:T(8,128)} custom-call(bf16[1024,512]{1,0:T(8,128)(2,1)} %get-tuple-element.132.x_ref.x_hbm, f32[1024,512]{1,0:T(8,128)} %get-tuple-element.82.dy1_ref, f32[2,512]{1,0:T(2,128)} %get-tuple-element.77.gain_ref, bf16[1024,3072]{1,0:T(8,128)(2,1)} %get-tuple-element.90.dk_ref, bf16[512,3072]{1,0:T(8,128)(2,1)} %get-tuple-element.91.w_ref), custom_call_target="tpu_custom_call" | custom-call | flops 3221225472 | bytes 25165824 | tf_op jit(solution)/shard_map/input_gradient/pallas_call | solution.py:585
  139.7 1.8 %add_convert_fusion.2 = (bf16[8,208,256]{2,1,0:T(8,128)(2,1)S(1)}, bf16[8,208,256]{2,1,0:T(8,128)(2,1)S(1)}) fusion(bf16[16,208,256]{2,1,0:T(8,128)(2,1)} %collective-permute-done.13, bf16[16,208,256]{2,1,0:T(8,128)(2,1)S(1)} %copy-done.1), kind=kLoop, calls=%fused_computation.2 | loop fusion | flops 3407872 | bytes 5111808 | tf_op jit(solution)/shard_map/convert_element_type | solution.py:417
  141.7 1.5 collective-permute-start.17
  143.3 8.6 %collective-permute-done.18 = bf16[2,160,512]{2,1,0:T(8,128)(2,1)S(1)} collective-permute-done((bf16[2,160,512]{2,1,0:T(8,128)(2,1)S(1)}, bf16[2,160,512]{2,1,0:T(8,128)(2,1)S(1)}, u32[]{:S(2)}, u32[]{:S(2)}) %collective-permute-start.18) | collective-permute-done | bytes 327712 | tf_op jit(solution)/shard_map/feed_back_near/ppermute | solution.py:405
  151.8 2.7 %collective-permute-done.17 = bf16[8,208,256]{2,1,0:T(8,128)(2,1)S(1)} collective-permute-done((bf16[8,208,256]{2,1,0:T(8,128)(2,1)S(1)}, bf16[8,208,256]{2,1,0:T(8,128)(2,1)S(1)}, u32[]{:S(2)}, u32[]{:S(2)}) %collective-permute-start.17) | collective-permute-done | bytes 852000 | tf_op jit(solution)/shard_map/mixer_back_second/ppermute | solution.py:405
  155.5 2.5 %copy.26 = f32[8,128,512]{2,1,0:T(8,128)} copy(f32[8,128,512]{2,0,1:T(8,128)S(1)} %bitcast.77) | data formatting | bytes 4194304 | tf_op jit(solution)/shard_map/transpose | solution.py:451
  158.0 1.3 copy.25
  159.3 3.9 %collective-permute-done.20 = bf16[160,512]{1,0:T(8,128)(2,1)S(1)} collective-permute-done((bf16[160,512]{1,0:T(8,128)(2,1)S(1)}, bf16[160,512]{1,0:T(8,128)(2,1)S(1)}, u32[]{:S(2)}, u32[]{:S(2)}) %collective-permute-start.20) | collective-permute-done | bytes 163872 | tf_op jit(solution)/shard_map/feed_back_far/ppermute | solution.py:405
  163.4 2.6 %collective-permute-start.22 = (bf16[208,256]{1,0:T(8,128)(2,1)S(1)}, bf16[208,256]{1,0:T(8,128)(2,1)S(1)}, u32[]{:S(2)}, u32[]{:S(2)}) collective-permute-start(bf16[208,256]{1,0:T(8,128)(2,1)S(1)} %get-tuple-element.123), channel_id=1, source_target_pairs={{0,8},{1,9},{2,10},{3,11},{4,12},{5,13},{6,14},{7,15},{8,0},{9,1},... | collective-permute-start | bytes 319496 | tf_op jit(solution)/shard_map/mixer_back_z/ppermute | solution.py:405
  166.0 1.8 %collective-permute-start.23 = (bf16[208,256]{1,0:T(8,128)(2,1)S(1)}, bf16[208,256]{1,0:T(8,128)(2,1)S(1)}, u32[]{:S(2)}, u32[]{:S(2)}) collective-permute-start(bf16[208,256]{1,0:T(8,128)(2,1)S(1)} %get-tuple-element.122), channel_id=1, source_target_pairs={{0,24},{1,25},{2,26},{3,27},{4,28},{5,29},{6,30},{7,31},{8,16},{9,... | collective-permute-start | bytes 319496 | tf_op jit(solution)/shard_map/mixer_back_z/ppermute | solution.py:405
  169.2 3.9 %collective-permute-done.21 = bf16[208,256]{1,0:T(8,128)(2,1)S(1)} collective-permute-done((bf16[208,256]{1,0:T(8,128)(2,1)S(1)}, bf16[208,256]{1,0:T(8,128)(2,1)S(1)}, u32[]{:S(2)}, u32[]{:S(2)}) %collective-permute-start.21) | collective-permute-done | bytes 106528 | tf_op jit(solution)/shard_map/mixer_back_z/ppermute | solution.py:405
  (100 shorter events, 13.0 us)
Async XLA Ops:
  3.4 11.1 %collective-permute-start = (bf16[208,256]{1,0:T(8,128)(2,1)}, bf16[208,256]{1,0:T(8,128)(2,1)S(1)}, u32[]{:S(2)}, u32[]{:S(2)}) collective-permute-start(bf16[208,256]{1,0:T(8,128)(2,1)} %pack.1), channel_id=1, source_target_pairs={{0,16},{1,17},{2,18},{3,19},{4,20},{5,21},{6,22},{7,23},{8,24},{9,... | collective-permute-start | bytes 319496 | tf_op jit(solution)/shard_map/mixer_z/ppermute | solution.py:405
  7.5 7.1 %collective-permute-start.1 = (bf16[208,256]{1,0:T(8,128)(2,1)}, bf16[208,256]{1,0:T(8,128)(2,1)S(1)}, u32[]{:S(2)}, u32[]{:S(2)}) collective-permute-start(bf16[208,256]{1,0:T(8,128)(2,1)} %pack.1), channel_id=1, source_target_pairs={{0,8},{1,9},{2,10},{3,11},{4,12},{5,13},{6,14},{7,15},{8,0},{9,1},... | collective-permute-start | bytes 319496 | tf_op jit(solution)/shard_map/mixer_z/ppermute | solution.py:405
  9.1 7.3 %collective-permute-start.2 = (bf16[208,256]{1,0:T(8,128)(2,1)}, bf16[208,256]{1,0:T(8,128)(2,1)S(1)}, u32[]{:S(2)}, u32[]{:S(2)}) collective-permute-start(bf16[208,256]{1,0:T(8,128)(2,1)} %pack.1), channel_id=1, source_target_pairs={{0,24},{1,25},{2,26},{3,27},{4,28},{5,29},{6,30},{7,31},{8,16},{9,... | collective-permute-start | bytes 319496 | tf_op jit(solution)/shard_map/mixer_z/ppermute | solution.py:405
  16.4 13.0 %collective-permute-start.3 = (bf16[4,208,256]{2,1,0:T(8,128)(2,1)S(1)}, bf16[4,208,256]{2,1,0:T(8,128)(2,1)S(1)}, u32[]{:S(2)}, u32[]{:S(2)}) collective-permute-start(bf16[4,208,256]{2,1,0:T(8,128)(2,1)S(1)} %pad_maximum_fusion.3), channel_id=1, source_target_pairs={{0,4},{1,3},{2,6},{3,1},{4,0},{5,7},{6,2},{7,5},{8,12},{9,11},{10,... | collective-permute-start | bytes 1277960 | tf_op jit(solution)/shard_map/mixer_first/ppermute | solution.py:405
  18.0 11.4 %collective-permute-start.4 = (bf16[160,512]{1,0:T(8,128)(2,1)S(1)}, bf16[160,512]{1,0:T(8,128)(2,1)S(1)}, u32[]{:S(2)}, u32[]{:S(2)}) collective-permute-start(bf16[160,512]{1,0:T(8,128)(2,1)S(1)} %pad_maximum_fusion.5), channel_id=1, source_target_pairs={{0,16},{1,17},{2,18},{3,19},{4,20},{5,21},{6,22},{7,23},{8,24},{9,... | collective-permute-start | bytes 491528 | tf_op jit(solution)/shard_map/feed_far/ppermute | solution.py:405
  29.5 23.7 %copy-start.4 = (bf16[8,208,256]{2,1,0:T(8,128)(2,1)}, bf16[8,208,256]{2,1,0:T(8,128)(2,1)S(1)}, u32[]{:S(2)}) copy-start(bf16[8,208,256]{2,1,0:T(8,128)(2,1)S(1)} %pad_maximum_fusion.1.g0) | copy-start | bytes 2555908
  29.5 12.8 %collective-permute-start.5 = (bf16[8,208,256]{2,1,0:T(8,128)(2,1)S(1)}, bf16[8,208,256]{2,1,0:T(8,128)(2,1)S(1)}, u32[]{:S(2)}, u32[]{:S(2)}) collective-permute-start(bf16[8,208,256]{2,1,0:T(8,128)(2,1)S(1)} %pad_maximum_fusion.1.g0), channel_id=1, source_target_pairs={{0,2},{1,5},{2,0},{3,7},{4,6},{5,1},{6,4},{7,3},{8,10},{9,13},{10,... | collective-permute-start | bytes 2555912 | tf_op jit(solution)/shard_map/mixer_second/ppermute | solution.py:405
  30.1 10.4 %collective-permute-start.6 = (bf16[2,160,512]{2,1,0:T(8,128)(2,1)S(1)}, bf16[2,160,512]{2,1,0:T(8,128)(2,1)S(1)}, u32[]{:S(2)}, u32[]{:S(2)}) collective-permute-start(bf16[2,160,512]{2,1,0:T(8,128)(2,1)S(1)} %pad_maximum_fusion.4), channel_id=1, source_target_pairs={{0,8},{1,9},{2,10},{3,11},{4,12},{5,13},{6,14},{7,15},{8,0},{9,1},... | collective-permute-start | bytes 983048 | tf_op jit(solution)/shard_map/feed_near/ppermute | solution.py:405
  30.1 13.8 %collective-permute-start.8 = (bf16[8,208,256]{2,1,0:T(8,128)(2,1)S(1)}, bf16[8,208,256]{2,1,0:T(8,128)(2,1)S(1)}, u32[]{:S(2)}, u32[]{:S(2)}) collective-permute-start(bf16[8,208,256]{2,1,0:T(8,128)(2,1)S(1)} %pad_maximum_fusion.1.g0), channel_id=1, source_target_pairs={{0,1},{1,0},{2,3},{3,2},{4,5},{5,4},{6,7},{7,6},{8,9},{9,8},{10,11... | collective-permute-start | bytes 2555912 | tf_op jit(solution)/shard_map/mixer_core/ppermute | solution.py:405
  42.3 10.9 %copy-start.17 = (bf16[8,208,256]{2,1,0:T(8,128)(2,1)}, bf16[8,208,256]{2,1,0:T(8,128)(2,1)S(1)}, u32[]{:S(2)}) copy-start(bf16[8,208,256]{2,1,0:T(8,128)(2,1)S(1)} %collective-permute-done.5.g1) | copy-start | bytes 2555908
  42.4 10.7 %collective-permute-start.9 = (bf16[8,208,256]{2,1,0:T(8,128)(2,1)S(1)}, bf16[8,208,256]{2,1,0:T(8,128)(2,1)}, u32[]{:S(2)}, u32[]{:S(2)}) collective-permute-start(bf16[8,208,256]{2,1,0:T(8,128)(2,1)S(1)} %collective-permute-done.5.g1), channel_id=1, source_target_pairs={{0,1},{1,0},{2,3},{3,2},{4,5},{5,4},{6,7},{7,6},{8,9},{9,8},{10,11... | collective-permute-start | bytes 2555912 | tf_op jit(solution)/shard_map/mixer_core_more/ppermute | solution.py:405
  42.4 10.7 %collective-permute-start.7 = (bf16[4,160,512]{2,1,0:T(8,128)(2,1)S(1)}, bf16[4,160,512]{2,1,0:T(8,128)(2,1)S(1)}, u32[]{:S(2)}, u32[]{:S(2)}) collective-permute-start(bf16[4,160,512]{2,1,0:T(8,128)(2,1)S(1)} %pad_maximum_fusion.2), channel_id=1, source_target_pairs={{0,4},{1,3},{2,6},{3,1},{4,0},{5,7},{6,2},{7,5},{8,12},{9,11},{10,... | collective-permute-start | bytes 1966088 | tf_op jit(solution)/shard_map/feed_first/ppermute | solution.py:405
  43.9 9.2 %copy-start.18 = (bf16[8,208,256]{2,1,0:T(8,128)(2,1)}, bf16[8,208,256]{2,1,0:T(8,128)(2,1)S(1)}, u32[]{:S(2)}) copy-start(bf16[8,208,256]{2,1,0:T(8,128)(2,1)S(1)} %collective-permute-done.8.g2) | copy-start | bytes 2555908
  53.2 18.9 %copy-start.2 = (bf16[8,160,512]{2,1,0:T(8,128)(2,1)}, bf16[8,160,512]{2,1,0:T(8,128)(2,1)S(1)}, u32[]{:S(2)}) copy-start(bf16[8,160,512]{2,1,0:T(8,128)(2,1)S(1)} %pad_maximum_fusion.g0) | copy-start | bytes 3932164
  53.2 18.9 %collective-permute-start.10 = (bf16[8,160,512]{2,1,0:T(8,128)(2,1)S(1)}, bf16[8,160,512]{2,1,0:T(8,128)(2,1)S(1)}, u32[]{:S(2)}, u32[]{:S(2)}) collective-permute-start(bf16[8,160,512]{2,1,0:T(8,128)(2,1)S(1)} %pad_maximum_fusion.g0), channel_id=1, source_target_pairs={{0,2},{1,5},{2,0},{3,7},{4,6},{5,1},{6,4},{7,3},{8,10},{9,13},{10,... | collective-permute-start | bytes 3932168 | tf_op jit(solution)/shard_map/feed_second/ppermute | solution.py:405
  53.8 19.3 %collective-permute-start.11 = (bf16[8,160,512]{2,1,0:T(8,128)(2,1)S(1)}, bf16[8,160,512]{2,1,0:T(8,128)(2,1)}, u32[]{:S(2)}, u32[]{:S(2)}) collective-permute-start(bf16[8,160,512]{2,1,0:T(8,128)(2,1)S(1)} %pad_maximum_fusion.g0), channel_id=1, source_target_pairs={{0,1},{1,0},{2,3},{3,2},{4,5},{5,4},{6,7},{7,6},{8,9},{9,8},{10,11... | collective-permute-start | bytes 3932168 | tf_op jit(solution)/shard_map/feed_core/ppermute | solution.py:405
  72.1 3.2 %collective-permute-start.12 = (bf16[8,160,512]{2,1,0:T(8,128)(2,1)S(1)}, bf16[8,160,512]{2,1,0:T(8,128)(2,1)}, u32[]{:S(2)}, u32[]{:S(2)}) collective-permute-start(bf16[8,160,512]{2,1,0:T(8,128)(2,1)S(1)} %collective-permute-done.10.g1), channel_id=1, source_target_pairs={{0,1},{1,0},{2,3},{3,2},{4,5},{5,4},{6,7},{7,6},{8,9},{9,8},{10,11... | collective-permute-start | bytes 3932168 | tf_op jit(solution)/shard_map/feed_core_more/ppermute | solution.py:405
  101.4 5.2 %collective-permute-start.14 = (bf16[16,160,512]{2,1,0:T(8,128)(2,1)}, bf16[16,160,512]{2,1,0:T(8,128)(2,1)S(1)}, u32[]{:S(2)}, u32[]{:S(2)}) collective-permute-start(bf16[16,160,512]{2,1,0:T(8,128)(2,1)} %get-tuple-element.95), channel_id=1, source_target_pairs={{0,1},{1,0},{2,3},{3,2},{4,5},{5,4},{6,7},{7,6},{8,9},{9,8},{10,11... | collective-permute-start | bytes 7864328 | tf_op jit(solution)/shard_map/feed_back_core/ppermute | solution.py:405
  110.2 17.8 %collective-permute-start.15 = (bf16[8,160,512]{2,1,0:T(8,128)(2,1)}, bf16[8,160,512]{2,1,0:T(8,128)(2,1)S(1)}, u32[]{:S(2)}, u32[]{:S(2)}) collective-permute-start(bf16[8,160,512]{2,1,0:T(8,128)(2,1)} %get-tuple-element.110), channel_id=1, source_target_pairs={{0,2},{1,5},{2,0},{3,7},{4,6},{5,1},{6,4},{7,3},{8,10},{9,13},{10,... | collective-permute-start | bytes 3932168 | tf_op jit(solution)/shard_map/feed_back_second/ppermute | solution.py:405
  126.2 13.5 %collective-permute-start.13 = (bf16[16,208,256]{2,1,0:T(8,128)(2,1)}, bf16[16,208,256]{2,1,0:T(8,128)(2,1)}, u32[]{:S(2)}, u32[]{:S(2)}) collective-permute-start(bf16[16,208,256]{2,1,0:T(8,128)(2,1)} %get-tuple-element.93), channel_id=1, source_target_pairs={{0,1},{1,0},{2,3},{3,2},{4,5},{5,4},{6,7},{7,6},{8,9},{9,8},{10,11... | collective-permute-start | bytes 5111816 | tf_op jit(solution)/shard_map/mixer_back_core/ppermute | solution.py:405
  129.2 12.3 %collective-permute-start.16 = (bf16[4,160,512]{2,1,0:T(8,128)(2,1)}, bf16[4,160,512]{2,1,0:T(8,128)(2,1)S(1)}, u32[]{:S(2)}, u32[]{:S(2)}) collective-permute-start(bf16[4,160,512]{2,1,0:T(8,128)(2,1)} %get-tuple-element.96), channel_id=1, source_target_pairs={{0,4},{1,3},{2,6},{3,1},{4,0},{5,7},{6,2},{7,5},{8,12},{9,11},{10,... | collective-permute-start | bytes 1966088 | tf_op jit(solution)/shard_map/feed_back_first/ppermute | solution.py:405
  130.6 9.1 %copy-start.1 = (bf16[16,208,256]{2,1,0:T(8,128)(2,1)S(1)}, bf16[16,208,256]{2,1,0:T(8,128)(2,1)}, u32[]{:S(2)}) copy-start(bf16[16,208,256]{2,1,0:T(8,128)(2,1)} %get-tuple-element.92) | copy-start | bytes 5111812
  141.7 13.7 %copy-start = (f32[1024,512]{1,0:T(8,128)S(1)}, f32[1024,512]{1,0:T(8,128)}, u32[]{:S(2)}) copy-start(f32[1024,512]{1,0:T(8,128)} %input_gradient.1) | copy-start | bytes 6291460
  141.7 12.8 %collective-permute-start.17 = (bf16[8,208,256]{2,1,0:T(8,128)(2,1)S(1)}, bf16[8,208,256]{2,1,0:T(8,128)(2,1)S(1)}, u32[]{:S(2)}, u32[]{:S(2)}) collective-permute-start(bf16[8,208,256]{2,1,0:T(8,128)(2,1)S(1)} %get-tuple-element.98), channel_id=1, source_target_pairs={{0,2},{1,5},{2,0},{3,7},{4,6},{5,1},{6,4},{7,3},{8,10},{9,13},{10,... | collective-permute-start | bytes 2555912 | tf_op jit(solution)/shard_map/mixer_back_second/ppermute | solution.py:405
  143.3 8.6 %collective-permute-start.18 = (bf16[2,160,512]{2,1,0:T(8,128)(2,1)S(1)}, bf16[2,160,512]{2,1,0:T(8,128)(2,1)S(1)}, u32[]{:S(2)}, u32[]{:S(2)}) collective-permute-start(bf16[2,160,512]{2,1,0:T(8,128)(2,1)S(1)} %get-tuple-element.99), channel_id=1, source_target_pairs={{0,8},{1,9},{2,10},{3,11},{4,12},{5,13},{6,14},{7,15},{8,0},{9,1},... | collective-permute-start | bytes 983048 | tf_op jit(solution)/shard_map/feed_back_near/ppermute | solution.py:405
  154.8 8.4 %collective-permute-start.19 = (bf16[4,208,256]{2,1,0:T(8,128)(2,1)S(1)}, bf16[4,208,256]{2,1,0:T(8,128)(2,1)S(1)}, u32[]{:S(2)}, u32[]{:S(2)}) collective-permute-start(bf16[4,208,256]{2,1,0:T(8,128)(2,1)S(1)} %get-tuple-element.104), channel_id=1, source_target_pairs={{0,4},{1,3},{2,6},{3,1},{4,0},{5,7},{6,2},{7,5},{8,12},{9,11},{10,... | collective-permute-start | bytes 1277960 | tf_op jit(solution)/shard_map/mixer_back_first/ppermute | solution.py:405
  155.5 7.7 %collective-permute-start.20 = (bf16[160,512]{1,0:T(8,128)(2,1)S(1)}, bf16[160,512]{1,0:T(8,128)(2,1)S(1)}, u32[]{:S(2)}, u32[]{:S(2)}) collective-permute-start(bf16[160,512]{1,0:T(8,128)(2,1)S(1)} %get-tuple-element.105), channel_id=1, source_target_pairs={{0,16},{1,17},{2,18},{3,19},{4,20},{5,21},{6,22},{7,23},{8,24},{9,... | collective-permute-start | bytes 491528 | tf_op jit(solution)/shard_map/feed_back_far/ppermute | solution.py:405
  163.3 11.1 %copy-start.9 = (bf16[16,1024]{1,0:T(8,128)(2,1)S(1)}, bf16[16,1024]{1,0:T(8,128)(2,1)}, u32[]{:S(2)}) copy-start(bf16[16,1024]{1,0:T(8,128)(2,1)} %cand_ref.1) | copy-start | bytes 98308
  163.3 11.3 %copy-start.10 = (bf16[16,1024]{1,0:T(8,128)(2,1)S(1)}, bf16[16,1024]{1,0:T(8,128)(2,1)}, u32[]{:S(2)}) copy-start(bf16[16,1024]{1,0:T(8,128)(2,1)} %input_ref.1) | copy-start | bytes 98308
  163.3 9.8 %collective-permute-start.21 = (bf16[208,256]{1,0:T(8,128)(2,1)S(1)}, bf16[208,256]{1,0:T(8,128)(2,1)S(1)}, u32[]{:S(2)}, u32[]{:S(2)}) collective-permute-start(bf16[208,256]{1,0:T(8,128)(2,1)S(1)} %get-tuple-element.121), channel_id=1, source_target_pairs={{0,16},{1,17},{2,18},{3,19},{4,20},{5,21},{6,22},{7,23},{8,24},{9,... | collective-permute-start | bytes 319496 | tf_op jit(solution)/shard_map/mixer_back_z/ppermute | solution.py:405
  163.4 9.7 %collective-permute-start.22 = (bf16[208,256]{1,0:T(8,128)(2,1)S(1)}, bf16[208,256]{1,0:T(8,128)(2,1)S(1)}, u32[]{:S(2)}, u32[]{:S(2)}) collective-permute-start(bf16[208,256]{1,0:T(8,128)(2,1)S(1)} %get-tuple-element.123), channel_id=1, source_target_pairs={{0,8},{1,9},{2,10},{3,11},{4,12},{5,13},{6,14},{7,15},{8,0},{9,1},... | collective-permute-start | bytes 319496 | tf_op jit(solution)/shard_map/mixer_back_z/ppermute | solution.py:405
  166.0 7.1 %collective-permute-start.23 = (bf16[208,256]{1,0:T(8,128)(2,1)S(1)}, bf16[208,256]{1,0:T(8,128)(2,1)S(1)}, u32[]{:S(2)}, u32[]{:S(2)}) collective-permute-start(bf16[208,256]{1,0:T(8,128)(2,1)S(1)} %get-tuple-element.122), channel_id=1, source_target_pairs={{0,24},{1,25},{2,26},{3,27},{4,28},{5,29},{6,30},{7,31},{8,16},{9,... | collective-permute-start | bytes 319496 | tf_op jit(solution)/shard_map/mixer_back_z/ppermute | solution.py:405
  (11 other events, 41.0 us)

commit v3 on v2

v3 whole, which is shorter than its diff:
```python
import functools

import jax
import jax.numpy as jnp
import numpy as np
from jax import lax
from jax.experimental import pallas as pl
from jax.experimental.pallas import tpu as pltpu
from jax.sharding import PartitionSpec as P

LEN = 1024
EPSILON = 1e-06
AXES = ("dp", "mp")
SLOTS = 32
CHUNKS = 8
LANES = 256
GROUP = 8
BF = jnp.bfloat16
F32 = jnp.float32
MIB = 1024 * 1024
C0 = 0.7978845608028654
C1 = C0 * 0.044715


def params(mib):
    return pltpu.CompilerParams(vmem_limit_bytes=mib * MIB)


def dot(a, b, dims=((1,), (0,))):
    return lax.dot_general(a, b, (dims, ((), ())), preferred_element_type=F32)


def whole(shape):
    return pl.BlockSpec(shape, lambda *_: (0,) * len(shape), pipeline_mode=pl.Buffered(1))


def aligned(start, size):
    return pl.ds(pl.multiple_of(start, size), size)


def spread(small, piece, width):
    lane = lax.broadcasted_iota(jnp.int32, (LANES, width), 0)
    column = lax.broadcasted_iota(jnp.int32, (LANES, width), 1)
    pick = (lane == column % piece).astype(BF)
    placed = dot(small.astype(BF), pick)
    row = lax.broadcasted_iota(jnp.int32, (SLOTS, width), 0)
    col = lax.broadcasted_iota(jnp.int32, (SLOTS, width), 1)
    return jnp.sum(jnp.where(col // piece == row, placed, 0.0), axis=0, keepdims=True)


def collect(vector, offset, piece):
    width = vector.shape[1]
    row = lax.broadcasted_iota(jnp.int32, (SLOTS, width), 0)
    col = lax.broadcasted_iota(jnp.int32, (SLOTS, width), 1)
    kept = jnp.where(col // piece == row, vector, 0.0).astype(BF)
    column = lax.broadcasted_iota(jnp.int32, (width, LANES), 0)
    lane = lax.broadcasted_iota(jnp.int32, (width, LANES), 1)
    pick = (lane == offset + column % piece).astype(BF)
    return dot(kept, pick)


def pack_mixer(forget_ref, input_ref, cand_ref, gmix_ref, gmlp_ref, bias_ref, out_ref, small):
    blocks = forget_ref.shape[1] // LANES
    for b in range(blocks):
        for w, ref in enumerate((forget_ref, input_ref, cand_ref)):
            at = (b * 3 + w) * 16
            out_ref[at : at + 16, :] = ref[:, b * LANES : (b + 1) * LANES]
    small[...] = jnp.zeros_like(small)
    for k, ref in enumerate((gmix_ref, gmlp_ref, bias_ref)):
        small[k : k + 1, 0 : ref.shape[1]] = ref[...].astype(F32)
    out_ref[48 * blocks :, :] = small[...].astype(BF)


def mixer_prepare(dev_ref, parts, x_ref, xn_ref, xnt_ref, gain_ref, bias_s, small):
    per = SLOTS // 4
    tail = parts[0].shape[1] - 16
    for s in range(SLOTS):
        rows = parts[s // per][s % per, tail : tail + 16, :].astype(F32)
        for k in range(3):
            small[k, pl.ds(dev_ref[s], 1), :] = rows[k : k + 1, :]
    width, chans = x_ref.shape[1], bias_s.shape[1]
    piece = width // SLOTS
    gmix = spread(small[0], piece, width)
    gain_ref[0:1, :] = gmix
    gain_ref[1:2, :] = spread(small[1], piece, width)
    bias_s[...] = spread(small[2], chans // SLOTS, chans)

    def rows(i, _):
        at = aligned(i * 256, 256)
        v = x_ref[at, :].astype(F32)
        scale = lax.rsqrt(jnp.mean(v * v, axis=-1, keepdims=True) + EPSILON)
        xn = ((v * scale) * gmix).astype(BF)
        xn_ref[at, :] = xn
        xnt_ref[:, at] = xn.T
        return 0

    lax.fori_loop(0, x_ref.shape[0] // 256, rows, 0)


def mixer_forward(dev_ref, x_ref, g0, g1, g2, g3, hb_ref, o_ref, u1_ref, u2_ref, w_ref, xnt_ref, gain_ref,
                  small, bias_s, xn_s, k_s, c2_s, f_s):
    step = pl.program_id(0)
    per = SLOTS // 4
    parts = (g0, g1, g2, g3)

    @pl.when(step == 0)
    def _():
        mixer_prepare(dev_ref, parts, x_ref, xn_s, xnt_ref, gain_ref, bias_s, small)

    for s in range(SLOTS):
        d = dev_ref[s]
        for w in range(3):
            src = aligned((step * 3 + w) * 16, 16)
            w_ref[aligned(d * 16, 16), w * LANES : (w + 1) * LANES] = parts[s // per][s % per, src, :]

    bias = bias_s[:, aligned(step * LANES, LANES)]
    k_s[...] = dot(xn_s[...], w_ref[...])
    kf_c, ki_c, kc_c = (slice(w * LANES, (w + 1) * LANES) for w in range(3))
    zeros = jnp.zeros((CHUNKS, LANES), F32)
    tile = GROUP * CHUNKS
    count = xn_s.shape[0] // tile

    def first(i, carry):
        h, prod = carry
        at = aligned(i * tile, tile)
        kf = k_s[at, kf_c]
        ki = k_s[at, ki_c] + bias
        kc = k_s[at, kc_c]
        low = jnp.minimum(jnp.minimum(kf, ki), 0.0)
        one = jnp.exp(low)
        ef = jnp.exp(low - kf)
        ei = jnp.exp(low - ki)
        a = one + ei
        b = one + ef
        inv = 1.0 / (a + b)
        forget = a * inv
        other = b * inv
        f_s[at, :] = forget
        o_ref[at, :] = other.astype(BF)
        drive = other * kc
        k_s[at, kf_c] = forget * (inv * ef)
        k_s[at, ki_c] = other * (inv * ei)
        c2_s[at, :] = drive
        for k in range(GROUP):
            part = slice(k * CHUNKS, (k + 1) * CHUNKS)
            h = forget[part] * h + drive[part]
            prod = prod * forget[part]
        return h, prod

    last, prod = lax.fori_loop(0, count, first, (zeros, zeros + 1.0))
    sub = lax.broadcasted_iota(jnp.int32, (CHUNKS, LANES), 0)
    start = zeros
    for s in range(CHUNKS - 1):
        moved = pltpu.roll(last + prod * start, 1, 0)
        start = jnp.where(sub == s + 1, moved, start)

    def second(i, h):
        at = aligned(i * tile, tile)
        forget = f_s[at, :]
        drive = c2_s[at, :]
        before, after = [], []
        for k in range(GROUP):
            part = slice(k * CHUNKS, (k + 1) * CHUNKS)
            before.append(h)
            h = forget[part] * h + drive[part]
            after.append(h)
        diff = jnp.concatenate(before, axis=0) - k_s[at, kc_c]
        hb_ref[at, :] = jnp.concatenate(after, axis=0).astype(BF)
        u1_ref[at, :] = (k_s[at, kf_c] * diff).astype(BF)
        u2_ref[at, :] = (k_s[at, ki_c] * -diff).astype(BF)
        return h

    lax.fori_loop(0, count, second, start)


def feed_forward(dev_ref, gain_ref, g0, g1, g2, g3, hb_ref, x_ref, dy_ref,
                 out_ref, dmix_ref, wo_ref, low_ref, high_ref, send_ref, small_ref,
                 y1_s, xn_s, xnt_s, dyt_s, acc_s, dxn_s, up_s, dn_s, upg_s, dng_s, wog_s):
    parts = (g0, g1, g2, g3)
    per = SLOTS // 4
    tokens, width = x_ref.shape
    chans = hb_ref.shape[1]
    rows = width // 8
    feed = 2 * rows
    gain = gain_ref[1:2, :]

    def target(s):
        return (low_ref, high_ref, send_ref, send_ref)[s // per], s % per + (per if s >= 3 * per else 0)

    for s in range(SLOTS):
        wo_ref[aligned(dev_ref[s] * 32, 32), :] = parts[s // per][s % per, feed:, :]

    def rows_in(i, _):
        at = aligned(i * 256, 256)
        y1 = x_ref[at, :].astype(F32) + dot(hb_ref[at, :], wo_ref[...])
        y1_s[at, :] = y1
        scale = lax.rsqrt(jnp.mean(y1 * y1, axis=-1, keepdims=True) + EPSILON)
        xn = ((y1 * scale) * gain).astype(BF)
        xn_s[at, :] = xn
        xnt_s[:, at] = xn.T
        return 0

    lax.fori_loop(0, tokens // 256, rows_in, 0)
    dyt_s[...] = dy_ref[...].T

    for base in (0, SLOTS // 2):
        slots = range(base, base + SLOTS // 2)
        for s in slots:
            d = dev_ref[s]
            block, at = d // 2 % 2, aligned(d // 4 * rows, rows)
            up_s[block, at, :] = parts[s // per][s % per, 0:rows, :]
            dn_s[block, at, :] = parts[s // per][s % per, rows:feed, :]
        for block in range(2):
            pre = dot(xn_s[...], up_s[block])
            dact = dot(dy_ref[...], dn_s[block])
            sq = pre * pre
            gate = 0.5 + 0.5 * jnp.tanh(pre * (C0 + C1 * sq))
            value = pre * gate
            act = value.astype(BF)
            slope = gate + value * (1.0 - gate) * (2.0 * C0 + 6.0 * C1 * sq)
            dpre = (slope * dact).astype(BF)
            upg_s[block] = dot(xnt_s[...], dpre).astype(BF)
            dng_s[block] = dot(dyt_s[...], act).astype(BF)
            out = dot(act, dn_s[block], ((1,), (1,)))
            dxn = dot(dpre, up_s[block], ((1,), (1,)))
            if base + block == 0:
                acc_s[...] = out
                dxn_s[...] = dxn
            else:
                acc_s[...] += out
                dxn_s[...] += dxn
        for s in slots:
            d = dev_ref[s]
            block, at = d // 2 % 2, aligned(d // 4 * rows, rows)
            ref, k = target(s)
            ref[k, 0:rows, :] = upg_s[block, at, :]
            ref[k, rows:feed, :] = dng_s[block, at, :]

    total = jnp.zeros((1, width), F32)
    for i in range(tokens // 256):
        at = slice(i * 256, (i + 1) * 256)
        y1 = y1_s[at, :]
        scale = lax.rsqrt(jnp.mean(y1 * y1, axis=-1, keepdims=True) + EPSILON)
        n2 = y1 * scale
        out_ref[at, :] = (y1 + acc_s[at, :]).astype(BF)
        dxn = dxn_s[at, :]
        dn = dxn * gain
        dy1 = dy_ref[at, :].astype(F32) + scale * (dn - n2 * jnp.mean(dn * n2, axis=-1, keepdims=True))
        dmix_ref[at, :] = dy1.astype(BF)
        total = total + jnp.sum(dxn * n2, axis=0, keepdims=True)
    small_ref[...] = collect(total, 0, width // SLOTS)

    span = 256
    for b in range(chans // span):
        wog_s[b * span : (b + 1) * span, :] = dot(
            hb_ref[:, b * span : (b + 1) * span], dmix_ref[...], ((0,), (0,))
        ).astype(BF)
    for s in range(SLOTS):
        ref, k = target(s)
        ref[k, feed:, :] = wog_s[aligned(dev_ref[s] * 32, 32), :]


def mixer_backward(dev_ref, dmix_ref, xnt_ref, wo_ref, small_ref, o_ref, u1_ref, u2_ref,
                   dk_ref, keep_ref, send_ref, bias_s, dh_s, grad_s):
    step = pl.program_id(0)
    blocks = pl.num_programs(0)
    width, tokens = xnt_ref.shape
    half = SLOTS // 2

    @pl.when(step == 0)
    def _():
        for b in range(dh_s.shape[0]):
            dh_s[b] = dot(dmix_ref[...], wo_ref[b * LANES : (b + 1) * LANES, :], ((1,), (1,)))

    zeros = jnp.zeros((CHUNKS, LANES), F32)
    tile = GROUP * CHUNKS
    count = tokens // tile

    def first(i, carry):
        g, prod, decay = carry
        at = aligned((count - 1 - i) * tile, tile)
        dh = dh_s[step, at, :]
        forget = 1.0 - o_ref[at, :].astype(F32)
        for k in reversed(range(GROUP)):
            part = slice(k * CHUNKS, (k + 1) * CHUNKS)
            g = dh[part] + decay * g
            prod = prod * decay
            decay = forget[part]
        return g, prod, decay

    ones = zeros + 1.0
    head, prod, decay = lax.fori_loop(0, count, first, (zeros, ones, ones))
    sub = lax.broadcasted_iota(jnp.int32, (CHUNKS, LANES), 0)
    start = zeros
    for s in reversed(range(1, CHUNKS)):
        moved = pltpu.roll(decay * (head + prod * start), CHUNKS - 1, 0)
        start = jnp.where(sub == s - 1, moved, start)

    def second(i, carry):
        g, decay, total = carry
        at = aligned((count - 1 - i) * tile, tile)
        dh = dh_s[step, at, :]
        other = o_ref[at, :].astype(F32)
        forget = 1.0 - other
        parts = [None] * GROUP
        for k in reversed(range(GROUP)):
            part = slice(k * CHUNKS, (k + 1) * CHUNKS)
            g = dh[part] + decay * g
            decay = forget[part]
            parts[k] = g
        grad = jnp.concatenate(parts, axis=0)
        dk_ref[at, 0:LANES] = (u1_ref[at, :].astype(F32) * grad).astype(BF)
        di = (u2_ref[at, :].astype(F32) * grad).astype(BF)
        dk_ref[at, LANES : 2 * LANES] = di
        dk_ref[at, 2 * LANES : 3 * LANES] = (other * grad).astype(BF)
        di = di.astype(F32)
        for k in range(GROUP):
            total = total + di[k * CHUNKS : (k + 1) * CHUNKS]
        return g, decay, total

    _, _, total = lax.fori_loop(0, count, second, (start, ones, zeros))
    bias_s[:, aligned(step * LANES, LANES)] = jnp.sum(total, axis=0, keepdims=True)

    grad_s[...] = dot(xnt_ref[...], dk_ref[...]).astype(BF)
    for s in range(SLOTS):
        target = keep_ref if s < half else send_ref
        src = aligned(dev_ref[s] * 16, 16)
        for w in range(3):
            dst = aligned((step * 3 + w) * 16, 16)
            target[s % half, dst, :] = grad_s[src, w * LANES : (w + 1) * LANES]

    @pl.when(step == blocks - 1)
    def _():
        bias = bias_s[...]
        piece = width // SLOTS
        values = small_ref[...] + collect(bias, 2 * piece, bias.shape[1] // SLOTS)
        dh_s[0, 0:SLOTS, :] = values
        row = lax.broadcasted_iota(jnp.int32, (16, LANES), 0)
        tail = keep_ref.shape[1] - 16
        for s in range(SLOTS):
            target = keep_ref if s < half else send_ref
            values = dh_s[0, pl.ds(dev_ref[s], 1), :]
            target[s % half, tail : tail + 16, :] = jnp.where(row == 0, values, 0.0).astype(BF)


def input_gradient(x_ref, dmix_ref, gain_ref, dk_ref, w_ref, out_ref):
    size = dk_ref.shape[2]
    dxn = dot(dk_ref[0], w_ref[:, :size], ((1,), (1,)))
    for b in range(1, dk_ref.shape[0]):
        dxn = dxn + dot(dk_ref[b], w_ref[:, b * size : (b + 1) * size], ((1,), (1,)))
    v = x_ref[...].astype(F32)
    scale = lax.rsqrt(jnp.mean(v * v, axis=-1, keepdims=True) + EPSILON)
    n1 = v * scale
    dn = dxn * gain_ref[0:1, :]
    out_ref[...] = dmix_ref[...].astype(F32) + scale * (dn - n1 * jnp.mean(dn * n1, axis=-1, keepdims=True))


def finish_mixer(own_ref, p0, p1, p2, forget_ref, input_ref, cand_ref, gain_ref,
                 fg_ref, ig_ref, cg_ref, gmix_ref, gmlp_ref, bias_ref):
    total = own_ref[...].astype(F32)
    for ref in (p0, p1, p2):
        total = total + ref[...].astype(F32)
    chans = fg_ref.shape[1]
    dots = jnp.zeros((16, 1), F32)
    for b in range(chans // LANES):
        cols = slice(b * LANES, (b + 1) * LANES)
        for w, (ref, weight) in enumerate(((fg_ref, forget_ref), (ig_ref, input_ref), (cg_ref, cand_ref))):
            grad = total[(b * 3 + w) * 16 : (b * 3 + w + 1) * 16]
            ref[:, cols] = grad
            dots = dots + jnp.sum(grad * weight[:, cols].astype(F32), axis=1, keepdims=True)
    row = jnp.broadcast_to(dots, (16, 128)).T[0:1, :]
    gmix_ref[...] = row / gain_ref[...].astype(F32)
    edge = total[chans // LANES * 48 : chans // LANES * 48 + 1]
    piece = gmlp_ref.shape[1]
    gmlp_ref[...] = edge[:, :piece]
    bias_ref[...] = edge[:, 2 * piece : 2 * piece + bias_ref.shape[1]]


def order_table():
    table = np.zeros((SLOTS, SLOTS), np.int32)
    for me in range(SLOTS):
        core, y, x, z = me & 1, me >> 1 & 1, me >> 2 & 1, me >> 3
        for slot in range(SLOTS):
            oc, second, first, oz = slot >> 4, slot >> 3 & 1, slot >> 2 & 1, (slot & 1) << 1 | slot >> 1 & 1
            c2 = core ^ oc
            x2 = x ^ (first if c2 == 0 else second)
            y2 = y ^ (second if c2 == 0 else first)
            table[me, slot] = ((z ^ oz) * 2 + x2) * 4 + y2 * 2 + c2
    return table


def flip(x0, y0, z0, c0, x1, y1, z1, c1):
    pairs = []
    for me in range(SLOTS):
        x, y, z, c = (x1, y1, z1, c1) if me & 1 else (x0, y0, z0, c0)
        pairs.append((me, me ^ (z << 3 | x << 2 | y << 1 | c)))
    return pairs


FAR, NEAR, BOTH = [flip(0, 0, k, 0, 0, 0, k, 0) for k in (2, 1, 3)]
FIRST = flip(1, 0, 0, 0, 0, 1, 0, 0)
SECOND = flip(0, 1, 0, 0, 1, 0, 0, 0)
CORE = flip(0, 0, 0, 1, 0, 0, 0, 1)


def send(value, pairs, name):
    with jax.named_scope(name):
        return lax.ppermute(value, AXES, pairs)


def after(value, *others):
    return lax.optimization_barrier((value,) + others)[0]


def after_all(*values):
    return lax.optimization_barrier(values)


def add(a, b):
    return (a.astype(F32) + b.astype(F32)).astype(BF)


def fold(low, high, pairs, name):
    got = send(high, pairs, name)
    half = low.shape[0] // 2
    return add(low[:half], got[:half]), add(low[half:], got[half:])


def pack(forget_weight, input_weight, candidate_weight, gain_mix, gain_mlp, input_gate_bias):
    rows = 3 * forget_weight.shape[1] // LANES * 16 + 16
    return pl.pallas_call(
        pack_mixer,
        out_shape=jax.ShapeDtypeStruct((rows, LANES), BF),
        scratch_shapes=[pltpu.VMEM((16, LANES), F32)],
        compiler_params=params(60),
        name="pack",
    )(forget_weight, input_weight, candidate_weight, gain_mix[None], gain_mlp[None], input_gate_bias[None])


def local(fast, tokens, gain_mix, gain_mlp, forget_weight, input_weight, candidate_weight, input_gate_bias,
          output_weight, up_weight, down_weight, cotangent):
    rows, width = tokens.shape
    chans = forget_weight.shape[1]
    blocks = chans // LANES
    shard = width // SLOTS

    def permute(v):
        return v.reshape(CHUNKS, rows // CHUNKS, width).transpose(1, 0, 2).reshape(rows, width)

    def restore(v):
        return v.reshape(rows // CHUNKS, CHUNKS, width).transpose(1, 0, 2).reshape(rows, width)

    xp = permute(tokens)
    dyp = permute(cotangent)
    if fast:
        me = lax.axis_index(AXES)
        table = order_table()
        dev = lax.dynamic_index_in_dim(jnp.asarray(table), me, keepdims=False)
        piece = pack(forget_weight, input_weight, candidate_weight, gain_mix, gain_mlp, input_gate_bias)
        four = jnp.stack([piece] + [send(piece, p, "mixer_z") for p in (FAR, NEAR, BOTH)])
        four, piece_f = after_all(four, jnp.concatenate([up_weight, down_weight.T, output_weight]), dev, xp, dyp)[:2]
        got, far_f = after_all(send(four, FIRST, "mixer_first"), send(piece_f, FAR, "feed_far"))
        eight = jnp.concatenate([four, got])
        two_f = jnp.stack([piece_f, far_f])
        eight, two_f = after_all(eight, two_f)
        more, got = after_all(send(eight, SECOND, "mixer_second"), send(two_f, NEAR, "feed_near"))
        four_f = jnp.concatenate([two_f, got])
        more, four_f = after_all(more, four_f)
        got, core, core_more = after_all(
            send(four_f, FIRST, "feed_first"), send(eight, CORE, "mixer_core"), send(more, CORE, "mixer_core_more")
        )
        eight_f = jnp.concatenate([four_f, got])
        mixer = (eight, more, core, core_more)
        mixer, eight_f = lax.optimization_barrier((mixer, eight_f))
        more_f = send(eight_f, SECOND, "feed_second")
    else:
        order = np.argsort(np.arange(SLOTS) % 2, kind="stable").astype(np.int32)
        dev = jnp.asarray(order)

        def full(v, axis=0, names=AXES):
            return lax.all_gather(v, names, axis=axis, tiled=True)

        gm, gl, gb = full(gain_mix), full(gain_mlp), full(input_gate_bias)
        weights = [full(w) for w in (forget_weight, input_weight, candidate_weight)]
        smalls = [v.reshape(SLOTS, -1) for v in (gm, gl, gb)]
        up = full(full(up_weight, 0, "dp"), 1, "mp")
        down = full(full(down_weight, 1, "dp"), 0, "mp")

        def regroup(w):
            return w.reshape(8, width // 8, 4, width).transpose(0, 2, 1, 3).reshape(SLOTS, width // 8, width)

        both = jnp.concatenate([regroup(up), regroup(down.T), full(output_weight).reshape(SLOTS, -1, width)], axis=1)

        def quarters(v):
            return tuple(jnp.stack([v[d] for d in order[k * 8 : (k + 1) * 8]]) for k in range(4))

        mixer = quarters(
            jnp.stack([pack(*[w[s * 16 : (s + 1) * 16] for w in weights], *[v[s] for v in smalls]) for s in range(SLOTS)])
        )
        feed = quarters(both)

    smem = pl.BlockSpec(memory_space=pltpu.SMEM)
    vmem = pl.BlockSpec(memory_space=pltpu.VMEM)
    part = 256

    def band(cols):
        return pl.BlockSpec((part, cols), lambda i: (i, 0))

    def shapes(*items):
        return [jax.ShapeDtypeStruct(shape, kind) for shape, kind in items]

    column = pl.BlockSpec((rows, LANES), lambda i: (0, i))
    block = pl.BlockSpec((None, rows, LANES), lambda i: (i, 0, 0))

    wide = pl.BlockSpec((width, 3 * LANES), lambda i: (0, i))
    hb, other, u1, u2, w3, xn1t, gains = pl.pallas_call(
        mixer_forward,
        grid=(blocks,),
        in_specs=[smem, whole((rows, width))] + [whole(mixer[0].shape)] * 4,
        out_specs=[column] + [block] * 3 + [wide, whole((width, rows)), whole((2, width))],
        out_shape=shapes(((rows, chans), BF), *[((blocks, rows, LANES), BF)] * 3,
                         ((width, 3 * chans), BF), ((width, rows), BF), ((2, width), F32)),
        scratch_shapes=[pltpu.VMEM((3, SLOTS, LANES), F32), pltpu.VMEM((1, chans), F32), pltpu.VMEM((rows, width), BF),
                        pltpu.VMEM((rows, 3 * LANES), F32), pltpu.VMEM((rows, LANES), F32),
                        pltpu.VMEM((rows, LANES), F32)],
        compiler_params=params(16),
        cost_estimate=pl.CostEstimate(flops=6 * rows * width * chans, bytes_accessed=32 << 20, transcendentals=0),
        name="mixer_forward",
    )(dev, xp, *mixer)
    if fast:
        last = after(more_f, hb)
        feed = (eight_f, more_f, send(eight_f, CORE, "feed_core"), send(last, CORE, "feed_core_more"))

    size = width // 8
    piece = feed[0].shape[1:]
    block_out, dmix, wo, low1, high1, send1, gmlp_small = pl.pallas_call(
        feed_forward,
        in_specs=[smem] + [vmem] * 8,
        out_specs=[vmem] * 7,
        out_shape=shapes(((rows, width), BF), ((rows, width), BF), ((chans, width), BF),
                         *[((count,) + piece, BF) for count in (SLOTS // 4, SLOTS // 4, SLOTS // 2)], ((SLOTS, LANES), F32)),
        scratch_shapes=[
            pltpu.VMEM((rows, width), F32),
            pltpu.VMEM((rows, width), BF),
            pltpu.VMEM((width, rows), BF),
            pltpu.VMEM((width, rows), BF),
            pltpu.VMEM((rows, width), F32),
            pltpu.VMEM((rows, width), F32),
            *[pltpu.VMEM((2, width, width), BF)] * 4,
            pltpu.VMEM((chans, width), BF),
        ],
        compiler_params=params(30),
        cost_estimate=pl.CostEstimate(flops=2 * rows * width * (24 * width + 2 * chans), bytes_accessed=60 << 20, transcendentals=0),
        name="feed_forward",
    )(dev, gains, *feed, hb, xp, dyp)

    if fast:
        half = SLOTS // 4
        got = send(send1, CORE, "feed_back_core")
        high = add(high1, got[half:])
        high, dmix = after_all(high, dmix)
    piece = (SLOTS // 2, 3 * blocks * 16 + 16, LANES)
    dk, keep2, send2 = pl.pallas_call(
        mixer_backward,
        grid=(blocks,),
        in_specs=[smem, whole((rows, width)), whole((width, rows)), whole((chans, width)), whole((SLOTS, LANES)),
                  block, block, block],
        out_specs=[pl.BlockSpec((None, rows, 3 * LANES), lambda i: (i, 0, 0))] + [whole(piece)] * 2,
        out_shape=shapes(((blocks, rows, 3 * LANES), BF), (piece, BF), (piece, BF)),
        scratch_shapes=[pltpu.VMEM((1, chans), F32), pltpu.VMEM((blocks, rows, LANES), F32),
                        pltpu.VMEM((width, 3 * LANES), BF)],
        compiler_params=params(16),
        cost_estimate=pl.CostEstimate(flops=8 * rows * width * chans, bytes_accessed=40 << 20, transcendentals=0),
        name="mixer_backward",
    )(dev, dmix, xn1t, wo, gmlp_small, other, u1, u2)

    def input_grad(dk_later):
        return pl.pallas_call(
            input_gradient,
            grid=(rows // part,),
            in_specs=[band(width), band(width), whole((2, width))] + [pl.BlockSpec((blocks, part, 3 * LANES), lambda i: (0, i, 0)), whole((width, 3 * chans))],
            out_specs=band(width),
            out_shape=jax.ShapeDtypeStruct((rows, width), F32),
            compiler_params=params(14),
            cost_estimate=pl.CostEstimate(flops=6 * rows * width * chans, bytes_accessed=24 << 20, transcendentals=0),
            name="input_gradient",
        )(xp, dmix, gains, dk_later, w3)

    def uncut(v):
        v = v[:, : 48 * blocks].reshape(-1, blocks, 3, 16, LANES)
        return [v[:, :, k].transpose(0, 2, 1, 3).reshape(-1, 16, chans) for k in range(3)]

    if fast:
        low = add(after(low1, dk), got[:half])
        low, high = fold(low, high, SECOND, "feed_back_second")
        low, high = fold(low, after(high, dk), FIRST, "feed_back_first")
        got = send(send2, CORE, "mixer_back_core")
        mlow, mhigh = add(keep2[:half], got[:half]), add(keep2[half:], got[half:])
        mlow, mhigh, low, high, dk = after_all(mlow, mhigh, low, high, dk)
        got, near, tokens_grad = after_all(
            send(mhigh, SECOND, "mixer_back_second"), send(high, NEAR, "feed_back_near"), input_grad(dk)
        )
        low, high = add(low[0], near[0]), add(low[1], near[1])
        half = SLOTS // 8
        mlow, mhigh = add(mlow[:half], got[:half]), add(mlow[half:], got[half:])
        mlow, mhigh, low, high = after_all(mlow, mhigh, low, high)
        got, far = after_all(send(mhigh, FIRST, "mixer_back_first"), send(high, FAR, "feed_back_far"))
        four = add(mlow, got)
        first = low.astype(F32) + far.astype(F32)
        parts = [send(four[k + 1], p, "mixer_back_z") for k, p in enumerate((FAR, NEAR, BOTH))]
        up_grad, down_grad, out_grad = first[:size], first[size : 2 * size].T, first[2 * size :]
        *grads, gmix_grad, gmlp_grad, bias_grad = pl.pallas_call(
            finish_mixer,
            out_shape=shapes(*[((16, chans), F32)] * 3, ((1, shard), F32), ((1, shard), F32), ((1, chans // SLOTS), F32)),
            compiler_params=params(16),
            name="finish",
        )(four[0], *parts, forget_weight, input_weight, candidate_weight, gain_mix[None])
        gmix_grad, gmlp_grad, bias_grad = gmix_grad[0], gmlp_grad[0], bias_grad[0]
    else:
        tokens_grad = input_grad(dk)
        first, total = (
            jnp.stack([jnp.concatenate(v)[k] for k in np.argsort(order)]).astype(F32)
            for v in ((low1, high1, send1), (keep2, send2))
        )

        def summed(v, axis=0, names=AXES):
            return lax.psum_scatter(v, names, scatter_dimension=axis, tiled=True)

        def joined(base):
            w = first[:, base : base + size]
            return w.reshape(8, 4, size, width).transpose(0, 2, 1, 3).reshape(width, 4 * width)

        up_grad = summed(summed(joined(0), 0, "dp"), 1, "mp")
        down_grad = summed(summed(joined(size).T, 1, "dp"), 0, "mp")
        out_grad = summed(first[:, 2 * size :].reshape(chans, width))
        grads = [summed(v.reshape(width, chans)) for v in uncut(total)]
        edge = total[:, 48 * blocks]
        gmlp_grad = summed(edge[:, :shard].reshape(-1))
        bias_grad = summed(edge[:, 2 * shard : 2 * shard + chans // SLOTS].reshape(-1))
        dots = sum(
            jnp.sum(w.astype(F32) * g, axis=1) for w, g in zip((forget_weight, input_weight, candidate_weight), grads)
        )
        gmix_grad = dots / gain_mix.astype(F32)

    return (restore(block_out), restore(tokens_grad), gmix_grad, gmlp_grad, grads[0], grads[1], grads[2], bias_grad,
            out_grad, up_grad, down_grad)


def solution(mesh):
    fast = mesh.shape["dp"] == 8 and mesh.shape["mp"] == 4
    every = P(AXES, None)
    in_specs = (every, P(AXES), P(AXES), every, every, every, P(AXES), every, P("dp", "mp"), P("mp", "dp"), every)
    out_specs = (every, every, P(AXES), P(AXES), every, every, every, P(AXES), every, P("dp", "mp"), P("mp", "dp"))
    return jax.shard_map(
        functools.partial(local, fast), mesh=mesh, in_specs=in_specs, out_specs=out_specs, check_vma=False
    )
```

time: 176 us -> 161 us (0.915)
  Pallas kernels: 69.1 us -> 50.3 us
  waiting for transfers between devices: 58 us -> 76.8 us
  other arithmetic: 9.97 us -> 2.54 us
  local copies, waits for them, and re-layouts: 12.4 us -> 8.67 us
  starting transfers between devices: 25 us -> 21.6 us
    ppermute x24, waiting for transfers between devices: 58 us -> 76.8 us  [send(): return lax.ppermute(value, AXES, pairs)]
    pallas_call x2 -> x3, Pallas kernels: 35 us -> 26.5 us  [the longest x1 20.8 us: local(): pl.pallas_call(feed_forward, in_specs=[smem] + [vmem] * 8, out_specs=[vme...]
    pallas_call x1, Pallas kernels: 18 us -> 12.4 us  [local(): pl.pallas_call(mixer_forward, grid=(blocks,), in_specs=[smem, whole((rows...]
    convert_element_type x7 -> x8, other arithmetic: 7.28 us -> 2.15 us  [add(): return (a.astype(F32) + b.astype(F32)).astype(BF)]
    pallas_call x1, Pallas kernels: 14.6 us -> 9.96 us  [local(): pl.pallas_call(mixer_backward, grid=(blocks,), in_specs=[smem, whole((row...]
    ppermute x24, starting transfers between devices: 25 us -> 21.6 us  [send(): return lax.ppermute(value, AXES, pairs)]
  transfers between devices with their start and end apart: 24 -> 24, of which waited for: 13 -> 16; matrix products, arithmetic and copies ran while one was open for 8% -> 6% of each run, Pallas kernels for 24% -> 17%
where the time goes in v3:
time: 161 us
  waiting for transfers between devices  76.8 us (48%)
  Pallas kernels  50.3 us (31%)
  starting transfers between devices  21.6 us (13%)
  local copies, waits for them, and re-layouts  8.67 us (5%)
  other arithmetic  2.54 us (2%)
    ppermute x24, waiting for transfers between devices, send(): return lax.ppermute(value, AXES, pairs)  76.8 us
    ppermute x24, starting transfers between devices, send(): return lax.ppermute(value, AXES, pairs)  21.6 us
    pallas_call x1, Pallas kernels, local(): pl.pallas_call(feed_forward, in_specs=[smem] + [vmem] * 8, out_specs=[vme...  20.8 us
    pallas_call x1, Pallas kernels, local(): pl.pallas_call(mixer_forward, grid=(blocks,), in_specs=[smem, whole((rows...  12.4 us
    pallas_call x1, Pallas kernels, local(): pl.pallas_call(mixer_backward, grid=(blocks,), in_specs=[smem, whole((row...  9.96 us
    pallas_call x1, Pallas kernels, input_grad(): pl.pallas_call(input_gradient, grid=(rows // part,), in_specs=[band(width...  4.98 us
    transpose x2, local copies, waits for them, and re-layouts, restore(): v.reshape(rows // CHUNKS, CHUNKS, width).transpose(1, 0, 2)  3.82 us
  transfers between devices with their start and end apart: 24, of which 16 were waited for; matrix products, arithmetic and copies ran while one was open for 6% of the time, Pallas kernels for 17%

profile of v3, /device:TPU:0, one launch (start us, length us, event | category | flops | bytes accessed | tf_op | source)
XLA Modules:
  0.0 160.8 jit_solution(16933565750511962322)
XLA Ops:
  0.6 1.5 pack.1
  2.1 5.0 %collective-permute-start.2 = (bf16[208,256]{1,0:T(8,128)(2,1)}, bf16[208,256]{1,0:T(8,128)(2,1)S(1)}, u32[]{:S(2)}, u32[]{:S(2)}) collective-permute-start(bf16[208,256]{1,0:T(8,128)(2,1)} %pack.1), channel_id=1, source_target_pairs={{0,24},{1,25},{2,26},{3,27},{4,28},{5,29},{6,30},{7,31},{8,16},{9,... | collective-permute-start | bytes 319496 | tf_op jit(solution)/shard_map/mixer_z/ppermute | solution.py:408
  7.7 2.7 %copy_bitcast_fusion = (bf16[1024,512]{1,0:T(8,128)(2,1)S(1)}, bf16[1024,512]{1,0:T(8,128)(2,1)S(1)}) fusion(bf16[8,128,512]{2,1,0:T(8,128)(2,1)} %bitcast.53, bf16[8,128,512]{2,1,0:T(8,128)(2,1)} %bitcast.54), kind=kLoop, calls=%fused_computation.7 | loop fusion | bytes 4194304 | tf_op jit(solution)/shard_map/reshape | solution.py:448
  11.2 2.5 %collective-permute-done.1 = bf16[208,256]{1,0:T(8,128)(2,1)S(1)} collective-permute-done((bf16[208,256]{1,0:T(8,128)(2,1)}, bf16[208,256]{1,0:T(8,128)(2,1)S(1)}, u32[]{:S(2)}, u32[]{:S(2)}) %collective-permute-start.1) | collective-permute-done | bytes 106528 | tf_op jit(solution)/shard_map/mixer_z/ppermute | solution.py:408
  13.7 2.6 %collective-permute-done = bf16[208,256]{1,0:T(8,128)(2,1)S(1)} collective-permute-done((bf16[208,256]{1,0:T(8,128)(2,1)}, bf16[208,256]{1,0:T(8,128)(2,1)S(1)}, u32[]{:S(2)}, u32[]{:S(2)}) %collective-permute-start) | collective-permute-done | bytes 106528 | tf_op jit(solution)/shard_map/mixer_z/ppermute | solution.py:408
  16.4 1.6 collective-permute-start.3
  18.0 1.3 collective-permute-start.4
  19.2 8.3 %collective-permute-done.4 = bf16[160,512]{1,0:T(8,128)(2,1)S(1)} collective-permute-done((bf16[160,512]{1,0:T(8,128)(2,1)S(1)}, bf16[160,512]{1,0:T(8,128)(2,1)S(1)}, u32[]{:S(2)}, u32[]{:S(2)}) %collective-permute-start.4) | collective-permute-done | bytes 163872 | tf_op jit(solution)/shard_map/feed_far/ppermute | solution.py:408
  28.5 9.6 %collective-permute-done.6 = bf16[2,160,512]{2,1,0:T(8,128)(2,1)S(1)} collective-permute-done((bf16[2,160,512]{2,1,0:T(8,128)(2,1)S(1)}, bf16[2,160,512]{2,1,0:T(8,128)(2,1)S(1)}, u32[]{:S(2)}, u32[]{:S(2)}) %collective-permute-start.6) | collective-permute-done | bytes 327712 | tf_op jit(solution)/shard_map/feed_near/ppermute | solution.py:408
  38.1 2.2 %collective-permute-done.5.g1 = bf16[8,208,256]{2,1,0:T(8,128)(2,1)S(1)} collective-permute-done((bf16[8,208,256]{2,1,0:T(8,128)(2,1)S(1)}, bf16[8,208,256]{2,1,0:T(8,128)(2,1)S(1)}, u32[]{:S(2)}, u32[]{:S(2)}) %collective-permute-start.5) | collective-permute-done | bytes 852000 | tf_op jit(solution)/shard_map/mixer_second/ppermute | solution.py:408
  40.5 1.6 collective-permute-start.7
  42.1 9.1 %collective-permute-done.7 = bf16[4,160,512]{2,1,0:T(8,128)(2,1)S(1)} collective-permute-done((bf16[4,160,512]{2,1,0:T(8,128)(2,1)S(1)}, bf16[4,160,512]{2,1,0:T(8,128)(2,1)S(1)}, u32[]{:S(2)}, u32[]{:S(2)}) %collective-permute-start.7) | collective-permute-done | bytes 655392 | tf_op jit(solution)/shard_map/feed_first/ppermute | solution.py:408
  52.1 12.4 %mixer_forward.1 = (bf16[1024,1024]{1,0:T(8,128)(2,1)S(1)}, bf16[4,1024,256]{2,1,0:T(8,128)(2,1)S(1)}, bf16[4,1024,256]{2,1,0:T(8,128)(2,1)S(1)}, bf16[4,1024,25...) custom-call(s32[32]{0:T(128)S(1)} %dynamic-slice_bitcast_fusion.dev_r, ...), custom_call_target="tpu_custom_call" | custom-call | flops 3221225472 | bytes 33554432 | tf_op jit(solution)/shard_map/mixer_forward/pallas_call | solution.py:516
  64.6 4.4 %collective-permute-done.10.g1 = bf16[8,160,512]{2,1,0:T(8,128)(2,1)S(1)} collective-permute-done((bf16[8,160,512]{2,1,0:T(8,128)(2,1)S(1)}, bf16[8,160,512]{2,1,0:T(8,128)(2,1)S(1)}, u32[]{:S(2)}, u32[]{:S(2)}) %collective-permute-start.10) | collective-permute-done | bytes 1310752 | tf_op jit(solution)/shard_map/feed_second/ppermute | solution.py:408
  69.0 3.0 %collective-permute-done.12.g3 = bf16[8,160,512]{2,1,0:T(8,128)(2,1)S(1)} collective-permute-done((bf16[8,160,512]{2,1,0:T(8,128)(2,1)S(1)}, bf16[8,160,512]{2,1,0:T(8,128)(2,1)S(1)}, u32[]{:S(2)}, u32[]{:S(2)}) %collective-permute-start.12) | collective-permute-done | bytes 1310752 | tf_op jit(solution)/shard_map/feed_core_more/ppermute | solution.py:408
  72.0 20.8 %feed_forward.1 = (bf16[1024,512]{1,0:T(8,128)(2,1)S(1)}, bf16[1024,512]{1,0:T(8,128)(2,1)S(1)}, bf16[1024,512]{1,0:T(8,128)(2,1)S(1)}, bf16[8,160,512]{2,1,0:T(...) custom-call(s32[32]{0:T(128)S(1)} %dynamic-slice_bitcast_fusion.dev_ref,, ...), custom_call_target="tpu_custom_call" | custom-call | flops 15032385536 | bytes 62914560 | tf_op jit(solution)/shard_map/feed_forward/pallas_call | solution.py:536
  93.0 4.8 %collective-permute-done.13 = bf16[16,160,512]{2,1,0:T(8,128)(2,1)S(1)} collective-permute-done((bf16[16,160,512]{2,1,0:T(8,128)(2,1)S(1)}, bf16[16,160,512]{2,1,0:T(8,128)(2,1)S(1)}, u32[]{:S(2)}, u32[]{:S(2)}) %collective-permute-start.13) | collective-permute-done | bytes 2621472 | tf_op jit(solution)/shard_map/feed_back_core/ppermute | solution.py:408
  98.6 10.0 %mixer_backward.1 = (bf16[4,1024,768]{2,1,0:T(8,128)(2,1)S(1)}, bf16[16,208,256]{2,1,0:T(8,128)(2,1)S(1)}, bf16[16,208,256]{2,1,0:T(8,128)(2,1)S(1)}) custom-call(s32[32]{0:T(128)S(1)} %dynamic-slice_bitcast_fusion.dev_ref, bf16[1024,512]{1,0:T(8,128)(2,1)S(1)} %get-tuple-element.96.dmix_ref, bf16[512,1024]{1,0:T(8,128)(2,1)S(1)} %get-tuple-element.97.xnt_ref, ...), custom_call_target="tpu_custom_call" | custom-call | flops 4294967296 | bytes 41943040 | tf_op jit(solution)/shard_map/mixer_backward/pallas_call | solution.py:563
  108.6 1.0 collective-permute-start.14
  110.0 5.8 %collective-permute-done.15 = bf16[8,160,512]{2,1,0:T(8,128)(2,1)S(1)} collective-permute-done((bf16[8,160,512]{2,1,0:T(8,128)(2,1)S(1)}, bf16[8,160,512]{2,1,0:T(8,128)(2,1)S(1)}, u32[]{:S(2)}, u32[]{:S(2)}) %collective-permute-start.15) | collective-permute-done | bytes 1310752 | tf_op jit(solution)/shard_map/feed_back_second/ppermute | solution.py:408
  116.2 1.6 collective-permute-start.16
  118.2 8.7 %collective-permute-done.16 = bf16[4,160,512]{2,1,0:T(8,128)(2,1)S(1)} collective-permute-done((bf16[4,160,512]{2,1,0:T(8,128)(2,1)S(1)}, bf16[4,160,512]{2,1,0:T(8,128)(2,1)S(1)}, u32[]{:S(2)}, u32[]{:S(2)}) %collective-permute-start.16) | collective-permute-done | bytes 655392 | tf_op jit(solution)/shard_map/feed_back_first/ppermute | solution.py:408
  127.5 5.0 %input_gradient.1 = f32[1024,512]{1,0:T(8,128)S(1)} custom-call(bf16[1024,512]{1,0:T(8,128)(2,1)S(1)} %get-tuple-element.148.x_ref, bf16[1024,512]{1,0:T(8,128)(2,1)S(1)} %get-tuple-element.96.dmix_ref, f32[2,512]{1,0:T(2,128)S(1)} %get-tuple-element.88.gain_ref, bf16[4,1024,768]{2,1,0:T(8,128)(2,1)S(1)} %get-tuple-element.112.dk_ref, ...), custom_call_target="tpu_custom_call" | custom-call | flops 3221225472 | bytes 25165824 | tf_op jit(solution)/shard_map/input_gradient/pallas_call | solution.py:578
  132.5 3.9 %collective-permute-done.18 = bf16[2,160,512]{2,1,0:T(8,128)(2,1)S(1)} collective-permute-done((bf16[2,160,512]{2,1,0:T(8,128)(2,1)S(1)}, bf16[2,160,512]{2,1,0:T(8,128)(2,1)S(1)}, u32[]{:S(2)}, u32[]{:S(2)}) %collective-permute-start.18) | collective-permute-done | bytes 327712 | tf_op jit(solution)/shard_map/feed_back_near/ppermute | solution.py:408
  136.4 3.4 %collective-permute-done.17 = bf16[8,208,256]{2,1,0:T(8,128)(2,1)S(1)} collective-permute-done((bf16[8,208,256]{2,1,0:T(8,128)(2,1)S(1)}, bf16[8,208,256]{2,1,0:T(8,128)(2,1)S(1)}, u32[]{:S(2)}, u32[]{:S(2)}) %collective-permute-start.17) | collective-permute-done | bytes 852000 | tf_op jit(solution)/shard_map/mixer_back_second/ppermute | solution.py:408
  140.1 1.6 collective-permute-start.19
  141.7 1.3 copy.25
  143.0 2.5 %copy.26 = f32[8,128,512]{2,1,0:T(8,128)} copy(f32[8,128,512]{2,0,1:T(8,128)S(1)} %bitcast.47) | data formatting | bytes 4194304 | tf_op jit(solution)/shard_map/transpose | solution.py:451
  145.5 5.5 %collective-permute-done.20 = bf16[160,512]{1,0:T(8,128)(2,1)S(1)} collective-permute-done((bf16[160,512]{1,0:T(8,128)(2,1)S(1)}, bf16[160,512]{1,0:T(8,128)(2,1)S(1)}, u32[]{:S(2)}, u32[]{:S(2)}) %collective-permute-start.20) | collective-permute-done | bytes 163872 | tf_op jit(solution)/shard_map/feed_back_far/ppermute | solution.py:408
  151.1 2.0 %collective-permute-start.23 = (bf16[208,256]{1,0:T(8,128)(2,1)S(1)}, bf16[208,256]{1,0:T(8,128)(2,1)S(1)}, u32[]{:S(2)}, u32[]{:S(2)}) collective-permute-start(bf16[208,256]{1,0:T(8,128)(2,1)S(1)} %get-tuple-element.141), channel_id=1, source_target_pairs={{0,24},{1,25},{2,26},{3,27},{4,28},{5,29},{6,30},{7,31},{8,16},{9,... | collective-permute-start | bytes 319496 | tf_op jit(solution)/shard_map/mixer_back_z/ppermute | solution.py:408
  153.2 2.4 %collective-permute-start.21 = (bf16[208,256]{1,0:T(8,128)(2,1)S(1)}, bf16[208,256]{1,0:T(8,128)(2,1)S(1)}, u32[]{:S(2)}, u32[]{:S(2)}) collective-permute-start(bf16[208,256]{1,0:T(8,128)(2,1)S(1)} %get-tuple-element.143), channel_id=1, source_target_pairs={{0,16},{1,17},{2,18},{3,19},{4,20},{5,21},{6,22},{7,23},{8,24},{9,... | collective-permute-start | bytes 319496 | tf_op jit(solution)/shard_map/mixer_back_z/ppermute | solution.py:408
  157.8 2.2 %collective-permute-done.22.p1 = bf16[208,256]{1,0:T(8,128)(2,1)S(1)} collective-permute-done((bf16[208,256]{1,0:T(8,128)(2,1)S(1)}, bf16[208,256]{1,0:T(8,128)(2,1)S(1)}, u32[]{:S(2)}, u32[]{:S(2)}) %collective-permute-start.22) | collective-permute-done | bytes 106528 | tf_op jit(solution)/shard_map/mixer_back_z/ppermute | solution.py:408
  (60 shorter events, 9.8 us)
Async XLA Ops:
  2.1 9.1 %collective-permute-start.2 = (bf16[208,256]{1,0:T(8,128)(2,1)}, bf16[208,256]{1,0:T(8,128)(2,1)S(1)}, u32[]{:S(2)}, u32[]{:S(2)}) collective-permute-start(bf16[208,256]{1,0:T(8,128)(2,1)} %pack.1), channel_id=1, source_target_pairs={{0,24},{1,25},{2,26},{3,27},{4,28},{5,29},{6,30},{7,31},{8,16},{9,... | collective-permute-start | bytes 319496 | tf_op jit(solution)/shard_map/mixer_z/ppermute | solution.py:408
  7.2 6.6 %collective-permute-start.1 = (bf16[208,256]{1,0:T(8,128)(2,1)}, bf16[208,256]{1,0:T(8,128)(2,1)S(1)}, u32[]{:S(2)}, u32[]{:S(2)}) collective-permute-start(bf16[208,256]{1,0:T(8,128)(2,1)} %pack.1), channel_id=1, source_target_pairs={{0,8},{1,9},{2,10},{3,11},{4,12},{5,13},{6,14},{7,15},{8,0},{9,1},... | collective-permute-start | bytes 319496 | tf_op jit(solution)/shard_map/mixer_z/ppermute | solution.py:408
  7.2 9.2 %collective-permute-start = (bf16[208,256]{1,0:T(8,128)(2,1)}, bf16[208,256]{1,0:T(8,128)(2,1)S(1)}, u32[]{:S(2)}, u32[]{:S(2)}) collective-permute-start(bf16[208,256]{1,0:T(8,128)(2,1)} %pack.1), channel_id=1, source_target_pairs={{0,16},{1,17},{2,18},{3,19},{4,20},{5,21},{6,22},{7,23},{8,24},{9,... | collective-permute-start | bytes 319496 | tf_op jit(solution)/shard_map/mixer_z/ppermute | solution.py:408
  7.7 2.8 %copy-start.5 = (bf16[512,64]{0,1:T(8,128)(2,1)S(1)}, bf16[512,64]{0,1:T(8,128)(2,1)}, u32[]{:S(2)}) copy-start(bf16[512,64]{0,1:T(8,128)(2,1)} %param.21) | copy-start | bytes 196612
  7.7 2.8 %copy-start.6 = (bf16[64,512]{1,0:T(8,128)(2,1)S(1)}, bf16[64,512]{1,0:T(8,128)(2,1)}, u32[]{:S(2)}) copy-start(bf16[64,512]{1,0:T(8,128)(2,1)} %param.20) | copy-start | bytes 196612
  7.7 2.8 %copy-start.7 = (bf16[32,512]{1,0:T(8,128)(2,1)S(1)}, bf16[32,512]{1,0:T(8,128)(2,1)}, u32[]{:S(2)}) copy-start(bf16[32,512]{1,0:T(8,128)(2,1)} %param.19) | copy-start | bytes 98308
  7.7 8.6 %copy-start.4 = (bf16[208,256]{1,0:T(8,128)(2,1)S(1)}, bf16[208,256]{1,0:T(8,128)(2,1)}, u32[]{:S(2)}) copy-start(bf16[208,256]{1,0:T(8,128)(2,1)} %pack.1) | copy-start | bytes 319492
  16.4 11.1 %collective-permute-start.3 = (bf16[4,208,256]{2,1,0:T(8,128)(2,1)S(1)}, bf16[4,208,256]{2,1,0:T(8,128)(2,1)S(1)}, u32[]{:S(2)}, u32[]{:S(2)}) collective-permute-start(bf16[4,208,256]{2,1,0:T(8,128)(2,1)S(1)} %pad_maximum_fusion.3), channel_id=1, source_target_pairs={{0,4},{1,3},{2,6},{3,1},{4,0},{5,7},{6,2},{7,5},{8,12},{9,11},{10,... | collective-permute-start | bytes 1277960 | tf_op jit(solution)/shard_map/mixer_first/ppermute | solution.py:408
  18.0 9.5 %collective-permute-start.4 = (bf16[160,512]{1,0:T(8,128)(2,1)S(1)}, bf16[160,512]{1,0:T(8,128)(2,1)S(1)}, u32[]{:S(2)}, u32[]{:S(2)}) collective-permute-start(bf16[160,512]{1,0:T(8,128)(2,1)S(1)} %pad_maximum_fusion.5), channel_id=1, source_target_pairs={{0,16},{1,17},{2,18},{3,19},{4,20},{5,21},{6,22},{7,23},{8,24},{9,... | collective-permute-start | bytes 491528 | tf_op jit(solution)/shard_map/feed_far/ppermute | solution.py:408
  27.6 12.8 %collective-permute-start.5 = (bf16[8,208,256]{2,1,0:T(8,128)(2,1)S(1)}, bf16[8,208,256]{2,1,0:T(8,128)(2,1)S(1)}, u32[]{:S(2)}, u32[]{:S(2)}) collective-permute-start(bf16[8,208,256]{2,1,0:T(8,128)(2,1)S(1)} %pad_maximum_fusion.1.g0), channel_id=1, source_target_pairs={{0,2},{1,5},{2,0},{3,7},{4,6},{5,1},{6,4},{7,3},{8,10},{9,13},{10,... | collective-permute-start | bytes 2555912 | tf_op jit(solution)/shard_map/mixer_second/ppermute | solution.py:408
  28.1 10.0 %collective-permute-start.6 = (bf16[2,160,512]{2,1,0:T(8,128)(2,1)S(1)}, bf16[2,160,512]{2,1,0:T(8,128)(2,1)S(1)}, u32[]{:S(2)}, u32[]{:S(2)}) collective-permute-start(bf16[2,160,512]{2,1,0:T(8,128)(2,1)S(1)} %pad_maximum_fusion.4), channel_id=1, source_target_pairs={{0,8},{1,9},{2,10},{3,11},{4,12},{5,13},{6,14},{7,15},{8,0},{9,1},... | collective-permute-start | bytes 983048 | tf_op jit(solution)/shard_map/feed_near/ppermute | solution.py:408
  28.1 14.0 %collective-permute-start.8 = (bf16[8,208,256]{2,1,0:T(8,128)(2,1)S(1)}, bf16[8,208,256]{2,1,0:T(8,128)(2,1)S(1)}, u32[]{:S(2)}, u32[]{:S(2)}) collective-permute-start(bf16[8,208,256]{2,1,0:T(8,128)(2,1)S(1)} %pad_maximum_fusion.1.g0), channel_id=1, source_target_pairs={{0,1},{1,0},{2,3},{3,2},{4,5},{5,4},{6,7},{7,6},{8,9},{9,8},{10,11... | collective-permute-start | bytes 2555912 | tf_op jit(solution)/shard_map/mixer_core/ppermute | solution.py:408
  40.4 10.7 %collective-permute-start.9 = (bf16[8,208,256]{2,1,0:T(8,128)(2,1)S(1)}, bf16[8,208,256]{2,1,0:T(8,128)(2,1)S(1)}, u32[]{:S(2)}, u32[]{:S(2)}) collective-permute-start(bf16[8,208,256]{2,1,0:T(8,128)(2,1)S(1)} %collective-permute-done.5.g1), channel_id=1, source_target_pairs={{0,1},{1,0},{2,3},{3,2},{4,5},{5,4},{6,7},{7,6},{8,9},{9,8},{10,11... | collective-permute-start | bytes 2555912 | tf_op jit(solution)/shard_map/mixer_core_more/ppermute | solution.py:408
  40.5 10.7 %collective-permute-start.7 = (bf16[4,160,512]{2,1,0:T(8,128)(2,1)S(1)}, bf16[4,160,512]{2,1,0:T(8,128)(2,1)S(1)}, u32[]{:S(2)}, u32[]{:S(2)}) collective-permute-start(bf16[4,160,512]{2,1,0:T(8,128)(2,1)S(1)} %pad_maximum_fusion.2), channel_id=1, source_target_pairs={{0,4},{1,3},{2,6},{3,1},{4,0},{5,7},{6,2},{7,5},{8,12},{9,11},{10,... | collective-permute-start | bytes 1966088 | tf_op jit(solution)/shard_map/feed_first/ppermute | solution.py:408
  51.3 17.7 %collective-permute-start.10 = (bf16[8,160,512]{2,1,0:T(8,128)(2,1)S(1)}, bf16[8,160,512]{2,1,0:T(8,128)(2,1)S(1)}, u32[]{:S(2)}, u32[]{:S(2)}) collective-permute-start(bf16[8,160,512]{2,1,0:T(8,128)(2,1)S(1)} %pad_maximum_fusion.g0), channel_id=1, source_target_pairs={{0,2},{1,5},{2,0},{3,7},{4,6},{5,1},{6,4},{7,3},{8,10},{9,13},{10,... | collective-permute-start | bytes 3932168 | tf_op jit(solution)/shard_map/feed_second/ppermute | solution.py:408
  51.8 17.2 %collective-permute-start.11 = (bf16[8,160,512]{2,1,0:T(8,128)(2,1)S(1)}, bf16[8,160,512]{2,1,0:T(8,128)(2,1)S(1)}, u32[]{:S(2)}, u32[]{:S(2)}) collective-permute-start(bf16[8,160,512]{2,1,0:T(8,128)(2,1)S(1)} %pad_maximum_fusion.g0), channel_id=1, source_target_pairs={{0,1},{1,0},{2,3},{3,2},{4,5},{5,4},{6,7},{7,6},{8,9},{9,8},{10,11... | collective-permute-start | bytes 3932168 | tf_op jit(solution)/shard_map/feed_core/ppermute | solution.py:408
  69.0 3.0 %collective-permute-start.12 = (bf16[8,160,512]{2,1,0:T(8,128)(2,1)S(1)}, bf16[8,160,512]{2,1,0:T(8,128)(2,1)S(1)}, u32[]{:S(2)}, u32[]{:S(2)}) collective-permute-start(bf16[8,160,512]{2,1,0:T(8,128)(2,1)S(1)} %collective-permute-done.10.g1), channel_id=1, source_target_pairs={{0,1},{1,0},{2,3},{3,2},{4,5},{5,4},{6,7},{7,6},{8,9},{9,8},{10,11... | collective-permute-start | bytes 3932168 | tf_op jit(solution)/shard_map/feed_core_more/ppermute | solution.py:408
  92.8 5.0 %collective-permute-start.13 = (bf16[16,160,512]{2,1,0:T(8,128)(2,1)S(1)}, bf16[16,160,512]{2,1,0:T(8,128)(2,1)S(1)}, u32[]{:S(2)}, u32[]{:S(2)}) collective-permute-start(bf16[16,160,512]{2,1,0:T(8,128)(2,1)S(1)} %get-tuple-element.94), channel_id=1, source_target_pairs={{0,1},{1,0},{2,3},{3,2},{4,5},{5,4},{6,7},{7,6},{8,9},{9,8},{10,11... | collective-permute-start | bytes 7864328 | tf_op jit(solution)/shard_map/feed_back_core/ppermute | solution.py:408
  98.1 17.7 %collective-permute-start.15 = (bf16[8,160,512]{2,1,0:T(8,128)(2,1)S(1)}, bf16[8,160,512]{2,1,0:T(8,128)(2,1)S(1)}, u32[]{:S(2)}, u32[]{:S(2)}) collective-permute-start(bf16[8,160,512]{2,1,0:T(8,128)(2,1)S(1)} %add_convert_fusion.1), channel_id=1, source_target_pairs={{0,2},{1,5},{2,0},{3,7},{4,6},{5,1},{6,4},{7,3},{8,10},{9,13},{10,... | collective-permute-start | bytes 3932168 | tf_op jit(solution)/shard_map/feed_back_second/ppermute | solution.py:408
  108.6 9.2 %collective-permute-start.14 = (bf16[16,208,256]{2,1,0:T(8,128)(2,1)S(1)}, bf16[16,208,256]{2,1,0:T(8,128)(2,1)S(1)}, u32[]{:S(2)}, u32[]{:S(2)}) collective-permute-start(bf16[16,208,256]{2,1,0:T(8,128)(2,1)S(1)} %get-tuple-element.104), channel_id=1, source_target_pairs={{0,1},{1,0},{2,3},{3,2},{4,5},{5,4},{6,7},{7,6},{8,9},{9,8},{10,11... | collective-permute-start | bytes 5111816 | tf_op jit(solution)/shard_map/mixer_back_core/ppermute | solution.py:408
  116.2 10.7 %collective-permute-start.16 = (bf16[4,160,512]{2,1,0:T(8,128)(2,1)S(1)}, bf16[4,160,512]{2,1,0:T(8,128)(2,1)S(1)}, u32[]{:S(2)}, u32[]{:S(2)}) collective-permute-start(bf16[4,160,512]{2,1,0:T(8,128)(2,1)S(1)} %get-tuple-element.109), channel_id=1, source_target_pairs={{0,4},{1,3},{2,6},{3,1},{4,0},{5,7},{6,2},{7,5},{8,12},{9,11},{10,... | collective-permute-start | bytes 1966088 | tf_op jit(solution)/shard_map/feed_back_first/ppermute | solution.py:408
  127.0 12.8 %collective-permute-start.17 = (bf16[8,208,256]{2,1,0:T(8,128)(2,1)S(1)}, bf16[8,208,256]{2,1,0:T(8,128)(2,1)S(1)}, u32[]{:S(2)}, u32[]{:S(2)}) collective-permute-start(bf16[8,208,256]{2,1,0:T(8,128)(2,1)S(1)} %get-tuple-element.110), channel_id=1, source_target_pairs={{0,2},{1,5},{2,0},{3,7},{4,6},{5,1},{6,4},{7,3},{8,10},{9,13},{10,... | collective-permute-start | bytes 2555912 | tf_op jit(solution)/shard_map/mixer_back_second/ppermute | solution.py:408
  127.5 8.9 %collective-permute-start.18 = (bf16[2,160,512]{2,1,0:T(8,128)(2,1)S(1)}, bf16[2,160,512]{2,1,0:T(8,128)(2,1)S(1)}, u32[]{:S(2)}, u32[]{:S(2)}) collective-permute-start(bf16[2,160,512]{2,1,0:T(8,128)(2,1)S(1)} %get-tuple-element.111), channel_id=1, source_target_pairs={{0,8},{1,9},{2,10},{3,11},{4,12},{5,13},{6,14},{7,15},{8,0},{9,1},... | collective-permute-start | bytes 983048 | tf_op jit(solution)/shard_map/feed_back_near/ppermute | solution.py:408
  140.1 10.9 %collective-permute-start.19 = (bf16[4,208,256]{2,1,0:T(8,128)(2,1)S(1)}, bf16[4,208,256]{2,1,0:T(8,128)(2,1)S(1)}, u32[]{:S(2)}, u32[]{:S(2)}) collective-permute-start(bf16[4,208,256]{2,1,0:T(8,128)(2,1)S(1)} %get-tuple-element.120), channel_id=1, source_target_pairs={{0,4},{1,3},{2,6},{3,1},{4,0},{5,7},{6,2},{7,5},{8,12},{9,11},{10,... | collective-permute-start | bytes 1277960 | tf_op jit(solution)/shard_map/mixer_back_first/ppermute | solution.py:408
  141.7 9.3 %collective-permute-start.20 = (bf16[160,512]{1,0:T(8,128)(2,1)S(1)}, bf16[160,512]{1,0:T(8,128)(2,1)S(1)}, u32[]{:S(2)}, u32[]{:S(2)}) collective-permute-start(bf16[160,512]{1,0:T(8,128)(2,1)S(1)} %get-tuple-element.121), channel_id=1, source_target_pairs={{0,16},{1,17},{2,18},{3,19},{4,20},{5,21},{6,22},{7,23},{8,24},{9,... | collective-permute-start | bytes 491528 | tf_op jit(solution)/shard_map/feed_back_far/ppermute | solution.py:408
  145.5 14.5 %copy-start = (bf16[16,1024]{1,0:T(8,128)(2,1)S(1)}, bf16[16,1024]{1,0:T(8,128)(2,1)}, u32[]{:S(2)}) copy-start(bf16[16,1024]{1,0:T(8,128)(2,1)} %forget_ref.3) | copy-start | bytes 98308
  145.5 14.5 %copy-start.1 = (bf16[16,1024]{1,0:T(8,128)(2,1)S(1)}, bf16[16,1024]{1,0:T(8,128)(2,1)}, u32[]{:S(2)}) copy-start(bf16[16,1024]{1,0:T(8,128)(2,1)} %input_ref.3) | copy-start | bytes 98308
  145.5 14.5 %copy-start.2 = (bf16[16,1024]{1,0:T(8,128)(2,1)S(1)}, bf16[16,1024]{1,0:T(8,128)(2,1)}, u32[]{:S(2)}) copy-start(bf16[16,1024]{1,0:T(8,128)(2,1)} %cand_ref.3) | copy-start | bytes 98308
  145.5 14.5 %copy-start.3 = (bf16[16]{0:T(256)(128)(2,1)S(1)}, bf16[16]{0:T(256)(128)(2,1)}, u32[]{:S(2)}) copy-start(bf16[16]{0:T(256)(128)(2,1)} %param.13) | copy-start | bytes 100
  151.1 6.7 %collective-permute-start.23 = (bf16[208,256]{1,0:T(8,128)(2,1)S(1)}, bf16[208,256]{1,0:T(8,128)(2,1)S(1)}, u32[]{:S(2)}, u32[]{:S(2)}) collective-permute-start(bf16[208,256]{1,0:T(8,128)(2,1)S(1)} %get-tuple-element.141), channel_id=1, source_target_pairs={{0,24},{1,25},{2,26},{3,27},{4,28},{5,29},{6,30},{7,31},{8,16},{9,... | collective-permute-start | bytes 319496 | tf_op jit(solution)/shard_map/mixer_back_z/ppermute | solution.py:408
  153.2 6.8 %collective-permute-start.22 = (bf16[208,256]{1,0:T(8,128)(2,1)S(1)}, bf16[208,256]{1,0:T(8,128)(2,1)S(1)}, u32[]{:S(2)}, u32[]{:S(2)}) collective-permute-start(bf16[208,256]{1,0:T(8,128)(2,1)S(1)} %get-tuple-element.142), channel_id=1, source_target_pairs={{0,8},{1,9},{2,10},{3,11},{4,12},{5,13},{6,14},{7,15},{8,0},{9,1},... | collective-permute-start | bytes 319496 | tf_op jit(solution)/shard_map/mixer_back_z/ppermute | solution.py:408
  153.2 6.8 %collective-permute-start.21 = (bf16[208,256]{1,0:T(8,128)(2,1)S(1)}, bf16[208,256]{1,0:T(8,128)(2,1)S(1)}, u32[]{:S(2)}, u32[]{:S(2)}) collective-permute-start(bf16[208,256]{1,0:T(8,128)(2,1)S(1)} %get-tuple-element.143), channel_id=1, source_target_pairs={{0,16},{1,17},{2,18},{3,19},{4,20},{5,21},{6,22},{7,23},{8,24},{9,... | collective-permute-start | bytes 319496 | tf_op jit(solution)/shard_map/mixer_back_z/ppermute | solution.py:408

commit v4 on v3

--- a/solution.py
+++ b/solution.py
@@ -173,73 +173,93 @@
     lax.fori_loop(0, count, second, start)
 
 
-def feed_forward(dev_ref, gain_ref, g0, g1, g2, g3, hb_ref, x_ref, dy_ref,
-                 out_ref, dmix_ref, wo_ref, low_ref, high_ref, send_ref, small_ref,
-                 y1_s, xn_s, xnt_s, dyt_s, acc_s, dxn_s, up_s, dn_s, upg_s, dng_s, wog_s):
-    parts = (g0, g1, g2, g3)
+def hidden_units(dev_ref, parts, xn_ref, xnt_ref, dy_ref, dyt_ref, targets, add_out, up_s, dn_s, upg_s, dng_s):
     per = SLOTS // 4
-    tokens, width = x_ref.shape
-    chans = hb_ref.shape[1]
-    rows = width // 8
-    feed = 2 * rows
-    gain = gain_ref[1:2, :]
-
-    def target(s):
-        return (low_ref, high_ref, send_ref, send_ref)[s // per], s % per + (per if s >= 3 * per else 0)
-
-    for s in range(SLOTS):
-        wo_ref[aligned(dev_ref[s] * 32, 32), :] = parts[s // per][s % per, feed:, :]
-
-    def rows_in(i, _):
-        at = aligned(i * 256, 256)
-        y1 = x_ref[at, :].astype(F32) + dot(hb_ref[at, :], wo_ref[...])
-        y1_s[at, :] = y1
-        scale = lax.rsqrt(jnp.mean(y1 * y1, axis=-1, keepdims=True) + EPSILON)
-        xn = ((y1 * scale) * gain).astype(BF)
-        xn_s[at, :] = xn
-        xnt_s[:, at] = xn.T
-        return 0
-
-    lax.fori_loop(0, tokens // 256, rows_in, 0)
-    dyt_s[...] = dy_ref[...].T
-
+    rows = up_s.shape[0] // 8
     for base in (0, SLOTS // 2):
         slots = range(base, base + SLOTS // 2)
         for s in slots:
             d = dev_ref[s]
-            block, at = d // 2 % 2, aligned(d // 4 * rows, rows)
-            up_s[block, at, :] = parts[s // per][s % per, 0:rows, :]
-            dn_s[block, at, :] = parts[s // per][s % per, rows:feed, :]
-        for block in range(2):
-            pre = dot(xn_s[...], up_s[block])
-            dact = dot(dy_ref[...], dn_s[block])
-            sq = pre * pre
-            gate = 0.5 + 0.5 * jnp.tanh(pre * (C0 + C1 * sq))
-            value = pre * gate
-            act = value.astype(BF)
-            slope = gate + value * (1.0 - gate) * (2.0 * C0 + 6.0 * C1 * sq)
-            dpre = (slope * dact).astype(BF)
-            upg_s[block] = dot(xnt_s[...], dpre).astype(BF)
-            dng_s[block] = dot(dyt_s[...], act).astype(BF)
-            out = dot(act, dn_s[block], ((1,), (1,)))
-            dxn = dot(dpre, up_s[block], ((1,), (1,)))
-            if base + block == 0:
-                acc_s[...] = out
-                dxn_s[...] = dxn
-            else:
-                acc_s[...] += out
-                dxn_s[...] += dxn
+            at, cols = aligned(d // 4 * rows, rows), aligned(d // 2 % 2 * LANES, LANES)
+            up_s[at, cols] = parts[s // per][s % per, 0:rows, :]
+            dn_s[at, cols] = parts[s // per][s % per, rows : 2 * rows, :]
+        pre = dot(xn_ref[...], up_s[...])
+        dact = dot(dy_ref[...], dn_s[...])
+        sq = pre * pre
+        gate = 0.5 + 0.5 * jnp.tanh(pre * (C0 + C1 * sq))
+        value = pre * gate
+        act = value.astype(BF)
+        slope = gate + value * (1.0 - gate) * (2.0 * C0 + 6.0 * C1 * sq)
+        dpre = (slope * dact).astype(BF)
+        upg_s[...] = dot(xnt_ref[...], dpre).astype(BF)
+        dng_s[...] = dot(dyt_ref[...], act).astype(BF)
+        add_out(base == 0, dot(act, dn_s[...], ((1,), (1,))), dot(dpre, up_s[...], ((1,), (1,))))
         for s in slots:
             d = dev_ref[s]
-            block, at = d // 2 % 2, aligned(d // 4 * rows, rows)
-            ref, k = target(s)
-            ref[k, 0:rows, :] = upg_s[block, at, :]
-            ref[k, rows:feed, :] = dng_s[block, at, :]
+            at, cols = aligned(d // 4 * rows, rows), aligned(d // 2 % 2 * LANES, LANES)
+            ref, k = target(targets, s)
+            ref[k, 0:rows, :] = upg_s[at, cols]
+            ref[k, rows : 2 * rows, :] = dng_s[at, cols]
+
+
+def target(targets, s):
+    per = SLOTS // 4
+    return (targets[0], s) if s < per else (targets[1], s - per) if s < 2 * per else (targets[2], s - 2 * per)
+
+
+def feed_first(dev_ref, gain_ref, g0, g1, g2, g3, hb_ref, x_ref, dy_ref,
+               y1_ref, xn_ref, xnt_ref, dyt_ref, acc_ref, dxn_ref, wo_ref, low_ref, high_ref, send_ref,
+               up_s, dn_s, upg_s, dng_s):
+    parts = (g0, g1, g2, g3)
+    per = SLOTS // 4
+    tokens, width = x_ref.shape
+    feed = width // 4
+    gain = gain_ref[1:2, :]
+    for s in range(SLOTS):
+        for c in range(width // LANES):
+            piece = parts[s // per][s % per, feed + c * 32 : feed + (c + 1) * 32, :]
+            wo_ref[aligned(dev_ref[s] * 32, 32), c * LANES : (c + 1) * LANES] = piece
+
+    def rows_in(i, _):
+        at = aligned(i * 256, 256)
+        y1 = x_ref[at, :].astype(F32) + dot(hb_ref[at, :], wo_ref[...])
+        y1_ref[at, :] = y1
+        scale = lax.rsqrt(jnp.mean(y1 * y1, axis=-1, keepdims=True) + EPSILON)
+        xn = ((y1 * scale) * gain).astype(BF)
+        xn_ref[at, :] = xn
+        xnt_ref[:, at] = xn.T
+        return 0
+
+    lax.fori_loop(0, tokens // 256, rows_in, 0)
+    dyt_ref[...] = dy_ref[...].T
+
+    def add_out(first, out, dxn):
+        acc_ref[...] = out if first else acc_ref[...] + out
+        dxn_ref[...] = dxn if first else dxn_ref[...] + dxn
+
+    hidden_units(dev_ref, parts, xn_ref, xnt_ref, dy_ref, dyt_ref, (low_ref, high_ref, send_ref), add_out,
+                 up_s, dn_s, upg_s, dng_s)
+
+
+def feed_last(dev_ref, gain_ref, g0, g1, g2, g3, hb_ref, dy_ref, y1_ref, xn_ref, xnt_ref, dyt_ref, acc_ref, dxn_ref,
+              out_ref, dmix_ref, low_ref, high_ref, send_ref, small_ref,
+              up_s, dn_s, upg_s, dng_s, acc_s, dxn_s, wog_s):
+    tokens, width = dy_ref.shape
+    chans = hb_ref.shape[1]
+    feed = width // 4
+    gain = gain_ref[1:2, :]
+    targets = (low_ref, high_ref, send_ref)
+
+    def add_out(first, out, dxn):
+        acc_s[...] = (acc_ref if first else acc_s)[...] + out
+        dxn_s[...] = (dxn_ref if first else dxn_s)[...] + dxn
+
+    hidden_units(dev_ref, (g0, g1, g2, g3), xn_ref, xnt_ref, dy_ref, dyt_ref, targets, add_out, up_s, dn_s, upg_s, dng_s)
 
     total = jnp.zeros((1, width), F32)
     for i in range(tokens // 256):
         at = slice(i * 256, (i + 1) * 256)
-        y1 = y1_s[at, :]
+        y1 = y1_ref[at, :]
         scale = lax.rsqrt(jnp.mean(y1 * y1, axis=-1, keepdims=True) + EPSILON)
         n2 = y1 * scale
         out_ref[at, :] = (y1 + acc_s[at, :]).astype(BF)
@@ -256,8 +276,10 @@
             hb_ref[:, b * span : (b + 1) * span], dmix_ref[...], ((0,), (0,))
         ).astype(BF)
     for s in range(SLOTS):
-        ref, k = target(s)
-        ref[k, feed:, :] = wog_s[aligned(dev_ref[s] * 32, 32), :]
+        ref, k = target(targets, s)
+        for c in range(width // LANES):
+            piece = wog_s[aligned(dev_ref[s] * 32, 32), c * LANES : (c + 1) * LANES]
+            ref[k, feed + c * 32 : feed + (c + 1) * 32, :] = piece
 
 
 def mixer_backward(dev_ref, dmix_ref, xnt_ref, wo_ref, small_ref, o_ref, u1_ref, u2_ref,
@@ -452,27 +474,32 @@
 
     xp = permute(tokens)
     dyp = permute(cotangent)
+    def pack_feed(up, down, out):
+        pieces = [v[:, c : c + LANES] for v in (up, down, out) for c in (0, LANES)]
+        return jnp.concatenate([pieces[0], pieces[2], pieces[4], pieces[5]]), jnp.concatenate([pieces[1], pieces[3]])
+
     if fast:
         me = lax.axis_index(AXES)
         table = order_table()
         dev = lax.dynamic_index_in_dim(jnp.asarray(table), me, keepdims=False)
         piece = pack(forget_weight, input_weight, candidate_weight, gain_mix, gain_mlp, input_gate_bias)
         four = jnp.stack([piece] + [send(piece, p, "mixer_z") for p in (FAR, NEAR, BOTH)])
-        four, piece_f = after_all(four, jnp.concatenate([up_weight, down_weight.T, output_weight]), dev, xp, dyp)[:2]
-        got, far_f = after_all(send(four, FIRST, "mixer_first"), send(piece_f, FAR, "feed_far"))
-        eight = jnp.concatenate([four, got])
-        two_f = jnp.stack([piece_f, far_f])
-        eight, two_f = after_all(eight, two_f)
-        more, got = after_all(send(eight, SECOND, "mixer_second"), send(two_f, NEAR, "feed_near"))
-        four_f = jnp.concatenate([two_f, got])
-        more, four_f = after_all(more, four_f)
-        got, core, core_more = after_all(
-            send(four_f, FIRST, "feed_first"), send(eight, CORE, "mixer_core"), send(more, CORE, "mixer_core_more")
+        piece1, piece2 = pack_feed(up_weight, down_weight.T, output_weight)
+        four, piece1, piece2, *_ = after_all(four, piece1, piece2, dev, xp, dyp)
+        got, far1 = after_all(send(four, FIRST, "mixer_first"), send(piece1, FAR, "feed1_far"))
+        eight, two1, piece2 = after_all(jnp.concatenate([four, got]), jnp.stack([piece1, far1]), piece2)
+        more, near1, far2 = after_all(
+            send(eight, SECOND, "mixer_second"), send(two1, NEAR, "feed1_near"), send(piece2, FAR, "feed2_far")
         )
-        eight_f = jnp.concatenate([four_f, got])
-        mixer = (eight, more, core, core_more)
-        mixer, eight_f = lax.optimization_barrier((mixer, eight_f))
-        more_f = send(eight_f, SECOND, "feed_second")
+        more, four1, two2 = after_all(more, jnp.concatenate([two1, near1]), jnp.stack([piece2, far2]))
+        got1, near2, core, core_more = after_all(
+            send(four1, FIRST, "feed1_first"), send(two2, NEAR, "feed2_near"),
+            send(eight, CORE, "mixer_core"), send(more, CORE, "mixer_core_more"),
+        )
+        eight1, four2 = jnp.concatenate([four1, got1]), jnp.concatenate([two2, near2])
+        mixer, eight1, four2 = after_all((eight, more, core, core_more), eight1, four2)
+        more1 = send(eight1, SECOND, "feed1_second")
+        got2 = send(four2, FIRST, "feed2_first")
     else:
         order = np.argsort(np.arange(SLOTS) % 2, kind="stable").astype(np.int32)
         dev = jnp.asarray(order)
@@ -489,7 +516,9 @@
         def regroup(w):
             return w.reshape(8, width // 8, 4, width).transpose(0, 2, 1, 3).reshape(SLOTS, width // 8, width)
 
-        both = jnp.concatenate([regroup(up), regroup(down.T), full(output_weight).reshape(SLOTS, -1, width)], axis=1)
+        both = [
+            pack_feed(*v) for v in zip(regroup(up), regroup(down.T), full(output_weight).reshape(SLOTS, -1, width))
+        ]
 
         def quarters(v):
             return tuple(jnp.stack([v[d] for d in order[k * 8 : (k + 1) * 8]]) for k in range(4))
@@ -497,7 +526,7 @@
         mixer = quarters(
             jnp.stack([pack(*[w[s * 16 : (s + 1) * 16] for w in weights], *[v[s] for v in smalls]) for s in range(SLOTS)])
         )
-        feed = quarters(both)
+        feed1, feed2 = (quarters([v[k] for v in both]) for k in range(2))
 
     smem = pl.BlockSpec(memory_space=pltpu.SMEM)
     vmem = pl.BlockSpec(memory_space=pltpu.VMEM)
@@ -528,39 +557,55 @@
         name="mixer_forward",
     )(dev, xp, *mixer)
     if fast:
-        last = after(more_f, hb)
-        feed = (eight_f, more_f, send(eight_f, CORE, "feed_core"), send(last, CORE, "feed_core_more"))
+        core1 = send(eight1, CORE, "feed1_core")
+        more1, got2, gains = after_all(more1, got2, gains)
+        eight2 = jnp.concatenate([four2, got2])
+        feed1 = (eight1, more1, core1, send(more1, CORE, "feed1_core_more"))
+        more2 = send(eight2, SECOND, "feed2_second")
 
     size = width // 8
-    piece = feed[0].shape[1:]
-    block_out, dmix, wo, low1, high1, send1, gmlp_small = pl.pallas_call(
-        feed_forward,
+    weights = [pltpu.VMEM((width, 2 * LANES), BF)] * 4
+
+    def pieces(count):
+        return [((slots, count, LANES), BF) for slots in (SLOTS // 4, SLOTS // 4, SLOTS // 2)]
+
+    y1, xn2, xn2t, dyt, acc, dxn2, wo, low1, high1, send1 = pl.pallas_call(
+        feed_first,
         in_specs=[smem] + [vmem] * 8,
-        out_specs=[vmem] * 7,
-        out_shape=shapes(((rows, width), BF), ((rows, width), BF), ((chans, width), BF),
-                         *[((count,) + piece, BF) for count in (SLOTS // 4, SLOTS // 4, SLOTS // 2)], ((SLOTS, LANES), F32)),
-        scratch_shapes=[
-            pltpu.VMEM((rows, width), F32),
-            pltpu.VMEM((rows, width), BF),
-            pltpu.VMEM((width, rows), BF),
-            pltpu.VMEM((width, rows), BF),
-            pltpu.VMEM((rows, width), F32),
-            pltpu.VMEM((rows, width), F32),
-            *[pltpu.VMEM((2, width, width), BF)] * 4,
-            pltpu.VMEM((chans, width), BF),
-        ],
-        compiler_params=params(30),
-        cost_estimate=pl.CostEstimate(flops=2 * rows * width * (24 * width + 2 * chans), bytes_accessed=60 << 20, transcendentals=0),
-        name="feed_forward",
-    )(dev, gains, *feed, hb, xp, dyp)
-
+        out_specs=[vmem] * 10,
+        out_shape=shapes(((rows, width), F32), ((rows, width), BF), ((width, rows), BF), ((width, rows), BF),
+                         ((rows, width), F32), ((rows, width), F32), ((chans, width), BF), *pieces(2 * size)),
+        scratch_shapes=weights,
+        compiler_params=params(20),
+        cost_estimate=pl.CostEstimate(flops=2 * rows * width * (12 * width + chans), bytes_accessed=30 << 20, transcendentals=0),
+        name="feed_first",
+    )(dev, gains, *feed1, hb, xp, dyp)
     if fast:
+        core2 = send(eight2, CORE, "feed2_core")
+        more2, y1, send1 = after_all(more2, y1, send1)
+        feed2 = (eight2, more2, core2, send(more2, CORE, "feed2_core_more"))
         half = SLOTS // 4
-        got = send(send1, CORE, "feed_back_core")
-        high = add(high1, got[half:])
-        high, dmix = after_all(high, dmix)
+        got1 = send(send1, CORE, "feed1_back_core")
+        high1, y1 = after_all(add(high1, got1[half:]), y1)
+        second1 = send(high1, SECOND, "feed1_back_second")
+    block_out, dmix, low2, high2, send2, gmlp_small = pl.pallas_call(
+        feed_last,
+        in_specs=[smem] + [vmem] * 13,
+        out_specs=[vmem] * 6,
+        out_shape=shapes(((rows, width), BF), ((rows, width), BF), *pieces(3 * size), ((SLOTS, LANES), F32)),
+        scratch_shapes=weights + [pltpu.VMEM((rows, width), F32)] * 2 + [pltpu.VMEM((chans, width), BF)],
+        compiler_params=params(20),
+        cost_estimate=pl.CostEstimate(flops=2 * rows * width * (12 * width + chans), bytes_accessed=30 << 20, transcendentals=0),
+        name="feed_last",
+    )(dev, gains, *feed2, hb, dyp, y1, xn2, xn2t, dyt, acc, dxn2)
+
+    if fast:
+        second1, dmix, send2 = after_all(second1, dmix, send2)
+        got2 = send(send2, CORE, "feed2_back_core")
+        high2, dmix = after_all(add(high2, got2[half:]), dmix)
+        second2 = send(high2, SECOND, "feed2_back_second")
     piece = (SLOTS // 2, 3 * blocks * 16 + 16, LANES)
-    dk, keep2, send2 = pl.pallas_call(
+    dk, keep3, send3 = pl.pallas_call(
         mixer_backward,
         grid=(blocks,),
         in_specs=[smem, whole((rows, width)), whole((width, rows)), whole((chans, width)), whole((SLOTS, LANES)),
@@ -591,11 +636,15 @@
         return [v[:, :, k].transpose(0, 2, 1, 3).reshape(-1, 16, chans) for k in range(3)]
 
     if fast:
-        low = add(after(low1, dk), got[:half])
-        low, high = fold(low, high, SECOND, "feed_back_second")
-        low, high = fold(low, after(high, dk), FIRST, "feed_back_first")
-        got = send(send2, CORE, "mixer_back_core")
-        mlow, mhigh = add(keep2[:half], got[:half]), add(keep2[half:], got[half:])
+        second1, second2, low1, low2, dk = after_all(second1, second2, low1, low2, dk)
+        low1, low2 = add(low1, got1[:half]), add(low2, got2[:half])
+        low, high = (
+            jnp.concatenate([add(low1[k], second1[k]), add(low2[k], second2[k])], axis=1)
+            for k in (slice(0, half // 2), slice(half // 2, half))
+        )
+        low, high = fold(low, high, FIRST, "feed_back_first")
+        got = send(send3, CORE, "mixer_back_core")
+        mlow, mhigh = add(keep3[:half], got[:half]), add(keep3[half:], got[half:])
         mlow, mhigh, low, high, dk = after_all(mlow, mhigh, low, high, dk)
         got, near, tokens_grad = after_all(
             send(mhigh, SECOND, "mixer_back_second"), send(high, NEAR, "feed_back_near"), input_grad(dk)
@@ -608,7 +657,11 @@
         four = add(mlow, got)
         first = low.astype(F32) + far.astype(F32)
         parts = [send(four[k + 1], p, "mixer_back_z") for k, p in enumerate((FAR, NEAR, BOTH))]
-        up_grad, down_grad, out_grad = first[:size], first[size : 2 * size].T, first[2 * size :]
+        up_grad, down_grad, out_grad = (
+            jnp.concatenate([first[a : a + count], first[b : b + count]], axis=1)
+            for a, b, count in ((0, 2 * size, size), (size, 3 * size, size), (4 * size, 4 * size + 32, 32))
+        )
+        down_grad = down_grad.T
         *grads, gmix_grad, gmlp_grad, bias_grad = pl.pallas_call(
             finish_mixer,
             out_shape=shapes(*[((16, chans), F32)] * 3, ((1, shard), F32), ((1, shard), F32), ((1, chans // SLOTS), F32)),
@@ -618,21 +671,22 @@
         gmix_grad, gmlp_grad, bias_grad = gmix_grad[0], gmlp_grad[0], bias_grad[0]
     else:
         tokens_grad = input_grad(dk)
-        first, total = (
+        first, last, total = (
             jnp.stack([jnp.concatenate(v)[k] for k in np.argsort(order)]).astype(F32)
-            for v in ((low1, high1, send1), (keep2, send2))
+            for v in ((low1, high1, send1), (low2, high2, send2), (keep3, send3))
         )
 
         def summed(v, axis=0, names=AXES):
             return lax.psum_scatter(v, names, scatter_dimension=axis, tiled=True)
 
         def joined(base):
-            w = first[:, base : base + size]
+            w = jnp.concatenate([first[:, base : base + size], last[:, base : base + size]], axis=2)
             return w.reshape(8, 4, size, width).transpose(0, 2, 1, 3).reshape(width, 4 * width)
 
         up_grad = summed(summed(joined(0), 0, "dp"), 1, "mp")
         down_grad = summed(summed(joined(size).T, 1, "dp"), 0, "mp")
-        out_grad = summed(first[:, 2 * size :].reshape(chans, width))
+        out_grad = jnp.concatenate([last[:, 2 * size : 2 * size + 32], last[:, 2 * size + 32 :]], axis=2)
+        out_grad = summed(out_grad.reshape(chans, width))
         grads = [summed(v.reshape(width, chans)) for v in uncut(total)]
         edge = total[:, 48 * blocks]
         gmlp_grad = summed(edge[:, :shard].reshape(-1))

time: 161 us -> 153 us (0.950)
  waiting for transfers between devices: 76.8 us -> 55.6 us
  starting transfers between devices: 21.6 us -> 30 us
  Pallas kernels: 50.3 us -> 52.5 us
  other arithmetic: 2.54 us -> 4.48 us
    ppermute x24 -> x32, waiting for transfers between devices: 76.8 us -> 55.6 us  [send(): return lax.ppermute(value, AXES, pairs)]
    ppermute x24 -> x32, starting transfers between devices: 21.6 us -> 30 us  [send(): return lax.ppermute(value, AXES, pairs)]
    pallas_call x1 -> x2, Pallas kernels: 20.8 us -> 22.9 us  [the longest x1 11.6 us: local(): pl.pallas_call(feed_last, in_specs=[smem] + [vmem] * 13, out_specs=[vmem]...]
  transfers between devices with their start and end apart: 24 -> 32, of which waited for: 16 -> 20; matrix products, arithmetic and copies ran while one was open for 6% -> 8% of each run, Pallas kernels for 17% -> 33%
where the time goes in v4:
time: 153 us
  waiting for transfers between devices  55.6 us (36%)
  Pallas kernels  52.5 us (34%)
  starting transfers between devices  30 us (20%)
  local copies, waits for them, and re-layouts  8.94 us (6%)
  other arithmetic  4.48 us (3%)
    ppermute x32, waiting for transfers between devices, send(): return lax.ppermute(value, AXES, pairs)  55.6 us
    ppermute x32, starting transfers between devices, send(): return lax.ppermute(value, AXES, pairs)  30 us
    pallas_call x1, Pallas kernels, local(): pl.pallas_call(mixer_forward, grid=(blocks,), in_specs=[smem, whole((rows...  12.4 us
    pallas_call x1, Pallas kernels, local(): pl.pallas_call(feed_last, in_specs=[smem] + [vmem] * 13, out_specs=[vmem]...  11.6 us
    pallas_call x1, Pallas kernels, local(): pl.pallas_call(feed_first, in_specs=[smem] + [vmem] * 8, out_specs=[vmem]...  11.4 us
    pallas_call x1, Pallas kernels, local(): pl.pallas_call(mixer_backward, grid=(blocks,), in_specs=[smem, whole((row...  10 us
    pallas_call x1, Pallas kernels, input_grad(): pl.pallas_call(input_gradient, grid=(rows // part,), in_specs=[band(width...  4.98 us
    transpose x2, local copies, waits for them, and re-layouts, restore(): v.reshape(rows // CHUNKS, CHUNKS, width).transpose(1, 0, 2)  3.82 us
  transfers between devices with their start and end apart: 32, of which 20 were waited for; matrix products, arithmetic and copies ran while one was open for 8% of the time, Pallas kernels for 33%

profile of v4, /device:TPU:0, one launch (start us, length us, event | category | flops | bytes accessed | tf_op | source)
XLA Modules:
  0.0 152.6 jit_solution(14233428405059434190)
XLA Ops:
  0.6 1.5 pack.1
  2.1 5.0 %collective-permute-start.2 = (bf16[208,256]{1,0:T(8,128)(2,1)}, bf16[208,256]{1,0:T(8,128)(2,1)S(1)}, u32[]{:S(2)}, u32[]{:S(2)}) collective-permute-start(bf16[208,256]{1,0:T(8,128)(2,1)} %pack.1), channel_id=1, source_target_pairs={{0,24},{1,25},{2,26},{3,27},{4,28},{5,29},{6,30},{7,31},{8,16},{9,... | collective-permute-start | bytes 319496 | tf_op jit(solution)/shard_map/mixer_z/ppermute | solution.py:430
  9.3 2.7 %copy_bitcast_fusion = (bf16[1024,512]{1,0:T(8,128)(2,1)S(1)}, bf16[1024,512]{1,0:T(8,128)(2,1)S(1)}) fusion(bf16[8,128,512]{2,1,0:T(8,128)(2,1)} %bitcast.55, bf16[8,128,512]{2,1,0:T(8,128)(2,1)} %bitcast.56), kind=kLoop, calls=%fused_computation.4 | loop fusion | bytes 4194304 | tf_op jit(solution)/shard_map/reshape | solution.py:470
  13.7 2.6 %collective-permute-done = bf16[208,256]{1,0:T(8,128)(2,1)S(1)} collective-permute-done((bf16[208,256]{1,0:T(8,128)(2,1)}, bf16[208,256]{1,0:T(8,128)(2,1)S(1)}, u32[]{:S(2)}, u32[]{:S(2)}) %collective-permute-start) | collective-permute-done | bytes 106528 | tf_op jit(solution)/shard_map/mixer_z/ppermute | solution.py:430
  16.4 1.6 %collective-permute-start.3 = (bf16[4,208,256]{2,1,0:T(8,128)(2,1)S(1)}, bf16[4,208,256]{2,1,0:T(8,128)(2,1)S(1)}, u32[]{:S(2)}, u32[]{:S(2)}) collective-permute-start(bf16[4,208,256]{2,1,0:T(8,128)(2,1)S(1)} %pad_maximum_fusion.3), channel_id=1, source_target_pairs={{0,4},{1,3},{2,6},{3,1},{4,0},{5,7},{6,2},{7,5},{8,12},{9,11},{10,... | collective-permute-start | bytes 1277960 | tf_op jit(solution)/shard_map/mixer_first/ppermute | solution.py:430
  19.2 5.5 %collective-permute-done.4 = bf16[192,256]{1,0:T(8,128)(2,1)S(1)} collective-permute-done((bf16[192,256]{1,0:T(8,128)(2,1)S(1)}, bf16[192,256]{1,0:T(8,128)(2,1)S(1)}, u32[]{:S(2)}, u32[]{:S(2)}) %collective-permute-start.4) | collective-permute-done | bytes 98336 | tf_op jit(solution)/shard_map/feed1_far/ppermute | solution.py:430
  24.8 1.5 collective-permute-start.5
  26.3 3.0 %collective-permute-start.7 = (bf16[128,256]{1,0:T(8,128)(2,1)S(1)}, bf16[128,256]{1,0:T(8,128)(2,1)S(1)}, u32[]{:S(2)}, u32[]{:S(2)}) collective-permute-start(bf16[128,256]{1,0:T(8,128)(2,1)S(1)} %pad_maximum_fusion.11), channel_id=1, source_target_pairs={{0,16},{1,17},{2,18},{3,19},{4,20},{5,21},{6,22},{7,23},{8,24},{9,... | collective-permute-start | bytes 196616 | tf_op jit(solution)/shard_map/feed2_far/ppermute | solution.py:430
  29.3 2.5 %collective-permute-done.7 = bf16[128,256]{1,0:T(8,128)(2,1)S(1)} collective-permute-done((bf16[128,256]{1,0:T(8,128)(2,1)S(1)}, bf16[128,256]{1,0:T(8,128)(2,1)S(1)}, u32[]{:S(2)}, u32[]{:S(2)}) %collective-permute-start.7) | collective-permute-done | bytes 65568 | tf_op jit(solution)/shard_map/feed2_far/ppermute | solution.py:430
  31.8 2.0 %collective-permute-done.6 = bf16[2,192,256]{2,1,0:T(8,128)(2,1)S(1)} collective-permute-done((bf16[2,192,256]{2,1,0:T(8,128)(2,1)S(1)}, bf16[2,192,256]{2,1,0:T(8,128)(2,1)S(1)}, u32[]{:S(2)}, u32[]{:S(2)}) %collective-permute-start.6) | collective-permute-done | bytes 196640 | tf_op jit(solution)/shard_map/feed1_near/ppermute | solution.py:430
  33.9 3.7 %collective-permute-done.5.g1 = bf16[8,208,256]{2,1,0:T(8,128)(2,1)S(1)} collective-permute-done((bf16[8,208,256]{2,1,0:T(8,128)(2,1)S(1)}, bf16[8,208,256]{2,1,0:T(8,128)(2,1)S(1)}, u32[]{:S(2)}, u32[]{:S(2)}) %collective-permute-start.5) | collective-permute-done | bytes 852000 | tf_op jit(solution)/shard_map/mixer_second/ppermute | solution.py:430
  37.7 1.6 %collective-permute-start.8 = (bf16[4,192,256]{2,1,0:T(8,128)(2,1)S(1)}, bf16[4,192,256]{2,1,0:T(8,128)(2,1)S(1)}, u32[]{:S(2)}, u32[]{:S(2)}) collective-permute-start(bf16[4,192,256]{2,1,0:T(8,128)(2,1)S(1)} %pad_maximum_fusion.4), channel_id=1, source_target_pairs={{0,4},{1,3},{2,6},{3,1},{4,0},{5,7},{6,2},{7,5},{8,12},{9,11},{10,... | collective-permute-start | bytes 1179656 | tf_op jit(solution)/shard_map/feed1_first/ppermute | solution.py:430
  39.3 5.5 %collective-permute-done.9 = bf16[2,128,256]{2,1,0:T(8,128)(2,1)S(1)} collective-permute-done((bf16[2,128,256]{2,1,0:T(8,128)(2,1)S(1)}, bf16[2,128,256]{2,1,0:T(8,128)(2,1)S(1)}, u32[]{:S(2)}, u32[]{:S(2)}) %collective-permute-start.9) | collective-permute-done | bytes 131104 | tf_op jit(solution)/shard_map/feed2_near/ppermute | solution.py:430
  45.6 1.5 collective-permute-start.12
  47.2 1.5 collective-permute-start.13
  48.6 12.4 %mixer_forward.1 = (bf16[1024,1024]{1,0:T(8,128)(2,1)S(1)}, bf16[4,1024,256]{2,1,0:T(8,128)(2,1)S(1)}, bf16[4,1024,256]{2,1,0:T(8,128)(2,1)S(1)}, bf16[4,1024,25...) custom-call(s32[32]{0:T(128)S(1)} %dynamic-slice_bitcast_fusion.dev_r, ...), custom_call_target="tpu_custom_call" | custom-call | flops 3221225472 | bytes 33554432 | tf_op jit(solution)/shard_map/mixer_forward/pallas_call | solution.py:545
  62.1 1.4 collective-permute-done.16.g3
  63.4 11.4 %feed_first.1 = (f32[1024,512]{1,0:T(8,128)S(1)}, bf16[1024,512]{1,0:T(8,128)(2,1)S(1)}, bf16[512,1024]{1,0:T(8,128)(2,1)S(1)}, bf16[512,1024]{1,0:T(8,128)(2,1)...) custom-call(s32[32]{0:T(128)S(1)} %dynamic-slice_bitcast_fusion.dev_, ...), custom_call_target="tpu_custom_call" | custom-call | flops 7516192768 | bytes 31457280 | tf_op jit(solution)/shard_map/feed_first/pallas_call | solution.py:572
  75.5 2.0 %collective-permute-done.19 = bf16[16,128,256]{2,1,0:T(8,128)(2,1)S(1)} collective-permute-done((bf16[16,128,256]{2,1,0:T(8,128)(2,1)S(1)}, bf16[16,128,256]{2,1,0:T(8,128)(2,1)S(1)}, u32[]{:S(2)}, u32[]{:S(2)}) %collective-permute-start.19) | collective-permute-done | bytes 1048608 | tf_op jit(solution)/shard_map/feed1_back_core/ppermute | solution.py:430
  79.0 11.6 %feed_last.1 = (bf16[1024,512]{1,0:T(8,128)(2,1)S(1)}, bf16[1024,512]{1,0:T(8,128)(2,1)S(1)}, bf16[8,192,256]{2,1,0:T(8,128)(2,1)S(1)}, bf16[8,192,256]{2,1,0:T(...) custom-call(s32[32]{0:T(128)S(1)} %dynamic-slice_bitcast_fusion.dev_ref, ...), custom_call_target="tpu_custom_call" | custom-call | flops 7516192768 | bytes 31457280 | tf_op jit(solution)/shard_map/feed_last/pallas_call | solution.py:591
  90.8 3.3 %collective-permute-done.21 = bf16[16,192,256]{2,1,0:T(8,128)(2,1)S(1)} collective-permute-done((bf16[16,192,256]{2,1,0:T(8,128)(2,1)S(1)}, bf16[16,192,256]{2,1,0:T(8,128)(2,1)S(1)}, u32[]{:S(2)}, u32[]{:S(2)}) %collective-permute-start.21) | collective-permute-done | bytes 1572896 | tf_op jit(solution)/shard_map/feed2_back_core/ppermute | solution.py:430
  95.2 10.0 %mixer_backward.1 = (bf16[4,1024,768]{2,1,0:T(8,128)(2,1)S(1)}, bf16[16,208,256]{2,1,0:T(8,128)(2,1)S(1)}, bf16[16,208,256]{2,1,0:T(8,128)(2,1)S(1)}) custom-call(s32[32]{0:T(128)S(1)} %dynamic-slice_bitcast_fusion.dev_ref, bf16[1024,512]{1,0:T(8,128)(2,1)S(1)} %get-tuple-element.147.dmix_ref, bf16[512,1024]{1,0:T(8,128)(2,1)S(1)} %get-tuple-element.148.xnt_ref, ...), custom_call_target="tpu_custom_call" | custom-call | flops 4294967296 | bytes 41943040 | tf_op jit(solution)/shard_map/mixer_backward/pallas_call | solution.py:608
  108.2 9.6 %collective-permute-done.24 = bf16[4,320,256]{2,1,0:T(8,128)(2,1)S(1)} collective-permute-done((bf16[4,320,256]{2,1,0:T(8,128)(2,1)S(1)}, bf16[4,320,256]{2,1,0:T(8,128)(2,1)S(1)}, u32[]{:S(2)}, u32[]{:S(2)}) %collective-permute-start.24) | collective-permute-done | bytes 655392 | tf_op jit(solution)/shard_map/feed_back_first/ppermute | solution.py:430
  119.3 5.0 %input_gradient.1 = f32[1024,512]{1,0:T(8,128)S(1)} custom-call(bf16[1024,512]{1,0:T(8,128)(2,1)S(1)} %get-tuple-element.218.x_ref, bf16[1024,512]{1,0:T(8,128)(2,1)S(1)} %get-tuple-element.147.dmix_ref, f32[2,512]{1,0:T(2,128)S(1)} %get-tuple-element.124.gain_ref, bf16[4,1024,768]{2,1,0:T(8,128)(2,1)S(1)} %get-tuple-element.168.dk_ref, ...), custom_call_target="tpu_custom_call" | custom-call | flops 3221225472 | bytes 25165824 | tf_op jit(solution)/shard_map/input_gradient/pallas_call | solution.py:623
  124.3 3.6 %collective-permute-done.26 = bf16[2,320,256]{2,1,0:T(8,128)(2,1)S(1)} collective-permute-done((bf16[2,320,256]{2,1,0:T(8,128)(2,1)S(1)}, bf16[2,320,256]{2,1,0:T(8,128)(2,1)S(1)}, u32[]{:S(2)}, u32[]{:S(2)}) %collective-permute-start.26) | collective-permute-done | bytes 327712 | tf_op jit(solution)/shard_map/feed_back_near/ppermute | solution.py:430
  127.9 3.3 %collective-permute-done.25 = bf16[8,208,256]{2,1,0:T(8,128)(2,1)S(1)} collective-permute-done((bf16[8,208,256]{2,1,0:T(8,128)(2,1)S(1)}, bf16[8,208,256]{2,1,0:T(8,128)(2,1)S(1)}, u32[]{:S(2)}, u32[]{:S(2)}) %collective-permute-start.25) | collective-permute-done | bytes 852000 | tf_op jit(solution)/shard_map/mixer_back_second/ppermute | solution.py:430
  135.2 2.5 %copy.26 = f32[8,128,512]{2,1,0:T(8,128)} copy(f32[8,128,512]{2,0,1:T(8,128)S(1)} %bitcast.49) | data formatting | bytes 4194304 | tf_op jit(solution)/shard_map/transpose | solution.py:473
  137.7 3.6 %collective-permute-done.28 = bf16[320,256]{1,0:T(8,128)(2,1)S(1)} collective-permute-done((bf16[320,256]{1,0:T(8,128)(2,1)S(1)}, bf16[320,256]{1,0:T(8,128)(2,1)S(1)}, u32[]{:S(2)}, u32[]{:S(2)}) %collective-permute-start.28) | collective-permute-done | bytes 163872 | tf_op jit(solution)/shard_map/feed_back_far/ppermute | solution.py:430
  141.6 2.1 %collective-permute-start.31 = (bf16[208,256]{1,0:T(8,128)(2,1)S(1)}, bf16[208,256]{1,0:T(8,128)(2,1)S(1)}, u32[]{:S(2)}, u32[]{:S(2)}) collective-permute-start(bf16[208,256]{1,0:T(8,128)(2,1)S(1)} %get-tuple-element.199), channel_id=1, source_target_pairs={{0,24},{1,25},{2,26},{3,27},{4,28},{5,29},{6,30},{7,31},{8,16},{9,... | collective-permute-start | bytes 319496 | tf_op jit(solution)/shard_map/mixer_back_z/ppermute | solution.py:430
  143.7 2.4 %collective-permute-start.29 = (bf16[208,256]{1,0:T(8,128)(2,1)S(1)}, bf16[208,256]{1,0:T(8,128)(2,1)S(1)}, u32[]{:S(2)}, u32[]{:S(2)}) collective-permute-start(bf16[208,256]{1,0:T(8,128)(2,1)S(1)} %get-tuple-element.201), channel_id=1, source_target_pairs={{0,16},{1,17},{2,18},{3,19},{4,20},{5,21},{6,22},{7,23},{8,24},{9,... | collective-permute-start | bytes 319496 | tf_op jit(solution)/shard_map/mixer_back_z/ppermute | solution.py:430
  148.8 1.6 %collective-permute-done.30.p1 = bf16[208,256]{1,0:T(8,128)(2,1)S(1)} collective-permute-done((bf16[208,256]{1,0:T(8,128)(2,1)S(1)}, bf16[208,256]{1,0:T(8,128)(2,1)S(1)}, u32[]{:S(2)}, u32[]{:S(2)}) %collective-permute-start.30) | collective-permute-done | bytes 106528 | tf_op jit(solution)/shard_map/mixer_back_z/ppermute | solution.py:430
  150.4 1.5 collective-permute-done.29.p0
  (85 shorter events, 22.9 us)
Async XLA Ops:
  2.1 10.7 %collective-permute-start.2 = (bf16[208,256]{1,0:T(8,128)(2,1)}, bf16[208,256]{1,0:T(8,128)(2,1)S(1)}, u32[]{:S(2)}, u32[]{:S(2)}) collective-permute-start(bf16[208,256]{1,0:T(8,128)(2,1)} %pack.1), channel_id=1, source_target_pairs={{0,24},{1,25},{2,26},{3,27},{4,28},{5,29},{6,30},{7,31},{8,16},{9,... | collective-permute-start | bytes 319496 | tf_op jit(solution)/shard_map/mixer_z/ppermute | solution.py:430
  7.2 6.6 %collective-permute-start.1 = (bf16[208,256]{1,0:T(8,128)(2,1)}, bf16[208,256]{1,0:T(8,128)(2,1)S(1)}, u32[]{:S(2)}, u32[]{:S(2)}) collective-permute-start(bf16[208,256]{1,0:T(8,128)(2,1)} %pack.1), channel_id=1, source_target_pairs={{0,8},{1,9},{2,10},{3,11},{4,12},{5,13},{6,14},{7,15},{8,0},{9,1},... | collective-permute-start | bytes 319496 | tf_op jit(solution)/shard_map/mixer_z/ppermute | solution.py:430
  7.2 9.2 %collective-permute-start = (bf16[208,256]{1,0:T(8,128)(2,1)}, bf16[208,256]{1,0:T(8,128)(2,1)S(1)}, u32[]{:S(2)}, u32[]{:S(2)}) collective-permute-start(bf16[208,256]{1,0:T(8,128)(2,1)} %pack.1), channel_id=1, source_target_pairs={{0,16},{1,17},{2,18},{3,19},{4,20},{5,21},{6,22},{7,23},{8,24},{9,... | collective-permute-start | bytes 319496 | tf_op jit(solution)/shard_map/mixer_z/ppermute | solution.py:430
  16.4 8.3 %collective-permute-start.3 = (bf16[4,208,256]{2,1,0:T(8,128)(2,1)S(1)}, bf16[4,208,256]{2,1,0:T(8,128)(2,1)S(1)}, u32[]{:S(2)}, u32[]{:S(2)}) collective-permute-start(bf16[4,208,256]{2,1,0:T(8,128)(2,1)S(1)} %pad_maximum_fusion.3), channel_id=1, source_target_pairs={{0,4},{1,3},{2,6},{3,1},{4,0},{5,7},{6,2},{7,5},{8,12},{9,11},{10,... | collective-permute-start | bytes 1277960 | tf_op jit(solution)/shard_map/mixer_first/ppermute | solution.py:430
  18.0 6.7 %collective-permute-start.4 = (bf16[192,256]{1,0:T(8,128)(2,1)S(1)}, bf16[192,256]{1,0:T(8,128)(2,1)S(1)}, u32[]{:S(2)}, u32[]{:S(2)}) collective-permute-start(bf16[192,256]{1,0:T(8,128)(2,1)S(1)} %pad_maximum_fusion.10), channel_id=1, source_target_pairs={{0,16},{1,17},{2,18},{3,19},{4,20},{5,21},{6,22},{7,23},{8,24},{9,... | collective-permute-start | bytes 294920 | tf_op jit(solution)/shard_map/feed1_far/ppermute | solution.py:430
  24.8 12.8 %collective-permute-start.5 = (bf16[8,208,256]{2,1,0:T(8,128)(2,1)S(1)}, bf16[8,208,256]{2,1,0:T(8,128)(2,1)S(1)}, u32[]{:S(2)}, u32[]{:S(2)}) collective-permute-start(bf16[8,208,256]{2,1,0:T(8,128)(2,1)S(1)} %pad_maximum_fusion.g0), channel_id=1, source_target_pairs={{0,2},{1,5},{2,0},{3,7},{4,6},{5,1},{6,4},{7,3},{8,10},{9,13},{10,... | collective-permute-start | bytes 2555912 | tf_op jit(solution)/shard_map/mixer_second/ppermute | solution.py:430
  26.3 7.6 %collective-permute-start.6 = (bf16[2,192,256]{2,1,0:T(8,128)(2,1)S(1)}, bf16[2,192,256]{2,1,0:T(8,128)(2,1)S(1)}, u32[]{:S(2)}, u32[]{:S(2)}) collective-permute-start(bf16[2,192,256]{2,1,0:T(8,128)(2,1)S(1)} %pad_maximum_fusion.7), channel_id=1, source_target_pairs={{0,8},{1,9},{2,10},{3,11},{4,12},{5,13},{6,14},{7,15},{8,0},{9,1},... | collective-permute-start | bytes 589832 | tf_op jit(solution)/shard_map/feed1_near/ppermute | solution.py:430
  26.3 5.5 %collective-permute-start.7 = (bf16[128,256]{1,0:T(8,128)(2,1)S(1)}, bf16[128,256]{1,0:T(8,128)(2,1)S(1)}, u32[]{:S(2)}, u32[]{:S(2)}) collective-permute-start(bf16[128,256]{1,0:T(8,128)(2,1)S(1)} %pad_maximum_fusion.11), channel_id=1, source_target_pairs={{0,16},{1,17},{2,18},{3,19},{4,20},{5,21},{6,22},{7,23},{8,24},{9,... | collective-permute-start | bytes 196616 | tf_op jit(solution)/shard_map/feed2_far/ppermute | solution.py:430
  29.3 9.9 %collective-permute-start.10 = (bf16[8,208,256]{2,1,0:T(8,128)(2,1)S(1)}, bf16[8,208,256]{2,1,0:T(8,128)(2,1)S(1)}, u32[]{:S(2)}, u32[]{:S(2)}) collective-permute-start(bf16[8,208,256]{2,1,0:T(8,128)(2,1)S(1)} %pad_maximum_fusion.g0), channel_id=1, source_target_pairs={{0,1},{1,0},{2,3},{3,2},{4,5},{5,4},{6,7},{7,6},{8,9},{9,8},{10,11... | collective-permute-start | bytes 2555912 | tf_op jit(solution)/shard_map/mixer_core/ppermute | solution.py:430
  37.6 7.9 %collective-permute-start.11 = (bf16[8,208,256]{2,1,0:T(8,128)(2,1)S(1)}, bf16[8,208,256]{2,1,0:T(8,128)(2,1)S(1)}, u32[]{:S(2)}, u32[]{:S(2)}) collective-permute-start(bf16[8,208,256]{2,1,0:T(8,128)(2,1)S(1)} %collective-permute-done.5.g1), channel_id=1, source_target_pairs={{0,1},{1,0},{2,3},{3,2},{4,5},{5,4},{6,7},{7,6},{8,9},{9,8},{10,11... | collective-permute-start | bytes 2555912 | tf_op jit(solution)/shard_map/mixer_core_more/ppermute | solution.py:430
  37.7 7.8 %collective-permute-start.8 = (bf16[4,192,256]{2,1,0:T(8,128)(2,1)S(1)}, bf16[4,192,256]{2,1,0:T(8,128)(2,1)S(1)}, u32[]{:S(2)}, u32[]{:S(2)}) collective-permute-start(bf16[4,192,256]{2,1,0:T(8,128)(2,1)S(1)} %pad_maximum_fusion.4), channel_id=1, source_target_pairs={{0,4},{1,3},{2,6},{3,1},{4,0},{5,7},{6,2},{7,5},{8,12},{9,11},{10,... | collective-permute-start | bytes 1179656 | tf_op jit(solution)/shard_map/feed1_first/ppermute | solution.py:430
  39.2 5.5 %collective-permute-start.9 = (bf16[2,128,256]{2,1,0:T(8,128)(2,1)S(1)}, bf16[2,128,256]{2,1,0:T(8,128)(2,1)S(1)}, u32[]{:S(2)}, u32[]{:S(2)}) collective-permute-start(bf16[2,128,256]{2,1,0:T(8,128)(2,1)S(1)} %pad_maximum_fusion.8), channel_id=1, source_target_pairs={{0,8},{1,9},{2,10},{3,11},{4,12},{5,13},{6,14},{7,15},{8,0},{9,1},... | collective-permute-start | bytes 393224 | tf_op jit(solution)/shard_map/feed2_near/ppermute | solution.py:430
  45.6 15.4 %collective-permute-start.12 = (bf16[8,192,256]{2,1,0:T(8,128)(2,1)S(1)}, bf16[8,192,256]{2,1,0:T(8,128)(2,1)S(1)}, u32[]{:S(2)}, u32[]{:S(2)}) collective-permute-start(bf16[8,192,256]{2,1,0:T(8,128)(2,1)S(1)} %pad_maximum_fusion.1.g0), channel_id=1, source_target_pairs={{0,2},{1,5},{2,0},{3,7},{4,6},{5,1},{6,4},{7,3},{8,10},{9,13},{10,... | collective-permute-start | bytes 2359304 | tf_op jit(solution)/shard_map/feed1_second/ppermute | solution.py:430
  47.1 14.9 %collective-permute-start.15 = (bf16[8,192,256]{2,1,0:T(8,128)(2,1)S(1)}, bf16[8,192,256]{2,1,0:T(8,128)(2,1)S(1)}, u32[]{:S(2)}, u32[]{:S(2)}) collective-permute-start(bf16[8,192,256]{2,1,0:T(8,128)(2,1)S(1)} %pad_maximum_fusion.1.g0), channel_id=1, source_target_pairs={{0,1},{1,0},{2,3},{3,2},{4,5},{5,4},{6,7},{7,6},{8,9},{9,8},{10,11... | collective-permute-start | bytes 2359304 | tf_op jit(solution)/shard_map/feed1_core/ppermute | solution.py:430
  47.2 13.9 %collective-permute-start.13 = (bf16[4,128,256]{2,1,0:T(8,128)(2,1)S(1)}, bf16[4,128,256]{2,1,0:T(8,128)(2,1)S(1)}, u32[]{:S(2)}, u32[]{:S(2)}) collective-permute-start(bf16[4,128,256]{2,1,0:T(8,128)(2,1)S(1)} %pad_maximum_fusion.6), channel_id=1, source_target_pairs={{0,4},{1,3},{2,6},{3,1},{4,0},{5,7},{6,2},{7,5},{8,12},{9,11},{10,... | collective-permute-start | bytes 786440 | tf_op jit(solution)/shard_map/feed2_first/ppermute | solution.py:430
  61.1 2.4 %collective-permute-start.16 = (bf16[8,192,256]{2,1,0:T(8,128)(2,1)S(1)}, bf16[8,192,256]{2,1,0:T(8,128)(2,1)S(1)}, u32[]{:S(2)}, u32[]{:S(2)}) collective-permute-start(bf16[8,192,256]{2,1,0:T(8,128)(2,1)S(1)} %collective-permute-done.12.g1), channel_id=1, source_target_pairs={{0,1},{1,0},{2,3},{3,2},{4,5},{5,4},{6,7},{7,6},{8,9},{9,8},{10,11... | collective-permute-start | bytes 2359304 | tf_op jit(solution)/shard_map/feed1_core_more/ppermute | solution.py:430
  61.2 13.6 %collective-permute-start.14 = (bf16[8,128,256]{2,1,0:T(8,128)(2,1)S(1)}, bf16[8,128,256]{2,1,0:T(8,128)(2,1)S(1)}, u32[]{:S(2)}, u32[]{:S(2)}) collective-permute-start(bf16[8,128,256]{2,1,0:T(8,128)(2,1)S(1)} %constant_dynamic-update-slice_fusion.g0), channel_id=1, source_target_pairs={{0,2},{1,5},{2,0},{3,7},{4,6},{5,1},{6,4},{7,3},{8,10},{9,13},{10,... | collective-permute-start | bytes 1572872 | tf_op jit(solution)/shard_map/feed2_second/ppermute | solution.py:430
  74.8 2.7 %collective-permute-start.19 = (bf16[16,128,256]{2,1,0:T(8,128)(2,1)S(1)}, bf16[16,128,256]{2,1,0:T(8,128)(2,1)S(1)}, u32[]{:S(2)}, u32[]{:S(2)}) collective-permute-start(bf16[16,128,256]{2,1,0:T(8,128)(2,1)S(1)} %get-tuple-element.132), channel_id=1, source_target_pairs={{0,1},{1,0},{2,3},{3,2},{4,5},{5,4},{6,7},{7,6},{8,9},{9,8},{10,11... | collective-permute-start | bytes 3145736 | tf_op jit(solution)/shard_map/feed1_back_core/ppermute | solution.py:430
  75.0 3.5 %collective-permute-start.17 = (bf16[8,128,256]{2,1,0:T(8,128)(2,1)S(1)}, bf16[8,128,256]{2,1,0:T(8,128)(2,1)S(1)}, u32[]{:S(2)}, u32[]{:S(2)}) collective-permute-start(bf16[8,128,256]{2,1,0:T(8,128)(2,1)S(1)} %constant_dynamic-update-slice_fusion.g0), channel_id=1, source_target_pairs={{0,1},{1,0},{2,3},{3,2},{4,5},{5,4},{6,7},{7,6},{8,9},{9,8},{10,11... | collective-permute-start | bytes 1572872 | tf_op jit(solution)/shard_map/feed2_core/ppermute | solution.py:430
  75.4 3.6 %collective-permute-start.18 = (bf16[8,128,256]{2,1,0:T(8,128)(2,1)S(1)}, bf16[8,128,256]{2,1,0:T(8,128)(2,1)S(1)}, u32[]{:S(2)}, u32[]{:S(2)}) collective-permute-start(bf16[8,128,256]{2,1,0:T(8,128)(2,1)S(1)} %collective-permute-done.14.g1), channel_id=1, source_target_pairs={{0,1},{1,0},{2,3},{3,2},{4,5},{5,4},{6,7},{7,6},{8,9},{9,8},{10,11... | collective-permute-start | bytes 1572872 | tf_op jit(solution)/shard_map/feed2_core_more/ppermute | solution.py:430
  77.7 12.9 %collective-permute-start.20 = (bf16[8,128,256]{2,1,0:T(8,128)(2,1)S(1)}, bf16[8,128,256]{2,1,0:T(8,128)(2,1)S(1)}, u32[]{:S(2)}, u32[]{:S(2)}) collective-permute-start(bf16[8,128,256]{2,1,0:T(8,128)(2,1)S(1)} %add_convert_fusion.5), channel_id=1, source_target_pairs={{0,2},{1,5},{2,0},{3,7},{4,6},{5,1},{6,4},{7,3},{8,10},{9,13},{10,... | collective-permute-start | bytes 1572872 | tf_op jit(solution)/shard_map/feed1_back_second/ppermute | solution.py:430
  90.6 3.5 %collective-permute-start.21 = (bf16[16,192,256]{2,1,0:T(8,128)(2,1)S(1)}, bf16[16,192,256]{2,1,0:T(8,128)(2,1)S(1)}, u32[]{:S(2)}, u32[]{:S(2)}) collective-permute-start(bf16[16,192,256]{2,1,0:T(8,128)(2,1)S(1)} %get-tuple-element.145), channel_id=1, source_target_pairs={{0,1},{1,0},{2,3},{3,2},{4,5},{5,4},{6,7},{7,6},{8,9},{9,8},{10,11... | collective-permute-start | bytes 4718600 | tf_op jit(solution)/shard_map/feed2_back_core/ppermute | solution.py:430
  94.3 12.1 %collective-permute-start.23 = (bf16[8,192,256]{2,1,0:T(8,128)(2,1)S(1)}, bf16[8,192,256]{2,1,0:T(8,128)(2,1)S(1)}, u32[]{:S(2)}, u32[]{:S(2)}) collective-permute-start(bf16[8,192,256]{2,1,0:T(8,128)(2,1)S(1)} %add_convert_fusion.3), channel_id=1, source_target_pairs={{0,2},{1,5},{2,0},{3,7},{4,6},{5,1},{6,4},{7,3},{8,10},{9,13},{10,... | collective-permute-start | bytes 2359304 | tf_op jit(solution)/shard_map/feed2_back_second/ppermute | solution.py:430
  105.2 12.7 %collective-permute-start.22 = (bf16[16,208,256]{2,1,0:T(8,128)(2,1)S(1)}, bf16[16,208,256]{2,1,0:T(8,128)(2,1)S(1)}, u32[]{:S(2)}, u32[]{:S(2)}) collective-permute-start(bf16[16,208,256]{2,1,0:T(8,128)(2,1)S(1)} %get-tuple-element.155), channel_id=1, source_target_pairs={{0,1},{1,0},{2,3},{3,2},{4,5},{5,4},{6,7},{7,6},{8,9},{9,8},{10,11... | collective-permute-start | bytes 5111816 | tf_op jit(solution)/shard_map/mixer_back_core/ppermute | solution.py:430
  107.1 10.7 %collective-permute-start.24 = (bf16[4,320,256]{2,1,0:T(8,128)(2,1)S(1)}, bf16[4,320,256]{2,1,0:T(8,128)(2,1)S(1)}, u32[]{:S(2)}, u32[]{:S(2)}) collective-permute-start(bf16[4,320,256]{2,1,0:T(8,128)(2,1)S(1)} %pad_maximum_fusion.2), channel_id=1, source_target_pairs={{0,4},{1,3},{2,6},{3,1},{4,0},{5,7},{6,2},{7,5},{8,12},{9,11},{10,... | collective-permute-start | bytes 1966088 | tf_op jit(solution)/shard_map/feed_back_first/ppermute | solution.py:430
  118.4 12.8 %collective-permute-start.25 = (bf16[8,208,256]{2,1,0:T(8,128)(2,1)S(1)}, bf16[8,208,256]{2,1,0:T(8,128)(2,1)S(1)}, u32[]{:S(2)}, u32[]{:S(2)}) collective-permute-start(bf16[8,208,256]{2,1,0:T(8,128)(2,1)S(1)} %get-tuple-element.166), channel_id=1, source_target_pairs={{0,2},{1,5},{2,0},{3,7},{4,6},{5,1},{6,4},{7,3},{8,10},{9,13},{10,... | collective-permute-start | bytes 2555912 | tf_op jit(solution)/shard_map/mixer_back_second/ppermute | solution.py:430
  119.3 8.6 %collective-permute-start.26 = (bf16[2,320,256]{2,1,0:T(8,128)(2,1)S(1)}, bf16[2,320,256]{2,1,0:T(8,128)(2,1)S(1)}, u32[]{:S(2)}, u32[]{:S(2)}) collective-permute-start(bf16[2,320,256]{2,1,0:T(8,128)(2,1)S(1)} %get-tuple-element.167), channel_id=1, source_target_pairs={{0,8},{1,9},{2,10},{3,11},{4,12},{5,13},{6,14},{7,15},{8,0},{9,1},... | collective-permute-start | bytes 983048 | tf_op jit(solution)/shard_map/feed_back_near/ppermute | solution.py:430
  131.5 9.7 %collective-permute-start.27 = (bf16[4,208,256]{2,1,0:T(8,128)(2,1)S(1)}, bf16[4,208,256]{2,1,0:T(8,128)(2,1)S(1)}, u32[]{:S(2)}, u32[]{:S(2)}) collective-permute-start(bf16[4,208,256]{2,1,0:T(8,128)(2,1)S(1)} %get-tuple-element.176), channel_id=1, source_target_pairs={{0,4},{1,3},{2,6},{3,1},{4,0},{5,7},{6,2},{7,5},{8,12},{9,11},{10,... | collective-permute-start | bytes 1277960 | tf_op jit(solution)/shard_map/mixer_back_first/ppermute | solution.py:430
  132.6 8.7 %collective-permute-start.28 = (bf16[320,256]{1,0:T(8,128)(2,1)S(1)}, bf16[320,256]{1,0:T(8,128)(2,1)S(1)}, u32[]{:S(2)}, u32[]{:S(2)}) collective-permute-start(bf16[320,256]{1,0:T(8,128)(2,1)S(1)} %get-tuple-element.177), channel_id=1, source_target_pairs={{0,16},{1,17},{2,18},{3,19},{4,20},{5,21},{6,22},{7,23},{8,24},{9,... | collective-permute-start | bytes 491528 | tf_op jit(solution)/shard_map/feed_back_far/ppermute | solution.py:430
  141.6 7.2 %collective-permute-start.31 = (bf16[208,256]{1,0:T(8,128)(2,1)S(1)}, bf16[208,256]{1,0:T(8,128)(2,1)S(1)}, u32[]{:S(2)}, u32[]{:S(2)}) collective-permute-start(bf16[208,256]{1,0:T(8,128)(2,1)S(1)} %get-tuple-element.199), channel_id=1, source_target_pairs={{0,24},{1,25},{2,26},{3,27},{4,28},{5,29},{6,30},{7,31},{8,16},{9,... | collective-permute-start | bytes 319496 | tf_op jit(solution)/shard_map/mixer_back_z/ppermute | solution.py:430
  143.7 6.7 %collective-permute-start.30 = (bf16[208,256]{1,0:T(8,128)(2,1)S(1)}, bf16[208,256]{1,0:T(8,128)(2,1)S(1)}, u32[]{:S(2)}, u32[]{:S(2)}) collective-permute-start(bf16[208,256]{1,0:T(8,128)(2,1)S(1)} %get-tuple-element.200), channel_id=1, source_target_pairs={{0,8},{1,9},{2,10},{3,11},{4,12},{5,13},{6,14},{7,15},{8,0},{9,1},... | collective-permute-start | bytes 319496 | tf_op jit(solution)/shard_map/mixer_back_z/ppermute | solution.py:430
  143.7 8.2 %collective-permute-start.29 = (bf16[208,256]{1,0:T(8,128)(2,1)S(1)}, bf16[208,256]{1,0:T(8,128)(2,1)S(1)}, u32[]{:S(2)}, u32[]{:S(2)}) collective-permute-start(bf16[208,256]{1,0:T(8,128)(2,1)S(1)} %get-tuple-element.201), channel_id=1, source_target_pairs={{0,16},{1,17},{2,18},{3,19},{4,20},{5,21},{6,22},{7,23},{8,24},{9,... | collective-permute-start | bytes 319496 | tf_op jit(solution)/shard_map/mixer_back_z/ppermute | solution.py:430
  (5 other events, 49.0 us)

commit v5 on v4

--- a/solution.py
+++ b/solution.py
@@ -114,18 +114,18 @@
             w_ref[aligned(d * 16, 16), w * LANES : (w + 1) * LANES] = parts[s // per][s % per, src, :]
 
     bias = bias_s[:, aligned(step * LANES, LANES)]
-    k_s[...] = dot(xn_s[...], w_ref[...])
     kf_c, ki_c, kc_c = (slice(w * LANES, (w + 1) * LANES) for w in range(3))
     zeros = jnp.zeros((CHUNKS, LANES), F32)
     tile = GROUP * CHUNKS
     count = xn_s.shape[0] // tile
+    span = 16 * CHUNKS
 
     def first(i, carry):
         h, prod = carry
-        at = aligned(i * tile, tile)
-        kf = k_s[at, kf_c]
-        ki = k_s[at, ki_c] + bias
-        kc = k_s[at, kc_c]
+        at = slice(i * span, (i + 1) * span)
+        k = dot(xn_s[at, :], w_ref[...])
+        kf, ki, kc = k[:, kf_c], k[:, ki_c] + bias, k[:, kc_c]
+        k_s[at, kc_c] = kc
         low = jnp.minimum(jnp.minimum(kf, ki), 0.0)
         one = jnp.exp(low)
         ef = jnp.exp(low - kf)
@@ -141,13 +141,16 @@
         k_s[at, kf_c] = forget * (inv * ef)
         k_s[at, ki_c] = other * (inv * ei)
         c2_s[at, :] = drive
-        for k in range(GROUP):
+        for k in range(span // CHUNKS):
             part = slice(k * CHUNKS, (k + 1) * CHUNKS)
             h = forget[part] * h + drive[part]
             prod = prod * forget[part]
         return h, prod
 
-    last, prod = lax.fori_loop(0, count, first, (zeros, zeros + 1.0))
+    carry = zeros, zeros + 1.0
+    for i in range(xn_s.shape[0] // span):
+        carry = first(i, carry)
+    last, prod = carry
     sub = lax.broadcasted_iota(jnp.int32, (CHUNKS, LANES), 0)
     start = zeros
     for s in range(CHUNKS - 1):
@@ -207,9 +210,7 @@
     return (targets[0], s) if s < per else (targets[1], s - per) if s < 2 * per else (targets[2], s - 2 * per)
 
 
-def feed_first(dev_ref, gain_ref, g0, g1, g2, g3, hb_ref, x_ref, dy_ref,
-               y1_ref, xn_ref, xnt_ref, dyt_ref, acc_ref, dxn_ref, wo_ref, low_ref, high_ref, send_ref,
-               up_s, dn_s, upg_s, dng_s):
+def feed_prepare(dev_ref, gain_ref, g0, g1, g2, g3, hb_ref, x_ref, dy_ref, y1_ref, xn_ref, xnt_ref, dyt_ref, wo_ref):
     parts = (g0, g1, g2, g3)
     per = SLOTS // 4
     tokens, width = x_ref.shape
@@ -233,37 +234,33 @@
     lax.fori_loop(0, tokens // 256, rows_in, 0)
     dyt_ref[...] = dy_ref[...].T
 
+
+def feed_half(dev_ref, g0, g1, g2, g3, xn_ref, xnt_ref, dy_ref, dyt_ref, *refs):
+    *before, acc_ref, dxn_ref, low_ref, high_ref, send_ref, up_s, dn_s, upg_s, dng_s = refs
+
     def add_out(first, out, dxn):
-        acc_ref[...] = out if first else acc_ref[...] + out
-        dxn_ref[...] = dxn if first else dxn_ref[...] + dxn
-
-    hidden_units(dev_ref, parts, xn_ref, xnt_ref, dy_ref, dyt_ref, (low_ref, high_ref, send_ref), add_out,
+        for ref, old, value in zip((acc_ref, dxn_ref), before or (None, None), (out, dxn)):
+            if not first:
+                old = ref
+            ref[...] = value if old is None else old[...] + value
+
+    hidden_units(dev_ref, (g0, g1, g2, g3), xn_ref, xnt_ref, dy_ref, dyt_ref, (low_ref, high_ref, send_ref), add_out,
                  up_s, dn_s, upg_s, dng_s)
 
 
-def feed_last(dev_ref, gain_ref, g0, g1, g2, g3, hb_ref, dy_ref, y1_ref, xn_ref, xnt_ref, dyt_ref, acc_ref, dxn_ref,
-              out_ref, dmix_ref, low_ref, high_ref, send_ref, small_ref,
-              up_s, dn_s, upg_s, dng_s, acc_s, dxn_s, wog_s):
+def feed_finish(dev_ref, gain_ref, hb_ref, dy_ref, y1_ref, acc_ref, dxn_ref,
+                out_ref, dmix_ref, low_ref, high_ref, send_ref, small_ref, wog_s):
     tokens, width = dy_ref.shape
     chans = hb_ref.shape[1]
-    feed = width // 4
     gain = gain_ref[1:2, :]
-    targets = (low_ref, high_ref, send_ref)
-
-    def add_out(first, out, dxn):
-        acc_s[...] = (acc_ref if first else acc_s)[...] + out
-        dxn_s[...] = (dxn_ref if first else dxn_s)[...] + dxn
-
-    hidden_units(dev_ref, (g0, g1, g2, g3), xn_ref, xnt_ref, dy_ref, dyt_ref, targets, add_out, up_s, dn_s, upg_s, dng_s)
-
     total = jnp.zeros((1, width), F32)
     for i in range(tokens // 256):
         at = slice(i * 256, (i + 1) * 256)
         y1 = y1_ref[at, :]
         scale = lax.rsqrt(jnp.mean(y1 * y1, axis=-1, keepdims=True) + EPSILON)
         n2 = y1 * scale
-        out_ref[at, :] = (y1 + acc_s[at, :]).astype(BF)
-        dxn = dxn_s[at, :]
+        out_ref[at, :] = (y1 + acc_ref[at, :]).astype(BF)
+        dxn = dxn_ref[at, :]
         dn = dxn * gain
         dy1 = dy_ref[at, :].astype(F32) + scale * (dn - n2 * jnp.mean(dn * n2, axis=-1, keepdims=True))
         dmix_ref[at, :] = dy1.astype(BF)
@@ -276,10 +273,10 @@
             hb_ref[:, b * span : (b + 1) * span], dmix_ref[...], ((0,), (0,))
         ).astype(BF)
     for s in range(SLOTS):
-        ref, k = target(targets, s)
+        ref, k = target((low_ref, high_ref, send_ref), s)
         for c in range(width // LANES):
             piece = wog_s[aligned(dev_ref[s] * 32, 32), c * LANES : (c + 1) * LANES]
-            ref[k, feed + c * 32 : feed + (c + 1) * 32, :] = piece
+            ref[k, c * 32 : (c + 1) * 32, :] = piece
 
 
 def mixer_backward(dev_ref, dmix_ref, xnt_ref, wo_ref, small_ref, o_ref, u1_ref, u2_ref,
@@ -499,7 +496,6 @@
         eight1, four2 = jnp.concatenate([four1, got1]), jnp.concatenate([two2, near2])
         mixer, eight1, four2 = after_all((eight, more, core, core_more), eight1, four2)
         more1 = send(eight1, SECOND, "feed1_second")
-        got2 = send(four2, FIRST, "feed2_first")
     else:
         order = np.argsort(np.arange(SLOTS) % 2, kind="stable").astype(np.int32)
         dev = jnp.asarray(order)
@@ -558,52 +554,76 @@
     )(dev, xp, *mixer)
     if fast:
         core1 = send(eight1, CORE, "feed1_core")
-        more1, got2, gains = after_all(more1, got2, gains)
-        eight2 = jnp.concatenate([four2, got2])
+        more1, four2, gains = after_all(more1, four2, gains)
         feed1 = (eight1, more1, core1, send(more1, CORE, "feed1_core_more"))
-        more2 = send(eight2, SECOND, "feed2_second")
+        got2 = send(four2, FIRST, "feed2_first")
 
     size = width // 8
-    weights = [pltpu.VMEM((width, 2 * LANES), BF)] * 4
 
     def pieces(count):
         return [((slots, count, LANES), BF) for slots in (SLOTS // 4, SLOTS // 4, SLOTS // 2)]
 
-    y1, xn2, xn2t, dyt, acc, dxn2, wo, low1, high1, send1 = pl.pallas_call(
-        feed_first,
+    y1, xn2, xn2t, dyt, wo = pl.pallas_call(
+        feed_prepare,
         in_specs=[smem] + [vmem] * 8,
-        out_specs=[vmem] * 10,
-        out_shape=shapes(((rows, width), F32), ((rows, width), BF), ((width, rows), BF), ((width, rows), BF),
-                         ((rows, width), F32), ((rows, width), F32), ((chans, width), BF), *pieces(2 * size)),
-        scratch_shapes=weights,
-        compiler_params=params(20),
-        cost_estimate=pl.CostEstimate(flops=2 * rows * width * (12 * width + chans), bytes_accessed=30 << 20, transcendentals=0),
-        name="feed_first",
+        out_specs=[vmem] * 5,
+        out_shape=shapes(((rows, width), F32), ((rows, width), BF), ((width, rows), BF), ((width, rows), BF), ((chans, width), BF)),
+        compiler_params=params(16),
+        cost_estimate=pl.CostEstimate(flops=2 * rows * width * chans, bytes_accessed=10 << 20, transcendentals=0),
+        name="feed_prepare",
     )(dev, gains, *feed1, hb, xp, dyp)
+
+    def feed(weights, *before):
+        return pl.pallas_call(
+            feed_half,
+            in_specs=[smem] + [vmem] * (8 + len(before)),
+            out_specs=[vmem] * 5,
+            out_shape=shapes(((rows, width), F32), ((rows, width), F32), *pieces(2 * size)),
+            scratch_shapes=[pltpu.VMEM((width, 2 * LANES), BF)] * 4,
+            compiler_params=params(20),
+            cost_estimate=pl.CostEstimate(flops=24 * rows * width * width, bytes_accessed=20 << 20, transcendentals=0),
+            name="feed_last" if before else "feed_first",
+        )(dev, *weights, xn2, xn2t, dyp, dyt, *before)
+
     if fast:
+        got2, y1, xn2, xn2t, dyt, wo = after_all(got2, y1, xn2, xn2t, dyt, wo)
+        eight2 = jnp.concatenate([four2, got2])
+        more2 = send(eight2, SECOND, "feed2_second")
         core2 = send(eight2, CORE, "feed2_core")
-        more2, y1, send1 = after_all(more2, y1, send1)
+    acc, dxn2, low1, high1, send1 = feed(feed1)
+    if fast:
+        half, quarter = SLOTS // 4, SLOTS // 8
+        more2, acc, dxn2, low1, high1, send1 = after_all(more2, acc, dxn2, low1, high1, send1)
         feed2 = (eight2, more2, core2, send(more2, CORE, "feed2_core_more"))
-        half = SLOTS // 4
         got1 = send(send1, CORE, "feed1_back_core")
-        high1, y1 = after_all(add(high1, got1[half:]), y1)
+        high1, acc, dxn2 = after_all(add(high1, got1[half:]), acc, dxn2)
         second1 = send(high1, SECOND, "feed1_back_second")
-    block_out, dmix, low2, high2, send2, gmlp_small = pl.pallas_call(
-        feed_last,
-        in_specs=[smem] + [vmem] * 13,
+    acc, dxn2, low2, high2, send2 = feed(feed2, acc, dxn2)
+    if fast:
+        low1 = add(low1, got1[:half])
+        second1, low1, acc, dxn2, low2, high2, send2 = after_all(second1, low1, acc, dxn2, low2, high2, send2)
+        low1, high1 = add(low1[:quarter], second1[:quarter]), add(low1[quarter:], second1[quarter:])
+        high1, acc, dxn2 = after_all(high1, acc, dxn2)
+        first1 = send(high1, FIRST, "feed1_back_first")
+        got2 = send(send2, CORE, "feed2_back_core")
+    block_out, dmix, low_o, high_o, send_o, gmlp_small = pl.pallas_call(
+        feed_finish,
+        in_specs=[smem] + [vmem] * 6,
         out_specs=[vmem] * 6,
-        out_shape=shapes(((rows, width), BF), ((rows, width), BF), *pieces(3 * size), ((SLOTS, LANES), F32)),
-        scratch_shapes=weights + [pltpu.VMEM((rows, width), F32)] * 2 + [pltpu.VMEM((chans, width), BF)],
-        compiler_params=params(20),
-        cost_estimate=pl.CostEstimate(flops=2 * rows * width * (12 * width + chans), bytes_accessed=30 << 20, transcendentals=0),
-        name="feed_last",
-    )(dev, gains, *feed2, hb, dyp, y1, xn2, xn2t, dyt, acc, dxn2)
-
+        out_shape=shapes(((rows, width), BF), ((rows, width), BF), *pieces(size), ((SLOTS, LANES), F32)),
+        scratch_shapes=[pltpu.VMEM((chans, width), BF)],
+        compiler_params=params(16),
+        cost_estimate=pl.CostEstimate(flops=2 * rows * width * chans, bytes_accessed=10 << 20, transcendentals=0),
+        name="feed_finish",
+    )(dev, gains, hb, dyp, y1, acc, dxn2)
     if fast:
-        second1, dmix, send2 = after_all(second1, dmix, send2)
-        got2 = send(send2, CORE, "feed2_back_core")
-        high2, dmix = after_all(add(high2, got2[half:]), dmix)
+        first1, got2, dmix, low_o, high_o, send_o = after_all(first1, got2, dmix, low_o, high_o, send_o)
+        got_o = send(send_o, CORE, "out_back_core")
+        low1, high1 = add(low1[:2], first1[:2]), add(low1[2:], first1[2:])
+        high2 = jnp.concatenate([add(high2, got2[half:]), add(high_o, got_o[half:])], axis=1)
+        high1, high2, dmix = after_all(high1, high2, dmix)
         second2 = send(high2, SECOND, "feed2_back_second")
+        near1 = send(high1, NEAR, "feed1_back_near")
     piece = (SLOTS // 2, 3 * blocks * 16 + 16, LANES)
     dk, keep3, send3 = pl.pallas_call(
         mixer_backward,
@@ -636,31 +656,31 @@
         return [v[:, :, k].transpose(0, 2, 1, 3).reshape(-1, 16, chans) for k in range(3)]
 
     if fast:
-        second1, second2, low1, low2, dk = after_all(second1, second2, low1, low2, dk)
-        low1, low2 = add(low1, got1[:half]), add(low2, got2[:half])
-        low, high = (
-            jnp.concatenate([add(low1[k], second1[k]), add(low2[k], second2[k])], axis=1)
-            for k in (slice(0, half // 2), slice(half // 2, half))
+        second2, near1, low1, low2, low_o, dk, send3, keep3 = after_all(second2, near1, low1, low2, low_o, dk, send3, keep3)
+        low1, high1 = add(low1[0], near1[0]), add(low1[1], near1[1])
+        low2 = jnp.concatenate([add(low2, got2[:half]), add(low_o, got_o[:half])], axis=1)
+        low2, high2 = add(low2[:quarter], second2[:quarter]), add(low2[quarter:], second2[quarter:])
+        high1, high2 = after_all(high1, high2)
+        got = send(send3, CORE, "mixer_back_core")
+        first2, far1 = send(high2, FIRST, "feed2_back_first"), send(high1, FAR, "feed1_back_far")
+        mlow, mhigh = add(keep3[:half], got[:half]), add(keep3[half:], got[half:])
+        first2, far1, mlow, mhigh, dk = after_all(first2, far1, mlow, mhigh, dk)
+        first = low1.astype(F32) + far1.astype(F32)
+        low2, high2 = add(low2[:2], first2[:2]), add(low2[2:], first2[2:])
+        mhigh, high2 = after_all(mhigh, high2)
+        got, near2, tokens_grad = after_all(
+            send(mhigh, SECOND, "mixer_back_second"), send(high2, NEAR, "feed2_back_near"), input_grad(dk)
         )
-        low, high = fold(low, high, FIRST, "feed_back_first")
-        got = send(send3, CORE, "mixer_back_core")
-        mlow, mhigh = add(keep3[:half], got[:half]), add(keep3[half:], got[half:])
-        mlow, mhigh, low, high, dk = after_all(mlow, mhigh, low, high, dk)
-        got, near, tokens_grad = after_all(
-            send(mhigh, SECOND, "mixer_back_second"), send(high, NEAR, "feed_back_near"), input_grad(dk)
-        )
-        low, high = add(low[0], near[0]), add(low[1], near[1])
-        half = SLOTS // 8
-        mlow, mhigh = add(mlow[:half], got[:half]), add(mlow[half:], got[half:])
-        mlow, mhigh, low, high = after_all(mlow, mhigh, low, high)
-        got, far = after_all(send(mhigh, FIRST, "mixer_back_first"), send(high, FAR, "feed_back_far"))
+        low2, high2 = add(low2[0], near2[0]), add(low2[1], near2[1])
+        mlow, mhigh = add(mlow[:quarter], got[:quarter]), add(mlow[quarter:], got[quarter:])
+        mlow, mhigh, low2, high2 = after_all(mlow, mhigh, low2, high2)
+        got, far2 = after_all(send(mhigh, FIRST, "mixer_back_first"), send(high2, FAR, "feed2_back_far"))
         four = add(mlow, got)
-        first = low.astype(F32) + far.astype(F32)
+        last = low2.astype(F32) + far2.astype(F32)
         parts = [send(four[k + 1], p, "mixer_back_z") for k, p in enumerate((FAR, NEAR, BOTH))]
-        up_grad, down_grad, out_grad = (
-            jnp.concatenate([first[a : a + count], first[b : b + count]], axis=1)
-            for a, b, count in ((0, 2 * size, size), (size, 3 * size, size), (4 * size, 4 * size + 32, 32))
-        )
+        up_grad = jnp.concatenate([first[:size], last[:size]], axis=1)
+        down_grad = jnp.concatenate([first[size:], last[size : 2 * size]], axis=1)
+        out_grad = jnp.concatenate([last[2 * size : 2 * size + 32], last[2 * size + 32 :]], axis=1)
         down_grad = down_grad.T
         *grads, gmix_grad, gmlp_grad, bias_grad = pl.pallas_call(
             finish_mixer,
@@ -671,9 +691,9 @@
         gmix_grad, gmlp_grad, bias_grad = gmix_grad[0], gmlp_grad[0], bias_grad[0]
     else:
         tokens_grad = input_grad(dk)
-        first, last, total = (
+        first, last, out_grad, total = (
             jnp.stack([jnp.concatenate(v)[k] for k in np.argsort(order)]).astype(F32)
-            for v in ((low1, high1, send1), (low2, high2, send2), (keep3, send3))
+            for v in ((low1, high1, send1), (low2, high2, send2), (low_o, high_o, send_o), (keep3, send3))
         )
 
         def summed(v, axis=0, names=AXES):
@@ -685,7 +705,7 @@
 
         up_grad = summed(summed(joined(0), 0, "dp"), 1, "mp")
         down_grad = summed(summed(joined(size).T, 1, "dp"), 0, "mp")
-        out_grad = jnp.concatenate([last[:, 2 * size : 2 * size + 32], last[:, 2 * size + 32 :]], axis=2)
+        out_grad = jnp.concatenate([out_grad[:, :32], out_grad[:, 32:]], axis=2)
         out_grad = summed(out_grad.reshape(chans, width))
         grads = [summed(v.reshape(width, chans)) for v in uncut(total)]
         edge = total[:, 48 * blocks]

time: 153 us -> 150 us (0.980)
  waiting for transfers between devices: 55.6 us -> 47.7 us
  starting transfers between devices: 30 us -> 36.4 us
    ppermute x32 -> x36, waiting for transfers between devices: 55.6 us -> 47.7 us  [send(): return lax.ppermute(value, AXES, pairs)]
    ppermute x32 -> x36, starting transfers between devices: 30 us -> 36.4 us  [send(): return lax.ppermute(value, AXES, pairs)]
    pallas_call x1, Pallas kernels: 12.4 us -> 9.05 us  [local(): pl.pallas_call(mixer_forward, grid=(blocks,), in_specs=[smem, whole((rows...]
    pallas_call x2 -> x4, Pallas kernels: 22.9 us -> 24.8 us  [the longest x2 17.9 us: feed(): pl.pallas_call(feed_half, in_specs=[smem] + [vmem] * (8 + len(before)), o...]
  transfers between devices with their start and end apart: 32 -> 36, of which waited for: 20 -> 25; matrix products, arithmetic and copies ran while one was open for 8% -> 8% of each run, Pallas kernels for 33% -> 33%
where the time goes in v5:
time: 150 us
  Pallas kernels  51.3 us (34%)
  waiting for transfers between devices  47.7 us (32%)
  starting transfers between devices  36.4 us (24%)
  local copies, waits for them, and re-layouts  8.93 us (6%)
  other arithmetic  4.57 us (3%)
    ppermute x36, waiting for transfers between devices, send(): return lax.ppermute(value, AXES, pairs)  47.7 us
    ppermute x36, starting transfers between devices, send(): return lax.ppermute(value, AXES, pairs)  36.4 us
    pallas_call x2, Pallas kernels, feed(): pl.pallas_call(feed_half, in_specs=[smem] + [vmem] * (8 + len(before)), o...  17.9 us
    pallas_call x1, Pallas kernels, local(): pl.pallas_call(mixer_backward, grid=(blocks,), in_specs=[smem, whole((row...  10 us
    pallas_call x1, Pallas kernels, local(): pl.pallas_call(mixer_forward, grid=(blocks,), in_specs=[smem, whole((rows...  9.05 us
    pallas_call x1, Pallas kernels, input_grad(): pl.pallas_call(input_gradient, grid=(rows // part,), in_specs=[band(width...  5.24 us
    transpose x2, local copies, waits for them, and re-layouts, restore(): v.reshape(rows // CHUNKS, CHUNKS, width).transpose(1, 0, 2)  3.82 us
    pallas_call x1, Pallas kernels, local(): pl.pallas_call(feed_prepare, in_specs=[smem] + [vmem] * 8, out_specs=[vme...  3.54 us
  transfers between devices with their start and end apart: 36, of which 25 were waited for; matrix products, arithmetic and copies ran while one was open for 8% of the time, Pallas kernels for 33%

profile of v5, /device:TPU:0, one launch (start us, length us, event | category | flops | bytes accessed | tf_op | source)
XLA Modules:
  0.0 149.9 jit_solution(12059951360839644994)
XLA Ops:
  2.1 5.0 %collective-permute-start.2 = (bf16[208,256]{1,0:T(8,128)(2,1)}, bf16[208,256]{1,0:T(8,128)(2,1)S(1)}, u32[]{:S(2)}, u32[]{:S(2)}) collective-permute-start(bf16[208,256]{1,0:T(8,128)(2,1)} %pack.1), channel_id=1, source_target_pairs={{0,24},{1,25},{2,26},{3,27},{4,28},{5,29},{6,30},{7,31},{8,16},{9,... | collective-permute-start | bytes 319496 | tf_op jit(solution)/shard_map/mixer_z/ppermute | solution.py:427
  9.3 2.7 %copy_bitcast_fusion = (bf16[1024,512]{1,0:T(8,128)(2,1)S(1)}, bf16[1024,512]{1,0:T(8,128)(2,1)S(1)}) fusion(bf16[8,128,512]{2,1,0:T(8,128)(2,1)} %bitcast.62, bf16[8,128,512]{2,1,0:T(8,128)(2,1)} %bitcast.63), kind=kLoop, calls=%fused_computation.2 | loop fusion | bytes 4194304 | tf_op jit(solution)/shard_map/reshape | solution.py:467
  13.7 2.6 %collective-permute-done = bf16[208,256]{1,0:T(8,128)(2,1)S(1)} collective-permute-done((bf16[208,256]{1,0:T(8,128)(2,1)}, bf16[208,256]{1,0:T(8,128)(2,1)S(1)}, u32[]{:S(2)}, u32[]{:S(2)}) %collective-permute-start) | collective-permute-done | bytes 106528 | tf_op jit(solution)/shard_map/mixer_z/ppermute | solution.py:427
  16.4 1.6 %collective-permute-start.3 = (bf16[4,208,256]{2,1,0:T(8,128)(2,1)S(1)}, bf16[4,208,256]{2,1,0:T(8,128)(2,1)S(1)}, u32[]{:S(2)}, u32[]{:S(2)}) collective-permute-start(bf16[4,208,256]{2,1,0:T(8,128)(2,1)S(1)} %pad_maximum_fusion.3), channel_id=1, source_target_pairs={{0,4},{1,3},{2,6},{3,1},{4,0},{5,7},{6,2},{7,5},{8,12},{9,11},{10,... | collective-permute-start | bytes 1277960 | tf_op jit(solution)/shard_map/mixer_first/ppermute | solution.py:427
  19.2 5.5 %collective-permute-done.4 = bf16[192,256]{1,0:T(8,128)(2,1)S(1)} collective-permute-done((bf16[192,256]{1,0:T(8,128)(2,1)S(1)}, bf16[192,256]{1,0:T(8,128)(2,1)S(1)}, u32[]{:S(2)}, u32[]{:S(2)}) %collective-permute-start.4) | collective-permute-done | bytes 98336 | tf_op jit(solution)/shard_map/feed1_far/ppermute | solution.py:427
  26.3 3.0 %collective-permute-start.7 = (bf16[128,256]{1,0:T(8,128)(2,1)S(1)}, bf16[128,256]{1,0:T(8,128)(2,1)S(1)}, u32[]{:S(2)}, u32[]{:S(2)}) collective-permute-start(bf16[128,256]{1,0:T(8,128)(2,1)S(1)} %pad_maximum_fusion.11), channel_id=1, source_target_pairs={{0,16},{1,17},{2,18},{3,19},{4,20},{5,21},{6,22},{7,23},{8,24},{9,... | collective-permute-start | bytes 196616 | tf_op jit(solution)/shard_map/feed2_far/ppermute | solution.py:427
  29.3 2.5 %collective-permute-done.7 = bf16[128,256]{1,0:T(8,128)(2,1)S(1)} collective-permute-done((bf16[128,256]{1,0:T(8,128)(2,1)S(1)}, bf16[128,256]{1,0:T(8,128)(2,1)S(1)}, u32[]{:S(2)}, u32[]{:S(2)}) %collective-permute-start.7) | collective-permute-done | bytes 65568 | tf_op jit(solution)/shard_map/feed2_far/ppermute | solution.py:427
  31.8 2.0 %collective-permute-done.6 = bf16[2,192,256]{2,1,0:T(8,128)(2,1)S(1)} collective-permute-done((bf16[2,192,256]{2,1,0:T(8,128)(2,1)S(1)}, bf16[2,192,256]{2,1,0:T(8,128)(2,1)S(1)}, u32[]{:S(2)}, u32[]{:S(2)}) %collective-permute-start.6) | collective-permute-done | bytes 196640 | tf_op jit(solution)/shard_map/feed1_near/ppermute | solution.py:427
  33.9 3.7 %collective-permute-done.5.g1 = bf16[8,208,256]{2,1,0:T(8,128)(2,1)S(1)} collective-permute-done((bf16[8,208,256]{2,1,0:T(8,128)(2,1)S(1)}, bf16[8,208,256]{2,1,0:T(8,128)(2,1)S(1)}, u32[]{:S(2)}, u32[]{:S(2)}) %collective-permute-start.5) | collective-permute-done | bytes 852000 | tf_op jit(solution)/shard_map/mixer_second/ppermute | solution.py:427
  37.7 1.6 %collective-permute-start.8 = (bf16[4,192,256]{2,1,0:T(8,128)(2,1)S(1)}, bf16[4,192,256]{2,1,0:T(8,128)(2,1)S(1)}, u32[]{:S(2)}, u32[]{:S(2)}) collective-permute-start(bf16[4,192,256]{2,1,0:T(8,128)(2,1)S(1)} %pad_maximum_fusion.5), channel_id=1, source_target_pairs={{0,4},{1,3},{2,6},{3,1},{4,0},{5,7},{6,2},{7,5},{8,12},{9,11},{10,... | collective-permute-start | bytes 1179656 | tf_op jit(solution)/shard_map/feed1_first/ppermute | solution.py:427
  39.3 5.5 %collective-permute-done.9 = bf16[2,128,256]{2,1,0:T(8,128)(2,1)S(1)} collective-permute-done((bf16[2,128,256]{2,1,0:T(8,128)(2,1)S(1)}, bf16[2,128,256]{2,1,0:T(8,128)(2,1)S(1)}, u32[]{:S(2)}, u32[]{:S(2)}) %collective-permute-start.9) | collective-permute-done | bytes 131104 | tf_op jit(solution)/shard_map/feed2_near/ppermute | solution.py:427
  45.6 1.5 %collective-permute-start.12 = (bf16[8,192,256]{2,1,0:T(8,128)(2,1)S(1)}, bf16[8,192,256]{2,1,0:T(8,128)(2,1)S(1)}, u32[]{:S(2)}, u32[]{:S(2)}) collective-permute-start(bf16[8,192,256]{2,1,0:T(8,128)(2,1)S(1)} %pad_maximum_fusion.1.g0), channel_id=1, source_target_pairs={{0,2},{1,5},{2,0},{3,7},{4,6},{5,1},{6,4},{7,3},{8,10},{9,13},{10,... | collective-permute-start | bytes 2359304 | tf_op jit(solution)/shard_map/feed1_second/ppermute | solution.py:427
  47.2 9.0 %mixer_forward.1 = (bf16[1024,1024]{1,0:T(8,128)(2,1)S(1)}, bf16[4,1024,256]{2,1,0:T(8,128)(2,1)S(1)}, bf16[4,1024,256]{2,1,0:T(8,128)(2,1)S(1)}, bf16[4,1024,25...) custom-call(s32[32]{0:T(128)S(1)} %dynamic-slice_bitcast_fusion.dev_r, ...), custom_call_target="tpu_custom_call" | custom-call | flops 3221225472 | bytes 33554432 | tf_op jit(solution)/shard_map/mixer_forward/pallas_call | solution.py:541
  60.0 3.5 %feed_prepare.1 = (f32[1024,512]{1,0:T(8,128)S(1)}, bf16[1024,512]{1,0:T(8,128)(2,1)S(1)}, bf16[512,1024]{1,0:T(8,128)(2,1)S(1)}, bf16[512,1024]{1,0:T(8,128)(2,1)S(1)}, bf16[1024,512]{1,0:T(8,128)(2,1)S(1)}) custom-call(s32[32]{0:T(128)S(1)} %dynamic-slice_bitcast_fusion.dev_ref, f32[2,512]{1,0:T(2,128)S(1)} %get-tuple-element.160.gain_ref, ...), custom_call_target="tpu_custom_call" | custom-call | flops 1073741824 | bytes 10485760 | tf_op jit(solution)/shard_map/feed_prepare/pallas_call | solution.py:566
  64.1 1.5 %collective-permute-start.16 = (bf16[8,128,256]{2,1,0:T(8,128)(2,1)S(1)}, bf16[8,128,256]{2,1,0:T(8,128)(2,1)S(1)}, u32[]{:S(2)}, u32[]{:S(2)}) collective-permute-start(bf16[8,128,256]{2,1,0:T(8,128)(2,1)S(1)} %constant_dynamic-update-slice_fusion.g0), channel_id=1, source_target_pairs={{0,2},{1,5},{2,0},{3,7},{4,6},{5,1},{6,4},{7,3},{8,10},{9,13},{10,... | collective-permute-start | bytes 1572872 | tf_op jit(solution)/shard_map/feed2_second/ppermute | solution.py:427
  65.6 8.8 %feed_first.1 = (f32[1024,512]{1,0:T(8,128)S(1)}, f32[1024,512]{1,0:T(8,128)S(1)}, bf16[8,128,256]{2,1,0:T(8,128)(2,1)S(1)}, bf16[8,128,256]{2,1,0:T(8,128)(2,1)S(1)}, bf16[16,128,256]{2,1,0:T(8,128)(2,1)S(1)}) custom-call(s32[32]{0:T(128)S(1)} %dynamic-slice_bitcast_fusion.dev_ref, bf16[8,192,256]{2,1,0:T(8,128)(2,1)S(1)} %pad_maximum_fusion.1.g0, ...), custom_call_target="tpu_custom_call" | custom-call | flops 6442450944 | bytes 20971520 | tf_op jit(solution)/shard_map/feed_first/pallas_call | solution.py:577
  75.0 2.1 %collective-permute-done.17 = bf16[16,128,256]{2,1,0:T(8,128)(2,1)S(1)} collective-permute-done((bf16[16,128,256]{2,1,0:T(8,128)(2,1)S(1)}, bf16[16,128,256]{2,1,0:T(8,128)(2,1)S(1)}, u32[]{:S(2)}, u32[]{:S(2)}) %collective-permute-start.17) | collective-permute-done | bytes 1048608 | tf_op jit(solution)/shard_map/feed1_back_core/ppermute | solution.py:427
  78.6 9.1 %feed_last.1 = (f32[1024,512]{1,0:T(8,128)S(1)}, f32[1024,512]{1,0:T(8,128)S(1)}, bf16[8,128,256]{2,1,0:T(8,128)(2,1)S(1)}, bf16[8,128,256]{2,1,0:T(8,128)(2,1)S(1)}, bf16[16,128,256]{2,1,0:T(8,128)(2,1)S(1)}) custom-call(s32[32]{0:T(128)S(1)} %dynamic-slice_bitcast_fusion.dev_ref, bf16[8,128,256]{2,1,0:T(8,128)(2,1)S(1)} %constant_dynamic-update-slice_fusion.g0, ...), custom_call_target="tpu_custom_call" | custom-call | flops 6442450944 | bytes 20971520 | tf_op jit(solution)/shard_map/feed_last/pallas_call | solution.py:577
  89.6 3.4 %feed_finish.1 = (bf16[1024,512]{1,0:T(8,128)(2,1)S(1)}, bf16[1024,512]{1,0:T(8,128)(2,1)S(1)}, bf16[8,64,256]{2,1,0:T(8,128)(2,1)S(1)}, bf16[8,64,256]{2,1,0:T(...) custom-call(s32[32]{0:T(128)S(1)} %dynamic-slice_bitcast_fusion.dev_ref, ...), custom_call_target="tpu_custom_call" | custom-call | flops 1073741824 | bytes 10485760 | tf_op jit(solution)/shard_map/feed_finish/pallas_call | solution.py:609
  93.0 1.6 %collective-permute-done.21 = bf16[4,128,256]{2,1,0:T(8,128)(2,1)S(1)} collective-permute-done((bf16[4,128,256]{2,1,0:T(8,128)(2,1)S(1)}, bf16[4,128,256]{2,1,0:T(8,128)(2,1)S(1)}, u32[]{:S(2)}, u32[]{:S(2)}) %collective-permute-start.21) | collective-permute-done | bytes 262176 | tf_op jit(solution)/shard_map/feed1_back_first/ppermute | solution.py:427
  94.8 1.7 %collective-permute-done.23 = bf16[16,64,256]{2,1,0:T(8,128)(2,1)S(1)} collective-permute-done((bf16[16,64,256]{2,1,0:T(8,128)(2,1)S(1)}, bf16[16,64,256]{2,1,0:T(8,128)(2,1)S(1)}, u32[]{:S(2)}, u32[]{:S(2)}) %collective-permute-start.23) | collective-permute-done | bytes 524320 | tf_op jit(solution)/shard_map/out_back_core/ppermute | solution.py:427
  97.4 10.0 %mixer_backward.1 = (bf16[4,1024,768]{2,1,0:T(8,128)(2,1)S(1)}, bf16[16,208,256]{2,1,0:T(8,128)(2,1)S(1)}, bf16[16,208,256]{2,1,0:T(8,128)(2,1)S(1)}) custom-call(s32[32]{0:T(128)S(1)} %dynamic-slice_bitcast_fusion.dev_ref, bf16[1024,512]{1,0:T(8,128)(2,1)S(1)} %get-tuple-element.216.dmix_ref, bf16[512,1024]{1,0:T(8,128)(2,1)S(1)} %get-tuple-element.217.xnt_ref, ...), custom_call_target="tpu_custom_call" | custom-call | flops 4294967296 | bytes 41943040 | tf_op jit(solution)/shard_map/mixer_backward/pallas_call | solution.py:628
  110.6 2.0 %collective-permute-start.27 = (bf16[128,256]{1,0:T(8,128)(2,1)S(1)}, bf16[128,256]{1,0:T(8,128)(2,1)S(1)}, u32[]{:S(2)}, u32[]{:S(2)}) collective-permute-start(bf16[128,256]{1,0:T(8,128)(2,1)S(1)} %fusion.3), channel_id=1, source_target_pairs={{0,16},{1,17},{2,18},{3,19},{4,20},{5,21},{6,22},{7,23},{8,24},{9,... | collective-permute-start | bytes 196616 | tf_op jit(solution)/shard_map/feed1_back_far/ppermute | solution.py:427
  113.1 3.6 %collective-permute-done.27 = bf16[128,256]{1,0:T(8,128)(2,1)S(1)} collective-permute-done((bf16[128,256]{1,0:T(8,128)(2,1)S(1)}, bf16[128,256]{1,0:T(8,128)(2,1)S(1)}, u32[]{:S(2)}, u32[]{:S(2)}) %collective-permute-start.27) | collective-permute-done | bytes 65568 | tf_op jit(solution)/shard_map/feed1_back_far/ppermute | solution.py:427
  120.7 5.2 %input_gradient.1 = f32[1024,512]{1,0:T(8,128)S(1)} custom-call(bf16[1024,512]{1,0:T(8,128)(2,1)S(1)} %get-tuple-element.294.x_ref, bf16[1024,512]{1,0:T(8,128)(2,1)S(1)} %get-tuple-element.216.dmix_ref, f32[2,512]{1,0:T(2,128)S(1)} %get-tuple-element.160.gain_ref, bf16[4,1024,768]{2,1,0:T(8,128)(2,1)S(1)} %get-tuple-element.240.dk_ref, ...), custom_call_target="tpu_custom_call" | custom-call | flops 3221225472 | bytes 25165824 | tf_op jit(solution)/shard_map/input_gradient/pallas_call | solution.py:643
  126.0 3.9 %collective-permute-done.29 = bf16[8,208,256]{2,1,0:T(8,128)(2,1)S(1)} collective-permute-done((bf16[8,208,256]{2,1,0:T(8,128)(2,1)S(1)}, bf16[8,208,256]{2,1,0:T(8,128)(2,1)S(1)}, u32[]{:S(2)}, u32[]{:S(2)}) %collective-permute-start.29) | collective-permute-done | bytes 852000 | tf_op jit(solution)/shard_map/mixer_back_second/ppermute | solution.py:427
  131.6 2.1 %collective-permute-start.32 = (bf16[192,256]{1,0:T(8,128)(2,1)S(1)}, bf16[192,256]{1,0:T(8,128)(2,1)S(1)}, u32[]{:S(2)}, u32[]{:S(2)}) collective-permute-start(bf16[192,256]{1,0:T(8,128)(2,1)S(1)} %get-tuple-element.248), channel_id=1, source_target_pairs={{0,16},{1,17},{2,18},{3,19},{4,20},{5,21},{6,22},{7,23},{8,24},{9,... | collective-permute-start | bytes 294920 | tf_op jit(solution)/shard_map/feed2_back_far/ppermute | solution.py:427
  133.7 2.5 %copy.26 = f32[8,128,512]{2,1,0:T(8,128)} copy(f32[8,128,512]{2,0,1:T(8,128)S(1)} %bitcast.56) | data formatting | bytes 4194304 | tf_op jit(solution)/shard_map/transpose | solution.py:470
  136.3 2.0 %collective-permute-done.32 = bf16[192,256]{1,0:T(8,128)(2,1)S(1)} collective-permute-done((bf16[192,256]{1,0:T(8,128)(2,1)S(1)}, bf16[192,256]{1,0:T(8,128)(2,1)S(1)}, u32[]{:S(2)}, u32[]{:S(2)}) %collective-permute-start.32) | collective-permute-done | bytes 98336 | tf_op jit(solution)/shard_map/feed2_back_far/ppermute | solution.py:427
  138.6 2.5 %collective-permute-start.35 = (bf16[208,256]{1,0:T(8,128)(2,1)S(1)}, bf16[208,256]{1,0:T(8,128)(2,1)S(1)}, u32[]{:S(2)}, u32[]{:S(2)}) collective-permute-start(bf16[208,256]{1,0:T(8,128)(2,1)S(1)} %get-tuple-element.273), channel_id=1, source_target_pairs={{0,24},{1,25},{2,26},{3,27},{4,28},{5,29},{6,30},{7,31},{8,16},{9,... | collective-permute-start | bytes 319496 | tf_op jit(solution)/shard_map/mixer_back_z/ppermute | solution.py:427
  141.3 1.7 %collective-permute-start.33 = (bf16[208,256]{1,0:T(8,128)(2,1)S(1)}, bf16[208,256]{1,0:T(8,128)(2,1)S(1)}, u32[]{:S(2)}, u32[]{:S(2)}) collective-permute-start(bf16[208,256]{1,0:T(8,128)(2,1)S(1)} %get-tuple-element.275), channel_id=1, source_target_pairs={{0,16},{1,17},{2,18},{3,19},{4,20},{5,21},{6,22},{7,23},{8,24},{9,... | collective-permute-start | bytes 319496 | tf_op jit(solution)/shard_map/mixer_back_z/ppermute | solution.py:427
  147.3 1.8 %collective-permute-done.33.p0 = bf16[208,256]{1,0:T(8,128)(2,1)S(1)} collective-permute-done((bf16[208,256]{1,0:T(8,128)(2,1)S(1)}, bf16[208,256]{1,0:T(8,128)(2,1)S(1)}, u32[]{:S(2)}, u32[]{:S(2)}) %collective-permute-start.33) | collective-permute-done | bytes 106528 | tf_op jit(solution)/shard_map/mixer_back_z/ppermute | solution.py:427
  (100 shorter events, 33.6 us)
Async XLA Ops:
  2.1 10.7 %collective-permute-start.2 = (bf16[208,256]{1,0:T(8,128)(2,1)}, bf16[208,256]{1,0:T(8,128)(2,1)S(1)}, u32[]{:S(2)}, u32[]{:S(2)}) collective-permute-start(bf16[208,256]{1,0:T(8,128)(2,1)} %pack.1), channel_id=1, source_target_pairs={{0,24},{1,25},{2,26},{3,27},{4,28},{5,29},{6,30},{7,31},{8,16},{9,... | collective-permute-start | bytes 319496 | tf_op jit(solution)/shard_map/mixer_z/ppermute | solution.py:427
  7.2 6.6 %collective-permute-start.1 = (bf16[208,256]{1,0:T(8,128)(2,1)}, bf16[208,256]{1,0:T(8,128)(2,1)S(1)}, u32[]{:S(2)}, u32[]{:S(2)}) collective-permute-start(bf16[208,256]{1,0:T(8,128)(2,1)} %pack.1), channel_id=1, source_target_pairs={{0,8},{1,9},{2,10},{3,11},{4,12},{5,13},{6,14},{7,15},{8,0},{9,1},... | collective-permute-start | bytes 319496 | tf_op jit(solution)/shard_map/mixer_z/ppermute | solution.py:427
  7.2 9.2 %collective-permute-start = (bf16[208,256]{1,0:T(8,128)(2,1)}, bf16[208,256]{1,0:T(8,128)(2,1)S(1)}, u32[]{:S(2)}, u32[]{:S(2)}) collective-permute-start(bf16[208,256]{1,0:T(8,128)(2,1)} %pack.1), channel_id=1, source_target_pairs={{0,16},{1,17},{2,18},{3,19},{4,20},{5,21},{6,22},{7,23},{8,24},{9,... | collective-permute-start | bytes 319496 | tf_op jit(solution)/shard_map/mixer_z/ppermute | solution.py:427
  16.4 8.3 %collective-permute-start.3 = (bf16[4,208,256]{2,1,0:T(8,128)(2,1)S(1)}, bf16[4,208,256]{2,1,0:T(8,128)(2,1)S(1)}, u32[]{:S(2)}, u32[]{:S(2)}) collective-permute-start(bf16[4,208,256]{2,1,0:T(8,128)(2,1)S(1)} %pad_maximum_fusion.3), channel_id=1, source_target_pairs={{0,4},{1,3},{2,6},{3,1},{4,0},{5,7},{6,2},{7,5},{8,12},{9,11},{10,... | collective-permute-start | bytes 1277960 | tf_op jit(solution)/shard_map/mixer_first/ppermute | solution.py:427
  18.0 6.7 %collective-permute-start.4 = (bf16[192,256]{1,0:T(8,128)(2,1)S(1)}, bf16[192,256]{1,0:T(8,128)(2,1)S(1)}, u32[]{:S(2)}, u32[]{:S(2)}) collective-permute-start(bf16[192,256]{1,0:T(8,128)(2,1)S(1)} %pad_maximum_fusion.10), channel_id=1, source_target_pairs={{0,16},{1,17},{2,18},{3,19},{4,20},{5,21},{6,22},{7,23},{8,24},{9,... | collective-permute-start | bytes 294920 | tf_op jit(solution)/shard_map/feed1_far/ppermute | solution.py:427
  24.8 12.8 %collective-permute-start.5 = (bf16[8,208,256]{2,1,0:T(8,128)(2,1)S(1)}, bf16[8,208,256]{2,1,0:T(8,128)(2,1)S(1)}, u32[]{:S(2)}, u32[]{:S(2)}) collective-permute-start(bf16[8,208,256]{2,1,0:T(8,128)(2,1)S(1)} %pad_maximum_fusion.g0), channel_id=1, source_target_pairs={{0,2},{1,5},{2,0},{3,7},{4,6},{5,1},{6,4},{7,3},{8,10},{9,13},{10,... | collective-permute-start | bytes 2555912 | tf_op jit(solution)/shard_map/mixer_second/ppermute | solution.py:427
  26.3 7.6 %collective-permute-start.6 = (bf16[2,192,256]{2,1,0:T(8,128)(2,1)S(1)}, bf16[2,192,256]{2,1,0:T(8,128)(2,1)S(1)}, u32[]{:S(2)}, u32[]{:S(2)}) collective-permute-start(bf16[2,192,256]{2,1,0:T(8,128)(2,1)S(1)} %pad_maximum_fusion.7), channel_id=1, source_target_pairs={{0,8},{1,9},{2,10},{3,11},{4,12},{5,13},{6,14},{7,15},{8,0},{9,1},... | collective-permute-start | bytes 589832 | tf_op jit(solution)/shard_map/feed1_near/ppermute | solution.py:427
  26.3 5.5 %collective-permute-start.7 = (bf16[128,256]{1,0:T(8,128)(2,1)S(1)}, bf16[128,256]{1,0:T(8,128)(2,1)S(1)}, u32[]{:S(2)}, u32[]{:S(2)}) collective-permute-start(bf16[128,256]{1,0:T(8,128)(2,1)S(1)} %pad_maximum_fusion.11), channel_id=1, source_target_pairs={{0,16},{1,17},{2,18},{3,19},{4,20},{5,21},{6,22},{7,23},{8,24},{9,... | collective-permute-start | bytes 196616 | tf_op jit(solution)/shard_map/feed2_far/ppermute | solution.py:427
  29.3 9.9 %collective-permute-start.10 = (bf16[8,208,256]{2,1,0:T(8,128)(2,1)S(1)}, bf16[8,208,256]{2,1,0:T(8,128)(2,1)S(1)}, u32[]{:S(2)}, u32[]{:S(2)}) collective-permute-start(bf16[8,208,256]{2,1,0:T(8,128)(2,1)S(1)} %pad_maximum_fusion.g0), channel_id=1, source_target_pairs={{0,1},{1,0},{2,3},{3,2},{4,5},{5,4},{6,7},{7,6},{8,9},{9,8},{10,11... | collective-permute-start | bytes 2555912 | tf_op jit(solution)/shard_map/mixer_core/ppermute | solution.py:427
  37.6 7.9 %collective-permute-start.11 = (bf16[8,208,256]{2,1,0:T(8,128)(2,1)S(1)}, bf16[8,208,256]{2,1,0:T(8,128)(2,1)S(1)}, u32[]{:S(2)}, u32[]{:S(2)}) collective-permute-start(bf16[8,208,256]{2,1,0:T(8,128)(2,1)S(1)} %collective-permute-done.5.g1), channel_id=1, source_target_pairs={{0,1},{1,0},{2,3},{3,2},{4,5},{5,4},{6,7},{7,6},{8,9},{9,8},{10,11... | collective-permute-start | bytes 2555912 | tf_op jit(solution)/shard_map/mixer_core_more/ppermute | solution.py:427
  37.7 7.8 %collective-permute-start.8 = (bf16[4,192,256]{2,1,0:T(8,128)(2,1)S(1)}, bf16[4,192,256]{2,1,0:T(8,128)(2,1)S(1)}, u32[]{:S(2)}, u32[]{:S(2)}) collective-permute-start(bf16[4,192,256]{2,1,0:T(8,128)(2,1)S(1)} %pad_maximum_fusion.5), channel_id=1, source_target_pairs={{0,4},{1,3},{2,6},{3,1},{4,0},{5,7},{6,2},{7,5},{8,12},{9,11},{10,... | collective-permute-start | bytes 1179656 | tf_op jit(solution)/shard_map/feed1_first/ppermute | solution.py:427
  39.2 5.5 %collective-permute-start.9 = (bf16[2,128,256]{2,1,0:T(8,128)(2,1)S(1)}, bf16[2,128,256]{2,1,0:T(8,128)(2,1)S(1)}, u32[]{:S(2)}, u32[]{:S(2)}) collective-permute-start(bf16[2,128,256]{2,1,0:T(8,128)(2,1)S(1)} %pad_maximum_fusion.8), channel_id=1, source_target_pairs={{0,8},{1,9},{2,10},{3,11},{4,12},{5,13},{6,14},{7,15},{8,0},{9,1},... | collective-permute-start | bytes 393224 | tf_op jit(solution)/shard_map/feed2_near/ppermute | solution.py:427
  45.6 12.1 %collective-permute-start.12 = (bf16[8,192,256]{2,1,0:T(8,128)(2,1)S(1)}, bf16[8,192,256]{2,1,0:T(8,128)(2,1)S(1)}, u32[]{:S(2)}, u32[]{:S(2)}) collective-permute-start(bf16[8,192,256]{2,1,0:T(8,128)(2,1)S(1)} %pad_maximum_fusion.1.g0), channel_id=1, source_target_pairs={{0,2},{1,5},{2,0},{3,7},{4,6},{5,1},{6,4},{7,3},{8,10},{9,13},{10,... | collective-permute-start | bytes 2359304 | tf_op jit(solution)/shard_map/feed1_second/ppermute | solution.py:427
  47.1 12.1 %collective-permute-start.14 = (bf16[8,192,256]{2,1,0:T(8,128)(2,1)S(1)}, bf16[8,192,256]{2,1,0:T(8,128)(2,1)S(1)}, u32[]{:S(2)}, u32[]{:S(2)}) collective-permute-start(bf16[8,192,256]{2,1,0:T(8,128)(2,1)S(1)} %pad_maximum_fusion.1.g0), channel_id=1, source_target_pairs={{0,1},{1,0},{2,3},{3,2},{4,5},{5,4},{6,7},{7,6},{8,9},{9,8},{10,11... | collective-permute-start | bytes 2359304 | tf_op jit(solution)/shard_map/feed1_core/ppermute | solution.py:427
  57.7 6.4 %collective-permute-start.13 = (bf16[4,128,256]{2,1,0:T(8,128)(2,1)S(1)}, bf16[4,128,256]{2,1,0:T(8,128)(2,1)S(1)}, u32[]{:S(2)}, u32[]{:S(2)}) collective-permute-start(bf16[4,128,256]{2,1,0:T(8,128)(2,1)S(1)} %pad_maximum_fusion.6), channel_id=1, source_target_pairs={{0,4},{1,3},{2,6},{3,1},{4,0},{5,7},{6,2},{7,5},{8,12},{9,11},{10,... | collective-permute-start | bytes 786440 | tf_op jit(solution)/shard_map/feed2_first/ppermute | solution.py:427
  64.1 10.3 %collective-permute-start.16 = (bf16[8,128,256]{2,1,0:T(8,128)(2,1)S(1)}, bf16[8,128,256]{2,1,0:T(8,128)(2,1)S(1)}, u32[]{:S(2)}, u32[]{:S(2)}) collective-permute-start(bf16[8,128,256]{2,1,0:T(8,128)(2,1)S(1)} %constant_dynamic-update-slice_fusion.g0), channel_id=1, source_target_pairs={{0,2},{1,5},{2,0},{3,7},{4,6},{5,1},{6,4},{7,3},{8,10},{9,13},{10,... | collective-permute-start | bytes 1572872 | tf_op jit(solution)/shard_map/feed2_second/ppermute | solution.py:427
  75.0 3.6 %collective-permute-start.20 = (bf16[8,128,256]{2,1,0:T(8,128)(2,1)S(1)}, bf16[8,128,256]{2,1,0:T(8,128)(2,1)S(1)}, u32[]{:S(2)}, u32[]{:S(2)}) collective-permute-start(bf16[8,128,256]{2,1,0:T(8,128)(2,1)S(1)} %collective-permute-done.16.g1), channel_id=1, source_target_pairs={{0,1},{1,0},{2,3},{3,2},{4,5},{5,4},{6,7},{7,6},{8,9},{9,8},{10,11... | collective-permute-start | bytes 1572872 | tf_op jit(solution)/shard_map/feed2_core_more/ppermute | solution.py:427
  77.5 10.3 %collective-permute-start.18 = (bf16[8,128,256]{2,1,0:T(8,128)(2,1)S(1)}, bf16[8,128,256]{2,1,0:T(8,128)(2,1)S(1)}, u32[]{:S(2)}, u32[]{:S(2)}) collective-permute-start(bf16[8,128,256]{2,1,0:T(8,128)(2,1)S(1)} %get-tuple-element.183), channel_id=1, source_target_pairs={{0,2},{1,5},{2,0},{3,7},{4,6},{5,1},{6,4},{7,3},{8,10},{9,13},{10,... | collective-permute-start | bytes 1572872 | tf_op jit(solution)/shard_map/feed1_back_second/ppermute | solution.py:427
  87.7 6.9 %collective-permute-start.22 = (bf16[16,128,256]{2,1,0:T(8,128)(2,1)S(1)}, bf16[16,128,256]{2,1,0:T(8,128)(2,1)S(1)}, u32[]{:S(2)}, u32[]{:S(2)}) collective-permute-start(bf16[16,128,256]{2,1,0:T(8,128)(2,1)S(1)} %get-tuple-element.201), channel_id=1, source_target_pairs={{0,1},{1,0},{2,3},{3,2},{4,5},{5,4},{6,7},{7,6},{8,9},{9,8},{10,11... | collective-permute-start | bytes 3145736 | tf_op jit(solution)/shard_map/feed2_back_core/ppermute | solution.py:427
  88.2 6.4 %collective-permute-start.21 = (bf16[4,128,256]{2,1,0:T(8,128)(2,1)S(1)}, bf16[4,128,256]{2,1,0:T(8,128)(2,1)S(1)}, u32[]{:S(2)}, u32[]{:S(2)}) collective-permute-start(bf16[4,128,256]{2,1,0:T(8,128)(2,1)S(1)} %get-tuple-element.200), channel_id=1, source_target_pairs={{0,4},{1,3},{2,6},{3,1},{4,0},{5,7},{6,2},{7,5},{8,12},{9,11},{10,... | collective-permute-start | bytes 786440 | tf_op jit(solution)/shard_map/feed1_back_first/ppermute | solution.py:427
  96.7 12.1 %collective-permute-start.24 = (bf16[8,192,256]{2,1,0:T(8,128)(2,1)S(1)}, bf16[8,192,256]{2,1,0:T(8,128)(2,1)S(1)}, u32[]{:S(2)}, u32[]{:S(2)}) collective-permute-start(bf16[8,192,256]{2,1,0:T(8,128)(2,1)S(1)} %pad_maximum_fusion.2), channel_id=1, source_target_pairs={{0,2},{1,5},{2,0},{3,7},{4,6},{5,1},{6,4},{7,3},{8,10},{9,13},{10,... | collective-permute-start | bytes 2359304 | tf_op jit(solution)/shard_map/feed2_back_second/ppermute | solution.py:427
  97.4 10.0 %collective-permute-start.25 = (bf16[2,128,256]{2,1,0:T(8,128)(2,1)S(1)}, bf16[2,128,256]{2,1,0:T(8,128)(2,1)S(1)}, u32[]{:S(2)}, u32[]{:S(2)}) collective-permute-start(bf16[2,128,256]{2,1,0:T(8,128)(2,1)S(1)} %get-tuple-element.213), channel_id=1, source_target_pairs={{0,8},{1,9},{2,10},{3,11},{4,12},{5,13},{6,14},{7,15},{8,0},{9,1},... | collective-permute-start | bytes 393224 | tf_op jit(solution)/shard_map/feed1_back_near/ppermute | solution.py:427
  108.7 3.9 %collective-permute-start.28 = (bf16[16,208,256]{2,1,0:T(8,128)(2,1)S(1)}, bf16[16,208,256]{2,1,0:T(8,128)(2,1)S(1)}, u32[]{:S(2)}, u32[]{:S(2)}) collective-permute-start(bf16[16,208,256]{2,1,0:T(8,128)(2,1)S(1)} %get-tuple-element.234), channel_id=1, source_target_pairs={{0,1},{1,0},{2,3},{3,2},{4,5},{5,4},{6,7},{7,6},{8,9},{9,8},{10,11... | collective-permute-start | bytes 5111816 | tf_op jit(solution)/shard_map/mixer_back_core/ppermute | solution.py:427
  109.2 7.8 %collective-permute-start.26 = (bf16[4,192,256]{2,1,0:T(8,128)(2,1)S(1)}, bf16[4,192,256]{2,1,0:T(8,128)(2,1)S(1)}, u32[]{:S(2)}, u32[]{:S(2)}) collective-permute-start(bf16[4,192,256]{2,1,0:T(8,128)(2,1)S(1)} %get-tuple-element.231), channel_id=1, source_target_pairs={{0,4},{1,3},{2,6},{3,1},{4,0},{5,7},{6,2},{7,5},{8,12},{9,11},{10,... | collective-permute-start | bytes 1179656 | tf_op jit(solution)/shard_map/feed2_back_first/ppermute | solution.py:427
  110.6 6.1 %collective-permute-start.27 = (bf16[128,256]{1,0:T(8,128)(2,1)S(1)}, bf16[128,256]{1,0:T(8,128)(2,1)S(1)}, u32[]{:S(2)}, u32[]{:S(2)}) collective-permute-start(bf16[128,256]{1,0:T(8,128)(2,1)S(1)} %fusion.3), channel_id=1, source_target_pairs={{0,16},{1,17},{2,18},{3,19},{4,20},{5,21},{6,22},{7,23},{8,24},{9,... | collective-permute-start | bytes 196616 | tf_op jit(solution)/shard_map/feed1_back_far/ppermute | solution.py:427
  117.1 12.8 %collective-permute-start.29 = (bf16[8,208,256]{2,1,0:T(8,128)(2,1)S(1)}, bf16[8,208,256]{2,1,0:T(8,128)(2,1)S(1)}, u32[]{:S(2)}, u32[]{:S(2)}) collective-permute-start(bf16[8,208,256]{2,1,0:T(8,128)(2,1)S(1)} %get-tuple-element.238), channel_id=1, source_target_pairs={{0,2},{1,5},{2,0},{3,7},{4,6},{5,1},{6,4},{7,3},{8,10},{9,13},{10,... | collective-permute-start | bytes 2555912 | tf_op jit(solution)/shard_map/mixer_back_second/ppermute | solution.py:427
  119.3 6.7 %collective-permute-start.30 = (bf16[2,192,256]{2,1,0:T(8,128)(2,1)S(1)}, bf16[2,192,256]{2,1,0:T(8,128)(2,1)S(1)}, u32[]{:S(2)}, u32[]{:S(2)}) collective-permute-start(bf16[2,192,256]{2,1,0:T(8,128)(2,1)S(1)} %get-tuple-element.239), channel_id=1, source_target_pairs={{0,8},{1,9},{2,10},{3,11},{4,12},{5,13},{6,14},{7,15},{8,0},{9,1},... | collective-permute-start | bytes 589832 | tf_op jit(solution)/shard_map/feed2_back_near/ppermute | solution.py:427
  130.2 8.2 %collective-permute-start.31 = (bf16[4,208,256]{2,1,0:T(8,128)(2,1)S(1)}, bf16[4,208,256]{2,1,0:T(8,128)(2,1)S(1)}, u32[]{:S(2)}, u32[]{:S(2)}) collective-permute-start(bf16[4,208,256]{2,1,0:T(8,128)(2,1)S(1)} %get-tuple-element.247), channel_id=1, source_target_pairs={{0,4},{1,3},{2,6},{3,1},{4,0},{5,7},{6,2},{7,5},{8,12},{9,11},{10,... | collective-permute-start | bytes 1277960 | tf_op jit(solution)/shard_map/mixer_back_first/ppermute | solution.py:427
  131.6 6.6 %collective-permute-start.32 = (bf16[192,256]{1,0:T(8,128)(2,1)S(1)}, bf16[192,256]{1,0:T(8,128)(2,1)S(1)}, u32[]{:S(2)}, u32[]{:S(2)}) collective-permute-start(bf16[192,256]{1,0:T(8,128)(2,1)S(1)} %get-tuple-element.248), channel_id=1, source_target_pairs={{0,16},{1,17},{2,18},{3,19},{4,20},{5,21},{6,22},{7,23},{8,24},{9,... | collective-permute-start | bytes 294920 | tf_op jit(solution)/shard_map/feed2_back_far/ppermute | solution.py:427
  138.6 7.4 %collective-permute-start.35 = (bf16[208,256]{1,0:T(8,128)(2,1)S(1)}, bf16[208,256]{1,0:T(8,128)(2,1)S(1)}, u32[]{:S(2)}, u32[]{:S(2)}) collective-permute-start(bf16[208,256]{1,0:T(8,128)(2,1)S(1)} %get-tuple-element.273), channel_id=1, source_target_pairs={{0,24},{1,25},{2,26},{3,27},{4,28},{5,29},{6,30},{7,31},{8,16},{9,... | collective-permute-start | bytes 319496 | tf_op jit(solution)/shard_map/mixer_back_z/ppermute | solution.py:427
  141.2 6.2 %collective-permute-start.34 = (bf16[208,256]{1,0:T(8,128)(2,1)S(1)}, bf16[208,256]{1,0:T(8,128)(2,1)S(1)}, u32[]{:S(2)}, u32[]{:S(2)}) collective-permute-start(bf16[208,256]{1,0:T(8,128)(2,1)S(1)} %get-tuple-element.274), channel_id=1, source_target_pairs={{0,8},{1,9},{2,10},{3,11},{4,12},{5,13},{6,14},{7,15},{8,0},{9,1},... | collective-permute-start | bytes 319496 | tf_op jit(solution)/shard_map/mixer_back_z/ppermute | solution.py:427
  141.3 7.8 %collective-permute-start.33 = (bf16[208,256]{1,0:T(8,128)(2,1)S(1)}, bf16[208,256]{1,0:T(8,128)(2,1)S(1)}, u32[]{:S(2)}, u32[]{:S(2)}) collective-permute-start(bf16[208,256]{1,0:T(8,128)(2,1)S(1)} %get-tuple-element.275), channel_id=1, source_target_pairs={{0,16},{1,17},{2,18},{3,19},{4,20},{5,21},{6,22},{7,23},{8,24},{9,... | collective-permute-start | bytes 319496 | tf_op jit(solution)/shard_map/mixer_back_z/ppermute | solution.py:427
  (9 other events, 69.3 us)

commit v6 on v5

--- a/solution.py
+++ b/solution.py
@@ -186,14 +186,18 @@
             at, cols = aligned(d // 4 * rows, rows), aligned(d // 2 % 2 * LANES, LANES)
             up_s[at, cols] = parts[s // per][s % per, 0:rows, :]
             dn_s[at, cols] = parts[s // per][s % per, rows : 2 * rows, :]
-        pre = dot(xn_ref[...], up_s[...])
-        dact = dot(dy_ref[...], dn_s[...])
-        sq = pre * pre
-        gate = 0.5 + 0.5 * jnp.tanh(pre * (C0 + C1 * sq))
-        value = pre * gate
-        act = value.astype(BF)
-        slope = gate + value * (1.0 - gate) * (2.0 * C0 + 6.0 * C1 * sq)
-        dpre = (slope * dact).astype(BF)
+        acts, dpres = [], []
+        for i in range(xn_ref.shape[0] // 128):
+            at = slice(i * 128, (i + 1) * 128)
+            pre = dot(xn_ref[at, :], up_s[...])
+            dact = dot(dy_ref[at, :], dn_s[...])
+            sq = pre * pre
+            gate = 0.5 + 0.5 * jnp.tanh(pre * (C0 + C1 * sq))
+            value = pre * gate
+            acts.append(value.astype(BF))
+            slope = gate + value * (1.0 - gate) * (2.0 * C0 + 6.0 * C1 * sq)
+            dpres.append((slope * dact).astype(BF))
+        act, dpre = jnp.concatenate(acts), jnp.concatenate(dpres)
         upg_s[...] = dot(xnt_ref[...], dpre).astype(BF)
         dng_s[...] = dot(dyt_ref[...], act).astype(BF)
         add_out(base == 0, dot(act, dn_s[...], ((1,), (1,))), dot(dpre, up_s[...], ((1,), (1,))))

time: 150 us -> 150 us (level)
  no operation moved by 1% of the time
where the time goes in v6:
time: 150 us; the launch traced here: 149 us
  Pallas kernels  50.9 us (34%)
  waiting for transfers between devices  47.7 us (32%)
  starting transfers between devices  36.5 us (24%)
  local copies, waits for them, and re-layouts  8.93 us (6%)
  other arithmetic  4.57 us (3%)
    ppermute x36, waiting for transfers between devices, send(): return lax.ppermute(value, AXES, pairs)  47.7 us
    ppermute x36, starting transfers between devices, send(): return lax.ppermute(value, AXES, pairs)  36.5 us
    pallas_call x2, Pallas kernels, feed(): pl.pallas_call(feed_half, in_specs=[smem] + [vmem] * (8 + len(before)), o...  17.4 us
    pallas_call x1, Pallas kernels, local(): pl.pallas_call(mixer_backward, grid=(blocks,), in_specs=[smem, whole((row...  10 us
    pallas_call x1, Pallas kernels, local(): pl.pallas_call(mixer_forward, grid=(blocks,), in_specs=[smem, whole((rows...  9.05 us
    pallas_call x1, Pallas kernels, input_grad(): pl.pallas_call(input_gradient, grid=(rows // part,), in_specs=[band(width...  5.24 us
    transpose x2, local copies, waits for them, and re-layouts, restore(): v.reshape(rows // CHUNKS, CHUNKS, width).transpose(1, 0, 2)  3.82 us
    pallas_call x1, Pallas kernels, local(): pl.pallas_call(feed_prepare, in_specs=[smem] + [vmem] * 8, out_specs=[vme...  3.54 us
  transfers between devices with their start and end apart: 36, of which 25 were waited for; matrix products, arithmetic and copies ran while one was open for 8% of the time, Pallas kernels for 33%

profile of v6, /device:TPU:0, one launch (start us, length us, event | category | flops | bytes accessed | tf_op | source)
XLA Modules:
  0.0 149.5 jit_solution(9666546721711412759)
XLA Ops:
  2.1 5.0 %collective-permute-start.2 = (bf16[208,256]{1,0:T(8,128)(2,1)}, bf16[208,256]{1,0:T(8,128)(2,1)S(1)}, u32[]{:S(2)}, u32[]{:S(2)}) collective-permute-start(bf16[208,256]{1,0:T(8,128)(2,1)} %pack.1), channel_id=1, source_target_pairs={{0,24},{1,25},{2,26},{3,27},{4,28},{5,29},{6,30},{7,31},{8,16},{9,... | collective-permute-start | bytes 319496 | tf_op jit(solution)/shard_map/mixer_z/ppermute | solution.py:431
  9.3 2.7 %copy_bitcast_fusion = (bf16[1024,512]{1,0:T(8,128)(2,1)S(1)}, bf16[1024,512]{1,0:T(8,128)(2,1)S(1)}) fusion(bf16[8,128,512]{2,1,0:T(8,128)(2,1)} %bitcast.62, bf16[8,128,512]{2,1,0:T(8,128)(2,1)} %bitcast.63), kind=kLoop, calls=%fused_computation.2 | loop fusion | bytes 4194304 | tf_op jit(solution)/shard_map/reshape | solution.py:471
  13.7 2.6 %collective-permute-done = bf16[208,256]{1,0:T(8,128)(2,1)S(1)} collective-permute-done((bf16[208,256]{1,0:T(8,128)(2,1)}, bf16[208,256]{1,0:T(8,128)(2,1)S(1)}, u32[]{:S(2)}, u32[]{:S(2)}) %collective-permute-start) | collective-permute-done | bytes 106528 | tf_op jit(solution)/shard_map/mixer_z/ppermute | solution.py:431
  16.4 1.6 %collective-permute-start.3 = (bf16[4,208,256]{2,1,0:T(8,128)(2,1)S(1)}, bf16[4,208,256]{2,1,0:T(8,128)(2,1)S(1)}, u32[]{:S(2)}, u32[]{:S(2)}) collective-permute-start(bf16[4,208,256]{2,1,0:T(8,128)(2,1)S(1)} %pad_maximum_fusion.3), channel_id=1, source_target_pairs={{0,4},{1,3},{2,6},{3,1},{4,0},{5,7},{6,2},{7,5},{8,12},{9,11},{10,... | collective-permute-start | bytes 1277960 | tf_op jit(solution)/shard_map/mixer_first/ppermute | solution.py:431
  19.2 5.5 %collective-permute-done.4 = bf16[192,256]{1,0:T(8,128)(2,1)S(1)} collective-permute-done((bf16[192,256]{1,0:T(8,128)(2,1)S(1)}, bf16[192,256]{1,0:T(8,128)(2,1)S(1)}, u32[]{:S(2)}, u32[]{:S(2)}) %collective-permute-start.4) | collective-permute-done | bytes 98336 | tf_op jit(solution)/shard_map/feed1_far/ppermute | solution.py:431
  24.8 1.5 %collective-permute-start.5 = (bf16[8,208,256]{2,1,0:T(8,128)(2,1)S(1)}, bf16[8,208,256]{2,1,0:T(8,128)(2,1)S(1)}, u32[]{:S(2)}, u32[]{:S(2)}) collective-permute-start(bf16[8,208,256]{2,1,0:T(8,128)(2,1)S(1)} %pad_maximum_fusion.g0), channel_id=1, source_target_pairs={{0,2},{1,5},{2,0},{3,7},{4,6},{5,1},{6,4},{7,3},{8,10},{9,13},{10,... | collective-permute-start | bytes 2555912 | tf_op jit(solution)/shard_map/mixer_second/ppermute | solution.py:431
  26.3 3.0 %collective-permute-start.7 = (bf16[128,256]{1,0:T(8,128)(2,1)S(1)}, bf16[128,256]{1,0:T(8,128)(2,1)S(1)}, u32[]{:S(2)}, u32[]{:S(2)}) collective-permute-start(bf16[128,256]{1,0:T(8,128)(2,1)S(1)} %pad_maximum_fusion.11), channel_id=1, source_target_pairs={{0,16},{1,17},{2,18},{3,19},{4,20},{5,21},{6,22},{7,23},{8,24},{9,... | collective-permute-start | bytes 196616 | tf_op jit(solution)/shard_map/feed2_far/ppermute | solution.py:431
  29.3 2.5 %collective-permute-done.7 = bf16[128,256]{1,0:T(8,128)(2,1)S(1)} collective-permute-done((bf16[128,256]{1,0:T(8,128)(2,1)S(1)}, bf16[128,256]{1,0:T(8,128)(2,1)S(1)}, u32[]{:S(2)}, u32[]{:S(2)}) %collective-permute-start.7) | collective-permute-done | bytes 65568 | tf_op jit(solution)/shard_map/feed2_far/ppermute | solution.py:431
  31.8 2.0 %collective-permute-done.6 = bf16[2,192,256]{2,1,0:T(8,128)(2,1)S(1)} collective-permute-done((bf16[2,192,256]{2,1,0:T(8,128)(2,1)S(1)}, bf16[2,192,256]{2,1,0:T(8,128)(2,1)S(1)}, u32[]{:S(2)}, u32[]{:S(2)}) %collective-permute-start.6) | collective-permute-done | bytes 196640 | tf_op jit(solution)/shard_map/feed1_near/ppermute | solution.py:431
  33.9 3.7 %collective-permute-done.5.g1 = bf16[8,208,256]{2,1,0:T(8,128)(2,1)S(1)} collective-permute-done((bf16[8,208,256]{2,1,0:T(8,128)(2,1)S(1)}, bf16[8,208,256]{2,1,0:T(8,128)(2,1)S(1)}, u32[]{:S(2)}, u32[]{:S(2)}) %collective-permute-start.5) | collective-permute-done | bytes 852000 | tf_op jit(solution)/shard_map/mixer_second/ppermute | solution.py:431
  37.7 1.6 %collective-permute-start.8 = (bf16[4,192,256]{2,1,0:T(8,128)(2,1)S(1)}, bf16[4,192,256]{2,1,0:T(8,128)(2,1)S(1)}, u32[]{:S(2)}, u32[]{:S(2)}) collective-permute-start(bf16[4,192,256]{2,1,0:T(8,128)(2,1)S(1)} %pad_maximum_fusion.5), channel_id=1, source_target_pairs={{0,4},{1,3},{2,6},{3,1},{4,0},{5,7},{6,2},{7,5},{8,12},{9,11},{10,... | collective-permute-start | bytes 1179656 | tf_op jit(solution)/shard_map/feed1_first/ppermute | solution.py:431
  39.3 5.5 %collective-permute-done.9 = bf16[2,128,256]{2,1,0:T(8,128)(2,1)S(1)} collective-permute-done((bf16[2,128,256]{2,1,0:T(8,128)(2,1)S(1)}, bf16[2,128,256]{2,1,0:T(8,128)(2,1)S(1)}, u32[]{:S(2)}, u32[]{:S(2)}) %collective-permute-start.9) | collective-permute-done | bytes 131104 | tf_op jit(solution)/shard_map/feed2_near/ppermute | solution.py:431
  45.6 1.5 %collective-permute-start.12 = (bf16[8,192,256]{2,1,0:T(8,128)(2,1)S(1)}, bf16[8,192,256]{2,1,0:T(8,128)(2,1)S(1)}, u32[]{:S(2)}, u32[]{:S(2)}) collective-permute-start(bf16[8,192,256]{2,1,0:T(8,128)(2,1)S(1)} %pad_maximum_fusion.1.g0), channel_id=1, source_target_pairs={{0,2},{1,5},{2,0},{3,7},{4,6},{5,1},{6,4},{7,3},{8,10},{9,13},{10,... | collective-permute-start | bytes 2359304 | tf_op jit(solution)/shard_map/feed1_second/ppermute | solution.py:431
  47.2 9.0 %mixer_forward.1 = (bf16[1024,1024]{1,0:T(8,128)(2,1)S(1)}, bf16[4,1024,256]{2,1,0:T(8,128)(2,1)S(1)}, bf16[4,1024,256]{2,1,0:T(8,128)(2,1)S(1)}, bf16[4,1024,25...) custom-call(s32[32]{0:T(128)S(1)} %dynamic-slice_bitcast_fusion.dev_r, ...), custom_call_target="tpu_custom_call" | custom-call | flops 3221225472 | bytes 33554432 | tf_op jit(solution)/shard_map/mixer_forward/pallas_call | solution.py:545
  60.0 3.5 %feed_prepare.1 = (f32[1024,512]{1,0:T(8,128)S(1)}, bf16[1024,512]{1,0:T(8,128)(2,1)S(1)}, bf16[512,1024]{1,0:T(8,128)(2,1)S(1)}, bf16[512,1024]{1,0:T(8,128)(2,1)S(1)}, bf16[1024,512]{1,0:T(8,128)(2,1)S(1)}) custom-call(s32[32]{0:T(128)S(1)} %dynamic-slice_bitcast_fusion.dev_ref, f32[2,512]{1,0:T(2,128)S(1)} %get-tuple-element.160.gain_ref, ...), custom_call_target="tpu_custom_call" | custom-call | flops 1073741824 | bytes 10485760 | tf_op jit(solution)/shard_map/feed_prepare/pallas_call | solution.py:570
  65.6 8.5 %feed_first.1 = (f32[1024,512]{1,0:T(8,128)S(1)}, f32[1024,512]{1,0:T(8,128)S(1)}, bf16[8,128,256]{2,1,0:T(8,128)(2,1)S(1)}, bf16[8,128,256]{2,1,0:T(8,128)(2,1)S(1)}, bf16[16,128,256]{2,1,0:T(8,128)(2,1)S(1)}) custom-call(s32[32]{0:T(128)S(1)} %dynamic-slice_bitcast_fusion.dev_ref, bf16[8,192,256]{2,1,0:T(8,128)(2,1)S(1)} %pad_maximum_fusion.1.g0, ...), custom_call_target="tpu_custom_call" | custom-call | flops 6442450944 | bytes 20971520 | tf_op jit(solution)/shard_map/feed_first/pallas_call | solution.py:581
  74.8 2.1 %collective-permute-done.17 = bf16[16,128,256]{2,1,0:T(8,128)(2,1)S(1)} collective-permute-done((bf16[16,128,256]{2,1,0:T(8,128)(2,1)S(1)}, bf16[16,128,256]{2,1,0:T(8,128)(2,1)S(1)}, u32[]{:S(2)}, u32[]{:S(2)}) %collective-permute-start.17) | collective-permute-done | bytes 1048608 | tf_op jit(solution)/shard_map/feed1_back_core/ppermute | solution.py:431
  78.4 8.9 %feed_last.1 = (f32[1024,512]{1,0:T(8,128)S(1)}, f32[1024,512]{1,0:T(8,128)S(1)}, bf16[8,128,256]{2,1,0:T(8,128)(2,1)S(1)}, bf16[8,128,256]{2,1,0:T(8,128)(2,1)S(1)}, bf16[16,128,256]{2,1,0:T(8,128)(2,1)S(1)}) custom-call(s32[32]{0:T(128)S(1)} %dynamic-slice_bitcast_fusion.dev_ref, bf16[8,128,256]{2,1,0:T(8,128)(2,1)S(1)} %constant_dynamic-update-slice_fusion.g0, ...), custom_call_target="tpu_custom_call" | custom-call | flops 6442450944 | bytes 20971520 | tf_op jit(solution)/shard_map/feed_last/pallas_call | solution.py:581
  89.2 3.4 %feed_finish.1 = (bf16[1024,512]{1,0:T(8,128)(2,1)S(1)}, bf16[1024,512]{1,0:T(8,128)(2,1)S(1)}, bf16[8,64,256]{2,1,0:T(8,128)(2,1)S(1)}, bf16[8,64,256]{2,1,0:T(...) custom-call(s32[32]{0:T(128)S(1)} %dynamic-slice_bitcast_fusion.dev_ref, ...), custom_call_target="tpu_custom_call" | custom-call | flops 1073741824 | bytes 10485760 | tf_op jit(solution)/shard_map/feed_finish/pallas_call | solution.py:613
  92.6 1.6 %collective-permute-done.21 = bf16[4,128,256]{2,1,0:T(8,128)(2,1)S(1)} collective-permute-done((bf16[4,128,256]{2,1,0:T(8,128)(2,1)S(1)}, bf16[4,128,256]{2,1,0:T(8,128)(2,1)S(1)}, u32[]{:S(2)}, u32[]{:S(2)}) %collective-permute-start.21) | collective-permute-done | bytes 262176 | tf_op jit(solution)/shard_map/feed1_back_first/ppermute | solution.py:431
  94.4 1.7 %collective-permute-done.23 = bf16[16,64,256]{2,1,0:T(8,128)(2,1)S(1)} collective-permute-done((bf16[16,64,256]{2,1,0:T(8,128)(2,1)S(1)}, bf16[16,64,256]{2,1,0:T(8,128)(2,1)S(1)}, u32[]{:S(2)}, u32[]{:S(2)}) %collective-permute-start.23) | collective-permute-done | bytes 524320 | tf_op jit(solution)/shard_map/out_back_core/ppermute | solution.py:431
  97.0 10.0 %mixer_backward.1 = (bf16[4,1024,768]{2,1,0:T(8,128)(2,1)S(1)}, bf16[16,208,256]{2,1,0:T(8,128)(2,1)S(1)}, bf16[16,208,256]{2,1,0:T(8,128)(2,1)S(1)}) custom-call(s32[32]{0:T(128)S(1)} %dynamic-slice_bitcast_fusion.dev_ref, bf16[1024,512]{1,0:T(8,128)(2,1)S(1)} %get-tuple-element.216.dmix_ref, bf16[512,1024]{1,0:T(8,128)(2,1)S(1)} %get-tuple-element.217.xnt_ref, ...), custom_call_target="tpu_custom_call" | custom-call | flops 4294967296 | bytes 41943040 | tf_op jit(solution)/shard_map/mixer_backward/pallas_call | solution.py:632
  110.2 2.0 %collective-permute-start.27 = (bf16[128,256]{1,0:T(8,128)(2,1)S(1)}, bf16[128,256]{1,0:T(8,128)(2,1)S(1)}, u32[]{:S(2)}, u32[]{:S(2)}) collective-permute-start(bf16[128,256]{1,0:T(8,128)(2,1)S(1)} %fusion.3), channel_id=1, source_target_pairs={{0,16},{1,17},{2,18},{3,19},{4,20},{5,21},{6,22},{7,23},{8,24},{9,... | collective-permute-start | bytes 196616 | tf_op jit(solution)/shard_map/feed1_back_far/ppermute | solution.py:431
  112.6 3.6 %collective-permute-done.27 = bf16[128,256]{1,0:T(8,128)(2,1)S(1)} collective-permute-done((bf16[128,256]{1,0:T(8,128)(2,1)S(1)}, bf16[128,256]{1,0:T(8,128)(2,1)S(1)}, u32[]{:S(2)}, u32[]{:S(2)}) %collective-permute-start.27) | collective-permute-done | bytes 65568 | tf_op jit(solution)/shard_map/feed1_back_far/ppermute | solution.py:431
  120.2 5.2 %input_gradient.1 = f32[1024,512]{1,0:T(8,128)S(1)} custom-call(bf16[1024,512]{1,0:T(8,128)(2,1)S(1)} %get-tuple-element.294.x_ref, bf16[1024,512]{1,0:T(8,128)(2,1)S(1)} %get-tuple-element.216.dmix_ref, f32[2,512]{1,0:T(2,128)S(1)} %get-tuple-element.160.gain_ref, bf16[4,1024,768]{2,1,0:T(8,128)(2,1)S(1)} %get-tuple-element.240.dk_ref, ...), custom_call_target="tpu_custom_call" | custom-call | flops 3221225472 | bytes 25165824 | tf_op jit(solution)/shard_map/input_gradient/pallas_call | solution.py:647
  125.6 3.9 %collective-permute-done.29 = bf16[8,208,256]{2,1,0:T(8,128)(2,1)S(1)} collective-permute-done((bf16[8,208,256]{2,1,0:T(8,128)(2,1)S(1)}, bf16[8,208,256]{2,1,0:T(8,128)(2,1)S(1)}, u32[]{:S(2)}, u32[]{:S(2)}) %collective-permute-start.29) | collective-permute-done | bytes 852000 | tf_op jit(solution)/shard_map/mixer_back_second/ppermute | solution.py:431
  131.2 2.0 %collective-permute-start.32 = (bf16[192,256]{1,0:T(8,128)(2,1)S(1)}, bf16[192,256]{1,0:T(8,128)(2,1)S(1)}, u32[]{:S(2)}, u32[]{:S(2)}) collective-permute-start(bf16[192,256]{1,0:T(8,128)(2,1)S(1)} %get-tuple-element.248), channel_id=1, source_target_pairs={{0,16},{1,17},{2,18},{3,19},{4,20},{5,21},{6,22},{7,23},{8,24},{9,... | collective-permute-start | bytes 294920 | tf_op jit(solution)/shard_map/feed2_back_far/ppermute | solution.py:431
  133.3 2.5 %copy.26 = f32[8,128,512]{2,1,0:T(8,128)} copy(f32[8,128,512]{2,0,1:T(8,128)S(1)} %bitcast.56) | data formatting | bytes 4194304 | tf_op jit(solution)/shard_map/transpose | solution.py:474
  135.8 2.0 %collective-permute-done.32 = bf16[192,256]{1,0:T(8,128)(2,1)S(1)} collective-permute-done((bf16[192,256]{1,0:T(8,128)(2,1)S(1)}, bf16[192,256]{1,0:T(8,128)(2,1)S(1)}, u32[]{:S(2)}, u32[]{:S(2)}) %collective-permute-start.32) | collective-permute-done | bytes 98336 | tf_op jit(solution)/shard_map/feed2_back_far/ppermute | solution.py:431
  138.2 2.5 %collective-permute-start.35 = (bf16[208,256]{1,0:T(8,128)(2,1)S(1)}, bf16[208,256]{1,0:T(8,128)(2,1)S(1)}, u32[]{:S(2)}, u32[]{:S(2)}) collective-permute-start(bf16[208,256]{1,0:T(8,128)(2,1)S(1)} %get-tuple-element.273), channel_id=1, source_target_pairs={{0,24},{1,25},{2,26},{3,27},{4,28},{5,29},{6,30},{7,31},{8,16},{9,... | collective-permute-start | bytes 319496 | tf_op jit(solution)/shard_map/mixer_back_z/ppermute | solution.py:431
  140.9 1.7 %collective-permute-start.33 = (bf16[208,256]{1,0:T(8,128)(2,1)S(1)}, bf16[208,256]{1,0:T(8,128)(2,1)S(1)}, u32[]{:S(2)}, u32[]{:S(2)}) collective-permute-start(bf16[208,256]{1,0:T(8,128)(2,1)S(1)} %get-tuple-element.275), channel_id=1, source_target_pairs={{0,16},{1,17},{2,18},{3,19},{4,20},{5,21},{6,22},{7,23},{8,24},{9,... | collective-permute-start | bytes 319496 | tf_op jit(solution)/shard_map/mixer_back_z/ppermute | solution.py:431
  146.9 1.8 %collective-permute-done.33.p0 = bf16[208,256]{1,0:T(8,128)(2,1)S(1)} collective-permute-done((bf16[208,256]{1,0:T(8,128)(2,1)S(1)}, bf16[208,256]{1,0:T(8,128)(2,1)S(1)}, u32[]{:S(2)}, u32[]{:S(2)}) %collective-permute-start.33) | collective-permute-done | bytes 106528 | tf_op jit(solution)/shard_map/mixer_back_z/ppermute | solution.py:431
  (100 shorter events, 33.6 us)
Async XLA Ops:
  2.1 10.7 %collective-permute-start.2 = (bf16[208,256]{1,0:T(8,128)(2,1)}, bf16[208,256]{1,0:T(8,128)(2,1)S(1)}, u32[]{:S(2)}, u32[]{:S(2)}) collective-permute-start(bf16[208,256]{1,0:T(8,128)(2,1)} %pack.1), channel_id=1, source_target_pairs={{0,24},{1,25},{2,26},{3,27},{4,28},{5,29},{6,30},{7,31},{8,16},{9,... | collective-permute-start | bytes 319496 | tf_op jit(solution)/shard_map/mixer_z/ppermute | solution.py:431
  7.2 6.6 %collective-permute-start.1 = (bf16[208,256]{1,0:T(8,128)(2,1)}, bf16[208,256]{1,0:T(8,128)(2,1)S(1)}, u32[]{:S(2)}, u32[]{:S(2)}) collective-permute-start(bf16[208,256]{1,0:T(8,128)(2,1)} %pack.1), channel_id=1, source_target_pairs={{0,8},{1,9},{2,10},{3,11},{4,12},{5,13},{6,14},{7,15},{8,0},{9,1},... | collective-permute-start | bytes 319496 | tf_op jit(solution)/shard_map/mixer_z/ppermute | solution.py:431
  7.2 9.2 %collective-permute-start = (bf16[208,256]{1,0:T(8,128)(2,1)}, bf16[208,256]{1,0:T(8,128)(2,1)S(1)}, u32[]{:S(2)}, u32[]{:S(2)}) collective-permute-start(bf16[208,256]{1,0:T(8,128)(2,1)} %pack.1), channel_id=1, source_target_pairs={{0,16},{1,17},{2,18},{3,19},{4,20},{5,21},{6,22},{7,23},{8,24},{9,... | collective-permute-start | bytes 319496 | tf_op jit(solution)/shard_map/mixer_z/ppermute | solution.py:431
  16.4 8.3 %collective-permute-start.3 = (bf16[4,208,256]{2,1,0:T(8,128)(2,1)S(1)}, bf16[4,208,256]{2,1,0:T(8,128)(2,1)S(1)}, u32[]{:S(2)}, u32[]{:S(2)}) collective-permute-start(bf16[4,208,256]{2,1,0:T(8,128)(2,1)S(1)} %pad_maximum_fusion.3), channel_id=1, source_target_pairs={{0,4},{1,3},{2,6},{3,1},{4,0},{5,7},{6,2},{7,5},{8,12},{9,11},{10,... | collective-permute-start | bytes 1277960 | tf_op jit(solution)/shard_map/mixer_first/ppermute | solution.py:431
  18.0 6.7 %collective-permute-start.4 = (bf16[192,256]{1,0:T(8,128)(2,1)S(1)}, bf16[192,256]{1,0:T(8,128)(2,1)S(1)}, u32[]{:S(2)}, u32[]{:S(2)}) collective-permute-start(bf16[192,256]{1,0:T(8,128)(2,1)S(1)} %pad_maximum_fusion.10), channel_id=1, source_target_pairs={{0,16},{1,17},{2,18},{3,19},{4,20},{5,21},{6,22},{7,23},{8,24},{9,... | collective-permute-start | bytes 294920 | tf_op jit(solution)/shard_map/feed1_far/ppermute | solution.py:431
  24.8 12.8 %collective-permute-start.5 = (bf16[8,208,256]{2,1,0:T(8,128)(2,1)S(1)}, bf16[8,208,256]{2,1,0:T(8,128)(2,1)S(1)}, u32[]{:S(2)}, u32[]{:S(2)}) collective-permute-start(bf16[8,208,256]{2,1,0:T(8,128)(2,1)S(1)} %pad_maximum_fusion.g0), channel_id=1, source_target_pairs={{0,2},{1,5},{2,0},{3,7},{4,6},{5,1},{6,4},{7,3},{8,10},{9,13},{10,... | collective-permute-start | bytes 2555912 | tf_op jit(solution)/shard_map/mixer_second/ppermute | solution.py:431
  26.3 7.6 %collective-permute-start.6 = (bf16[2,192,256]{2,1,0:T(8,128)(2,1)S(1)}, bf16[2,192,256]{2,1,0:T(8,128)(2,1)S(1)}, u32[]{:S(2)}, u32[]{:S(2)}) collective-permute-start(bf16[2,192,256]{2,1,0:T(8,128)(2,1)S(1)} %pad_maximum_fusion.7), channel_id=1, source_target_pairs={{0,8},{1,9},{2,10},{3,11},{4,12},{5,13},{6,14},{7,15},{8,0},{9,1},... | collective-permute-start | bytes 589832 | tf_op jit(solution)/shard_map/feed1_near/ppermute | solution.py:431
  26.3 5.5 %collective-permute-start.7 = (bf16[128,256]{1,0:T(8,128)(2,1)S(1)}, bf16[128,256]{1,0:T(8,128)(2,1)S(1)}, u32[]{:S(2)}, u32[]{:S(2)}) collective-permute-start(bf16[128,256]{1,0:T(8,128)(2,1)S(1)} %pad_maximum_fusion.11), channel_id=1, source_target_pairs={{0,16},{1,17},{2,18},{3,19},{4,20},{5,21},{6,22},{7,23},{8,24},{9,... | collective-permute-start | bytes 196616 | tf_op jit(solution)/shard_map/feed2_far/ppermute | solution.py:431
  29.3 9.9 %collective-permute-start.10 = (bf16[8,208,256]{2,1,0:T(8,128)(2,1)S(1)}, bf16[8,208,256]{2,1,0:T(8,128)(2,1)S(1)}, u32[]{:S(2)}, u32[]{:S(2)}) collective-permute-start(bf16[8,208,256]{2,1,0:T(8,128)(2,1)S(1)} %pad_maximum_fusion.g0), channel_id=1, source_target_pairs={{0,1},{1,0},{2,3},{3,2},{4,5},{5,4},{6,7},{7,6},{8,9},{9,8},{10,11... | collective-permute-start | bytes 2555912 | tf_op jit(solution)/shard_map/mixer_core/ppermute | solution.py:431
  37.6 7.9 %collective-permute-start.11 = (bf16[8,208,256]{2,1,0:T(8,128)(2,1)S(1)}, bf16[8,208,256]{2,1,0:T(8,128)(2,1)S(1)}, u32[]{:S(2)}, u32[]{:S(2)}) collective-permute-start(bf16[8,208,256]{2,1,0:T(8,128)(2,1)S(1)} %collective-permute-done.5.g1), channel_id=1, source_target_pairs={{0,1},{1,0},{2,3},{3,2},{4,5},{5,4},{6,7},{7,6},{8,9},{9,8},{10,11... | collective-permute-start | bytes 2555912 | tf_op jit(solution)/shard_map/mixer_core_more/ppermute | solution.py:431
  37.7 7.8 %collective-permute-start.8 = (bf16[4,192,256]{2,1,0:T(8,128)(2,1)S(1)}, bf16[4,192,256]{2,1,0:T(8,128)(2,1)S(1)}, u32[]{:S(2)}, u32[]{:S(2)}) collective-permute-start(bf16[4,192,256]{2,1,0:T(8,128)(2,1)S(1)} %pad_maximum_fusion.5), channel_id=1, source_target_pairs={{0,4},{1,3},{2,6},{3,1},{4,0},{5,7},{6,2},{7,5},{8,12},{9,11},{10,... | collective-permute-start | bytes 1179656 | tf_op jit(solution)/shard_map/feed1_first/ppermute | solution.py:431
  39.2 5.5 %collective-permute-start.9 = (bf16[2,128,256]{2,1,0:T(8,128)(2,1)S(1)}, bf16[2,128,256]{2,1,0:T(8,128)(2,1)S(1)}, u32[]{:S(2)}, u32[]{:S(2)}) collective-permute-start(bf16[2,128,256]{2,1,0:T(8,128)(2,1)S(1)} %pad_maximum_fusion.8), channel_id=1, source_target_pairs={{0,8},{1,9},{2,10},{3,11},{4,12},{5,13},{6,14},{7,15},{8,0},{9,1},... | collective-permute-start | bytes 393224 | tf_op jit(solution)/shard_map/feed2_near/ppermute | solution.py:431
  45.6 12.1 %collective-permute-start.12 = (bf16[8,192,256]{2,1,0:T(8,128)(2,1)S(1)}, bf16[8,192,256]{2,1,0:T(8,128)(2,1)S(1)}, u32[]{:S(2)}, u32[]{:S(2)}) collective-permute-start(bf16[8,192,256]{2,1,0:T(8,128)(2,1)S(1)} %pad_maximum_fusion.1.g0), channel_id=1, source_target_pairs={{0,2},{1,5},{2,0},{3,7},{4,6},{5,1},{6,4},{7,3},{8,10},{9,13},{10,... | collective-permute-start | bytes 2359304 | tf_op jit(solution)/shard_map/feed1_second/ppermute | solution.py:431
  47.1 12.1 %collective-permute-start.14 = (bf16[8,192,256]{2,1,0:T(8,128)(2,1)S(1)}, bf16[8,192,256]{2,1,0:T(8,128)(2,1)S(1)}, u32[]{:S(2)}, u32[]{:S(2)}) collective-permute-start(bf16[8,192,256]{2,1,0:T(8,128)(2,1)S(1)} %pad_maximum_fusion.1.g0), channel_id=1, source_target_pairs={{0,1},{1,0},{2,3},{3,2},{4,5},{5,4},{6,7},{7,6},{8,9},{9,8},{10,11... | collective-permute-start | bytes 2359304 | tf_op jit(solution)/shard_map/feed1_core/ppermute | solution.py:431
  57.7 6.4 %collective-permute-start.13 = (bf16[4,128,256]{2,1,0:T(8,128)(2,1)S(1)}, bf16[4,128,256]{2,1,0:T(8,128)(2,1)S(1)}, u32[]{:S(2)}, u32[]{:S(2)}) collective-permute-start(bf16[4,128,256]{2,1,0:T(8,128)(2,1)S(1)} %pad_maximum_fusion.6), channel_id=1, source_target_pairs={{0,4},{1,3},{2,6},{3,1},{4,0},{5,7},{6,2},{7,5},{8,12},{9,11},{10,... | collective-permute-start | bytes 786440 | tf_op jit(solution)/shard_map/feed2_first/ppermute | solution.py:431
  64.1 10.1 %collective-permute-start.16 = (bf16[8,128,256]{2,1,0:T(8,128)(2,1)S(1)}, bf16[8,128,256]{2,1,0:T(8,128)(2,1)S(1)}, u32[]{:S(2)}, u32[]{:S(2)}) collective-permute-start(bf16[8,128,256]{2,1,0:T(8,128)(2,1)S(1)} %constant_dynamic-update-slice_fusion.g0), channel_id=1, source_target_pairs={{0,2},{1,5},{2,0},{3,7},{4,6},{5,1},{6,4},{7,3},{8,10},{9,13},{10,... | collective-permute-start | bytes 1572872 | tf_op jit(solution)/shard_map/feed2_second/ppermute | solution.py:431
  74.2 3.7 %collective-permute-start.19 = (bf16[8,128,256]{2,1,0:T(8,128)(2,1)S(1)}, bf16[8,128,256]{2,1,0:T(8,128)(2,1)S(1)}, u32[]{:S(2)}, u32[]{:S(2)}) collective-permute-start(bf16[8,128,256]{2,1,0:T(8,128)(2,1)S(1)} %constant_dynamic-update-slice_fusion.g0), channel_id=1, source_target_pairs={{0,1},{1,0},{2,3},{3,2},{4,5},{5,4},{6,7},{7,6},{8,9},{9,8},{10,11... | collective-permute-start | bytes 1572872 | tf_op jit(solution)/shard_map/feed2_core/ppermute | solution.py:431
  77.2 10.0 %collective-permute-start.18 = (bf16[8,128,256]{2,1,0:T(8,128)(2,1)S(1)}, bf16[8,128,256]{2,1,0:T(8,128)(2,1)S(1)}, u32[]{:S(2)}, u32[]{:S(2)}) collective-permute-start(bf16[8,128,256]{2,1,0:T(8,128)(2,1)S(1)} %get-tuple-element.183), channel_id=1, source_target_pairs={{0,2},{1,5},{2,0},{3,7},{4,6},{5,1},{6,4},{7,3},{8,10},{9,13},{10,... | collective-permute-start | bytes 1572872 | tf_op jit(solution)/shard_map/feed1_back_second/ppermute | solution.py:431
  87.3 6.9 %collective-permute-start.22 = (bf16[16,128,256]{2,1,0:T(8,128)(2,1)S(1)}, bf16[16,128,256]{2,1,0:T(8,128)(2,1)S(1)}, u32[]{:S(2)}, u32[]{:S(2)}) collective-permute-start(bf16[16,128,256]{2,1,0:T(8,128)(2,1)S(1)} %get-tuple-element.201), channel_id=1, source_target_pairs={{0,1},{1,0},{2,3},{3,2},{4,5},{5,4},{6,7},{7,6},{8,9},{9,8},{10,11... | collective-permute-start | bytes 3145736 | tf_op jit(solution)/shard_map/feed2_back_core/ppermute | solution.py:431
  87.7 6.4 %collective-permute-start.21 = (bf16[4,128,256]{2,1,0:T(8,128)(2,1)S(1)}, bf16[4,128,256]{2,1,0:T(8,128)(2,1)S(1)}, u32[]{:S(2)}, u32[]{:S(2)}) collective-permute-start(bf16[4,128,256]{2,1,0:T(8,128)(2,1)S(1)} %get-tuple-element.200), channel_id=1, source_target_pairs={{0,4},{1,3},{2,6},{3,1},{4,0},{5,7},{6,2},{7,5},{8,12},{9,11},{10,... | collective-permute-start | bytes 786440 | tf_op jit(solution)/shard_map/feed1_back_first/ppermute | solution.py:431
  96.2 12.1 %collective-permute-start.24 = (bf16[8,192,256]{2,1,0:T(8,128)(2,1)S(1)}, bf16[8,192,256]{2,1,0:T(8,128)(2,1)S(1)}, u32[]{:S(2)}, u32[]{:S(2)}) collective-permute-start(bf16[8,192,256]{2,1,0:T(8,128)(2,1)S(1)} %pad_maximum_fusion.2), channel_id=1, source_target_pairs={{0,2},{1,5},{2,0},{3,7},{4,6},{5,1},{6,4},{7,3},{8,10},{9,13},{10,... | collective-permute-start | bytes 2359304 | tf_op jit(solution)/shard_map/feed2_back_second/ppermute | solution.py:431
  97.0 10.0 %collective-permute-start.25 = (bf16[2,128,256]{2,1,0:T(8,128)(2,1)S(1)}, bf16[2,128,256]{2,1,0:T(8,128)(2,1)S(1)}, u32[]{:S(2)}, u32[]{:S(2)}) collective-permute-start(bf16[2,128,256]{2,1,0:T(8,128)(2,1)S(1)} %get-tuple-element.213), channel_id=1, source_target_pairs={{0,8},{1,9},{2,10},{3,11},{4,12},{5,13},{6,14},{7,15},{8,0},{9,1},... | collective-permute-start | bytes 393224 | tf_op jit(solution)/shard_map/feed1_back_near/ppermute | solution.py:431
  108.3 3.9 %collective-permute-start.28 = (bf16[16,208,256]{2,1,0:T(8,128)(2,1)S(1)}, bf16[16,208,256]{2,1,0:T(8,128)(2,1)S(1)}, u32[]{:S(2)}, u32[]{:S(2)}) collective-permute-start(bf16[16,208,256]{2,1,0:T(8,128)(2,1)S(1)} %get-tuple-element.234), channel_id=1, source_target_pairs={{0,1},{1,0},{2,3},{3,2},{4,5},{5,4},{6,7},{7,6},{8,9},{9,8},{10,11... | collective-permute-start | bytes 5111816 | tf_op jit(solution)/shard_map/mixer_back_core/ppermute | solution.py:431
  108.8 7.8 %collective-permute-start.26 = (bf16[4,192,256]{2,1,0:T(8,128)(2,1)S(1)}, bf16[4,192,256]{2,1,0:T(8,128)(2,1)S(1)}, u32[]{:S(2)}, u32[]{:S(2)}) collective-permute-start(bf16[4,192,256]{2,1,0:T(8,128)(2,1)S(1)} %get-tuple-element.231), channel_id=1, source_target_pairs={{0,4},{1,3},{2,6},{3,1},{4,0},{5,7},{6,2},{7,5},{8,12},{9,11},{10,... | collective-permute-start | bytes 1179656 | tf_op jit(solution)/shard_map/feed2_back_first/ppermute | solution.py:431
  110.2 6.1 %collective-permute-start.27 = (bf16[128,256]{1,0:T(8,128)(2,1)S(1)}, bf16[128,256]{1,0:T(8,128)(2,1)S(1)}, u32[]{:S(2)}, u32[]{:S(2)}) collective-permute-start(bf16[128,256]{1,0:T(8,128)(2,1)S(1)} %fusion.3), channel_id=1, source_target_pairs={{0,16},{1,17},{2,18},{3,19},{4,20},{5,21},{6,22},{7,23},{8,24},{9,... | collective-permute-start | bytes 196616 | tf_op jit(solution)/shard_map/feed1_back_far/ppermute | solution.py:431
  116.7 12.8 %collective-permute-start.29 = (bf16[8,208,256]{2,1,0:T(8,128)(2,1)S(1)}, bf16[8,208,256]{2,1,0:T(8,128)(2,1)S(1)}, u32[]{:S(2)}, u32[]{:S(2)}) collective-permute-start(bf16[8,208,256]{2,1,0:T(8,128)(2,1)S(1)} %get-tuple-element.238), channel_id=1, source_target_pairs={{0,2},{1,5},{2,0},{3,7},{4,6},{5,1},{6,4},{7,3},{8,10},{9,13},{10,... | collective-permute-start | bytes 2555912 | tf_op jit(solution)/shard_map/mixer_back_second/ppermute | solution.py:431
  118.8 6.8 %collective-permute-start.30 = (bf16[2,192,256]{2,1,0:T(8,128)(2,1)S(1)}, bf16[2,192,256]{2,1,0:T(8,128)(2,1)S(1)}, u32[]{:S(2)}, u32[]{:S(2)}) collective-permute-start(bf16[2,192,256]{2,1,0:T(8,128)(2,1)S(1)} %get-tuple-element.239), channel_id=1, source_target_pairs={{0,8},{1,9},{2,10},{3,11},{4,12},{5,13},{6,14},{7,15},{8,0},{9,1},... | collective-permute-start | bytes 589832 | tf_op jit(solution)/shard_map/feed2_back_near/ppermute | solution.py:431
  129.8 8.2 %collective-permute-start.31 = (bf16[4,208,256]{2,1,0:T(8,128)(2,1)S(1)}, bf16[4,208,256]{2,1,0:T(8,128)(2,1)S(1)}, u32[]{:S(2)}, u32[]{:S(2)}) collective-permute-start(bf16[4,208,256]{2,1,0:T(8,128)(2,1)S(1)} %get-tuple-element.247), channel_id=1, source_target_pairs={{0,4},{1,3},{2,6},{3,1},{4,0},{5,7},{6,2},{7,5},{8,12},{9,11},{10,... | collective-permute-start | bytes 1277960 | tf_op jit(solution)/shard_map/mixer_back_first/ppermute | solution.py:431
  131.2 6.6 %collective-permute-start.32 = (bf16[192,256]{1,0:T(8,128)(2,1)S(1)}, bf16[192,256]{1,0:T(8,128)(2,1)S(1)}, u32[]{:S(2)}, u32[]{:S(2)}) collective-permute-start(bf16[192,256]{1,0:T(8,128)(2,1)S(1)} %get-tuple-element.248), channel_id=1, source_target_pairs={{0,16},{1,17},{2,18},{3,19},{4,20},{5,21},{6,22},{7,23},{8,24},{9,... | collective-permute-start | bytes 294920 | tf_op jit(solution)/shard_map/feed2_back_far/ppermute | solution.py:431
  138.2 7.4 %collective-permute-start.35 = (bf16[208,256]{1,0:T(8,128)(2,1)S(1)}, bf16[208,256]{1,0:T(8,128)(2,1)S(1)}, u32[]{:S(2)}, u32[]{:S(2)}) collective-permute-start(bf16[208,256]{1,0:T(8,128)(2,1)S(1)} %get-tuple-element.273), channel_id=1, source_target_pairs={{0,24},{1,25},{2,26},{3,27},{4,28},{5,29},{6,30},{7,31},{8,16},{9,... | collective-permute-start | bytes 319496 | tf_op jit(solution)/shard_map/mixer_back_z/ppermute | solution.py:431
  140.7 6.2 %collective-permute-start.34 = (bf16[208,256]{1,0:T(8,128)(2,1)S(1)}, bf16[208,256]{1,0:T(8,128)(2,1)S(1)}, u32[]{:S(2)}, u32[]{:S(2)}) collective-permute-start(bf16[208,256]{1,0:T(8,128)(2,1)S(1)} %get-tuple-element.274), channel_id=1, source_target_pairs={{0,8},{1,9},{2,10},{3,11},{4,12},{5,13},{6,14},{7,15},{8,0},{9,1},... | collective-permute-start | bytes 319496 | tf_op jit(solution)/shard_map/mixer_back_z/ppermute | solution.py:431
  140.9 7.8 %collective-permute-start.33 = (bf16[208,256]{1,0:T(8,128)(2,1)S(1)}, bf16[208,256]{1,0:T(8,128)(2,1)S(1)}, u32[]{:S(2)}, u32[]{:S(2)}) collective-permute-start(bf16[208,256]{1,0:T(8,128)(2,1)S(1)} %get-tuple-element.275), channel_id=1, source_target_pairs={{0,16},{1,17},{2,18},{3,19},{4,20},{5,21},{6,22},{7,23},{8,24},{9,... | collective-permute-start | bytes 319496 | tf_op jit(solution)/shard_map/mixer_back_z/ppermute | solution.py:431
  (9 other events, 69.3 us)

commit v7 on v6

--- a/solution.py
+++ b/solution.py
@@ -225,17 +225,14 @@
             piece = parts[s // per][s % per, feed + c * 32 : feed + (c + 1) * 32, :]
             wo_ref[aligned(dev_ref[s] * 32, 32), c * LANES : (c + 1) * LANES] = piece
 
-    def rows_in(i, _):
-        at = aligned(i * 256, 256)
+    for i in range(tokens // 256):
+        at = slice(i * 256, (i + 1) * 256)
         y1 = x_ref[at, :].astype(F32) + dot(hb_ref[at, :], wo_ref[...])
         y1_ref[at, :] = y1
         scale = lax.rsqrt(jnp.mean(y1 * y1, axis=-1, keepdims=True) + EPSILON)
         xn = ((y1 * scale) * gain).astype(BF)
         xn_ref[at, :] = xn
         xnt_ref[:, at] = xn.T
-        return 0
-
-    lax.fori_loop(0, tokens // 256, rows_in, 0)
     dyt_ref[...] = dy_ref[...].T
 
 
@@ -500,6 +497,7 @@
         eight1, four2 = jnp.concatenate([four1, got1]), jnp.concatenate([two2, near2])
         mixer, eight1, four2 = after_all((eight, more, core, core_more), eight1, four2)
         more1 = send(eight1, SECOND, "feed1_second")
+        got2 = send(four2, FIRST, "feed2_first")
     else:
         order = np.argsort(np.arange(SLOTS) % 2, kind="stable").astype(np.int32)
         dev = jnp.asarray(order)
@@ -558,9 +556,9 @@
     )(dev, xp, *mixer)
     if fast:
         core1 = send(eight1, CORE, "feed1_core")
-        more1, four2, gains = after_all(more1, four2, gains)
+        more1, got2, gains = after_all(more1, got2, gains)
+        eight2 = jnp.concatenate([four2, got2])
         feed1 = (eight1, more1, core1, send(more1, CORE, "feed1_core_more"))
-        got2 = send(four2, FIRST, "feed2_first")
 
     size = width // 8
 
@@ -590,14 +588,12 @@
         )(dev, *weights, xn2, xn2t, dyp, dyt, *before)
 
     if fast:
-        got2, y1, xn2, xn2t, dyt, wo = after_all(got2, y1, xn2, xn2t, dyt, wo)
-        eight2 = jnp.concatenate([four2, got2])
         more2 = send(eight2, SECOND, "feed2_second")
         core2 = send(eight2, CORE, "feed2_core")
     acc, dxn2, low1, high1, send1 = feed(feed1)
     if fast:
         half, quarter = SLOTS // 4, SLOTS // 8
-        more2, acc, dxn2, low1, high1, send1 = after_all(more2, acc, dxn2, low1, high1, send1)
+        more2, core2, acc, dxn2, low1, high1, send1 = after_all(more2, core2, acc, dxn2, low1, high1, send1)
         feed2 = (eight2, more2, core2, send(more2, CORE, "feed2_core_more"))
         got1 = send(send1, CORE, "feed1_back_core")
         high1, acc, dxn2 = after_all(add(high1, got1[half:]), acc, dxn2)

time: 150 us -> 150 us (level)
  transfers between devices with their start and end apart: 36 -> 36, of which waited for: 25 -> 22; matrix products, arithmetic and copies ran while one was open for 8% -> 8% of each run, Pallas kernels for 33% -> 32%
where the time goes in v7:
time: 150 us; the launch traced here: 149 us
  Pallas kernels  49.6 us (33%)
  waiting for transfers between devices  47.4 us (32%)
  starting transfers between devices  37.7 us (25%)
  local copies, waits for them, and re-layouts  8.93 us (6%)
  other arithmetic  4.54 us (3%)
    ppermute x36, waiting for transfers between devices, send(): return lax.ppermute(value, AXES, pairs)  47.4 us
    ppermute x36, starting transfers between devices, send(): return lax.ppermute(value, AXES, pairs)  37.7 us
    pallas_call x2, Pallas kernels, feed(): pl.pallas_call(feed_half, in_specs=[smem] + [vmem] * (8 + len(before)), o...  17.4 us
    pallas_call x1, Pallas kernels, local(): pl.pallas_call(mixer_backward, grid=(blocks,), in_specs=[smem, whole((row...  10 us
    pallas_call x1, Pallas kernels, local(): pl.pallas_call(mixer_forward, grid=(blocks,), in_specs=[smem, whole((rows...  9.23 us
    pallas_call x1, Pallas kernels, input_grad(): pl.pallas_call(input_gradient, grid=(rows // part,), in_specs=[band(width...  5.24 us
    transpose x2, local copies, waits for them, and re-layouts, restore(): v.reshape(rows // CHUNKS, CHUNKS, width).transpose(1, 0, 2)  3.82 us
    pallas_call x1, Pallas kernels, local(): pl.pallas_call(feed_finish, in_specs=[smem] + [vmem] * 6, out_specs=[vmem...  3.4 us
  transfers between devices with their start and end apart: 36, of which 22 were waited for; matrix products, arithmetic and copies ran while one was open for 8% of the time, Pallas kernels for 32%

profile of v7, /device:TPU:0, one launch (start us, length us, event | category | flops | bytes accessed | tf_op | source)
XLA Modules:
  0.0 149.2 jit_solution(7803435075059475806)
XLA Ops:
  2.1 5.0 %collective-permute-start.2 = (bf16[208,256]{1,0:T(8,128)(2,1)}, bf16[208,256]{1,0:T(8,128)(2,1)S(1)}, u32[]{:S(2)}, u32[]{:S(2)}) collective-permute-start(bf16[208,256]{1,0:T(8,128)(2,1)} %pack.1), channel_id=1, source_target_pairs={{0,24},{1,25},{2,26},{3,27},{4,28},{5,29},{6,30},{7,31},{8,16},{9,... | collective-permute-start | bytes 319496 | tf_op jit(solution)/shard_map/mixer_z/ppermute | solution.py:428
  9.3 2.7 %copy_bitcast_fusion = (bf16[1024,512]{1,0:T(8,128)(2,1)S(1)}, bf16[1024,512]{1,0:T(8,128)(2,1)S(1)}) fusion(bf16[8,128,512]{2,1,0:T(8,128)(2,1)} %bitcast.62, bf16[8,128,512]{2,1,0:T(8,128)(2,1)} %bitcast.63), kind=kLoop, calls=%fused_computation.2 | loop fusion | bytes 4194304 | tf_op jit(solution)/shard_map/reshape | solution.py:468
  13.7 2.6 %collective-permute-done = bf16[208,256]{1,0:T(8,128)(2,1)S(1)} collective-permute-done((bf16[208,256]{1,0:T(8,128)(2,1)}, bf16[208,256]{1,0:T(8,128)(2,1)S(1)}, u32[]{:S(2)}, u32[]{:S(2)}) %collective-permute-start) | collective-permute-done | bytes 106528 | tf_op jit(solution)/shard_map/mixer_z/ppermute | solution.py:428
  16.4 1.6 %collective-permute-start.3 = (bf16[4,208,256]{2,1,0:T(8,128)(2,1)S(1)}, bf16[4,208,256]{2,1,0:T(8,128)(2,1)S(1)}, u32[]{:S(2)}, u32[]{:S(2)}) collective-permute-start(bf16[4,208,256]{2,1,0:T(8,128)(2,1)S(1)} %pad_maximum_fusion.3), channel_id=1, source_target_pairs={{0,4},{1,3},{2,6},{3,1},{4,0},{5,7},{6,2},{7,5},{8,12},{9,11},{10,... | collective-permute-start | bytes 1277960 | tf_op jit(solution)/shard_map/mixer_first/ppermute | solution.py:428
  19.2 5.5 %collective-permute-done.4 = bf16[192,256]{1,0:T(8,128)(2,1)S(1)} collective-permute-done((bf16[192,256]{1,0:T(8,128)(2,1)S(1)}, bf16[192,256]{1,0:T(8,128)(2,1)S(1)}, u32[]{:S(2)}, u32[]{:S(2)}) %collective-permute-start.4) | collective-permute-done | bytes 98336 | tf_op jit(solution)/shard_map/feed1_far/ppermute | solution.py:428
  26.3 3.0 %collective-permute-start.7 = (bf16[128,256]{1,0:T(8,128)(2,1)S(1)}, bf16[128,256]{1,0:T(8,128)(2,1)S(1)}, u32[]{:S(2)}, u32[]{:S(2)}) collective-permute-start(bf16[128,256]{1,0:T(8,128)(2,1)S(1)} %pad_maximum_fusion.11), channel_id=1, source_target_pairs={{0,16},{1,17},{2,18},{3,19},{4,20},{5,21},{6,22},{7,23},{8,24},{9,... | collective-permute-start | bytes 196616 | tf_op jit(solution)/shard_map/feed2_far/ppermute | solution.py:428
  29.3 2.5 %collective-permute-done.7 = bf16[128,256]{1,0:T(8,128)(2,1)S(1)} collective-permute-done((bf16[128,256]{1,0:T(8,128)(2,1)S(1)}, bf16[128,256]{1,0:T(8,128)(2,1)S(1)}, u32[]{:S(2)}, u32[]{:S(2)}) %collective-permute-start.7) | collective-permute-done | bytes 65568 | tf_op jit(solution)/shard_map/feed2_far/ppermute | solution.py:428
  31.8 2.0 %collective-permute-done.6 = bf16[2,192,256]{2,1,0:T(8,128)(2,1)S(1)} collective-permute-done((bf16[2,192,256]{2,1,0:T(8,128)(2,1)S(1)}, bf16[2,192,256]{2,1,0:T(8,128)(2,1)S(1)}, u32[]{:S(2)}, u32[]{:S(2)}) %collective-permute-start.6) | collective-permute-done | bytes 196640 | tf_op jit(solution)/shard_map/feed1_near/ppermute | solution.py:428
  33.9 3.7 %collective-permute-done.5.g1 = bf16[8,208,256]{2,1,0:T(8,128)(2,1)S(1)} collective-permute-done((bf16[8,208,256]{2,1,0:T(8,128)(2,1)S(1)}, bf16[8,208,256]{2,1,0:T(8,128)(2,1)S(1)}, u32[]{:S(2)}, u32[]{:S(2)}) %collective-permute-start.5) | collective-permute-done | bytes 852000 | tf_op jit(solution)/shard_map/mixer_second/ppermute | solution.py:428
  37.7 1.6 %collective-permute-start.8 = (bf16[4,192,256]{2,1,0:T(8,128)(2,1)S(1)}, bf16[4,192,256]{2,1,0:T(8,128)(2,1)S(1)}, u32[]{:S(2)}, u32[]{:S(2)}) collective-permute-start(bf16[4,192,256]{2,1,0:T(8,128)(2,1)S(1)} %pad_maximum_fusion.5), channel_id=1, source_target_pairs={{0,4},{1,3},{2,6},{3,1},{4,0},{5,7},{6,2},{7,5},{8,12},{9,11},{10,... | collective-permute-start | bytes 1179656 | tf_op jit(solution)/shard_map/feed1_first/ppermute | solution.py:428
  39.3 5.5 %collective-permute-done.9 = bf16[2,128,256]{2,1,0:T(8,128)(2,1)S(1)} collective-permute-done((bf16[2,128,256]{2,1,0:T(8,128)(2,1)S(1)}, bf16[2,128,256]{2,1,0:T(8,128)(2,1)S(1)}, u32[]{:S(2)}, u32[]{:S(2)}) %collective-permute-start.9) | collective-permute-done | bytes 131104 | tf_op jit(solution)/shard_map/feed2_near/ppermute | solution.py:428
  48.6 9.2 %mixer_forward.1 = (bf16[1024,1024]{1,0:T(8,128)(2,1)S(1)}, bf16[4,1024,256]{2,1,0:T(8,128)(2,1)S(1)}, bf16[4,1024,256]{2,1,0:T(8,128)(2,1)S(1)}, bf16[4,1024,25...) custom-call(s32[32]{0:T(128)S(1)} %dynamic-slice_bitcast_fusion.dev_r, ...), custom_call_target="tpu_custom_call" | custom-call | flops 3221225472 | bytes 33554432 | tf_op jit(solution)/shard_map/mixer_forward/pallas_call | solution.py:543
  57.9 2.6 %collective-permute-done.12.g1 = bf16[8,192,256]{2,1,0:T(8,128)(2,1)S(1)} collective-permute-done((bf16[8,192,256]{2,1,0:T(8,128)(2,1)S(1)}, bf16[8,192,256]{2,1,0:T(8,128)(2,1)S(1)}, u32[]{:S(2)}, u32[]{:S(2)}) %collective-permute-start.12) | collective-permute-done | bytes 786464 | tf_op jit(solution)/shard_map/feed1_second/ppermute | solution.py:428
  62.8 2.1 %feed_prepare.1 = (f32[1024,512]{1,0:T(8,128)S(1)}, bf16[1024,512]{1,0:T(8,128)(2,1)S(1)}, bf16[512,1024]{1,0:T(8,128)(2,1)S(1)}, bf16[512,1024]{1,0:T(8,128)(2,1)S(1)}, bf16[1024,512]{1,0:T(8,128)(2,1)S(1)}) custom-call(s32[32]{0:T(128)S(1)} %dynamic-slice_bitcast_fusion.dev_ref, f32[2,512]{1,0:T(2,128)S(1)} %get-tuple-element.155.gain_ref, ...), custom_call_target="tpu_custom_call" | custom-call | flops 1073741824 | bytes 10485760 | tf_op jit(solution)/shard_map/feed_prepare/pallas_call | solution.py:568
  64.9 8.6 %feed_first.1 = (f32[1024,512]{1,0:T(8,128)S(1)}, f32[1024,512]{1,0:T(8,128)S(1)}, bf16[8,128,256]{2,1,0:T(8,128)(2,1)S(1)}, bf16[8,128,256]{2,1,0:T(8,128)(2,1)S(1)}, bf16[16,128,256]{2,1,0:T(8,128)(2,1)S(1)}) custom-call(s32[32]{0:T(128)S(1)} %dynamic-slice_bitcast_fusion.dev_ref, bf16[8,192,256]{2,1,0:T(8,128)(2,1)S(1)} %pad_maximum_fusion.1.g0, ...), custom_call_target="tpu_custom_call" | custom-call | flops 6442450944 | bytes 20971520 | tf_op jit(solution)/shard_map/feed_first/pallas_call | solution.py:579
  74.1 2.1 %collective-permute-done.18 = bf16[16,128,256]{2,1,0:T(8,128)(2,1)S(1)} collective-permute-done((bf16[16,128,256]{2,1,0:T(8,128)(2,1)S(1)}, bf16[16,128,256]{2,1,0:T(8,128)(2,1)S(1)}, u32[]{:S(2)}, u32[]{:S(2)}) %collective-permute-start.18) | collective-permute-done | bytes 1048608 | tf_op jit(solution)/shard_map/feed1_back_core/ppermute | solution.py:428
  76.6 1.5 %collective-permute-start.19 = (bf16[8,128,256]{2,1,0:T(8,128)(2,1)S(1)}, bf16[8,128,256]{2,1,0:T(8,128)(2,1)S(1)}, u32[]{:S(2)}, u32[]{:S(2)}) collective-permute-start(bf16[8,128,256]{2,1,0:T(8,128)(2,1)S(1)} %get-tuple-element.172), channel_id=1, source_target_pairs={{0,2},{1,5},{2,0},{3,7},{4,6},{5,1},{6,4},{7,3},{8,10},{9,13},{10,... | collective-permute-start | bytes 1572872 | tf_op jit(solution)/shard_map/feed1_back_second/ppermute | solution.py:428
  78.1 8.9 %feed_last.1 = (f32[1024,512]{1,0:T(8,128)S(1)}, f32[1024,512]{1,0:T(8,128)S(1)}, bf16[8,128,256]{2,1,0:T(8,128)(2,1)S(1)}, bf16[8,128,256]{2,1,0:T(8,128)(2,1)S(1)}, bf16[16,128,256]{2,1,0:T(8,128)(2,1)S(1)}) custom-call(s32[32]{0:T(128)S(1)} %dynamic-slice_bitcast_fusion.dev_ref, bf16[8,128,256]{2,1,0:T(8,128)(2,1)S(1)} %constant_dynamic-update-slice_fusion.g0, ...), custom_call_target="tpu_custom_call" | custom-call | flops 6442450944 | bytes 20971520 | tf_op jit(solution)/shard_map/feed_last/pallas_call | solution.py:579
  87.2 1.6 %collective-permute-start.21 = (bf16[4,128,256]{2,1,0:T(8,128)(2,1)S(1)}, bf16[4,128,256]{2,1,0:T(8,128)(2,1)S(1)}, u32[]{:S(2)}, u32[]{:S(2)}) collective-permute-start(bf16[4,128,256]{2,1,0:T(8,128)(2,1)S(1)} %get-tuple-element.190), channel_id=1, source_target_pairs={{0,4},{1,3},{2,6},{3,1},{4,0},{5,7},{6,2},{7,5},{8,12},{9,11},{10,... | collective-permute-start | bytes 786440 | tf_op jit(solution)/shard_map/feed1_back_first/ppermute | solution.py:428
  88.8 3.4 %feed_finish.1 = (bf16[1024,512]{1,0:T(8,128)(2,1)S(1)}, bf16[1024,512]{1,0:T(8,128)(2,1)S(1)}, bf16[8,64,256]{2,1,0:T(8,128)(2,1)S(1)}, bf16[8,64,256]{2,1,0:T(...) custom-call(s32[32]{0:T(128)S(1)} %dynamic-slice_bitcast_fusion.dev_ref, ...), custom_call_target="tpu_custom_call" | custom-call | flops 1073741824 | bytes 10485760 | tf_op jit(solution)/shard_map/feed_finish/pallas_call | solution.py:609
  93.9 1.7 %collective-permute-done.23 = bf16[16,64,256]{2,1,0:T(8,128)(2,1)S(1)} collective-permute-done((bf16[16,64,256]{2,1,0:T(8,128)(2,1)S(1)}, bf16[16,64,256]{2,1,0:T(8,128)(2,1)S(1)}, u32[]{:S(2)}, u32[]{:S(2)}) %collective-permute-start.23) | collective-permute-done | bytes 524320 | tf_op jit(solution)/shard_map/out_back_core/ppermute | solution.py:428
  97.1 10.0 %mixer_backward.1 = (bf16[4,1024,768]{2,1,0:T(8,128)(2,1)S(1)}, bf16[16,208,256]{2,1,0:T(8,128)(2,1)S(1)}, bf16[16,208,256]{2,1,0:T(8,128)(2,1)S(1)}) custom-call(s32[32]{0:T(128)S(1)} %dynamic-slice_bitcast_fusion.dev_ref, bf16[1024,512]{1,0:T(8,128)(2,1)S(1)} %get-tuple-element.206.dmix_ref, bf16[512,1024]{1,0:T(8,128)(2,1)S(1)} %get-tuple-element.207.xnt_ref, ...), custom_call_target="tpu_custom_call" | custom-call | flops 4294967296 | bytes 41943040 | tf_op jit(solution)/shard_map/mixer_backward/pallas_call | solution.py:628
  108.2 1.6 %collective-permute-start.26 = (bf16[4,192,256]{2,1,0:T(8,128)(2,1)S(1)}, bf16[4,192,256]{2,1,0:T(8,128)(2,1)S(1)}, u32[]{:S(2)}, u32[]{:S(2)}) collective-permute-start(bf16[4,192,256]{2,1,0:T(8,128)(2,1)S(1)} %get-tuple-element.221), channel_id=1, source_target_pairs={{0,4},{1,3},{2,6},{3,1},{4,0},{5,7},{6,2},{7,5},{8,12},{9,11},{10,... | collective-permute-start | bytes 1179656 | tf_op jit(solution)/shard_map/feed2_back_first/ppermute | solution.py:428
  109.7 1.7 %collective-permute-start.27 = (bf16[128,256]{1,0:T(8,128)(2,1)S(1)}, bf16[128,256]{1,0:T(8,128)(2,1)S(1)}, u32[]{:S(2)}, u32[]{:S(2)}) collective-permute-start(bf16[128,256]{1,0:T(8,128)(2,1)S(1)} %fusion.3), channel_id=1, source_target_pairs={{0,16},{1,17},{2,18},{3,19},{4,20},{5,21},{6,22},{7,23},{8,24},{9,... | collective-permute-start | bytes 196616 | tf_op jit(solution)/shard_map/feed1_back_far/ppermute | solution.py:428
  111.9 4.2 %collective-permute-done.27 = bf16[128,256]{1,0:T(8,128)(2,1)S(1)} collective-permute-done((bf16[128,256]{1,0:T(8,128)(2,1)S(1)}, bf16[128,256]{1,0:T(8,128)(2,1)S(1)}, u32[]{:S(2)}, u32[]{:S(2)}) %collective-permute-start.27) | collective-permute-done | bytes 65568 | tf_op jit(solution)/shard_map/feed1_back_far/ppermute | solution.py:428
  119.6 5.2 %input_gradient.1 = f32[1024,512]{1,0:T(8,128)S(1)} custom-call(bf16[1024,512]{1,0:T(8,128)(2,1)S(1)} %get-tuple-element.284.x_ref, bf16[1024,512]{1,0:T(8,128)(2,1)S(1)} %get-tuple-element.206.dmix_ref, f32[2,512]{1,0:T(2,128)S(1)} %get-tuple-element.155.gain_ref, bf16[4,1024,768]{2,1,0:T(8,128)(2,1)S(1)} %get-tuple-element.230.dk_ref, ...), custom_call_target="tpu_custom_call" | custom-call | flops 3221225472 | bytes 25165824 | tf_op jit(solution)/shard_map/input_gradient/pallas_call | solution.py:643
  125.1 3.8 %collective-permute-done.29 = bf16[8,208,256]{2,1,0:T(8,128)(2,1)S(1)} collective-permute-done((bf16[8,208,256]{2,1,0:T(8,128)(2,1)S(1)}, bf16[8,208,256]{2,1,0:T(8,128)(2,1)S(1)}, u32[]{:S(2)}, u32[]{:S(2)}) %collective-permute-start.29) | collective-permute-done | bytes 852000 | tf_op jit(solution)/shard_map/mixer_back_second/ppermute | solution.py:428
  130.8 1.7 %collective-permute-start.32 = (bf16[192,256]{1,0:T(8,128)(2,1)S(1)}, bf16[192,256]{1,0:T(8,128)(2,1)S(1)}, u32[]{:S(2)}, u32[]{:S(2)}) collective-permute-start(bf16[192,256]{1,0:T(8,128)(2,1)S(1)} %get-tuple-element.238), channel_id=1, source_target_pairs={{0,16},{1,17},{2,18},{3,19},{4,20},{5,21},{6,22},{7,23},{8,24},{9,... | collective-permute-start | bytes 294920 | tf_op jit(solution)/shard_map/feed2_back_far/ppermute | solution.py:428
  132.5 2.5 %copy.26 = f32[8,128,512]{2,1,0:T(8,128)} copy(f32[8,128,512]{2,0,1:T(8,128)S(1)} %bitcast.56) | data formatting | bytes 4194304 | tf_op jit(solution)/shard_map/transpose | solution.py:471
  135.1 2.4 %collective-permute-done.32 = bf16[192,256]{1,0:T(8,128)(2,1)S(1)} collective-permute-done((bf16[192,256]{1,0:T(8,128)(2,1)S(1)}, bf16[192,256]{1,0:T(8,128)(2,1)S(1)}, u32[]{:S(2)}, u32[]{:S(2)}) %collective-permute-start.32) | collective-permute-done | bytes 98336 | tf_op jit(solution)/shard_map/feed2_back_far/ppermute | solution.py:428
  137.7 2.5 %collective-permute-start.35 = (bf16[208,256]{1,0:T(8,128)(2,1)S(1)}, bf16[208,256]{1,0:T(8,128)(2,1)S(1)}, u32[]{:S(2)}, u32[]{:S(2)}) collective-permute-start(bf16[208,256]{1,0:T(8,128)(2,1)S(1)} %get-tuple-element.263), channel_id=1, source_target_pairs={{0,24},{1,25},{2,26},{3,27},{4,28},{5,29},{6,30},{7,31},{8,16},{9,... | collective-permute-start | bytes 319496 | tf_op jit(solution)/shard_map/mixer_back_z/ppermute | solution.py:428
  146.0 2.4 %collective-permute-done.33.p0 = bf16[208,256]{1,0:T(8,128)(2,1)S(1)} collective-permute-done((bf16[208,256]{1,0:T(8,128)(2,1)S(1)}, bf16[208,256]{1,0:T(8,128)(2,1)S(1)}, u32[]{:S(2)}, u32[]{:S(2)}) %collective-permute-start.33) | collective-permute-done | bytes 106528 | tf_op jit(solution)/shard_map/mixer_back_z/ppermute | solution.py:428
  (100 shorter events, 32.7 us)
Async XLA Ops:
  2.1 10.7 %collective-permute-start.2 = (bf16[208,256]{1,0:T(8,128)(2,1)}, bf16[208,256]{1,0:T(8,128)(2,1)S(1)}, u32[]{:S(2)}, u32[]{:S(2)}) collective-permute-start(bf16[208,256]{1,0:T(8,128)(2,1)} %pack.1), channel_id=1, source_target_pairs={{0,24},{1,25},{2,26},{3,27},{4,28},{5,29},{6,30},{7,31},{8,16},{9,... | collective-permute-start | bytes 319496 | tf_op jit(solution)/shard_map/mixer_z/ppermute | solution.py:428
  7.2 6.6 %collective-permute-start.1 = (bf16[208,256]{1,0:T(8,128)(2,1)}, bf16[208,256]{1,0:T(8,128)(2,1)S(1)}, u32[]{:S(2)}, u32[]{:S(2)}) collective-permute-start(bf16[208,256]{1,0:T(8,128)(2,1)} %pack.1), channel_id=1, source_target_pairs={{0,8},{1,9},{2,10},{3,11},{4,12},{5,13},{6,14},{7,15},{8,0},{9,1},... | collective-permute-start | bytes 319496 | tf_op jit(solution)/shard_map/mixer_z/ppermute | solution.py:428
  7.2 9.2 %collective-permute-start = (bf16[208,256]{1,0:T(8,128)(2,1)}, bf16[208,256]{1,0:T(8,128)(2,1)S(1)}, u32[]{:S(2)}, u32[]{:S(2)}) collective-permute-start(bf16[208,256]{1,0:T(8,128)(2,1)} %pack.1), channel_id=1, source_target_pairs={{0,16},{1,17},{2,18},{3,19},{4,20},{5,21},{6,22},{7,23},{8,24},{9,... | collective-permute-start | bytes 319496 | tf_op jit(solution)/shard_map/mixer_z/ppermute | solution.py:428
  16.4 8.3 %collective-permute-start.3 = (bf16[4,208,256]{2,1,0:T(8,128)(2,1)S(1)}, bf16[4,208,256]{2,1,0:T(8,128)(2,1)S(1)}, u32[]{:S(2)}, u32[]{:S(2)}) collective-permute-start(bf16[4,208,256]{2,1,0:T(8,128)(2,1)S(1)} %pad_maximum_fusion.3), channel_id=1, source_target_pairs={{0,4},{1,3},{2,6},{3,1},{4,0},{5,7},{6,2},{7,5},{8,12},{9,11},{10,... | collective-permute-start | bytes 1277960 | tf_op jit(solution)/shard_map/mixer_first/ppermute | solution.py:428
  18.0 6.7 %collective-permute-start.4 = (bf16[192,256]{1,0:T(8,128)(2,1)S(1)}, bf16[192,256]{1,0:T(8,128)(2,1)S(1)}, u32[]{:S(2)}, u32[]{:S(2)}) collective-permute-start(bf16[192,256]{1,0:T(8,128)(2,1)S(1)} %pad_maximum_fusion.10), channel_id=1, source_target_pairs={{0,16},{1,17},{2,18},{3,19},{4,20},{5,21},{6,22},{7,23},{8,24},{9,... | collective-permute-start | bytes 294920 | tf_op jit(solution)/shard_map/feed1_far/ppermute | solution.py:428
  24.8 12.8 %collective-permute-start.5 = (bf16[8,208,256]{2,1,0:T(8,128)(2,1)S(1)}, bf16[8,208,256]{2,1,0:T(8,128)(2,1)S(1)}, u32[]{:S(2)}, u32[]{:S(2)}) collective-permute-start(bf16[8,208,256]{2,1,0:T(8,128)(2,1)S(1)} %pad_maximum_fusion.g0), channel_id=1, source_target_pairs={{0,2},{1,5},{2,0},{3,7},{4,6},{5,1},{6,4},{7,3},{8,10},{9,13},{10,... | collective-permute-start | bytes 2555912 | tf_op jit(solution)/shard_map/mixer_second/ppermute | solution.py:428
  26.3 7.6 %collective-permute-start.6 = (bf16[2,192,256]{2,1,0:T(8,128)(2,1)S(1)}, bf16[2,192,256]{2,1,0:T(8,128)(2,1)S(1)}, u32[]{:S(2)}, u32[]{:S(2)}) collective-permute-start(bf16[2,192,256]{2,1,0:T(8,128)(2,1)S(1)} %pad_maximum_fusion.7), channel_id=1, source_target_pairs={{0,8},{1,9},{2,10},{3,11},{4,12},{5,13},{6,14},{7,15},{8,0},{9,1},... | collective-permute-start | bytes 589832 | tf_op jit(solution)/shard_map/feed1_near/ppermute | solution.py:428
  26.3 5.5 %collective-permute-start.7 = (bf16[128,256]{1,0:T(8,128)(2,1)S(1)}, bf16[128,256]{1,0:T(8,128)(2,1)S(1)}, u32[]{:S(2)}, u32[]{:S(2)}) collective-permute-start(bf16[128,256]{1,0:T(8,128)(2,1)S(1)} %pad_maximum_fusion.11), channel_id=1, source_target_pairs={{0,16},{1,17},{2,18},{3,19},{4,20},{5,21},{6,22},{7,23},{8,24},{9,... | collective-permute-start | bytes 196616 | tf_op jit(solution)/shard_map/feed2_far/ppermute | solution.py:428
  29.3 9.9 %collective-permute-start.10 = (bf16[8,208,256]{2,1,0:T(8,128)(2,1)S(1)}, bf16[8,208,256]{2,1,0:T(8,128)(2,1)S(1)}, u32[]{:S(2)}, u32[]{:S(2)}) collective-permute-start(bf16[8,208,256]{2,1,0:T(8,128)(2,1)S(1)} %pad_maximum_fusion.g0), channel_id=1, source_target_pairs={{0,1},{1,0},{2,3},{3,2},{4,5},{5,4},{6,7},{7,6},{8,9},{9,8},{10,11... | collective-permute-start | bytes 2555912 | tf_op jit(solution)/shard_map/mixer_core/ppermute | solution.py:428
  37.6 7.9 %collective-permute-start.11 = (bf16[8,208,256]{2,1,0:T(8,128)(2,1)S(1)}, bf16[8,208,256]{2,1,0:T(8,128)(2,1)S(1)}, u32[]{:S(2)}, u32[]{:S(2)}) collective-permute-start(bf16[8,208,256]{2,1,0:T(8,128)(2,1)S(1)} %collective-permute-done.5.g1), channel_id=1, source_target_pairs={{0,1},{1,0},{2,3},{3,2},{4,5},{5,4},{6,7},{7,6},{8,9},{9,8},{10,11... | collective-permute-start | bytes 2555912 | tf_op jit(solution)/shard_map/mixer_core_more/ppermute | solution.py:428
  37.7 7.8 %collective-permute-start.8 = (bf16[4,192,256]{2,1,0:T(8,128)(2,1)S(1)}, bf16[4,192,256]{2,1,0:T(8,128)(2,1)S(1)}, u32[]{:S(2)}, u32[]{:S(2)}) collective-permute-start(bf16[4,192,256]{2,1,0:T(8,128)(2,1)S(1)} %pad_maximum_fusion.5), channel_id=1, source_target_pairs={{0,4},{1,3},{2,6},{3,1},{4,0},{5,7},{6,2},{7,5},{8,12},{9,11},{10,... | collective-permute-start | bytes 1179656 | tf_op jit(solution)/shard_map/feed1_first/ppermute | solution.py:428
  39.2 5.5 %collective-permute-start.9 = (bf16[2,128,256]{2,1,0:T(8,128)(2,1)S(1)}, bf16[2,128,256]{2,1,0:T(8,128)(2,1)S(1)}, u32[]{:S(2)}, u32[]{:S(2)}) collective-permute-start(bf16[2,128,256]{2,1,0:T(8,128)(2,1)S(1)} %pad_maximum_fusion.8), channel_id=1, source_target_pairs={{0,8},{1,9},{2,10},{3,11},{4,12},{5,13},{6,14},{7,15},{8,0},{9,1},... | collective-permute-start | bytes 393224 | tf_op jit(solution)/shard_map/feed2_near/ppermute | solution.py:428
  45.6 14.9 %collective-permute-start.12 = (bf16[8,192,256]{2,1,0:T(8,128)(2,1)S(1)}, bf16[8,192,256]{2,1,0:T(8,128)(2,1)S(1)}, u32[]{:S(2)}, u32[]{:S(2)}) collective-permute-start(bf16[8,192,256]{2,1,0:T(8,128)(2,1)S(1)} %pad_maximum_fusion.1.g0), channel_id=1, source_target_pairs={{0,2},{1,5},{2,0},{3,7},{4,6},{5,1},{6,4},{7,3},{8,10},{9,13},{10,... | collective-permute-start | bytes 2359304 | tf_op jit(solution)/shard_map/feed1_second/ppermute | solution.py:428
  47.1 15.4 %collective-permute-start.14 = (bf16[8,192,256]{2,1,0:T(8,128)(2,1)S(1)}, bf16[8,192,256]{2,1,0:T(8,128)(2,1)S(1)}, u32[]{:S(2)}, u32[]{:S(2)}) collective-permute-start(bf16[8,192,256]{2,1,0:T(8,128)(2,1)S(1)} %pad_maximum_fusion.1.g0), channel_id=1, source_target_pairs={{0,1},{1,0},{2,3},{3,2},{4,5},{5,4},{6,7},{7,6},{8,9},{9,8},{10,11... | collective-permute-start | bytes 2359304 | tf_op jit(solution)/shard_map/feed1_core/ppermute | solution.py:428
  47.2 10.7 %collective-permute-start.13 = (bf16[4,128,256]{2,1,0:T(8,128)(2,1)S(1)}, bf16[4,128,256]{2,1,0:T(8,128)(2,1)S(1)}, u32[]{:S(2)}, u32[]{:S(2)}) collective-permute-start(bf16[4,128,256]{2,1,0:T(8,128)(2,1)S(1)} %pad_maximum_fusion.6), channel_id=1, source_target_pairs={{0,4},{1,3},{2,6},{3,1},{4,0},{5,7},{6,2},{7,5},{8,12},{9,11},{10,... | collective-permute-start | bytes 786440 | tf_op jit(solution)/shard_map/feed2_first/ppermute | solution.py:428
  60.6 12.9 %collective-permute-start.17 = (bf16[8,128,256]{2,1,0:T(8,128)(2,1)S(1)}, bf16[8,128,256]{2,1,0:T(8,128)(2,1)S(1)}, u32[]{:S(2)}, u32[]{:S(2)}) collective-permute-start(bf16[8,128,256]{2,1,0:T(8,128)(2,1)S(1)} %constant_dynamic-update-slice_fusion.g0), channel_id=1, source_target_pairs={{0,1},{1,0},{2,3},{3,2},{4,5},{5,4},{6,7},{7,6},{8,9},{9,8},{10,11... | collective-permute-start | bytes 1572872 | tf_op jit(solution)/shard_map/feed2_core/ppermute | solution.py:428
  61.1 12.4 %collective-permute-start.16 = (bf16[8,128,256]{2,1,0:T(8,128)(2,1)S(1)}, bf16[8,128,256]{2,1,0:T(8,128)(2,1)S(1)}, u32[]{:S(2)}, u32[]{:S(2)}) collective-permute-start(bf16[8,128,256]{2,1,0:T(8,128)(2,1)S(1)} %constant_dynamic-update-slice_fusion.g0), channel_id=1, source_target_pairs={{0,2},{1,5},{2,0},{3,7},{4,6},{5,1},{6,4},{7,3},{8,10},{9,13},{10,... | collective-permute-start | bytes 1572872 | tf_op jit(solution)/shard_map/feed2_second/ppermute | solution.py:428
  73.7 4.4 %collective-permute-start.20 = (bf16[8,128,256]{2,1,0:T(8,128)(2,1)S(1)}, bf16[8,128,256]{2,1,0:T(8,128)(2,1)S(1)}, u32[]{:S(2)}, u32[]{:S(2)}) collective-permute-start(bf16[8,128,256]{2,1,0:T(8,128)(2,1)S(1)} %collective-permute-done.16.g1), channel_id=1, source_target_pairs={{0,1},{1,0},{2,3},{3,2},{4,5},{5,4},{6,7},{7,6},{8,9},{9,8},{10,11... | collective-permute-start | bytes 1572872 | tf_op jit(solution)/shard_map/feed2_core_more/ppermute | solution.py:428
  76.6 10.4 %collective-permute-start.19 = (bf16[8,128,256]{2,1,0:T(8,128)(2,1)S(1)}, bf16[8,128,256]{2,1,0:T(8,128)(2,1)S(1)}, u32[]{:S(2)}, u32[]{:S(2)}) collective-permute-start(bf16[8,128,256]{2,1,0:T(8,128)(2,1)S(1)} %get-tuple-element.172), channel_id=1, source_target_pairs={{0,2},{1,5},{2,0},{3,7},{4,6},{5,1},{6,4},{7,3},{8,10},{9,13},{10,... | collective-permute-start | bytes 1572872 | tf_op jit(solution)/shard_map/feed1_back_second/ppermute | solution.py:428
  87.0 6.7 %collective-permute-start.22 = (bf16[16,128,256]{2,1,0:T(8,128)(2,1)S(1)}, bf16[16,128,256]{2,1,0:T(8,128)(2,1)S(1)}, u32[]{:S(2)}, u32[]{:S(2)}) collective-permute-start(bf16[16,128,256]{2,1,0:T(8,128)(2,1)S(1)} %get-tuple-element.191), channel_id=1, source_target_pairs={{0,1},{1,0},{2,3},{3,2},{4,5},{5,4},{6,7},{7,6},{8,9},{9,8},{10,11... | collective-permute-start | bytes 3145736 | tf_op jit(solution)/shard_map/feed2_back_core/ppermute | solution.py:428
  87.2 6.4 %collective-permute-start.21 = (bf16[4,128,256]{2,1,0:T(8,128)(2,1)S(1)}, bf16[4,128,256]{2,1,0:T(8,128)(2,1)S(1)}, u32[]{:S(2)}, u32[]{:S(2)}) collective-permute-start(bf16[4,128,256]{2,1,0:T(8,128)(2,1)S(1)} %get-tuple-element.190), channel_id=1, source_target_pairs={{0,4},{1,3},{2,6},{3,1},{4,0},{5,7},{6,2},{7,5},{8,12},{9,11},{10,... | collective-permute-start | bytes 786440 | tf_op jit(solution)/shard_map/feed1_back_first/ppermute | solution.py:428
  95.7 12.1 %collective-permute-start.24 = (bf16[8,192,256]{2,1,0:T(8,128)(2,1)S(1)}, bf16[8,192,256]{2,1,0:T(8,128)(2,1)S(1)}, u32[]{:S(2)}, u32[]{:S(2)}) collective-permute-start(bf16[8,192,256]{2,1,0:T(8,128)(2,1)S(1)} %pad_maximum_fusion.2), channel_id=1, source_target_pairs={{0,2},{1,5},{2,0},{3,7},{4,6},{5,1},{6,4},{7,3},{8,10},{9,13},{10,... | collective-permute-start | bytes 2359304 | tf_op jit(solution)/shard_map/feed2_back_second/ppermute | solution.py:428
  97.1 10.0 %collective-permute-start.25 = (bf16[2,128,256]{2,1,0:T(8,128)(2,1)S(1)}, bf16[2,128,256]{2,1,0:T(8,128)(2,1)S(1)}, u32[]{:S(2)}, u32[]{:S(2)}) collective-permute-start(bf16[2,128,256]{2,1,0:T(8,128)(2,1)S(1)} %get-tuple-element.203), channel_id=1, source_target_pairs={{0,8},{1,9},{2,10},{3,11},{4,12},{5,13},{6,14},{7,15},{8,0},{9,1},... | collective-permute-start | bytes 393224 | tf_op jit(solution)/shard_map/feed1_back_near/ppermute | solution.py:428
  108.2 7.9 %collective-permute-start.26 = (bf16[4,192,256]{2,1,0:T(8,128)(2,1)S(1)}, bf16[4,192,256]{2,1,0:T(8,128)(2,1)S(1)}, u32[]{:S(2)}, u32[]{:S(2)}) collective-permute-start(bf16[4,192,256]{2,1,0:T(8,128)(2,1)S(1)} %get-tuple-element.221), channel_id=1, source_target_pairs={{0,4},{1,3},{2,6},{3,1},{4,0},{5,7},{6,2},{7,5},{8,12},{9,11},{10,... | collective-permute-start | bytes 1179656 | tf_op jit(solution)/shard_map/feed2_back_first/ppermute | solution.py:428
  109.7 6.4 %collective-permute-start.27 = (bf16[128,256]{1,0:T(8,128)(2,1)S(1)}, bf16[128,256]{1,0:T(8,128)(2,1)S(1)}, u32[]{:S(2)}, u32[]{:S(2)}) collective-permute-start(bf16[128,256]{1,0:T(8,128)(2,1)S(1)} %fusion.3), channel_id=1, source_target_pairs={{0,16},{1,17},{2,18},{3,19},{4,20},{5,21},{6,22},{7,23},{8,24},{9,... | collective-permute-start | bytes 196616 | tf_op jit(solution)/shard_map/feed1_back_far/ppermute | solution.py:428
  116.2 12.8 %collective-permute-start.29 = (bf16[8,208,256]{2,1,0:T(8,128)(2,1)S(1)}, bf16[8,208,256]{2,1,0:T(8,128)(2,1)S(1)}, u32[]{:S(2)}, u32[]{:S(2)}) collective-permute-start(bf16[8,208,256]{2,1,0:T(8,128)(2,1)S(1)} %get-tuple-element.228), channel_id=1, source_target_pairs={{0,2},{1,5},{2,0},{3,7},{4,6},{5,1},{6,4},{7,3},{8,10},{9,13},{10,... | collective-permute-start | bytes 2555912 | tf_op jit(solution)/shard_map/mixer_back_second/ppermute | solution.py:428
  118.8 6.3 %collective-permute-start.30 = (bf16[2,192,256]{2,1,0:T(8,128)(2,1)S(1)}, bf16[2,192,256]{2,1,0:T(8,128)(2,1)S(1)}, u32[]{:S(2)}, u32[]{:S(2)}) collective-permute-start(bf16[2,192,256]{2,1,0:T(8,128)(2,1)S(1)} %get-tuple-element.229), channel_id=1, source_target_pairs={{0,8},{1,9},{2,10},{3,11},{4,12},{5,13},{6,14},{7,15},{8,0},{9,1},... | collective-permute-start | bytes 589832 | tf_op jit(solution)/shard_map/feed2_back_near/ppermute | solution.py:428
  129.3 8.2 %collective-permute-start.31 = (bf16[4,208,256]{2,1,0:T(8,128)(2,1)S(1)}, bf16[4,208,256]{2,1,0:T(8,128)(2,1)S(1)}, u32[]{:S(2)}, u32[]{:S(2)}) collective-permute-start(bf16[4,208,256]{2,1,0:T(8,128)(2,1)S(1)} %get-tuple-element.237), channel_id=1, source_target_pairs={{0,4},{1,3},{2,6},{3,1},{4,0},{5,7},{6,2},{7,5},{8,12},{9,11},{10,... | collective-permute-start | bytes 1277960 | tf_op jit(solution)/shard_map/mixer_back_first/ppermute | solution.py:428
  130.8 6.6 %collective-permute-start.32 = (bf16[192,256]{1,0:T(8,128)(2,1)S(1)}, bf16[192,256]{1,0:T(8,128)(2,1)S(1)}, u32[]{:S(2)}, u32[]{:S(2)}) collective-permute-start(bf16[192,256]{1,0:T(8,128)(2,1)S(1)} %get-tuple-element.238), channel_id=1, source_target_pairs={{0,16},{1,17},{2,18},{3,19},{4,20},{5,21},{6,22},{7,23},{8,24},{9,... | collective-permute-start | bytes 294920 | tf_op jit(solution)/shard_map/feed2_back_far/ppermute | solution.py:428
  137.7 7.4 %collective-permute-start.35 = (bf16[208,256]{1,0:T(8,128)(2,1)S(1)}, bf16[208,256]{1,0:T(8,128)(2,1)S(1)}, u32[]{:S(2)}, u32[]{:S(2)}) collective-permute-start(bf16[208,256]{1,0:T(8,128)(2,1)S(1)} %get-tuple-element.263), channel_id=1, source_target_pairs={{0,24},{1,25},{2,26},{3,27},{4,28},{5,29},{6,30},{7,31},{8,16},{9,... | collective-permute-start | bytes 319496 | tf_op jit(solution)/shard_map/mixer_back_z/ppermute | solution.py:428
  140.2 5.8 %collective-permute-start.34 = (bf16[208,256]{1,0:T(8,128)(2,1)S(1)}, bf16[208,256]{1,0:T(8,128)(2,1)S(1)}, u32[]{:S(2)}, u32[]{:S(2)}) collective-permute-start(bf16[208,256]{1,0:T(8,128)(2,1)S(1)} %get-tuple-element.264), channel_id=1, source_target_pairs={{0,8},{1,9},{2,10},{3,11},{4,12},{5,13},{6,14},{7,15},{8,0},{9,1},... | collective-permute-start | bytes 319496 | tf_op jit(solution)/shard_map/mixer_back_z/ppermute | solution.py:428
  140.7 7.7 %collective-permute-start.33 = (bf16[208,256]{1,0:T(8,128)(2,1)S(1)}, bf16[208,256]{1,0:T(8,128)(2,1)S(1)}, u32[]{:S(2)}, u32[]{:S(2)}) collective-permute-start(bf16[208,256]{1,0:T(8,128)(2,1)S(1)} %get-tuple-element.265), channel_id=1, source_target_pairs={{0,16},{1,17},{2,18},{3,19},{4,20},{5,21},{6,22},{7,23},{8,24},{9,... | collective-permute-start | bytes 319496 | tf_op jit(solution)/shard_map/mixer_back_z/ppermute | solution.py:428
  (9 other events, 71.2 us)
